TPU v7x, 32 devices: a whole 2x2x4 slice. The times are simulated.
32 devices in a mesh: dp: 32 (over z, y, x, core).
Axes of the slice: x: 2, y: 2, z: 4, core: 2. Of those that a mesh axis runs over, the one named last changes fastest.
Arguments:
- frames: bfloat16 [160, 1536, 120], P('dp'), may hold values from -6 to 6
- lengths: int32 [160], P('dp'), may hold values from 384 to 1536, as said below
- cotangent: bfloat16 [160, 1536, 120], P('dp'), may hold values from -6 to 6
- master: float32 [339968], P('dp')
- moment_one: float32 [339968], P('dp')
- moment_two: float32 [339968], P('dp'), as said below
- average: float32 [339968], P('dp')
Outputs:
- output: bfloat16 [160, 1536, 120], P('dp')
- input_grad: float32 [160, 1536, 120], P('dp')
- weight_grad: float32 [339968], P('dp')
- new_master: float32 [339968], P('dp')
- new_moment_one: float32 [339968], P('dp')
- new_moment_two: float32 [339968], P('dp')
- new_average: float32 [339968], P('dp')
Inputs may be any that keep to these rules, and one draw needn't show every extreme that they name: `lengths`: each length is a multiple of 3, and some utterance has all 1536 frames. `moment_two`: second moments are positive.
All inputs are finite; a program needn't handle non-finite values.
Results may differ from a plain program's by a relative error of at most 0.012.
The roundings to bfloat16 on the way count: a program that leaves them out, or rounds other values in their place, can miss the bound.
Values may be sent and summed in bfloat16 or wider, within the bound.
No kernel may reach another device: no remote copies, remote signals or barrier semaphores. Data moves between devices by JAX's collectives and lax.ppermute only.
A program may use at most 320 MiB of HBM per device.

v0:
```python
import math

import jax
import jax.numpy as jnp
import numpy as np
from jax import lax
from jax.experimental import pallas as pl
from jax.experimental.pallas import tpu as pltpu
from jax.sharding import PartitionSpec as P

D = 120
HEADS = 4
FF = 480
KERNEL = 15
GROUP = 3
REL = 127
STEP = 5
MAXLEN = 1536
LG = 512
HEAD = 90
HP = 96
GP = HEADS * HP
HALF = KERNEL // 2

EPS_NORM = 1e-05
EPS_ADAM = 1e-08
NEG_FILL = -1000000000.0
LOG2E = math.log2(math.e)
SCALE = HEAD ** (-0.5)

f32 = jnp.float32
bf16 = jnp.bfloat16
VMEM_BYTES = 58 * 2**20

REL_AT = 174240
TAIL_AT = 175260
TAIL = 1456
ROWS_HEAD = 1452
ROWS_TAIL = 1352
TABLE = 2824
F1 = 0
AT = 967
CV = TAIL
F2 = TAIL + 383
FN = TAIL + 1350
LIVE = 337500

C_F1, C_AT, C_CV, C_BN, C_F2, C_FN, C_DWB, C_DW = 0, 2, 4, 6, 8, 10, 12, 13


def dot(a, b):
    return lax.dot_general(a, b, (((1,), (0,)), ((), ())), preferred_element_type=f32)


def dot_nt(a, b):
    return lax.dot_general(a, b, (((1,), (1,)), ((), ())), preferred_element_type=f32)


def dot_tn(a, b):
    return lax.dot_general(a, b, (((0,), (0,)), ((), ())), preferred_element_type=f32)


def lane_iota(shape):
    return lax.broadcasted_iota(jnp.int32, shape, len(shape) - 1)


def row_iota(shape):
    return lax.broadcasted_iota(jnp.int32, shape, 0)


def segments():
    found = []
    for h in range(HEADS):
        for r in range(GROUP):
            lo, hi = max(HEAD * h, D * r), min(HEAD * h + HEAD, D * r + D)
            if lo < hi:
                found.append((HP * h + lo - HEAD * h, r, lo - D * r, hi - lo))
    return found


def pad8(values):
    return jnp.concatenate([values, jnp.zeros((8, values.shape[1]), f32)], axis=0)


def ext(values):
    width = values.shape[1]
    ones = jnp.where(row_iota((8, width)) == 0, 1.0, 0.0).astype(f32)
    return jnp.concatenate([values, ones], axis=0).astype(bf16)


def norm(values):
    mean = jnp.sum(values, axis=0, keepdims=True) * (1.0 / D)
    centre = values - mean
    var = jnp.sum(centre * centre, axis=0, keepdims=True) * (1.0 / D)
    rstd = lax.rsqrt(var + EPS_NORM)
    return centre * rstd, rstd


def norm_back(upstream, xhat, rstd, gain):
    scaled = upstream * gain
    mean_one = jnp.sum(scaled, axis=0, keepdims=True) * (1.0 / D)
    mean_two = jnp.sum(scaled * xhat, axis=0, keepdims=True) * (1.0 / D)
    return rstd * (scaled - mean_one - xhat * mean_two)


def fold(values):
    total = values[:, 0:128]
    for at in range(128, values.shape[1], 128):
        total = total + values[:, at : at + 128]
    return total


def permute_in(values, pm):
    low = pad8(values).astype(bf16)
    stack = jnp.concatenate([low[:, 384 * b : 384 * b + 384] for b in range(4)], axis=0)
    out = dot(stack, pm)
    tiles = [out[128 * b : 128 * b + D, 128 * r : 128 * r + 128] for r in range(3) for b in range(4)]
    return jnp.concatenate(tiles, axis=1)


def stack_out(values):
    low = pad8(values).astype(bf16)
    blocks = []
    for b in range(4):
        blocks.append(
            jnp.concatenate([low[:, 512 * r + 128 * b : 512 * r + 128 * b + 128] for r in range(3)], axis=1)
        )
    return jnp.concatenate(blocks, axis=0)


def unstack_out(out):
    return jnp.concatenate([out[128 * b : 128 * b + D, :] for b in range(4)], axis=1)


def permute_out(values, pm):
    return unstack_out(dot_nt(stack_out(values), pm))


def permute_out_wide(values, pm):
    high = values.astype(bf16).astype(f32)
    rest = values - high
    mid = rest.astype(bf16).astype(f32)
    return unstack_out(dot_nt(stack_out(high), pm) + dot_nt(stack_out(mid), pm))


def plane_mask(r, length):
    return jnp.where(lane_iota((1, LG)) * GROUP + r < length, 1.0, 0.0).astype(f32)


def sigmoid(values):
    return 0.5 + 0.5 * jnp.tanh(0.5 * values)


def plane(r):
    return pl.ds(pl.multiple_of(r * LG, LG), LG)


def plane_rows(r):
    return pl.ds(pl.multiple_of(r * 128, 128), 128)


def planes(body):
    def step(r, carry):
        body(r)
        return carry

    lax.fori_loop(0, GROUP, step, 0)


def shifted_planes(tiles):
    zero = jnp.zeros((8, 128), f32)
    padded = [jnp.concatenate([tile, zero], axis=1) for tile in tiles]
    made = {}

    def get(m):
        r, s = m % GROUP, m // GROUP
        if s == 0:
            return tiles[r]
        if m not in made:
            made[m] = pltpu.roll(padded[r], (-s) % (LG + 128), 1)[:, :LG]
        return made[m]

    return get


def prepare_body(
    g_ref, up1_ref, upp1_ref, dn1_ref, dnp1_ref, up2_ref, upp2_ref, dn2_ref, dnp2_ref, pw_ref, pwp_ref, pr_ref, prp_ref,
    wqkv_ref, wqkvt_ref, wo_ref, wob_ref, cols_ref, tab_ref, pm_ref, flat, tb, wt, big, rows,
):
    parts, part_rows = g_ref.shape[0], g_ref.shape[1]
    for d in range(parts):
        flat[part_rows * d : part_rows * (d + 1), :] = g_ref[d].astype(f32)
    tb[...] = jnp.zeros_like(tb)
    for start, count, base in ((0, ROWS_HEAD, 0), (TAIL_AT, ROWS_TAIL, TAIL)):
        for r in range(16):
            at = start + D * r
            first, col = at // 128, at % 128
            many = (count - r + 15) // 16
            here = flat[pl.ds(first, many, stride=15), :]
            then = flat[pl.ds(first + 1, many, stride=15), :]
            lanes = lane_iota((many, 128))
            got = jnp.where(lanes >= col, here, then)
            if col:
                got = pltpu.roll(got, 128 - col, 1)
            tb[pl.ds(base + r, many, stride=16), :] = jnp.where(lanes < D, got, 0.0)

    def with_row(block, row):
        tail = jnp.where(row_iota((8, 128)) == 0, row, 0.0)
        return jnp.concatenate([block, tail], axis=0)

    for base, up_ref, upp_ref, dn_ref, dnp_ref in (
        (F1, up1_ref, upp1_ref, dn1_ref, dnp1_ref),
        (F2, up2_ref, upp2_ref, dn2_ref, dnp2_ref),
    ):
        parts_t = []
        for q in range(4):
            block = tb[pl.ds(base + 2 + q, D, stride=4), :]
            parts_t.append(with_row(block, tb[base + 482 + q : base + 483 + q, :]).T[:D, :])
        up_t = jnp.concatenate(parts_t, axis=0)
        up_ref[...] = up_t.astype(bf16)
        full = jnp.concatenate([up_t, jnp.zeros((32, 128), f32)], axis=0)
        upp_ref[...] = full.T[:, :FF].astype(bf16)
        down = tb[base + 486 : base + 966, :]
        dnp_ref[...] = down.astype(bf16)
        bias = jnp.where(row_iota((32, 128)) == 0, tb[base + 966 : base + 967, :], 0.0)
        dn_ref[...] = jnp.concatenate([down, bias], axis=0).T.astype(bf16)

    parts_t = []
    for q in range(2):
        block = tb[pl.ds(CV + 2 + q, D, stride=2), :]
        parts_t.append(with_row(block, tb[CV + 242 + q : CV + 243 + q, :]).T[:D, :])
    pw_t = jnp.concatenate(parts_t, axis=0)
    pw_ref[...] = pw_t.astype(bf16)
    pwp_ref[...] = jnp.concatenate([pw_t, jnp.zeros((16, 128), f32)], axis=0).T[:, :240].astype(bf16)
    block = with_row(tb[CV + 262 : CV + 382, :], tb[CV + 382 : CV + 383, :])
    prp_ref[...] = block.astype(bf16)
    pr_ref[...] = block.T.astype(bf16)

    none = jnp.zeros((1, 128), f32)
    for w, at, bias_at in ((0, AT + 2, AT + 122), (1, AT + 123, None), (2, AT + 243, AT + 363)):
        bias = none if bias_at is None else tb[bias_at : bias_at + 1, :]
        wt[...] = with_row(tb[at : at + D, :], bias).T
        big[...] = jnp.zeros_like(big)
        for to, r, src, many in segments():
            big[to : to + many, 128 * r : 128 * r + 128] = wt[src : src + many, :]
        made = big[...]
        wqkv_ref[GP * w : GP * w + GP, :] = made.astype(bf16)
        wqkvt_ref[:, GP * w : GP * w + GP] = made.T.astype(bf16)
    wt[...] = with_row(tb[AT + 364 : AT + 484, :], none)
    big[...] = jnp.zeros_like(big)
    for to, r, src, many in segments():
        big[to : to + many, 128 * r : 128 * r + 128] = wt[src : src + many, :]
    wob_ref[...] = big[...].astype(bf16)
    for r in range(GROUP):
        big[HEAD : HEAD + 1, 128 * r : 128 * r + 128] = tb[AT + 484 : AT + 485, :]
    wo_ref[...] = big[...].T.astype(bf16)

    rows[...] = jnp.zeros_like(rows)
    listed = []
    for base in (F1, AT, CV, CV + 260, F2, FN):
        listed += [base, base + 1]
    listed += [CV + 259] + [CV + 244 + k for k in range(KERNEL)]
    for to, src in enumerate(listed):
        rows[to : to + 1, :] = tb[src : src + 1, :]
    cols_ref[...] = rows[...].T

    rel_rows = []
    lanes = lane_iota((1, 128))
    for h in range(HEADS):
        at = REL_AT + (2 * REL + 1) * h
        first, col = at // 128, at % 128
        pieces = []
        for k in range(2):
            got = jnp.where(lanes >= col, flat[first + k : first + k + 1, :], flat[first + k + 1 : first + k + 2, :])
            pieces.append(pltpu.roll(got, (128 - col) % 128, 1) if col else got)
        rel_rows.append(jnp.concatenate(pieces, axis=1))
    rel = jnp.concatenate(rel_rows + [jnp.zeros((4, 256), f32)], axis=0)
    rel = jnp.where(lane_iota((8, 256)) < 2 * REL + 1, rel, 0.0)
    base = dot(rel.astype(bf16), distance_select()) * LOG2E
    for h in range(HEADS):
        spread = jnp.broadcast_to(base[h : h + 1, :], (LG, 2 * LG))
        tab_ref[h] = pltpu.roll(spread, 0, 1, stride=1, stride_axis=0)[:, :LG]
    t = row_iota((384, 384))
    c = lane_iota((384, 384))
    pm_ref[...] = jnp.where(t == GROUP * (c % 128) + c // 128, 1.0, 0.0).astype(bf16)


def distance_select():
    l = lane_iota((256, 2 * LG))
    gap = jnp.where(l < LG, -l, 2 * LG - l)
    index = jnp.clip(gap, -REL, REL) + REL
    return jnp.where(row_iota((256, 2 * LG)) == index, 1.0, 0.0).astype(bf16)


def diagonal_sum(values):
    wide = jnp.concatenate([values, jnp.zeros((LG, LG), f32)], axis=1)
    half = LG // 2
    while half:
        upper, lower = wide[:half], wide[half : 2 * half]
        if half % 128 == 0:
            lower = jnp.concatenate([lower[:, half:], lower[:, :half]], axis=1)
        else:
            lower = pltpu.roll(lower, 2 * LG - half, 1)
        wide = upper + lower
        half //= 2
    return wide


def prepare(gathered):
    total = gathered.shape[0] * gathered.shape[1]

    def o(shape, kind=bf16):
        return jax.ShapeDtypeStruct(shape, kind)

    ffn = [o((FF, 128)), o((128, FF)), o((128, 512)), o((FF, 128))]
    return pl.pallas_call(
        prepare_body,
        out_shape=ffn
        + ffn
        + [o((240, 128)), o((128, 240)), o((128, 128)), o((128, 128))]
        + [o((3 * GP, GP)), o((GP, 3 * GP)), o((GP, GP)), o((GP, GP))]
        + [o((128, 128), f32), o((HEADS, LG, LG), f32), o((384, 384))],
        scratch_shapes=[
            pltpu.VMEM((total, 128), f32),
            pltpu.VMEM((TABLE, 128), f32),
            pltpu.VMEM((128, 128), f32),
            pltpu.VMEM((GP, GP), f32),
            pltpu.VMEM((128, 128), f32),
        ],
        compiler_params=pltpu.CompilerParams(vmem_limit_bytes=VMEM_BYTES),
        name="prepare",
    )(gathered)


def column(cols, k):
    return cols[:D, k : k + 1]


def valid_keys(length):
    return row_iota((LG, 1)) * GROUP < length


def set_tail(hid):
    hid[FF:, :] = jnp.where(row_iota((512 - FF, hid.shape[1])) == 0, 1.0, 0.0).astype(bf16)


def first_body(
    len_ref, x_ref, cols_ref, up_ref, dn_ref, wqkv_ref, wo_ref, pw_ref, tab_ref, pm_ref,
    xp_ref, one_ref, qkv_ref, att_ref, lse_ref, aa_ref, dep_ref, st_ref,
    hid, nrm, gat, run,
):
    u = pl.program_id(0)
    length = len_ref[u]

    @pl.when(u == 0)
    def _():
        set_tail(hid)
        run[...] = jnp.zeros_like(run)

    xp_ref[0] = permute_in(x_ref[0].astype(f32), pm_ref[...]).astype(bf16)
    cols = cols_ref

    def ffn(r):
        at = plane(r)
        x = xp_ref[0, :, at].astype(f32)
        xhat, _ = norm(x)
        low = ext(xhat * column(cols, C_F1) + column(cols, C_F1 + 1))
        half = 0.5 * dot(up_ref[...], low)
        hid[:FF, :] = (half + half * jnp.tanh(half)).astype(bf16)
        one = x + 0.5 * dot(dn_ref[...], hid[...])[:D]
        one_ref[0, :, at] = one
        xhat, _ = norm(one)
        nrm[plane_rows(r), :] = ext(xhat * column(cols, C_AT) + column(cols, C_AT + 1))

    planes(ffn)
    qkv_ref[0] = dot(wqkv_ref[...], nrm[...]).astype(bf16)
    keys = valid_keys(length)

    def head(h, carry):
        def rows(w):
            return pl.ds(pl.multiple_of(GP * w + HP * h, 32), HP)

        key = qkv_ref[0, rows(1), :]
        value = qkv_ref[0, rows(2), :]
        for part in range(2):
            at = slice(256 * part, 256 * part + 256)
            query = qkv_ref[0, rows(0), at]
            scores = dot_tn(key, query) * (SCALE * LOG2E) + tab_ref[h, :, at]
            scores = jnp.where(keys, scores, NEG_FILL * LOG2E)
            peak = jnp.max(scores, axis=0, keepdims=True)
            power = jnp.exp2(scores - peak)
            total = jnp.sum(power, axis=0, keepdims=True)
            probs = (power * (1.0 / total)).astype(bf16)
            mixed = dot(value, probs)
            mark = (row_iota((HP, 256)) == HEAD) & (h == 0)
            att_ref[0, rows(0), at] = jnp.where(mark, 1.0, mixed).astype(bf16)
            lse_ref[0, pl.ds(h, 1), at] = peak + jnp.log2(total)
        return carry

    lax.fori_loop(0, HEADS, head, 0)
    mixed = dot(wo_ref[...], att_ref[0])
    for r in range(GROUP):
        at = slice(LG * r, LG * r + LG)
        aa_ref[0, :, at] = one_ref[0, :, at] + mixed[128 * r : 128 * r + D]

    def gate(r):
        at = plane(r)
        xhat, _ = norm(aa_ref[0, :, at])
        pre = dot(pw_ref[...], ext(xhat * column(cols, C_CV) + column(cols, C_CV + 1)))
        gat[:, at] = pre[:D] * sigmoid(pre[D:]) * plane_mask(r, length)

    planes(gate)

    def conv(f, carry):
        rows = pl.ds(pl.multiple_of(8 * f, 8), 8)
        get = shifted_planes([gat[rows, LG * r : LG * r + LG] for r in range(GROUP)])
        here = cols[rows, :]
        for r in range(GROUP):
            total = jnp.broadcast_to(here[:, C_DWB : C_DWB + 1], (8, LG))
            for k in range(KERNEL):
                total = total + here[:, C_DW + k : C_DW + k + 1] * get(r + k - HALF)
            dep_ref[0, rows, LG * r : LG * r + LG] = total
        return carry

    lax.fori_loop(0, D // 8, conv, 0)

    count = length.astype(f32)
    mask = jnp.concatenate([plane_mask(r, length) for r in range(GROUP)], axis=1)
    dep = dep_ref[0]
    mean = jnp.sum(dep * mask, axis=1, keepdims=True) / count
    gap = (dep - mean) * mask
    spread = jnp.sum(gap * gap, axis=1, keepdims=True)
    old_mean, old_spread, old_count = run[0], run[1], run[2]
    new_count = old_count + count
    step = mean - old_mean
    new_mean = old_mean + step * (count / new_count)
    new_spread = old_spread + spread + step * step * (old_count * count / new_count)
    run[0] = new_mean
    run[1] = new_spread
    run[2] = new_count
    lanes = lane_iota((D, 128))
    picked = jnp.where(lanes == 0, new_mean, jnp.where(lanes == 1, new_spread, jnp.where(lanes == 2, new_count, 0.0)))
    st_ref[...] = pad8(picked).T[0:8]


def whole(shape):
    zeros = (0,) * len(shape)
    return pl.BlockSpec(shape, lambda u: zeros)


def per_utt(shape):
    zeros = (0,) * len(shape)
    return pl.BlockSpec((1,) + shape, lambda u: (u,) + zeros)


SMEM = pl.BlockSpec(memory_space=pltpu.SMEM)


def first(lengths, x, weights):
    cols, up, dn, wqkv, wo, pw, tab, pm = weights
    utts = x.shape[0]
    per = [
        ((D, MAXLEN), bf16),
        ((D, MAXLEN), f32),
        ((3 * GP, LG), bf16),
        ((GP, LG), bf16),
        ((8, LG), f32),
        ((D, MAXLEN), f32),
        ((D, MAXLEN), f32),
    ]
    return pl.pallas_call(
        first_body,
        grid=(utts,),
        in_specs=[SMEM, per_utt((D, MAXLEN))] + [whole(w.shape) for w in weights],
        out_specs=[per_utt(s) for s, k in per] + [whole((8, 128))],
        out_shape=[jax.ShapeDtypeStruct((utts,) + s, k) for s, k in per] + [jax.ShapeDtypeStruct((8, 128), f32)],
        scratch_shapes=[
            pltpu.VMEM((512, LG), bf16),
            pltpu.VMEM((GP, LG), bf16),
            pltpu.VMEM((D, MAXLEN), f32),
            pltpu.VMEM((3, D, 128), f32),
        ],
        compiler_params=pltpu.CompilerParams(vmem_limit_bytes=VMEM_BYTES),
        name="first",
    )(lengths, x, *weights)


def second_body(
    len_ref, stats_ref, cot_ref, aa_ref, dep_ref, cols_ref, up_ref, upp_ref, dn_ref, dnp_ref, pr_ref, prp_ref, pm_ref,
    out_ref, bgd_ref, gc_ref, sums_ref, stc_ref, gdn_ref, gup_ref, gpr_ref, vec_ref,
    hid, cotp, outp, acc,
):
    u = pl.program_id(0)
    length = len_ref[u]
    cols = cols_ref

    @pl.when(u == 0)
    def _():
        set_tail(hid)
        parts = stats_ref.shape[0]
        count = jnp.zeros((1, 128), f32)
        total = jnp.zeros((1, 128), f32)
        for d in range(parts):
            many = stats_ref[d, 2:3, :]
            count = count + many
            total = total + many * stats_ref[d, 0:1, :]
        here = lane_iota((1, 128)) < D
        count = jnp.where(here, count, 1.0)
        mean = total / count
        spread = jnp.zeros((1, 128), f32)
        for d in range(parts):
            gap = stats_ref[d, 0:1, :] - mean
            spread = spread + stats_ref[d, 1:2, :] + stats_ref[d, 2:3, :] * gap * gap
        scale = lax.rsqrt(spread / count + EPS_NORM)
        at = row_iota((128, 128))
        table = jnp.where(at == 0, mean, jnp.where(at == 1, scale, jnp.where(at == 2, 1.0 / count, 0.0)))
        stc_ref[...] = table.T
        gdn_ref[...] = jnp.zeros_like(gdn_ref)
        gup_ref[...] = jnp.zeros_like(gup_ref)
        gpr_ref[...] = jnp.zeros_like(gpr_ref)
        vec_ref[...] = jnp.zeros_like(vec_ref)
        acc[...] = jnp.zeros_like(acc)

    cotp[...] = permute_in(cot_ref[0].astype(f32), pm_ref[...])

    def tile(r):
        at = plane(r)
        mask = plane_mask(r, length)
        normal = (dep_ref[0, :, at] - stc_ref[:D, 0:1]) * stc_ref[:D, 1:2]
        z = normal * column(cols, C_BN) + column(cols, C_BN + 1)
        z_sig = sigmoid(z)
        act = z * z_sig
        act_low = ext(act)
        after_conv = aa_ref[0, :, at] + dot(pr_ref[...], act_low)[:D]
        xhat, rstd = norm(after_conv)
        low = ext(xhat * column(cols, C_F2) + column(cols, C_F2 + 1))
        pre = dot(up_ref[...], low)
        sig = sigmoid(pre)
        hidden = pre * sig
        hid[:FF, :] = hidden.astype(bf16)
        slope = sig + hidden * (1.0 - sig)
        after_two = after_conv + 0.5 * dot(dn_ref[...], hid[...])[:D]
        xhat_f, rstd_f = norm(after_two)
        outp[:, at] = (xhat_f * column(cols, C_FN) + column(cols, C_FN + 1)) * mask
        up_grad = cotp[:, at] * mask
        vec_ref[2] += fold(up_grad * xhat_f)
        vec_ref[3] += fold(up_grad)
        grad_two = norm_back(up_grad, xhat_f, rstd_f, column(cols, C_FN))
        branch = pad8(0.5 * grad_two).astype(bf16)
        gdn_ref[...] += dot_nt(hid[...], branch)
        pre_low = (slope * dot(dnp_ref[...], branch)).astype(bf16)
        gup_ref[...] += dot_nt(pre_low, low)
        back = dot(upp_ref[...], pre_low)[:D]
        vec_ref[0] += fold(back * xhat)
        vec_ref[1] += fold(back)
        grad_conv = grad_two + norm_back(back, xhat, rstd, column(cols, C_F2))
        gc_ref[0, :, at] = grad_conv
        project = pad8(grad_conv).astype(bf16)
        gpr_ref[...] += dot_nt(act_low, project)
        batch = (z_sig + act * (1.0 - z_sig)) * dot(prp_ref[...], project)[:D]
        bgd_ref[0, :, at] = batch
        acc[0] += fold(batch * normal)
        acc[1] += fold(batch)

    planes(tile)
    out_ref[0] = permute_out(outp[...], pm_ref[...]).astype(bf16)
    lanes = lane_iota((D, 128))
    gain = jnp.sum(acc[0], axis=1, keepdims=True)
    shift = jnp.sum(acc[1], axis=1, keepdims=True)
    sums_ref[...] = pad8(jnp.where(lanes == 0, gain, jnp.where(lanes == 1, shift, 0.0))).T[0:8]


def second(lengths, stats, cot, aa, dep, weights):
    utts = cot.shape[0]
    big = (D, MAXLEN)
    outs = [
        (per_utt(big), (utts,) + big, bf16),
        (per_utt(big), (utts,) + big, f32),
        (per_utt(big), (utts,) + big, f32),
    ]
    for s in ((8, 128), (128, 128), (512, 128), (FF, 128), (128, 128), (4, D, 128)):
        outs.append((whole(s), s, f32))
    return pl.pallas_call(
        second_body,
        grid=(utts,),
        in_specs=[SMEM, whole(stats.shape)] + [per_utt(big)] * 3 + [whole(w.shape) for w in weights],
        out_specs=[o[0] for o in outs],
        out_shape=[jax.ShapeDtypeStruct(o[1], o[2]) for o in outs],
        scratch_shapes=[
            pltpu.VMEM((512, LG), bf16),
            pltpu.VMEM(big, f32),
            pltpu.VMEM(big, f32),
            pltpu.VMEM((2, D, 128), f32),
        ],
        compiler_params=pltpu.CompilerParams(vmem_limit_bytes=VMEM_BYTES),
        name="second",
    )(lengths, stats, cot, aa, dep, *weights)


def third_body(
    len_ref, sums_ref, stc_ref, bgd_ref, gc_ref, xp_ref, one_ref, qkv_ref, att_ref, lse_ref, aa_ref, dep_ref,
    cols_ref, up_ref, upp_ref, dnp_ref, wqkv_t_ref, wob_ref, pw_ref, pwp_ref, tab_ref, pm_ref,
    gin_ref, gdn_ref, gup_ref, gpw_ref, gqkv_ref, go_ref, rel_ref, vec_ref,
    hid, nrm, cn, gat, sig_s, dgs, olg, agr, back_s, ng, relacc, tot,
):
    u = pl.program_id(0)
    length = len_ref[u]
    cols = cols_ref

    @pl.when(u == 0)
    def _():
        set_tail(hid)
        parts = sums_ref.shape[0]
        total = sums_ref[0]
        for d in range(1, parts):
            total = total + sums_ref[d]
        tot[...] = jnp.concatenate([total, jnp.zeros((120, 128), f32)], axis=0).T
        for ref in (gdn_ref, gup_ref, gpw_ref, gqkv_ref, go_ref, vec_ref, relacc):
            ref[...] = jnp.zeros_like(ref)

    def conv_in(r):
        at = plane(r)
        mask = plane_mask(r, length)
        gain = column(cols, C_BN)
        scale = stc_ref[:D, 1:2]
        per = stc_ref[:D, 2:3]
        normal = (dep_ref[0, :, at] - stc_ref[:D, 0:1]) * scale
        shift_part = gain * tot[:D, 1:2] * per * scale
        gain_part = gain * tot[:D, 0:1] * per * scale
        dgs[:, at] = bgd_ref[0, :, at] * (gain * scale) - mask * (shift_part + normal * gain_part)
        xhat, _ = norm(aa_ref[0, :, at])
        low = ext(xhat * column(cols, C_CV) + column(cols, C_CV + 1))
        cn[:, at] = low
        pre = dot(pw_ref[...], low)
        sig = sigmoid(pre[D:])
        sig_s[:, at] = sig
        gat[:, at] = pre[:D] * sig * mask

    planes(conv_in)

    def conv(f, carry):
        rows = pl.ds(pl.multiple_of(8 * f, 8), 8)
        get = shifted_planes([dgs[rows, LG * r : LG * r + LG] for r in range(GROUP)])
        here = cols[rows, :]
        taps = [None] * KERNEL
        bias = None
        made = []
        for r in range(GROUP):
            gated = gat[rows, LG * r : LG * r + LG]
            total = None
            for k in range(KERNEL):
                moved = get(r - k + HALF)
                term = here[:, C_DW + k : C_DW + k + 1] * moved
                total = term if total is None else total + term
                tap = fold(gated * moved)
                taps[k] = tap if taps[k] is None else taps[k] + tap
            part = fold(get(r))
            bias = part if bias is None else bias + part
            made.append(total)
        for r in range(GROUP):
            ng[rows, LG * r : LG * r + LG] = made[r]
        vec_ref[6, rows, :] += bias
        for k in range(KERNEL):
            vec_ref[7 + k, rows, :] += taps[k]
        return carry

    lax.fori_loop(0, D // 8, conv, 0)

    def conv_out(r):
        at = plane(r)
        grad = ng[:, at]
        sig = sig_s[:, at]
        left = grad * plane_mask(r, length) * sig
        right = grad * gat[:, at] * (1.0 - sig)
        pre_low = jnp.concatenate([left, right], axis=0).astype(bf16)
        gpw_ref[...] += dot_nt(pre_low, cn[:, at])
        back = dot(pwp_ref[...], pre_low)[:D]
        xhat, rstd = norm(aa_ref[0, :, at])
        vec_ref[0] += fold(back * xhat)
        vec_ref[1] += fold(back)
        grad_attn = gc_ref[0, :, at] + norm_back(back, xhat, rstd, column(cols, C_CV))
        dgs[:, at] = grad_attn
        olg[plane_rows(r), :] = pad8(grad_attn).astype(bf16)
        xhat, _ = norm(one_ref[0, :, at])
        nrm[plane_rows(r), :] = ext(xhat * column(cols, C_AT) + column(cols, C_AT + 1))

    planes(conv_out)
    go_ref[...] += dot_nt(att_ref[0], olg[...])
    agr[...] = dot(wob_ref[...], olg[...]).astype(bf16)
    keys = valid_keys(length)

    def head(h, carry):
        def rows(w):
            return pl.ds(pl.multiple_of(GP * w + HP * h, 32), HP)

        key = qkv_ref[0, rows(1), :]
        value = qkv_ref[0, rows(2), :]
        key_grad = jnp.zeros((HP, LG), f32)
        value_grad = jnp.zeros((HP, LG), f32)
        for part in range(2):
            at = slice(256 * part, 256 * part + 256)
            query = qkv_ref[0, rows(0), at]
            grad = agr[rows(0), at]
            scores = dot_tn(key, query) * (SCALE * LOG2E) + tab_ref[h, :, at]
            scores = jnp.where(keys, scores, NEG_FILL * LOG2E)
            probs = jnp.exp2(scores - lse_ref[0, pl.ds(h, 1), at])
            prob_grad = dot_tn(value, grad)
            inner = jnp.sum(probs * prob_grad, axis=0, keepdims=True)
            score_low = (probs * (prob_grad - inner)).astype(bf16)
            relacc[h, :, at] += score_low.astype(f32)
            back_s[rows(0), at] = (dot(key, score_low) * SCALE).astype(bf16)
            key_grad = key_grad + dot_nt(query, score_low)
            value_grad = value_grad + dot_nt(grad, probs.astype(bf16))
        back_s[rows(1), :] = (key_grad * SCALE).astype(bf16)
        back_s[rows(2), :] = value_grad.astype(bf16)
        return carry

    lax.fori_loop(0, HEADS, head, 0)
    gqkv_ref[...] += dot_nt(back_s[...], nrm[...])
    normed_grad = dot(wqkv_t_ref[...], back_s[...])
    for r in range(GROUP):
        ng[:, LG * r : LG * r + LG] = normed_grad[128 * r : 128 * r + D]

    def ffn(r):
        at = plane(r)
        back = ng[:, at]
        xhat, rstd = norm(one_ref[0, :, at])
        vec_ref[2] += fold(back * xhat)
        vec_ref[3] += fold(back)
        grad_one = dgs[:, at] + norm_back(back, xhat, rstd, column(cols, C_AT))
        xhat, rstd = norm(xp_ref[0, :, at].astype(f32))
        low = ext(xhat * column(cols, C_F1) + column(cols, C_F1 + 1))
        pre = dot(up_ref[...], low)
        sig = sigmoid(pre)
        hidden = pre * sig
        hid[:FF, :] = hidden.astype(bf16)
        slope = sig + hidden * (1.0 - sig)
        branch = pad8(0.5 * grad_one).astype(bf16)
        gdn_ref[...] += dot_nt(hid[...], branch)
        pre_low = (slope * dot(dnp_ref[...], branch)).astype(bf16)
        gup_ref[...] += dot_nt(pre_low, low)
        back = dot(upp_ref[...], pre_low)[:D]
        vec_ref[4] += fold(back * xhat)
        vec_ref[5] += fold(back)
        sig_s[:, at] = grad_one + norm_back(back, xhat, rstd, column(cols, C_F1))

    planes(ffn)
    gin_ref[0] = permute_out_wide(sig_s[...], pm_ref[...])

    @pl.when(u == pl.num_programs(0) - 1)
    def _():
        found = []
        for h in range(HEADS):
            found.append(diagonal_sum(relacc[h]))
        stacked = jnp.concatenate(found + [jnp.zeros((4, 2 * LG), f32)], axis=0)
        high = stacked.astype(bf16)
        rest = stacked - high.astype(f32)
        mid = rest.astype(bf16)
        rest = rest - mid.astype(f32)
        select = distance_select()
        rel_ref[...] = dot_nt(high, select) + dot_nt(mid, select) + dot_nt(rest.astype(bf16), select)


def third(lengths, sums, stc, bgd, gc, saved, weights):
    utts = bgd.shape[0]
    big = (D, MAXLEN)
    outs = [(per_utt(big), (utts,) + big)]
    for s in ((512, 128), (FF, 128), (240, 128), (3 * GP, GP), (GP, GP), (8, 256), (22, D, 128)):
        outs.append((whole(s), s))
    return pl.pallas_call(
        third_body,
        grid=(utts,),
        in_specs=[SMEM, whole(sums.shape), whole(stc.shape), per_utt(big), per_utt(big)]
        + [per_utt(s.shape[1:]) for s in saved]
        + [whole(w.shape) for w in weights],
        out_specs=[o[0] for o in outs],
        out_shape=[jax.ShapeDtypeStruct(o[1], f32) for o in outs],
        scratch_shapes=[
            pltpu.VMEM((512, LG), bf16),
            pltpu.VMEM((GP, LG), bf16),
            pltpu.VMEM((128, MAXLEN), bf16),
            pltpu.VMEM(big, f32),
            pltpu.VMEM(big, f32),
            pltpu.VMEM(big, f32),
            pltpu.VMEM((GP, LG), bf16),
            pltpu.VMEM((GP, LG), bf16),
            pltpu.VMEM((3 * GP, LG), bf16),
            pltpu.VMEM(big, f32),
            pltpu.VMEM((HEADS, LG, LG), f32),
            pltpu.VMEM((128, 128), f32),
        ],
        compiler_params=pltpu.CompilerParams(vmem_limit_bytes=VMEM_BYTES),
        name="third",
    )(lengths, sums, stc, bgd, gc, *saved, *weights)


def pack_body(
    dn1_ref, up1_ref, dn2_ref, up2_ref, pr_ref, pw_ref, qkv_ref, o_ref, rel_ref, vecs2_ref, vecs3_ref, sums_ref,
    out_ref, tb, flat, wt,
):
    tb[...] = jnp.zeros_like(tb)
    flat[...] = jnp.zeros_like(flat)
    lanes = lane_iota((D, 128))
    table = jnp.zeros((D, 128), f32)
    listed = []
    for ref, at in (
        (vecs2_ref, (F2, F2 + 1, FN, FN + 1)),
        (vecs3_ref, (CV, CV + 1, AT, AT + 1, F1, F1 + 1, CV + 259) + tuple(CV + 244 + k for k in range(KERNEL))),
    ):
        for k, to in enumerate(at):
            table = jnp.where(lanes == len(listed), jnp.sum(ref[k], axis=1, keepdims=True), table)
            listed.append(to)
    wt[...] = pad8(table).T
    keep = lane_iota((1, 128)) < D
    for k, to in enumerate(listed):
        tb[to : to + 1, :] = wt[k : k + 1, :]
    tb[CV + 260 : CV + 262, :] = sums_ref[0:2, :]

    def clean(block):
        return jnp.where(lane_iota(block.shape) < D, block, 0.0)

    for base, dn_ref, up_ref in ((F1, dn1_ref, up1_ref), (F2, dn2_ref, up2_ref)):
        tb[base + 486 : base + 967, :] = clean(dn_ref[0 : FF + 1, :])
        for q in range(4):
            block = pad8(up_ref[D * q : D * q + D, :]).T
            tb[pl.ds(base + 2 + q, D, stride=4), :] = block[:D]
            tb[base + 482 + q : base + 483 + q, :] = block[D : D + 1]
    for q in range(2):
        block = pad8(pw_ref[D * q : D * q + D, :]).T
        tb[pl.ds(CV + 2 + q, D, stride=2), :] = block[:D]
        tb[CV + 242 + q : CV + 243 + q, :] = block[D : D + 1]
    tb[CV + 262 : CV + 383, :] = clean(pr_ref[0 : D + 1, :])

    def gathered(ref, base):
        wt[...] = jnp.zeros_like(wt)
        for to, r, src, many in segments():
            wt[src : src + many, :] += ref[base + to : base + to + many, 128 * r : 128 * r + 128]
        return wt[...]

    for w, at, bias_at in ((0, AT + 2, AT + 122), (1, AT + 123, None), (2, AT + 243, AT + 363)):
        block = gathered(qkv_ref, GP * w).T
        tb[at : at + D, :] = block[:D]
        if bias_at is not None:
            tb[bias_at : bias_at + 1, :] = block[D : D + 1]
    tb[AT + 364 : AT + 484, :] = clean(gathered(o_ref, 0)[:D])
    bias = o_ref[HEAD : HEAD + 1, 0:128] + o_ref[HEAD : HEAD + 1, 128:256] + o_ref[HEAD : HEAD + 1, 256:384]
    tb[AT + 484 : AT + 485, :] = jnp.where(keep, bias, 0.0)

    last = (LIVE - 1) // 128
    for y_first, y_count, offset, base in (
        (0, REL_AT // 128 + 1, 0, 0),
        (TAIL_AT // 128, last - TAIL_AT // 128 + 1, 128 * (TAIL_AT // 128) - TAIL_AT + D, TAIL - 1),
    ):
        for k in range(15):
            at = 128 * k + offset
            first_row, col = at // D, at % D
            many = (y_count - k + 14) // 15
            here = lane_iota((many, 128))
            got = tb[pl.ds(base + first_row, many, stride=16), :]
            if col:
                got = pltpu.roll(got, 128 - col, 1)
            then = pltpu.roll(tb[pl.ds(base + first_row + 1, many, stride=16), :], D - col, 1)
            got = jnp.where(here < D - col, got, then)
            if 2 * D - col < 128:
                then = pltpu.roll(tb[pl.ds(base + first_row + 2, many, stride=16), :], 2 * D - col, 1)
                got = jnp.where(here < 2 * D - col, got, then)
            flat[pl.ds(y_first + k, many, stride=15), :] = got
    here = lane_iota((1, 128))
    width = 2 * REL + 1
    for h in range(HEADS):
        at = REL_AT + width * h
        for y in range(at // 128, (at + width - 1) // 128 + 1):
            lo, hi = max(at - 128 * y, 0), min(at + width - 128 * y, 128)
            shift = (at - 128 * y) % 256
            turned = rel_ref[h : h + 1, :]
            if shift:
                turned = pltpu.roll(turned, shift, 1)
            flat[y : y + 1, :] += jnp.where((here >= lo) & (here < hi), turned[:, :128], 0.0)
    rows = out_ref.shape[1]
    for d in range(out_ref.shape[0]):
        out_ref[d] = flat[rows * d : rows * (d + 1), :]


def pack(parts, rows, grads):
    return pl.pallas_call(
        pack_body,
        out_shape=jax.ShapeDtypeStruct((parts, rows, 128), f32),
        scratch_shapes=[
            pltpu.VMEM((TABLE, 128), f32),
            pltpu.VMEM((parts * rows, 128), f32),
            pltpu.VMEM((128, 128), f32),
        ],
        compiler_params=pltpu.CompilerParams(vmem_limit_bytes=VMEM_BYTES),
        name="pack",
    )(*grads)


def update_tables(total_len):
    rates = np.zeros(total_len, np.float32)
    decays = np.zeros(total_len, np.float32)
    vector, gain, ffn = (D, 0.1, 0.0), (D, 0.3, 0.0), lambda n, fan: (n, fan**-0.5, 0.01)
    block = [gain, vector, ffn(D * FF, D), (FF, 0.1, 0.0), ffn(FF * D, FF), vector]
    square = ffn(D * D, D)
    pieces = block + [gain, vector, square, vector, square, square, vector, ffn(D * D, 6.0 * D / MAXLEN), vector]
    pieces += [(HEADS * (2 * REL + 1), 0.5, 0.0)]
    pieces += [gain, vector, ffn(2 * D * D, D), (2 * D, 0.1, 0.0), ffn(KERNEL * D, KERNEL), vector, gain, vector]
    pieces += [square, vector] + block + [gain, vector]
    offset = 0
    for entries, rate, decay in pieces:
        rates[offset : offset + entries] = rate
        decays[offset : offset + entries] = decay
        offset += entries
    return rates, decays


def everyone(values, devices):
    return lax.all_to_all(jnp.broadcast_to(values[None], (devices,) + values.shape), "dp", 0, 0)


def local(frames, lengths, cotangent, master, moment_one, moment_two, average):
    shard_len = master.shape[0]
    devices = lax.axis_size("dp")
    rows = shard_len // 128
    gathered = everyone(master.astype(bf16).reshape(rows, 128), devices)
    (
        up1, upp1, dn1, dnp1, up2, upp2, dn2, dnp2, pw, pwp, pr, prp, wqkv, wqkvt, wo, wob, cols, tab, pm,
    ) = prepare(gathered)
    x = jnp.transpose(frames, (0, 2, 1))
    cot = jnp.transpose(cotangent, (0, 2, 1))
    xp, one, qkv, att, lse, aa, dep, st = first(lengths, x, (cols, up1, dn1, wqkv, wo, pw, tab, pm))
    stats = everyone(st, devices)
    out, bgd, gc, sums, stc, gdn2, gup2, gpr, vec2 = second(
        lengths, stats, cot, aa, dep, (cols, up2, upp2, dn2, dnp2, pr, prp, pm)
    )
    all_sums = everyone(sums, devices)
    gin, gdn1, gup1, gpw, gqkv, go, rel, vec3 = third(
        lengths, all_sums, stc, bgd, gc, (xp, one, qkv, att, lse, aa, dep),
        (cols, up1, upp1, dnp1, wqkvt, wob, pw, pwp, tab, pm),
    )
    flat = pack(devices, rows, (gdn1, gup1, gdn2, gup2, gpr, gpw, gqkv, go, rel, vec2, vec3, sums))
    reduced = jnp.sum(lax.all_to_all(flat, "dp", 0, 0), axis=0).reshape(shard_len)
    rates_np, decays_np = update_tables(shard_len * devices)
    start_at = lax.axis_index("dp") * shard_len
    rates = lax.dynamic_slice_in_dim(jnp.asarray(rates_np), start_at, shard_len)
    decays = lax.dynamic_slice_in_dim(jnp.asarray(decays_np), start_at, shard_len)
    correction = 1.0 - 0.5**STEP
    new_one = 0.5 * moment_one + 0.5 * reduced
    new_two = 0.5 * moment_two + 0.5 * reduced * reduced
    direction = new_one / correction / (jnp.sqrt(new_two / correction) + EPS_ADAM)
    new_master = master - rates * (direction + decays * master)
    new_average = 0.75 * average + 0.25 * new_master
    return (
        jnp.transpose(out, (0, 2, 1)),
        jnp.transpose(gin, (0, 2, 1)),
        reduced,
        new_master,
        new_one,
        new_two,
        new_average,
    )


def solution(mesh):
    three = P("dp", None, None)
    one = P("dp")
    in_specs = (three, one, three, one, one, one, one)
    out_specs = (three, three, one, one, one, one, one)
    return jax.shard_map(local, mesh=mesh, in_specs=in_specs, out_specs=out_specs, check_vma=False)
```

profile of v0, /device:TPU:0, one launch (start us, length us, event | category | flops | bytes accessed | tf_op | source)
XLA Modules:
  0.0 301.6 jit_solution(5141053847949797802)
XLA Ops:
  0.6 0.8 convert_bitcast_fusion
  1.4 0.1 broadcast_in_dim.9
  1.5 26.4 %all_to_all.20.g_ref = bf16[32,83,128]{2,1,0:T(8,128)(2,1)} all-to-all(bf16[32,83,128]{2,1,0:T(8,128)(2,1)S(1)} %broadcast_in_dim.9), channel_id=1, replica_groups=mesh['dp'=32] {'dp'}, dimensions={0} | all-to-all | bytes 1359872 | tf_op jit(solution)/shard_map/all_to_all | solution.py:917
  28.0 7.1 %prepare.1 = (bf16[480,128]{1,0:T(8,128)(2,1)}, bf16[128,480]{1,0:T(8,128)(2,1)}, bf16[128,512]{1,0:T(8,128)(2,1)}, bf16[480,128]{1,0:T(8,128)(2,1)}, bf16[480,1...) custom-call(bf16[32,83,128]{2,1,0:T(8,128)(2,1)} %all_to_all.20.g_ref), custom_call_target="tpu_custom_call" | custom-call | tf_op jit(solution)/shard_map/prepare/pallas_call | solution.py:316
  35.0 65.5 %first.1 = (bf16[5,120,1536]{2,1,0:T(8,128)(2,1)}, f32[5,120,1536]{2,1,0:T(8,128)}, bf16[5,1152,512]{2,1,0:T(8,128)(2,1)}, bf16[5,384,512]{2,1,0:T(8,128)(2,1)},...) custom-call(s32[5]{0:T(128)} %len_ref.5, ...), custom_call_target="tpu_custom_call" | custom-call | tf_op jit(solution)/shard_map/first/pallas_call | solution.py:471
  100.5 0.7 broadcast_in_dim.10
  101.2 11.8 %all_to_all.21.stats_ref = f32[32,8,128]{2,1,0:T(8,128)} all-to-all(f32[32,8,128]{2,1,0:T(8,128)S(1)} %broadcast_in_dim.10), channel_id=1, replica_groups=mesh['dp'=32] {'dp'}, dimensions={0} | all-to-all | bytes 262144 | tf_op jit(solution)/shard_map/all_to_all | solution.py:917
  113.0 38.2 %second.1 = (bf16[5,120,1536]{2,1,0:T(8,128)(2,1)}, f32[5,120,1536]{2,1,0:T(8,128)}, f32[5,120,1536]{2,1,0:T(8,128)}, f32[8,128]{1,0:T(8,128)}, f32[128,128]{1,0...) custom-call(s32[5]{0:T(128)} %len_ref.5, ...), custom_call_target="tpu_custom_call" | custom-call | tf_op jit(solution)/shard_map/second/pallas_call | solution.py:583
  151.2 0.7 broadcast_in_dim.22
  151.9 10.6 %all_to_all.22.sums_ref = f32[32,8,128]{2,1,0:T(8,128)} all-to-all(f32[32,8,128]{2,1,0:T(8,128)S(1)} %broadcast_in_dim.22), channel_id=1, replica_groups=mesh['dp'=32] {'dp'}, dimensions={0} | all-to-all | bytes 262144 | tf_op jit(solution)/shard_map/all_to_all | solution.py:917
  162.5 93.8 %third.1 = (f32[5,120,1536]{2,1,0:T(8,128)}, f32[512,128]{1,0:T(8,128)}, f32[480,128]{1,0:T(8,128)}, f32[240,128]{1,0:T(8,128)}, f32[1152,384]{1,0:T(8,128)}, /*...) custom-call(s32[5]{0:T(128)} %len_ref.5, f32[32,8,128]{2,1,0:T(8,128)} %all_to_all.22.sums_ref, ...), custom_call_target="tpu_custom_call" | custom-call | tf_op jit(solution)/shard_map/third/pallas_call | solution.py:770
  256.3 5.7 %pack.1 = f32[32,83,128]{2,1,0:T(8,128)} custom-call(f32[512,128]{1,0:T(8,128)} %get-tuple-element.84.dn1_ref, f32[480,128]{1,0:T(8,128)} %get-tuple-element.85.up1_ref, f32[512,128]{1,0:T(8,128)} %get-tuple-element.86.dn2_ref, f32[480,128]{1,0:T(8,128)} %get-tuple-element.87.up2_ref, f32[128,128]{1,0:T(8,128)} %get-tuple-element.88.pr_ref, ...), custom_call_target="tpu_custom_call" | custom-call | tf_op jit(solution)/shard_map/pack/pallas_call | solution.py:885
  261.9 0.0 copy-start.1
  261.9 0.0 copy-start.2
  261.9 0.0 copy-start.3
  261.9 0.0 copy-start.4
  262.0 2.8 all-to-all-start.3
  264.8 35.1 %all-to-all-done.3 = f32[32,83,128]{2,1,0:T(8,128)S(1)} async-done(((f32[32,83,128]{2,1,0:T(8,128)}), f32[32,83,128]{2,1,0:T(8,128)S(1)}, u32[]{:S(2)}, u32[]{:S(2)}) %all-to-all-start.3) | async-done | bytes 1359904 | tf_op jit(solution)/shard_map/all_to_all | solution.py:941
  299.9 0.1 reduce_sum.9
  300.0 0.0 copy-done.1
  300.0 0.0 copy-done.2
  300.0 0.0 copy-done.3
  300.0 0.0 copy-done.4
  300.0 0.0 copy-start
  300.0 1.6 multiply_add_fusion.1
  301.6 0.0 copy-done
Async XLA Ops:
  261.9 38.0 %copy-start.1 = (f32[10624]{0:T(1024)S(1)}, f32[10624]{0:T(1024)}, u32[]{:S(2)}) copy-start(f32[10624]{0:T(1024)} %param.12) | copy-start | bytes 127492
  261.9 38.0 %copy-start.2 = (f32[10624]{0:T(1024)S(1)}, f32[10624]{0:T(1024)}, u32[]{:S(2)}) copy-start(f32[10624]{0:T(1024)} %param.15) | copy-start | bytes 127492
  261.9 38.0 %copy-start.3 = (f32[10624]{0:T(1024)S(1)}, f32[10624]{0:T(1024)}, u32[]{:S(2)}) copy-start(f32[10624]{0:T(1024)} %param.13) | copy-start | bytes 127492
  261.9 38.0 %copy-start.4 = (f32[10624]{0:T(1024)S(1)}, f32[10624]{0:T(1024)}, u32[]{:S(2)}) copy-start(f32[10624]{0:T(1024)} %param.14) | copy-start | bytes 127492
  262.0 37.9 %all-to-all-start.3 = ((f32[32,83,128]{2,1,0:T(8,128)}), f32[32,83,128]{2,1,0:T(8,128)S(1)}, u32[]{:S(2)}, u32[]{:S(2)}) async-start(f32[32,83,128]{2,1,0:T(8,128)} %pack.1), calls=%async_computation.3 | async-start | bytes 2883584 | tf_op jit(solution)/shard_map/all_to_all | solution.py:941
  300.0 1.6 copy-start
where the time goes:
time: 302 us
  Pallas kernels  210 us (70%)
  blocking collectives  48.8 us (16%)
  waiting for transfers between devices  35.1 us (12%)
    pallas_call x1, Pallas kernels, third(): pl.pallas_call(third_body, grid=(utts,), in_specs=[SMEM, whole(sums.shape...  93.8 us
    pallas_call x1, Pallas kernels, first(): pl.pallas_call(first_body, grid=(utts,), in_specs=[SMEM, per_utt((D, MAXL...  65.5 us
    all_to_all x3, blocking collectives, everyone(): lax.all_to_all(jnp.broadcast_to(values[None], (devices,) + values.shape),...  48.8 us
    pallas_call x1, Pallas kernels, second(): pl.pallas_call(second_body, grid=(utts,), in_specs=[SMEM, whole(stats.sha...  38.2 us
    all_to_all x1, waiting for transfers between devices, local(): lax.all_to_all(flat, 'dp', 0, 0)  35.1 us
    pallas_call x1, Pallas kernels, prepare(): pl.pallas_call(prepare_body, out_shape=ffn + ffn + [o((240, 128)), o((128...  7.05 us
  transfers between devices with their start and end apart: 1, of which 1 were waited for; matrix products, arithmetic and copies ran while one was open for 0% of the time, Pallas kernels for 0%

commit v1 on v0

v1 whole, which is shorter than its diff:
```python
import math

import jax
import jax.numpy as jnp
import numpy as np
from jax import lax
from jax.experimental import pallas as pl
from jax.experimental.pallas import tpu as pltpu
from jax.sharding import PartitionSpec as P

D = 120
HEADS = 4
FF = 480
KERNEL = 15
GROUP = 3
REL = 127
STEP = 5
MAXLEN = 1536
LG = 512
HEAD = 90
HP = 96
GP = HEADS * HP
HALF = KERNEL // 2
WIN = (0, 112, 240)
WROWS = 144
MARKS = tuple(HP * r + HEAD - WIN[r] for r in range(GROUP))

EPS_NORM = 1e-05
EPS_ADAM = 1e-08
NEG_FILL = -1000000000.0
LOG2E = math.log2(math.e)
SCALE = HEAD ** (-0.5)

f32 = jnp.float32
bf16 = jnp.bfloat16
VMEM_BYTES = 58 * 2**20

REL_AT = 174240
TAIL_AT = 175260
TAIL = 1456
ROWS_HEAD = 1452
ROWS_TAIL = 1352
TABLE = 2824
F1 = 0
AT = 967
CV = TAIL
F2 = TAIL + 383
FN = TAIL + 1350
LIVE = 337500

C_F1, C_AT, C_CV, C_BN, C_F2, C_FN, C_DWB, C_DW = 0, 2, 4, 6, 8, 10, 12, 13


def dot(a, b):
    return lax.dot_general(a, b, (((1,), (0,)), ((), ())), preferred_element_type=f32)


def dot_nt(a, b):
    return lax.dot_general(a, b, (((1,), (1,)), ((), ())), preferred_element_type=f32)


def dot_tn(a, b):
    return lax.dot_general(a, b, (((0,), (0,)), ((), ())), preferred_element_type=f32)


def lane_iota(shape):
    return lax.broadcasted_iota(jnp.int32, shape, len(shape) - 1)


def row_iota(shape):
    return lax.broadcasted_iota(jnp.int32, shape, 0)


def segments():
    found = []
    for h in range(HEADS):
        for r in range(GROUP):
            lo, hi = max(HEAD * h, D * r), min(HEAD * h + HEAD, D * r + D)
            if lo < hi:
                found.append((HP * h + lo - HEAD * h, r, lo - D * r, hi - lo))
    return found


def pad8(values):
    return jnp.concatenate([values, jnp.zeros((8, values.shape[1]), f32)], axis=0)


def ext(values):
    width = values.shape[1]
    ones = jnp.where(row_iota((8, width)) == 0, 1.0, 0.0).astype(f32)
    return jnp.concatenate([values, ones], axis=0).astype(bf16)


def norm(values):
    mean = jnp.sum(values, axis=0, keepdims=True) * (1.0 / D)
    centre = values - mean
    var = jnp.sum(centre * centre, axis=0, keepdims=True) * (1.0 / D)
    rstd = lax.rsqrt(var + EPS_NORM)
    return centre * rstd, rstd


def norm_back(upstream, xhat, rstd, gain):
    scaled = upstream * gain
    mean_one = jnp.sum(scaled, axis=0, keepdims=True) * (1.0 / D)
    mean_two = jnp.sum(scaled * xhat, axis=0, keepdims=True) * (1.0 / D)
    return rstd * (scaled - mean_one - xhat * mean_two)


def fold(values):
    total = values[:, 0:128]
    for at in range(128, values.shape[1], 128):
        total = total + values[:, at : at + 128]
    return total


def permute_in(values, pm):
    low = pad8(values).astype(bf16)
    stack = jnp.concatenate([low[:, 384 * b : 384 * b + 384] for b in range(4)], axis=0)
    out = dot(stack, pm)
    tiles = [out[128 * b : 128 * b + D, 128 * r : 128 * r + 128] for r in range(3) for b in range(4)]
    return jnp.concatenate(tiles, axis=1)


def stack_out(values):
    low = pad8(values).astype(bf16)
    blocks = []
    for b in range(4):
        blocks.append(
            jnp.concatenate([low[:, 512 * r + 128 * b : 512 * r + 128 * b + 128] for r in range(3)], axis=1)
        )
    return jnp.concatenate(blocks, axis=0)


def unstack_out(out):
    return jnp.concatenate([out[128 * b : 128 * b + D, :] for b in range(4)], axis=1)


def permute_out(values, pm):
    return unstack_out(dot_nt(stack_out(values), pm))


def permute_out_wide(values, pm):
    high = values.astype(bf16).astype(f32)
    rest = values - high
    mid = rest.astype(bf16).astype(f32)
    return unstack_out(dot_nt(stack_out(high), pm) + dot_nt(stack_out(mid), pm))


def plane_mask(r, length):
    return jnp.where(lane_iota((1, LG)) * GROUP + r < length, 1.0, 0.0).astype(f32)


def span(r):
    return slice(LG * r, LG * r + LG)


def skewed(count, stages):
    held = [None] * count
    for step in range(count + len(stages) - 1):
        for k, stage in enumerate(stages):
            n = step - k
            if 0 <= n < count:
                held[n] = stage(n, held[n])


def window(ref, r, base=0):
    return ref[base + WIN[r] : base + WIN[r] + WROWS, :]


def join_windows(parts):
    a, b, c = parts
    return jnp.concatenate([a[:112], a[112:128] + b[:16], b[16:128], b[128:144] + c[:16], c[16:]], axis=0)


def shifted_planes(tiles):
    lanes = lane_iota((8, 128))
    zero = jnp.zeros((8, 128), f32)
    made = {}
    for m in range(-HALF, HALF + GROUP):
        r, s = m % GROUP, m // GROUP
        if s == 0:
            made[m] = tiles[r]
            continue
        turned = [pltpu.roll(tiles[r][:, 128 * k : 128 * k + 128], (-s) % 128, 1) for k in range(4)]
        if s > 0:
            pairs = zip(turned, turned[1:] + [zero])
            parts = [jnp.where(lanes < 128 - s, a, b) for a, b in pairs]
        else:
            pairs = zip([zero] + turned[:-1], turned)
            parts = [jnp.where(lanes < -s, a, b) for a, b in pairs]
        made[m] = jnp.concatenate(parts, axis=1)
    return made


def prepare_body(
    me_ref, g_ref, up1_ref, upp1_ref, dn1_ref, dnp1_ref, up2_ref, upp2_ref, dn2_ref, dnp2_ref, pw_ref, pwp_ref, pr_ref, prp_ref,
    wqkv_ref, wqkvt_ref, wo_ref, wob_ref, cols_ref, tab_ref, pm_ref, flat, tb, wt, wins, rows,
):
    parts, part_rows = g_ref.shape[0], g_ref.shape[1]
    for d in range(parts):
        flat[part_rows * d : part_rows * (d + 1), :] = g_ref[place(me_ref[0] ^ d, parts)].astype(f32)
    tb[...] = jnp.zeros_like(tb)
    for start, count, base in ((0, ROWS_HEAD, 0), (TAIL_AT, ROWS_TAIL, TAIL)):
        for r in range(16):
            at = start + D * r
            first, col = at // 128, at % 128
            many = (count - r + 15) // 16
            here = flat[pl.ds(first, many, stride=15), :]
            then = flat[pl.ds(first + 1, many, stride=15), :]
            lanes = lane_iota((many, 128))
            got = jnp.where(lanes >= col, here, then)
            if col:
                got = pltpu.roll(got, 128 - col, 1)
            tb[pl.ds(base + r, many, stride=16), :] = jnp.where(lanes < D, got, 0.0)

    def with_row(block, row):
        tail = jnp.where(row_iota((8, 128)) == 0, row, 0.0)
        return jnp.concatenate([block, tail], axis=0)

    for base, up_ref, upp_ref, dn_ref, dnp_ref in (
        (F1, up1_ref, upp1_ref, dn1_ref, dnp1_ref),
        (F2, up2_ref, upp2_ref, dn2_ref, dnp2_ref),
    ):
        parts_t = []
        for q in range(4):
            block = tb[pl.ds(base + 2 + q, D, stride=4), :]
            parts_t.append(with_row(block, tb[base + 482 + q : base + 483 + q, :]).T[:D, :])
        up_t = jnp.concatenate(parts_t, axis=0)
        up_ref[...] = (0.5 * up_t).astype(bf16)
        full = jnp.concatenate([up_t, jnp.zeros((32, 128), f32)], axis=0)
        upp_ref[...] = full.T[:, :FF].astype(bf16)
        down = tb[base + 486 : base + 966, :]
        dnp_ref[...] = (0.25 * down).astype(bf16)
        bias = jnp.where(row_iota((32, 128)) == 0, tb[base + 966 : base + 967, :], 0.0)
        dn_ref[...] = (0.5 * jnp.concatenate([down, bias], axis=0)).T.astype(bf16)

    parts_t = []
    for q in range(2):
        block = tb[pl.ds(CV + 2 + q, D, stride=2), :]
        parts_t.append(with_row(block, tb[CV + 242 + q : CV + 243 + q, :]).T[:D, :])
    pw_t = jnp.concatenate(parts_t, axis=0)
    pw_ref[...] = (0.5 * pw_t).astype(bf16)
    pwp_ref[...] = jnp.concatenate([pw_t, jnp.zeros((16, 128), f32)], axis=0).T[:, :240].astype(bf16)
    block = with_row(tb[CV + 262 : CV + 382, :], tb[CV + 382 : CV + 383, :])
    prp_ref[...] = (0.5 * block).astype(bf16)
    pr_ref[...] = block.T.astype(bf16)

    none = jnp.zeros((1, 128), f32)
    wins[...] = jnp.zeros_like(wins)
    for w, at, bias_at in ((0, AT + 2, AT + 122), (1, AT + 123, None), (2, AT + 243, AT + 363)):
        bias = none if bias_at is None else tb[bias_at : bias_at + 1, :]
        wt[...] = with_row(tb[at : at + D, :], bias).T
        for to, r, src, many in segments():
            start = WROWS * w + to - WIN[r]
            wins[r, start : start + many, :] = wt[src : src + many, :]
    for r in range(GROUP):
        made = wins[r]
        wqkv_ref[r] = made[: 3 * WROWS].astype(bf16)
        wqkvt_ref[r] = made.T[:, : 3 * WROWS].astype(bf16)
    wt[...] = with_row(tb[AT + 364 : AT + 484, :], none)
    wins[:, 0:256, :] = jnp.zeros((GROUP, 256, 128), f32)
    for to, r, src, many in segments():
        start = to - WIN[r]
        wins[r, start : start + many, :] = wt[src : src + many, :]
    for r in range(GROUP):
        wob_ref[r] = wins[r, 0:WROWS, :].astype(bf16)
        wins[r, MARKS[r] : MARKS[r] + 1, :] = tb[AT + 484 : AT + 485, :]
        wo_ref[r] = wins[r, 0:256, :].T[:, :WROWS].astype(bf16)

    rows[...] = jnp.zeros_like(rows)
    listed = []
    for base in (F1, AT, CV, CV + 260, F2, FN):
        listed += [base, base + 1]
    listed += [CV + 259] + [CV + 244 + k for k in range(KERNEL)]
    for to, src in enumerate(listed):
        rows[to : to + 1, :] = tb[src : src + 1, :]
    cols_ref[...] = rows[...].T

    rel_rows = []
    lanes = lane_iota((1, 128))
    for h in range(HEADS):
        at = REL_AT + (2 * REL + 1) * h
        first, col = at // 128, at % 128
        pieces = []
        for k in range(2):
            got = jnp.where(lanes >= col, flat[first + k : first + k + 1, :], flat[first + k + 1 : first + k + 2, :])
            pieces.append(pltpu.roll(got, (128 - col) % 128, 1) if col else got)
        rel_rows.append(jnp.concatenate(pieces, axis=1))
    rel = jnp.concatenate(rel_rows + [jnp.zeros((4, 256), f32)], axis=0)
    rel = jnp.where(lane_iota((8, 256)) < 2 * REL + 1, rel, 0.0)
    base = dot(rel.astype(bf16), distance_select()) * LOG2E
    for h in range(HEADS):
        spread = jnp.broadcast_to(base[h : h + 1, :], (LG, 2 * LG))
        tab_ref[h] = pltpu.roll(spread, 0, 1, stride=1, stride_axis=0)[:, :LG]
    t = row_iota((384, 384))
    c = lane_iota((384, 384))
    pm_ref[...] = jnp.where(t == GROUP * (c % 128) + c // 128, 1.0, 0.0).astype(bf16)


def distance_select():
    l = lane_iota((256, 2 * LG))
    gap = jnp.where(l < LG, -l, 2 * LG - l)
    index = jnp.clip(gap, -REL, REL) + REL
    return jnp.where(row_iota((256, 2 * LG)) == index, 1.0, 0.0).astype(bf16)


def diagonal_sum(values):
    wide = jnp.concatenate([values, jnp.zeros((LG, LG), f32)], axis=1)
    half = LG // 2
    while half:
        upper, lower = wide[:half], wide[half : 2 * half]
        if half % 128 == 0:
            lower = jnp.concatenate([lower[:, half:], lower[:, :half]], axis=1)
        else:
            lower = pltpu.roll(lower, 2 * LG - half, 1)
        wide = upper + lower
        half //= 2
    return wide


SMEM = pl.BlockSpec(memory_space=pltpu.SMEM)


def prepare(me, gathered):
    total = gathered.shape[0] * gathered.shape[1]

    def o(shape, kind=bf16):
        return jax.ShapeDtypeStruct(shape, kind)

    ffn = [o((FF, 128)), o((128, FF)), o((128, 512)), o((FF, 128))]
    return pl.pallas_call(
        prepare_body,
        in_specs=[SMEM, pl.BlockSpec(memory_space=pltpu.VMEM)],
        out_shape=ffn
        + ffn
        + [o((240, 128)), o((128, 240)), o((128, 128)), o((128, 128))]
        + [o((GROUP, 3 * WROWS, 128)), o((GROUP, 128, 3 * WROWS)), o((GROUP, 128, WROWS)), o((GROUP, WROWS, 128))]
        + [o((128, 128), f32), o((HEADS, LG, LG), f32), o((384, 384))],
        scratch_shapes=[
            pltpu.VMEM((total, 128), f32),
            pltpu.VMEM((TABLE, 128), f32),
            pltpu.VMEM((128, 128), f32),
            pltpu.VMEM((GROUP, 512, 128), f32),
            pltpu.VMEM((128, 128), f32),
        ],
        compiler_params=pltpu.CompilerParams(vmem_limit_bytes=VMEM_BYTES),
        name="prepare",
    )(me, gathered)


def column(cols, k):
    return cols[:D, k : k + 1]


def valid_keys(length):
    return row_iota((LG, 1)) * GROUP < length


def set_tail(hid):
    hid[FF:, :] = jnp.where(row_iota((512 - FF, hid.shape[1])) == 0, 1.0, 0.0).astype(bf16)


def conv_columns(cols, cb):
    for k in range(KERNEL + 1):
        cb[k] = jnp.broadcast_to(cols[:D, C_DWB + k : C_DWB + k + 1], (D, 128))


def wide(tile, copies=4):
    return jnp.concatenate([tile] * copies, axis=1)


def first_body(
    len_ref, x_ref, cols_ref, up_ref, dn_ref, wqkv_ref, wo_ref, pw_ref, tab_ref, pm_ref,
    xf_ref, lf_ref, xa_ref, nrm_ref, qkv_ref, prob_ref, att_ref, aa_ref, xc_ref, cn_ref, gat_ref, sig_ref, rgt_ref,
    rs_ref, dep_ref, st_ref,
    hid, xp, one, cb, run,
):
    u = pl.program_id(0)
    length = len_ref[u]

    @pl.when(u == 0)
    def _():
        set_tail(hid)
        run[...] = jnp.zeros_like(run)
        conv_columns(cols_ref, cb)

    xp[...] = permute_in(x_ref[0].astype(f32), pm_ref[...])
    cols = cols_ref

    def ffn_up(r, held):
        xhat, rstd = norm(xp[:, span(r)])
        xf_ref[0, :, span(r)] = xhat
        rs_ref[0, 0:1, span(r)] = rstd
        low = ext(xhat * column(cols, C_F1) + column(cols, C_F1 + 1))
        lf_ref[0, :, span(r)] = low
        return dot(up_ref[...], low)

    def ffn_down(r, half):
        hid[:FF, span(r)] = (half + half * jnp.tanh(half)).astype(bf16)
        return dot(dn_ref[...], hid[:, span(r)])[:D]

    def ffn_norm(r, branch):
        after = xp[:, span(r)] + branch
        one[:, span(r)] = after
        xhat, rstd = norm(after)
        xa_ref[0, :, span(r)] = xhat
        rs_ref[0, 1:2, span(r)] = rstd
        low = ext(xhat * column(cols, C_AT) + column(cols, C_AT + 1))
        nrm_ref[0, 128 * r : 128 * r + 128, :] = low
        return dot(wqkv_ref[r], low)

    made = [None] * GROUP

    def ffn_keep(r, found):
        made[r] = found

    skewed(GROUP, (ffn_up, ffn_down, ffn_norm, ffn_keep))
    for w in range(3):
        joined = join_windows([made[r][WROWS * w : WROWS * w + WROWS] for r in range(GROUP)])
        qkv_ref[0, GP * w : GP * w + GP, :] = joined.astype(bf16)
    keys = valid_keys(length)

    def rows(w, h):
        return slice(GP * w + HP * h, GP * w + HP * h + HP)

    def score(h, held):
        return dot_tn(qkv_ref[0, rows(1, h), :], qkv_ref[0, rows(0, h), :])

    def soften(h, raw):
        scores = raw * (SCALE * LOG2E) + tab_ref[h]
        scores = jnp.where(keys, scores, NEG_FILL * LOG2E)
        peak = jnp.max(scores, axis=0, keepdims=True)
        power = jnp.exp2(scores - peak)
        total = jnp.sum(power, axis=0, keepdims=True)
        prob_ref[0, h] = (power * (1.0 / total)).astype(bf16)
        mixed = dot(qkv_ref[0, rows(2, h), :], prob_ref[0, h])
        if h < GROUP:
            mixed = jnp.where(row_iota((HP, LG)) == HEAD, 1.0, mixed)
        att_ref[0, rows(0, h), :] = mixed.astype(bf16)

    skewed(HEADS, (score, soften))

    def project(r, held):
        return dot(wo_ref[r], window(att_ref.at[0], r))[:D]

    def gate_in(r, mixed):
        after = one[:, span(r)] + mixed
        aa_ref[0, :, span(r)] = after
        xhat, rstd = norm(after)
        xc_ref[0, :, span(r)] = xhat
        rs_ref[0, 2:3, span(r)] = rstd
        low = ext(xhat * column(cols, C_CV) + column(cols, C_CV + 1))
        cn_ref[0, :, span(r)] = low
        return dot(pw_ref[...], low)

    def gate_out(r, pre):
        mask = plane_mask(r, length)
        sig = (0.5 + 0.5 * jnp.tanh(pre[D:])) * mask
        gated = (pre[:D] + pre[:D]) * sig
        gat_ref[0, :, span(r)] = gated
        sig_ref[0, :, span(r)] = sig
        rgt_ref[0, :, span(r)] = gated * (1.0 - sig)

    skewed(GROUP, (project, gate_in, gate_out))

    def shift(f, held):
        return shifted_planes([gat_ref[0, 8 * f : 8 * f + 8, span(r)] for r in range(GROUP)])

    def taps(f, moved):
        at = slice(8 * f, 8 * f + 8)
        for r in range(GROUP):
            total = wide(cb[0, at, :])
            for k in range(KERNEL):
                total = total + wide(cb[1 + k, at, :]) * moved[r + k - HALF]
            dep_ref[0, at, span(r)] = total

    skewed(D // 8, (shift, taps))

    count = length.astype(f32)
    mask = jnp.concatenate([plane_mask(r, length) for r in range(GROUP)], axis=1)
    dep = dep_ref[0]
    mean = jnp.sum(dep * mask, axis=1, keepdims=True) / count
    gap = (dep - mean) * mask
    spread = jnp.sum(gap * gap, axis=1, keepdims=True)
    old_mean, old_spread, old_count = run[0], run[1], run[2]
    new_count = old_count + count
    step = mean - old_mean
    new_mean = old_mean + step * (count / new_count)
    new_spread = old_spread + spread + step * step * (old_count * count / new_count)
    run[0] = new_mean
    run[1] = new_spread
    run[2] = new_count

    @pl.when(u == pl.num_programs(0) - 1)
    def _():
        lanes = lane_iota((D, 128))
        picked = jnp.where(lanes == 0, run[0], jnp.where(lanes == 1, run[1], jnp.where(lanes == 2, run[2], 0.0)))
        line = pad8(picked).T[0:8]
        for d in range(st_ref.shape[0]):
            st_ref[d] = line


def whole(shape):
    zeros = (0,) * len(shape)
    return pl.BlockSpec(shape, lambda u: zeros)


def per_utt(shape):
    zeros = (0,) * len(shape)
    return pl.BlockSpec((1,) + shape, lambda u: (u,) + zeros)


def first(devices, lengths, x, weights):
    utts = x.shape[0]
    big = (D, MAXLEN)
    low = (128, MAXLEN)
    per = [
        (big, f32),
        (low, bf16),
        (big, f32),
        ((GP, LG), bf16),
        ((3 * GP, LG), bf16),
        ((HEADS, LG, LG), bf16),
        ((GP, LG), bf16),
        (big, f32),
        (big, f32),
        (low, bf16),
        (big, f32),
        (big, f32),
        (big, f32),
        ((8, MAXLEN), f32),
        (big, f32),
    ]
    line = (devices, 8, 128)
    return pl.pallas_call(
        first_body,
        grid=(utts,),
        in_specs=[SMEM, per_utt(big)] + [whole(w.shape) for w in weights],
        out_specs=[per_utt(s) for s, k in per] + [whole(line)],
        out_shape=[jax.ShapeDtypeStruct((utts,) + s, k) for s, k in per] + [jax.ShapeDtypeStruct(line, f32)],
        scratch_shapes=[
            pltpu.VMEM((512, MAXLEN), bf16),
            pltpu.VMEM(big, f32),
            pltpu.VMEM(big, f32),
            pltpu.VMEM((KERNEL + 1, D, 128), f32),
            pltpu.VMEM((3, D, 128), f32),
        ],
        compiler_params=pltpu.CompilerParams(vmem_limit_bytes=VMEM_BYTES),
        name="first",
    )(lengths, x, *weights)


def second_body(
    len_ref, stats_ref, cot_ref, aa_ref, dep_ref, cols_ref, up_ref, upp_ref, dn_ref, dnp_ref, pr_ref, prp_ref, pm_ref,
    out_ref, bgd_ref, gc_ref, sums_ref, stc_ref, gdn_ref, gup_ref, gpr_ref, vec_ref,
    hid, cotp, outp, acc,
):
    u = pl.program_id(0)
    length = len_ref[u]
    cols = cols_ref

    @pl.when(u == 0)
    def _():
        set_tail(hid)
        parts = stats_ref.shape[0]
        count = jnp.zeros((1, 128), f32)
        total = jnp.zeros((1, 128), f32)
        for d in range(parts):
            many = stats_ref[d, 2:3, :]
            count = count + many
            total = total + many * stats_ref[d, 0:1, :]
        here = lane_iota((1, 128)) < D
        count = jnp.where(here, count, 1.0)
        mean = total / count
        spread = jnp.zeros((1, 128), f32)
        for d in range(parts):
            gap = stats_ref[d, 0:1, :] - mean
            spread = spread + stats_ref[d, 1:2, :] + stats_ref[d, 2:3, :] * gap * gap
        scale = lax.rsqrt(spread / count + EPS_NORM)
        at = row_iota((128, 128))
        table = jnp.where(at == 0, mean, jnp.where(at == 1, scale, jnp.where(at == 2, 1.0 / count, 0.0)))
        stc_ref[...] = table.T
        gdn_ref[...] = jnp.zeros_like(gdn_ref)
        gup_ref[...] = jnp.zeros_like(gup_ref)
        gpr_ref[...] = jnp.zeros_like(gpr_ref)
        vec_ref[...] = jnp.zeros_like(vec_ref)
        acc[...] = jnp.zeros_like(acc)

    cotp[...] = permute_in(cot_ref[0].astype(f32), pm_ref[...])
    half_gain = 0.5 * column(cols, C_BN)
    half_bias = 0.5 * column(cols, C_BN + 1)

    def enter(r, held):
        normal = (dep_ref[0, :, span(r)] - stc_ref[:D, 0:1]) * stc_ref[:D, 1:2]
        z = normal * half_gain + half_bias
        t = jnp.tanh(z)
        act = z + z * t
        act_low = ext(act)
        slope = (1.0 + t) * (1.0 + z * (1.0 - t))
        return act_low, normal, slope, dot(pr_ref[...], act_low)[:D]

    def ffn_up(r, held):
        act_low, normal, slope, moved = held
        after_conv = aa_ref[0, :, span(r)] + moved
        xhat, rstd = norm(after_conv)
        low = ext(xhat * column(cols, C_F2) + column(cols, C_F2 + 1))
        return act_low, normal, slope, after_conv, xhat, rstd, low, dot(up_ref[...], low)

    def ffn_down(r, held):
        act_low, normal, slope, after_conv, xhat, rstd, low, half = held
        t = jnp.tanh(half)
        hid[:FF, span(r)] = (half + half * t).astype(bf16)
        bend = (1.0 + t) * (1.0 + half * (1.0 - t))
        return act_low, normal, slope, after_conv, xhat, rstd, low, bend, dot(dn_ref[...], hid[:, span(r)])[:D]

    def finish(r, held):
        act_low, normal, slope, after_conv, xhat, rstd, low, bend, branch = held
        mask = plane_mask(r, length)
        xhat_f, rstd_f = norm(after_conv + branch)
        outp[:, span(r)] = (xhat_f * column(cols, C_FN) + column(cols, C_FN + 1)) * mask
        up_grad = cotp[:, span(r)] * mask
        vec_ref[2] += fold(up_grad * xhat_f)
        vec_ref[3] += fold(up_grad)
        grad_two = norm_back(up_grad, xhat_f, rstd_f, column(cols, C_FN))
        branch = pad8(grad_two).astype(bf16)
        gdn_ref[...] += dot_nt(hid[:, span(r)], branch)
        return act_low, normal, slope, xhat, rstd, low, bend, grad_two, dot(dnp_ref[...], branch)

    def ffn_back(r, held):
        act_low, normal, slope, xhat, rstd, low, bend, grad_two, back = held
        pre_low = (bend * back).astype(bf16)
        gup_ref[...] += dot_nt(pre_low, low)
        return act_low, normal, slope, xhat, rstd, grad_two, dot(upp_ref[...], pre_low)[:D]

    def leave(r, held):
        act_low, normal, slope, xhat, rstd, grad_two, back = held
        vec_ref[0] += fold(back * xhat)
        vec_ref[1] += fold(back)
        grad_conv = grad_two + norm_back(back, xhat, rstd, column(cols, C_F2))
        gc_ref[0, :, span(r)] = grad_conv
        project = pad8(grad_conv).astype(bf16)
        gpr_ref[...] += dot_nt(act_low, project)
        return normal, slope, dot(prp_ref[...], project)[:D]

    def last(r, held):
        normal, slope, back = held
        batch = slope * back
        bgd_ref[0, :, span(r)] = batch
        acc[0] += fold(batch * normal)
        acc[1] += fold(batch)

    skewed(GROUP, (enter, ffn_up, ffn_down, finish, ffn_back, leave, last))
    out_ref[0] = permute_out(outp[...], pm_ref[...]).astype(bf16)

    @pl.when(u == pl.num_programs(0) - 1)
    def _():
        lanes = lane_iota((D, 128))
        gain = jnp.sum(acc[0], axis=1, keepdims=True)
        shift = jnp.sum(acc[1], axis=1, keepdims=True)
        line = pad8(jnp.where(lanes == 0, gain, jnp.where(lanes == 1, shift, 0.0))).T[0:8]
        for d in range(sums_ref.shape[0]):
            sums_ref[d] = line


def second(lengths, stats, cot, aa, dep, weights):
    utts = cot.shape[0]
    big = (D, MAXLEN)
    outs = [
        (per_utt(big), (utts,) + big, bf16),
        (per_utt(big), (utts,) + big, f32),
        (per_utt(big), (utts,) + big, f32),
    ]
    for s in (stats.shape, (128, 128), (512, 128), (FF, 128), (128, 128), (4, D, 128)):
        outs.append((whole(s), s, f32))
    return pl.pallas_call(
        second_body,
        grid=(utts,),
        in_specs=[SMEM, whole(stats.shape)] + [per_utt(big)] * 3 + [whole(w.shape) for w in weights],
        out_specs=[o[0] for o in outs],
        out_shape=[jax.ShapeDtypeStruct(o[1], o[2]) for o in outs],
        scratch_shapes=[
            pltpu.VMEM((512, MAXLEN), bf16),
            pltpu.VMEM(big, f32),
            pltpu.VMEM(big, f32),
            pltpu.VMEM((2, D, 128), f32),
        ],
        compiler_params=pltpu.CompilerParams(vmem_limit_bytes=VMEM_BYTES),
        name="second",
    )(lengths, stats, cot, aa, dep, *weights)


def third_body(
    len_ref, sums_ref, stc_ref, bgd_ref, gc_ref, dep_ref, xf_ref, lf_ref, xa_ref, nrm_ref, qkv_ref, prob_ref, att_ref, xc_ref,
    cn_ref, gat_ref, sig_ref, rgt_ref, rs_ref,
    cols_ref, up_ref, upp_ref, dnp_ref, wqkv_t_ref, wob_ref, pwp_ref, pm_ref,
    gin_ref, gdn_ref, gup_ref, gpw_ref, gqkv_ref, go_ref, rel_ref, vec_ref,
    hid, dgs, olg, agr, back_s, gg, relacc, cb, tot,
):
    u = pl.program_id(0)
    length = len_ref[u]
    cols = cols_ref

    @pl.when(u == 0)
    def _():
        set_tail(hid)
        conv_columns(cols_ref, cb)
        parts = sums_ref.shape[0]
        total = sums_ref[0]
        for d in range(1, parts):
            total = total + sums_ref[d]
        tot[...] = jnp.concatenate([total, jnp.zeros((120, 128), f32)], axis=0).T
        for ref in (gdn_ref, gup_ref, gpw_ref, gqkv_ref, go_ref, vec_ref, relacc):
            ref[...] = jnp.zeros_like(ref)

    scale = stc_ref[:D, 1:2]
    lead = column(cols, C_BN) * scale
    share = lead * stc_ref[:D, 2:3]
    shift_part = share * tot[:D, 1:2]
    gain_part = share * tot[:D, 0:1] * scale
    for r in range(GROUP):
        normal = dep_ref[0, :, span(r)] - stc_ref[:D, 0:1]
        mask = plane_mask(r, length)
        dgs[:, span(r)] = bgd_ref[0, :, span(r)] * lead - mask * (shift_part + normal * gain_part)

    def shift(f, held):
        return shifted_planes([dgs[8 * f : 8 * f + 8, span(r)] for r in range(GROUP)])

    def taps(f, moved):
        at = slice(8 * f, 8 * f + 8)
        gated = [gat_ref[0, at, span(r)] for r in range(GROUP)]
        totals = [None] * GROUP
        for k in range(KERNEL):
            weight = wide(cb[1 + k, at, :])
            tap = None
            for r in range(GROUP):
                here = moved[r - k + HALF]
                term = weight * here
                totals[r] = term if totals[r] is None else totals[r] + term
                part = gated[r] * here
                tap = part if tap is None else tap + part
            vec_ref[7 + k, at, :] += fold(tap)
        vec_ref[6, at, :] += fold(moved[0] + moved[1] + moved[2])
        for r in range(GROUP):
            gg[at, span(r)] = totals[r]

    skewed(D // 8, (shift, taps))

    def gate(r, held):
        grad = gg[:, span(r)]
        left = grad * sig_ref[0, :, span(r)]
        right = grad * rgt_ref[0, :, span(r)]
        pre_low = jnp.concatenate([left, right], axis=0).astype(bf16)
        gpw_ref[...] += dot_nt(pre_low, cn_ref[0, :, span(r)])
        return dot(pwp_ref[...], pre_low)[:D]

    def residual(r, back):
        xhat = xc_ref[0, :, span(r)]
        vec_ref[0] += fold(back * xhat)
        vec_ref[1] += fold(back)
        grad = gc_ref[0, :, span(r)] + norm_back(back, xhat, rs_ref[0, 2:3, span(r)], column(cols, C_CV))
        dgs[:, span(r)] = grad
        low = pad8(grad).astype(bf16)
        olg[128 * r : 128 * r + 128, :] = low
        return dot(wob_ref[r], low)

    made = [None] * GROUP

    def keep(r, found):
        go_ref[r] += dot_nt(window(att_ref.at[0], r), olg[128 * r : 128 * r + 128, :])
        made[r] = found

    skewed(GROUP, (gate, residual, keep))
    agr[...] = join_windows(made).astype(bf16)

    def rows(w, h):
        return slice(GP * w + HP * h, GP * w + HP * h + HP)

    def enter(h, held):
        grad = agr[rows(0, h), :]
        back_s[rows(2, h), :] = dot_nt(grad, prob_ref[0, h]).astype(bf16)
        return dot_tn(qkv_ref[0, rows(2, h), :], grad)

    def soften(h, prob_grad):
        probs = prob_ref[0, h].astype(f32)
        inner = jnp.sum(probs * prob_grad, axis=0, keepdims=True)
        score = probs * (prob_grad - inner)
        relacc[h] += score
        low = score.astype(bf16)
        back_s[rows(0, h), :] = (dot(qkv_ref[0, rows(1, h), :], low) * SCALE).astype(bf16)
        back_s[rows(1, h), :] = (dot_nt(qkv_ref[0, rows(0, h), :], low) * SCALE).astype(bf16)

    skewed(HEADS, (enter, soften))

    def project(r, held):
        stack = jnp.concatenate([window(back_s, r, GP * w) for w in range(3)], axis=0)
        gqkv_ref[r] += dot_nt(stack, nrm_ref[0, 128 * r : 128 * r + 128, :])
        return dot(wqkv_t_ref[r], stack)[:D], dot(up_ref[...], lf_ref[0, :, span(r)])

    def ffn_in(r, held):
        back, half = held
        xhat = xa_ref[0, :, span(r)]
        vec_ref[2] += fold(back * xhat)
        vec_ref[3] += fold(back)
        grad = dgs[:, span(r)] + norm_back(back, xhat, rs_ref[0, 1:2, span(r)], column(cols, C_AT))
        low = pad8(grad).astype(bf16)
        return grad, low, half, dot(dnp_ref[...], low)

    def ffn_mid(r, held):
        grad, branch, half, back = held
        t = jnp.tanh(half)
        hid[:FF, span(r)] = (half + half * t).astype(bf16)
        pre_low = ((1.0 + t) * (1.0 + half * (1.0 - t)) * back).astype(bf16)
        gdn_ref[...] += dot_nt(hid[:, span(r)], branch)
        gup_ref[...] += dot_nt(pre_low, lf_ref[0, :, span(r)])
        return grad, dot(upp_ref[...], pre_low)[:D]

    def ffn_out(r, held):
        grad, back = held
        xhat = xf_ref[0, :, span(r)]
        vec_ref[4] += fold(back * xhat)
        vec_ref[5] += fold(back)
        gg[:, span(r)] = grad + norm_back(back, xhat, rs_ref[0, 0:1, span(r)], column(cols, C_F1))

    skewed(GROUP, (project, ffn_in, ffn_mid, ffn_out))
    gin_ref[0] = permute_out_wide(gg[...], pm_ref[...])

    @pl.when(u == pl.num_programs(0) - 1)
    def _():
        found = []
        for h in range(HEADS):
            found.append(diagonal_sum(relacc[h]))
        stacked = jnp.concatenate(found + [jnp.zeros((4, 2 * LG), f32)], axis=0)
        high = stacked.astype(bf16)
        rest = stacked - high.astype(f32)
        mid = rest.astype(bf16)
        rest = rest - mid.astype(f32)
        select = distance_select()
        rel_ref[...] = dot_nt(high, select) + dot_nt(mid, select) + dot_nt(rest.astype(bf16), select)


def third(lengths, sums, stc, saved, weights):
    utts = saved[0].shape[0]
    big = (D, MAXLEN)
    outs = [(per_utt(big), (utts,) + big)]
    for s in ((512, 128), (FF, 128), (240, 128), (GROUP, 3 * WROWS, 128), (GROUP, WROWS, 128), (8, 256), (22, D, 128)):
        outs.append((whole(s), s))
    return pl.pallas_call(
        third_body,
        grid=(utts,),
        in_specs=[SMEM, whole(sums.shape), whole(stc.shape)]
        + [per_utt(s.shape[1:]) for s in saved]
        + [whole(w.shape) for w in weights],
        out_specs=[o[0] for o in outs],
        out_shape=[jax.ShapeDtypeStruct(o[1], f32) for o in outs],
        scratch_shapes=[
            pltpu.VMEM((512, MAXLEN), bf16),
            pltpu.VMEM(big, f32),
            pltpu.VMEM((GP, LG), bf16),
            pltpu.VMEM((GP, LG), bf16),
            pltpu.VMEM((3 * GP, LG), bf16),
            pltpu.VMEM(big, f32),
            pltpu.VMEM((HEADS, LG, LG), f32),
            pltpu.VMEM((KERNEL + 1, D, 128), f32),
            pltpu.VMEM((128, 128), f32),
        ],
        compiler_params=pltpu.CompilerParams(vmem_limit_bytes=VMEM_BYTES),
        name="third",
    )(lengths, sums, stc, *saved, *weights)


def pack_body(
    me_ref, dn1_ref, up1_ref, dn2_ref, up2_ref, pr_ref, pw_ref, qkv_ref, o_ref, rel_ref, vecs2_ref, vecs3_ref, sums_ref,
    keep_ref, send_ref, tb, flat, stage, wt,
):
    tb[...] = jnp.zeros_like(tb)
    flat[...] = jnp.zeros_like(flat)
    lanes = lane_iota((D, 128))
    table = jnp.zeros((D, 128), f32)
    listed = []
    for ref, at in (
        (vecs2_ref, (F2, F2 + 1, FN, FN + 1)),
        (vecs3_ref, (CV, CV + 1, AT, AT + 1, F1, F1 + 1, CV + 259) + tuple(CV + 244 + k for k in range(KERNEL))),
    ):
        for k, to in enumerate(at):
            table = jnp.where(lanes == len(listed), jnp.sum(ref[k], axis=1, keepdims=True), table)
            listed.append(to)
    wt[...] = pad8(table).T
    keep = lane_iota((1, 128)) < D
    for k, to in enumerate(listed):
        tb[to : to + 1, :] = wt[k : k + 1, :]
    tb[CV + 260 : CV + 262, :] = sums_ref[0, 0:2, :]

    def clean(block):
        return jnp.where(lane_iota(block.shape) < D, block, 0.0)

    for base, dn_ref, up_ref in ((F1, dn1_ref, up1_ref), (F2, dn2_ref, up2_ref)):
        tb[base + 486 : base + 967, :] = 0.5 * clean(dn_ref[0 : FF + 1, :])
        for q in range(4):
            block = pad8(up_ref[D * q : D * q + D, :]).T
            tb[pl.ds(base + 2 + q, D, stride=4), :] = block[:D]
            tb[base + 482 + q : base + 483 + q, :] = block[D : D + 1]
    for q in range(2):
        block = pad8(pw_ref[D * q : D * q + D, :]).T
        tb[pl.ds(CV + 2 + q, D, stride=2), :] = block[:D]
        tb[CV + 242 + q : CV + 243 + q, :] = block[D : D + 1]
    tb[CV + 262 : CV + 383, :] = clean(pr_ref[0 : D + 1, :])

    def gathered(ref, base):
        wt[...] = jnp.zeros_like(wt)
        for to, r, src, many in segments():
            start = base + to - WIN[r]
            wt[src : src + many, :] += ref[r, start : start + many, :]
        return wt[...]

    for w, at, bias_at in ((0, AT + 2, AT + 122), (1, AT + 123, None), (2, AT + 243, AT + 363)):
        block = gathered(qkv_ref, WROWS * w).T
        tb[at : at + D, :] = block[:D]
        if bias_at is not None:
            tb[bias_at : bias_at + 1, :] = block[D : D + 1]
    tb[AT + 364 : AT + 484, :] = clean(gathered(o_ref, 0)[:D])
    bias = sum(o_ref[r, MARKS[r] : MARKS[r] + 1, :] for r in range(GROUP))
    tb[AT + 484 : AT + 485, :] = jnp.where(keep, bias, 0.0)

    last = (LIVE - 1) // 128
    for y_first, y_count, offset, base in (
        (0, REL_AT // 128 + 1, 0, 0),
        (TAIL_AT // 128, last - TAIL_AT // 128 + 1, 128 * (TAIL_AT // 128) - TAIL_AT + D, TAIL - 1),
    ):
        for k in range(15):
            at = 128 * k + offset
            first_row, col = at // D, at % D
            many = (y_count - k + 14) // 15
            here = lane_iota((many, 128))
            got = tb[pl.ds(base + first_row, many, stride=16), :]
            if col:
                got = pltpu.roll(got, 128 - col, 1)
            then = pltpu.roll(tb[pl.ds(base + first_row + 1, many, stride=16), :], D - col, 1)
            got = jnp.where(here < D - col, got, then)
            if 2 * D - col < 128:
                then = pltpu.roll(tb[pl.ds(base + first_row + 2, many, stride=16), :], 2 * D - col, 1)
                got = jnp.where(here < 2 * D - col, got, then)
            flat[pl.ds(y_first + k, many, stride=15), :] = got
    here = lane_iota((1, 128))
    width = 2 * REL + 1
    for h in range(HEADS):
        at = REL_AT + width * h
        for y in range(at // 128, (at + width - 1) // 128 + 1):
            lo, hi = max(at - 128 * y, 0), min(at + width - 128 * y, 128)
            shift = (at - 128 * y) % 256
            turned = rel_ref[h : h + 1, :]
            if shift:
                turned = pltpu.roll(turned, shift, 1)
            flat[y : y + 1, :] += jnp.where((here >= lo) & (here < hi), turned[:, :128], 0.0)
    parts, rows = 2 * keep_ref.shape[0], keep_ref.shape[1]
    for d in range(parts):
        stage[d] = flat[rows * d : rows * (d + 1), :]
    for offset in range(0, parts, 2):
        keep_ref[place(offset, parts)] = stage[me_ref[0] ^ offset]
        send_ref[place(offset, parts)] = stage[me_ref[0] ^ (offset + 1)]


def pack(parts, rows, me, grads):
    half = jax.ShapeDtypeStruct((parts // 2, rows, 128), f32)
    return pl.pallas_call(
        pack_body,
        in_specs=[SMEM] + [pl.BlockSpec(memory_space=pltpu.VMEM)] * len(grads),
        out_shape=[half, half],
        scratch_shapes=[
            pltpu.VMEM((TABLE, 128), f32),
            pltpu.VMEM((parts * rows, 128), f32),
            pltpu.VMEM((parts, rows, 128), f32),
            pltpu.VMEM((128, 128), f32),
        ],
        compiler_params=pltpu.CompilerParams(vmem_limit_bytes=VMEM_BYTES),
        name="pack",
    )(me, *grads)


def update_tables(total_len):
    rates = np.zeros(total_len, np.float32)
    decays = np.zeros(total_len, np.float32)
    vector, gain, ffn = (D, 0.1, 0.0), (D, 0.3, 0.0), lambda n, fan: (n, fan**-0.5, 0.01)
    block = [gain, vector, ffn(D * FF, D), (FF, 0.1, 0.0), ffn(FF * D, FF), vector]
    square = ffn(D * D, D)
    pieces = block + [gain, vector, square, vector, square, square, vector, ffn(D * D, 6.0 * D / MAXLEN), vector]
    pieces += [(HEADS * (2 * REL + 1), 0.5, 0.0)]
    pieces += [gain, vector, ffn(2 * D * D, D), (2 * D, 0.1, 0.0), ffn(KERNEL * D, KERNEL), vector, gain, vector]
    pieces += [square, vector] + block + [gain, vector]
    offset = 0
    for entries, rate, decay in pieces:
        rates[offset : offset + entries] = rate
        decays[offset : offset + entries] = decay
        offset += entries
    return rates, decays


def digits(devices):
    found, stride = [], 1
    while stride < devices:
        size = min(2 if stride == 1 else 4, devices // stride)
        found.append((stride, size))
        stride *= size
    return found


def place(offset, devices):
    at, weight = 0, devices
    for stride, size in digits(devices):
        weight //= size
        at = at + ((offset // stride) % size) * weight
    return at


def partner(values, offset, devices):
    return lax.ppermute(values, "dp", [(i, i ^ offset) for i in range(devices)])


def gather(values, devices):
    held = values[None]
    for stride, size in reversed(digits(devices)):
        held = jnp.concatenate([held] + [partner(held, stride * j, devices) for j in range(1, size)], axis=0)
    return held


def scatter_sum(keep, send, devices):
    total = keep + partner(send, 1, devices)
    for stride, size in digits(devices)[1:]:
        parts = total.reshape((size, total.shape[0] // size) + total.shape[1:])
        total = parts[0]
        for j in range(1, size):
            total = total + partner(parts[j], stride * j, devices)
    return total


def local(frames, lengths, cotangent, master, moment_one, moment_two, average):
    shard_len = master.shape[0]
    devices = lax.axis_size("dp")
    rows = shard_len // 128
    me = lax.axis_index("dp").astype(jnp.int32).reshape(1)
    gathered = gather(master.astype(bf16).reshape(rows, 128), devices)
    (
        up1, upp1, dn1, dnp1, up2, upp2, dn2, dnp2, pw, pwp, pr, prp, wqkv, wqkvt, wo, wob, cols, tab, pm,
    ) = prepare(me, gathered)
    x = jnp.transpose(frames, (0, 2, 1))
    cot = jnp.transpose(cotangent, (0, 2, 1))
    xf, lf, xa, nrm, qkv, prob, att, aa, xc, cn, gat, sig, rgt, rs, dep, st = first(
        devices, lengths, x, (cols, up1, dn1, wqkv, wo, pw, tab, pm)
    )
    stats = lax.all_to_all(st, "dp", 0, 0)
    out, bgd, gc, sums, stc, gdn2, gup2, gpr, vec2 = second(
        lengths, stats, cot, aa, dep, (cols, up2, upp2, dn2, dnp2, pr, prp, pm)
    )
    all_sums = lax.all_to_all(sums, "dp", 0, 0)
    gin, gdn1, gup1, gpw, gqkv, go, rel, vec3 = third(
        lengths, all_sums, stc,
        (bgd, gc, dep, xf, lf, xa, nrm, qkv, prob, att, xc, cn, gat, sig, rgt, rs),
        (cols, up1, upp1, dnp1, wqkvt, wob, pwp, pm),
    )
    keep, send = pack(devices, rows, me, (gdn1, gup1, gdn2, gup2, gpr, gpw, gqkv, go, rel, vec2, vec3, sums))
    reduced = scatter_sum(keep, send, devices).reshape(shard_len)
    rates_np, decays_np = update_tables(shard_len * devices)
    start_at = lax.axis_index("dp") * shard_len
    rates = lax.dynamic_slice_in_dim(jnp.asarray(rates_np), start_at, shard_len)
    decays = lax.dynamic_slice_in_dim(jnp.asarray(decays_np), start_at, shard_len)
    correction = 1.0 - 0.5**STEP
    new_one = 0.5 * moment_one + 0.5 * reduced
    new_two = 0.5 * moment_two + 0.5 * reduced * reduced
    direction = new_one / correction / (jnp.sqrt(new_two / correction) + EPS_ADAM)
    new_master = master - rates * (direction + decays * master)
    new_average = 0.75 * average + 0.25 * new_master
    return (
        jnp.transpose(out, (0, 2, 1)),
        jnp.transpose(gin, (0, 2, 1)),
        reduced,
        new_master,
        new_one,
        new_two,
        new_average,
    )


def solution(mesh):
    three = P("dp", None, None)
    one = P("dp")
    in_specs = (three, one, three, one, one, one, one)
    out_specs = (three, three, one, one, one, one, one)
    return jax.shard_map(local, mesh=mesh, in_specs=in_specs, out_specs=out_specs, check_vma=False)
```

time: 302 us -> 196 us (0.65)
  Pallas kernels: 210 us -> 123 us
  blocking collectives: 48.8 us -> 23 us
  starting transfers between devices: 2.83 us -> 17.5 us
  waiting for transfers between devices: 35.1 us -> 25.2 us
    pallas_call x1, Pallas kernels: 93.8 us -> 52.7 us  [third(): pl.pallas_call(third_body, grid=(utts,), in_specs=[SMEM, whole(sums.shape...]
    all_to_all x1 -> x0, waiting for transfers between devices: 35.1 us -> none  [local(): lax.all_to_all(flat, 'dp', 0, 0)]
    pallas_call x3, Pallas kernels: 78.2 us -> 47.2 us  [the longest x1 35.4 us: first(): pl.pallas_call(first_body, grid=(utts,), in_specs=[SMEM, per_utt(big)] +...]
    all_to_all x3 -> x2, blocking collectives: 48.8 us -> 23 us  [the longest x1 11.5 us: local(): stats = lax.all_to_all(st, 'dp', 0, 0)]
    ppermute x0 -> x14, waiting for transfers between devices: none -> 25.2 us  [partner(): return lax.ppermute(values, 'dp', [(i, i ^ offset) for i in range(devices)])]
    ppermute x0 -> x14, starting transfers between devices: none -> 17.5 us  [partner(): return lax.ppermute(values, 'dp', [(i, i ^ offset) for i in range(devices)])]
    pallas_call x1, Pallas kernels: 38.2 us -> 22.8 us  [second(): pl.pallas_call(second_body, grid=(utts,), in_specs=[SMEM, whole(stats.sha...]
  transfers between devices with their start and end apart: 1 -> 14, of which waited for: 1 -> 13; matrix products, arithmetic and copies ran while one was open for 0% -> 0% of each run, Pallas kernels for 0% -> 0%
where the time goes in v1:
time: 196 us; the launch traced here: 195 us
  Pallas kernels  123 us (63%)
  waiting for transfers between devices  25.2 us (13%)
  blocking collectives  23 us (12%)
  starting transfers between devices  17.5 us (9%)
  other arithmetic  3.77 us (2%)
  local copies, waits for them, and re-layouts  2.41 us (1%)
    pallas_call x1, Pallas kernels, third(): pl.pallas_call(third_body, grid=(utts,), in_specs=[SMEM, whole(sums.shape...  52.7 us
    pallas_call x1, Pallas kernels, first(): pl.pallas_call(first_body, grid=(utts,), in_specs=[SMEM, per_utt(big)] +...  35.4 us
    ppermute x14, waiting for transfers between devices, partner(): return lax.ppermute(values, 'dp', [(i, i ^ offset) for i in range(devices)])  25.2 us
    pallas_call x1, Pallas kernels, second(): pl.pallas_call(second_body, grid=(utts,), in_specs=[SMEM, whole(stats.sha...  22.8 us
    ppermute x14, starting transfers between devices, partner(): return lax.ppermute(values, 'dp', [(i, i ^ offset) for i in range(devices)])  17.5 us
    all_to_all x1, blocking collectives, local(): stats = lax.all_to_all(st, 'dp', 0, 0)  11.5 us
    all_to_all x1, blocking collectives, local(): all_sums = lax.all_to_all(sums, 'dp', 0, 0)  11.5 us
    pallas_call x1, Pallas kernels, prepare(): pl.pallas_call(prepare_body, in_specs=[SMEM, pl.BlockSpec(memory_space=pl...  6.49 us
  transfers between devices with their start and end apart: 14, of which 13 were waited for; matrix products, arithmetic and copies ran while one was open for 0% of the time, Pallas kernels for 0%

profile of v1, /device:TPU:0, one launch (start us, length us, event | category | flops | bytes accessed | tf_op | source)
XLA Modules:
  0.0 195.4 jit_solution(9806371866987076290)
XLA Ops:
  0.6 0.8 constant_dynamic-update-slice_fusion.6
  1.4 3.0 %collective-permute-start = (bf16[1,83,128]{2,1,0:T(8,128)(2,1)S(1)}, bf16[1,83,128]{2,1,0:T(8,128)(2,1)S(1)}, u32[]{:S(2)}, u32[]{:S(2)}) collective-permute-start(bf16[1,83,128]{2,1,0:T(8,128)(2,1)S(1)} %get-tuple-element.121), channel_id=1, source_target_pairs={{0,8},{1,9},{2,10},{3,11},{4,12},{5,13},{6,14},{7,15},{8,0},{9,1},... | collective-permute-start | bytes 63752 | tf_op jit(solution)/shard_map/ppermute | solution.py:1015
  4.5 2.6 %collective-permute-start.1 = (bf16[1,83,128]{2,1,0:T(8,128)(2,1)S(1)}, bf16[1,83,128]{2,1,0:T(8,128)(2,1)S(1)}, u32[]{:S(2)}, u32[]{:S(2)}) collective-permute-start(bf16[1,83,128]{2,1,0:T(8,128)(2,1)S(1)} %get-tuple-element.121), channel_id=1, source_target_pairs={{0,16},{1,17},{2,18},{3,19},{4,20},{5,21},{6,22},{7,23},{8,24},{9,... | collective-permute-start | bytes 63752 | tf_op jit(solution)/shard_map/ppermute | solution.py:1015
  7.0 0.0 collective-permute-start.2
  7.1 0.0 collective-permute-done
  7.1 2.4 %collective-permute-done.1 = bf16[1,83,128]{2,1,0:T(8,128)(2,1)S(1)} collective-permute-done((bf16[1,83,128]{2,1,0:T(8,128)(2,1)S(1)}, bf16[1,83,128]{2,1,0:T(8,128)(2,1)S(1)}, u32[]{:S(2)}, u32[]{:S(2)}) %collective-permute-start.1) | collective-permute-done | bytes 21280 | tf_op jit(solution)/shard_map/ppermute | solution.py:1015
  9.4 3.2 %collective-permute-done.2 = bf16[1,83,128]{2,1,0:T(8,128)(2,1)S(1)} collective-permute-done((bf16[1,83,128]{2,1,0:T(8,128)(2,1)S(1)}, bf16[1,83,128]{2,1,0:T(8,128)(2,1)S(1)}, u32[]{:S(2)}, u32[]{:S(2)}) %collective-permute-start.2) | collective-permute-done | bytes 21280 | tf_op jit(solution)/shard_map/ppermute | solution.py:1015
  12.7 1.6 collective-permute-start.3
  14.2 1.5 collective-permute-start.4
  15.7 0.5 collective-permute-start.5
  16.3 1.5 collective-permute-done.3
  17.8 1.2 collective-permute-done.4
  19.1 2.1 %collective-permute-done.5 = bf16[4,83,128]{2,1,0:T(8,128)(2,1)S(1)} collective-permute-done((bf16[4,83,128]{2,1,0:T(8,128)(2,1)S(1)}, bf16[4,83,128]{2,1,0:T(8,128)(2,1)S(1)}, u32[]{:S(2)}, u32[]{:S(2)}) %collective-permute-start.5) | collective-permute-done | bytes 85024 | tf_op jit(solution)/shard_map/ppermute | solution.py:1015
  21.2 0.1 collective-permute-start.6
  21.3 1.7 collective-permute-done.6
  23.0 0.1 constant_dynamic-update-slice_fusion.7.g_ref
  23.0 0.0 copy-start
  23.0 0.8 copy-done
  23.9 6.5 %prepare.1 = (bf16[480,128]{1,0:T(8,128)(2,1)}, bf16[128,480]{1,0:T(8,128)(2,1)}, bf16[128,512]{1,0:T(8,128)(2,1)}, bf16[480,128]{1,0:T(8,128)(2,1)}, bf16[480,1...) custom-call(s32[1]{0:T(128)} %bitcast.1.me_ref, ...), custom_call_target="tpu_custom_call" | custom-call | tf_op jit(solution)/shard_map/prepare/pallas_call | solution.py:331
  30.4 35.4 %first.1 = (f32[5,120,1536]{2,1,0:T(8,128)}, bf16[5,128,1536]{2,1,0:T(8,128)(2,1)}, f32[5,120,1536]{2,1,0:T(8,128)}, bf16[5,384,512]{2,1,0:T(8,128)(2,1)}, bf16[...) custom-call(s32[5]{0:T(128)} %len_ref.5, ...), custom_call_target="tpu_custom_call" | custom-call | tf_op jit(solution)/shard_map/first/pallas_call | solution.py:535
  65.8 11.5 %all_to_all.10.stats_ref = f32[32,8,128]{2,1,0:T(8,128)} all-to-all(f32[32,8,128]{2,1,0:T(8,128)} %get-tuple-element.69), channel_id=1, replica_groups=mesh['dp'=32] {'dp'}, dimensions={0} | all-to-all | bytes 262144 | tf_op jit(solution)/shard_map/all_to_all | solution.py:1049
  77.3 22.8 %second.1 = (bf16[5,120,1536]{2,1,0:T(8,128)(2,1)}, f32[5,120,1536]{2,1,0:T(8,128)}, f32[5,120,1536]{2,1,0:T(8,128)}, f32[32,8,128]{2,1,0:T(8,128)}, f32[128,128...) custom-call(s32[5]{0:T(128)} %len_ref.5, ...), custom_call_target="tpu_custom_call" | custom-call | tf_op jit(solution)/shard_map/second/pallas_call | solution.py:675
  100.1 11.5 %all_to_all.11.sums_ref = f32[32,8,128]{2,1,0:T(8,128)} all-to-all(f32[32,8,128]{2,1,0:T(8,128)} %get-tuple-element.79.sums_ref), channel_id=1, replica_groups=mesh['dp'=32] {'dp'}, dimensions={0} | all-to-all | bytes 262144 | tf_op jit(solution)/shard_map/all_to_all | solution.py:1053
  111.6 52.7 %third.1 = (f32[5,120,1536]{2,1,0:T(8,128)}, f32[512,128]{1,0:T(8,128)}, f32[480,128]{1,0:T(8,128)}, f32[240,128]{1,0:T(8,128)}, f32[3,432,128]{2,1,0:T(8,128)},...) custom-call(s32[5]{0:T(128)} %len_ref.5, f32[32,8,128]{2,1,0:T(8,128)} %all_to_all.11.sums_ref, ...), custom_call_target="tpu_custom_call" | custom-call | tf_op jit(solution)/shard_map/third/pallas_call | solution.py:847
  164.3 5.3 %pack.1 = (f32[16,83,128]{2,1,0:T(8,128)}, f32[16,83,128]{2,1,0:T(8,128)}) custom-call(s32[1]{0:T(128)} %bitcast.1.me_ref, f32[512,128]{1,0:T(8,128)} %get-tuple-element.102.dn1_ref, f32[480,128]{1,0:T(8,128)} %get-tuple-element.103.up1_ref, f32[512,128]{1,0:T(8,128)} %get-tuple-element.104.dn2_ref, f32[480,128]{1,0:T(8,128)} %get-tuple-element.105.up2_ref, ...), custom_call_target="tpu_custom_call" | custom-call | tf_op jit(solution)/shard_map/pack/pallas_call | solution.py:964
  169.6 0.0 copy-start.1
  169.6 0.0 copy-start.2
  169.6 0.0 copy-start.3
  169.6 0.0 copy-start.4
  169.6 1.3 copy.16
  170.9 0.3 collective-permute-start.7
  171.2 1.9 collective-permute-done.7
  173.1 1.3 copy_add_fusion
  174.5 0.9 collective-permute-start.10
  175.5 1.3 collective-permute-start.8
  176.7 1.4 collective-permute-start.9
  178.1 4.8 %collective-permute-done.10 = f32[4,83,128]{2,1,0:T(8,128)S(1)} collective-permute-done((f32[4,83,128]{2,1,0:T(8,128)S(1)}, f32[4,83,128]{2,1,0:T(8,128)S(1)}, u32[]{:S(2)}, u32[]{:S(2)}) %collective-permute-start.10) | collective-permute-done | bytes 170016 | tf_op jit(solution)/shard_map/ppermute | solution.py:1015
  182.9 2.2 %collective-permute-done.8 = f32[4,83,128]{2,1,0:T(8,128)S(1)} collective-permute-done((f32[4,83,128]{2,1,0:T(8,128)S(1)}, f32[4,83,128]{2,1,0:T(8,128)S(1)}, u32[]{:S(2)}, u32[]{:S(2)}) %collective-permute-start.8) | collective-permute-done | bytes 170016 | tf_op jit(solution)/shard_map/ppermute | solution.py:1015
  185.2 0.9 collective-permute-done.9
  186.1 0.6 collective-permute-start.11
  186.7 1.1 collective-permute-start.12
  187.9 2.7 %collective-permute-start.13 = (f32[1,83,128]{2,1,0:T(8,128)S(1)}, f32[1,83,128]{2,1,0:T(8,128)S(1)}, u32[]{:S(2)}, u32[]{:S(2)}) collective-permute-start(f32[1,83,128]{2,1,0:T(8,128)S(1)} %get-tuple-element.126), channel_id=1, source_target_pairs={{0,24},{1,25},{2,26},{3,27},{4,28},{5,29},{6,30},{7,31},{8,16},{9,... | collective-permute-start | bytes 127496 | tf_op jit(solution)/shard_map/ppermute | solution.py:1015
  190.5 0.1 collective-permute-done.11
  190.7 2.2 %collective-permute-done.12 = f32[1,83,128]{2,1,0:T(8,128)S(1)} collective-permute-done((f32[1,83,128]{2,1,0:T(8,128)S(1)}, f32[1,83,128]{2,1,0:T(8,128)S(1)}, u32[]{:S(2)}, u32[]{:S(2)}) %collective-permute-start.12) | collective-permute-done | bytes 42528 | tf_op jit(solution)/shard_map/ppermute | solution.py:1015
  192.9 1.0 collective-permute-done.13
  193.8 0.0 copy-done.1
  193.8 0.0 copy-done.2
  193.8 0.0 copy-done.3
  193.8 0.0 copy-done.4
  193.8 1.6 multiply_add_fusion.1
  (11 shorter events, 0.3 us)
Async XLA Ops:
  1.4 5.6 %collective-permute-start = (bf16[1,83,128]{2,1,0:T(8,128)(2,1)S(1)}, bf16[1,83,128]{2,1,0:T(8,128)(2,1)S(1)}, u32[]{:S(2)}, u32[]{:S(2)}) collective-permute-start(bf16[1,83,128]{2,1,0:T(8,128)(2,1)S(1)} %get-tuple-element.121), channel_id=1, source_target_pairs={{0,8},{1,9},{2,10},{3,11},{4,12},{5,13},{6,14},{7,15},{8,0},{9,1},... | collective-permute-start | bytes 63752 | tf_op jit(solution)/shard_map/ppermute | solution.py:1015
  4.5 5.0 %collective-permute-start.1 = (bf16[1,83,128]{2,1,0:T(8,128)(2,1)S(1)}, bf16[1,83,128]{2,1,0:T(8,128)(2,1)S(1)}, u32[]{:S(2)}, u32[]{:S(2)}) collective-permute-start(bf16[1,83,128]{2,1,0:T(8,128)(2,1)S(1)} %get-tuple-element.121), channel_id=1, source_target_pairs={{0,16},{1,17},{2,18},{3,19},{4,20},{5,21},{6,22},{7,23},{8,24},{9,... | collective-permute-start | bytes 63752 | tf_op jit(solution)/shard_map/ppermute | solution.py:1015
  7.0 5.6 %collective-permute-start.2 = (bf16[1,83,128]{2,1,0:T(8,128)(2,1)S(1)}, bf16[1,83,128]{2,1,0:T(8,128)(2,1)S(1)}, u32[]{:S(2)}, u32[]{:S(2)}) collective-permute-start(bf16[1,83,128]{2,1,0:T(8,128)(2,1)S(1)} %get-tuple-element.121), channel_id=1, source_target_pairs={{0,24},{1,25},{2,26},{3,27},{4,28},{5,29},{6,30},{7,31},{8,16},{9,... | collective-permute-start | bytes 63752 | tf_op jit(solution)/shard_map/ppermute | solution.py:1015
  12.7 5.1 %collective-permute-start.3 = (bf16[4,83,128]{2,1,0:T(8,128)(2,1)S(1)}, bf16[4,83,128]{2,1,0:T(8,128)(2,1)S(1)}, u32[]{:S(2)}, u32[]{:S(2)}) collective-permute-start(bf16[4,83,128]{2,1,0:T(8,128)(2,1)S(1)} %pad_maximum_fusion), channel_id=1, source_target_pairs={{0,2},{1,3},{2,0},{3,1},{4,6},{5,7},{6,4},{7,5},{8,10},{9,11},{10,... | collective-permute-start | bytes 254984 | tf_op jit(solution)/shard_map/ppermute | solution.py:1015
  14.2 4.8 %collective-permute-start.4 = (bf16[4,83,128]{2,1,0:T(8,128)(2,1)S(1)}, bf16[4,83,128]{2,1,0:T(8,128)(2,1)S(1)}, u32[]{:S(2)}, u32[]{:S(2)}) collective-permute-start(bf16[4,83,128]{2,1,0:T(8,128)(2,1)S(1)} %pad_maximum_fusion), channel_id=1, source_target_pairs={{0,4},{1,5},{2,6},{3,7},{4,0},{5,1},{6,2},{7,3},{8,12},{9,13},{10,... | collective-permute-start | bytes 254984 | tf_op jit(solution)/shard_map/ppermute | solution.py:1015
  15.7 5.4 %collective-permute-start.5 = (bf16[4,83,128]{2,1,0:T(8,128)(2,1)S(1)}, bf16[4,83,128]{2,1,0:T(8,128)(2,1)S(1)}, u32[]{:S(2)}, u32[]{:S(2)}) collective-permute-start(bf16[4,83,128]{2,1,0:T(8,128)(2,1)S(1)} %pad_maximum_fusion), channel_id=1, source_target_pairs={{0,6},{1,7},{2,4},{3,5},{4,2},{5,3},{6,0},{7,1},{8,14},{9,15},{10,... | collective-permute-start | bytes 254984 | tf_op jit(solution)/shard_map/ppermute | solution.py:1015
  21.2 1.7 collective-permute-start.6
  23.0 0.9 copy-start
  169.6 24.2 %copy-start.1 = (f32[10624]{0:T(1024)S(1)}, f32[10624]{0:T(1024)}, u32[]{:S(2)}) copy-start(f32[10624]{0:T(1024)} %param.12) | copy-start | bytes 127492
  169.6 24.2 %copy-start.2 = (f32[10624]{0:T(1024)S(1)}, f32[10624]{0:T(1024)}, u32[]{:S(2)}) copy-start(f32[10624]{0:T(1024)} %param.15) | copy-start | bytes 127492
  169.6 24.2 %copy-start.3 = (f32[10624]{0:T(1024)S(1)}, f32[10624]{0:T(1024)}, u32[]{:S(2)}) copy-start(f32[10624]{0:T(1024)} %param.13) | copy-start | bytes 127492
  169.6 24.2 %copy-start.4 = (f32[10624]{0:T(1024)S(1)}, f32[10624]{0:T(1024)}, u32[]{:S(2)}) copy-start(f32[10624]{0:T(1024)} %param.14) | copy-start | bytes 127492
  170.9 2.2 %collective-permute-start.7 = (f32[16,83,128]{2,0,1:T(8,128)S(1)}, f32[16,83,128]{2,0,1:T(8,128)S(1)}, u32[]{:S(2)}, u32[]{:S(2)}) collective-permute-start(f32[16,83,128]{2,0,1:T(8,128)S(1)} %copy.16), channel_id=1, source_target_pairs={{0,1},{1,0},{2,3},{3,2},{4,5},{5,4},{6,7},{7,6},{8,9},{9,8},{10,11... | collective-permute-start | bytes 2039816 | tf_op jit(solution)/shard_map/ppermute | solution.py:1015
  174.5 8.4 %collective-permute-start.10 = (f32[4,83,128]{2,1,0:T(8,128)S(1)}, f32[4,83,128]{2,1,0:T(8,128)S(1)}, u32[]{:S(2)}, u32[]{:S(2)}) collective-permute-start(f32[4,83,128]{2,1,0:T(8,128)S(1)} %get-tuple-element.123), channel_id=1, source_target_pairs={{0,6},{1,7},{2,4},{3,5},{4,2},{5,3},{6,0},{7,1},{8,14},{9,15},{10,... | collective-permute-start | bytes 509960 | tf_op jit(solution)/shard_map/ppermute | solution.py:1015
  175.5 9.7 %collective-permute-start.8 = (f32[4,83,128]{2,1,0:T(8,128)S(1)}, f32[4,83,128]{2,1,0:T(8,128)S(1)}, u32[]{:S(2)}, u32[]{:S(2)}) collective-permute-start(f32[4,83,128]{2,1,0:T(8,128)S(1)} %get-tuple-element.122), channel_id=1, source_target_pairs={{0,2},{1,3},{2,0},{3,1},{4,6},{5,7},{6,4},{7,5},{8,10},{9,11},{10,... | collective-permute-start | bytes 509960 | tf_op jit(solution)/shard_map/ppermute | solution.py:1015
  176.7 9.3 %collective-permute-start.9 = (f32[4,83,128]{2,1,0:T(8,128)S(1)}, f32[4,83,128]{2,1,0:T(8,128)S(1)}, u32[]{:S(2)}, u32[]{:S(2)}) collective-permute-start(f32[4,83,128]{2,1,0:T(8,128)S(1)} %get-tuple-element.124), channel_id=1, source_target_pairs={{0,4},{1,5},{2,6},{3,7},{4,0},{5,1},{6,2},{7,3},{8,12},{9,13},{10,... | collective-permute-start | bytes 509960 | tf_op jit(solution)/shard_map/ppermute | solution.py:1015
  186.1 4.6 %collective-permute-start.11 = (f32[1,83,128]{2,1,0:T(8,128)S(1)}, f32[1,83,128]{2,1,0:T(8,128)S(1)}, u32[]{:S(2)}, u32[]{:S(2)}) collective-permute-start(f32[1,83,128]{2,1,0:T(8,128)S(1)} %get-tuple-element.125), channel_id=1, source_target_pairs={{0,8},{1,9},{2,10},{3,11},{4,12},{5,13},{6,14},{7,15},{8,0},{9,1},... | collective-permute-start | bytes 127496 | tf_op jit(solution)/shard_map/ppermute | solution.py:1015
  186.7 6.1 %collective-permute-start.12 = (f32[1,83,128]{2,1,0:T(8,128)S(1)}, f32[1,83,128]{2,1,0:T(8,128)S(1)}, u32[]{:S(2)}, u32[]{:S(2)}) collective-permute-start(f32[1,83,128]{2,1,0:T(8,128)S(1)} %get-tuple-element.127), channel_id=1, source_target_pairs={{0,16},{1,17},{2,18},{3,19},{4,20},{5,21},{6,22},{7,23},{8,24},{9,... | collective-permute-start | bytes 127496 | tf_op jit(solution)/shard_map/ppermute | solution.py:1015
  187.9 5.9 %collective-permute-start.13 = (f32[1,83,128]{2,1,0:T(8,128)S(1)}, f32[1,83,128]{2,1,0:T(8,128)S(1)}, u32[]{:S(2)}, u32[]{:S(2)}) collective-permute-start(f32[1,83,128]{2,1,0:T(8,128)S(1)} %get-tuple-element.126), channel_id=1, source_target_pairs={{0,24},{1,25},{2,26},{3,27},{4,28},{5,29},{6,30},{7,31},{8,16},{9,... | collective-permute-start | bytes 127496 | tf_op jit(solution)/shard_map/ppermute | solution.py:1015

commit v2 on v1

--- a/solution.py
+++ b/solution.py
@@ -192,59 +192,149 @@
     return made
 
 
-def prepare_body(
-    me_ref, g_ref, up1_ref, upp1_ref, dn1_ref, dnp1_ref, up2_ref, upp2_ref, dn2_ref, dnp2_ref, pw_ref, pwp_ref, pr_ref, prp_ref,
-    wqkv_ref, wqkvt_ref, wo_ref, wob_ref, cols_ref, tab_ref, pm_ref, flat, tb, wt, wins, rows,
-):
+def shifted(tiles, m):
+    r, s = m % GROUP, m // GROUP
+    if s == 0:
+        return tiles[r]
+    lanes = lane_iota((8, 128))
+    zero = jnp.zeros((8, 128), f32)
+    turned = [pltpu.roll(tiles[r][:, 128 * k : 128 * k + 128], (-s) % 128, 1) for k in range(4)]
+    if s > 0:
+        pairs = zip(turned, turned[1:] + [zero])
+        parts = [jnp.where(lanes < 128 - s, a, b) for a, b in pairs]
+    else:
+        pairs = zip([zero] + turned[:-1], turned)
+        parts = [jnp.where(lanes < -s, a, b) for a, b in pairs]
+    return jnp.concatenate(parts, axis=1)
+
+
+SMEM = pl.BlockSpec(memory_space=pltpu.SMEM)
+VMEM = pl.BlockSpec(memory_space=pltpu.VMEM)
+BIG = (D, MAXLEN)
+LOW = (128, MAXLEN)
+
+
+def whole(shape):
+    zeros = (0,) * len(shape)
+    return pl.BlockSpec(shape, lambda u: zeros)
+
+
+def per_utt(shape):
+    zeros = (0,) * len(shape)
+    return pl.BlockSpec((1,) + shape, lambda u: (u,) + zeros)
+
+
+def o(shape, kind=bf16):
+    return jax.ShapeDtypeStruct(shape, kind)
+
+
+def params(flops=0, moved=0):
+    cost = pl.CostEstimate(flops=flops, bytes_accessed=moved, transcendentals=0)
+    return dict(compiler_params=pltpu.CompilerParams(vmem_limit_bytes=VMEM_BYTES), cost_estimate=cost)
+
+
+def permutation():
+    t = row_iota((384, 384))
+    c = lane_iota((384, 384))
+    return jnp.where(t == GROUP * (c % 128) + c // 128, 1.0, 0.0).astype(bf16)
+
+
+def enter_body(x_ref, cot_ref, xp_ref, cp_ref, xf_ref, rs_ref, pm_ref):
+    @pl.when(pl.program_id(0) == 0)
+    def _():
+        pm_ref[...] = permutation()
+
+    x = permute_in(x_ref[0].astype(f32), pm_ref[...])
+    xp_ref[0] = x.astype(bf16)
+    xhat, rstd = norm(x)
+    xf_ref[0] = xhat
+    rs_ref[0] = jnp.broadcast_to(rstd, (8, MAXLEN))
+    cp_ref[0] = permute_in(cot_ref[0].astype(f32), pm_ref[...]).astype(bf16)
+
+
+def enter(x, cot):
+    utts = x.shape[0]
+    return pl.pallas_call(
+        enter_body,
+        grid=(utts,),
+        in_specs=[per_utt(BIG)] * 2,
+        out_specs=[per_utt(BIG)] * 3 + [per_utt((8, MAXLEN)), whole((384, 384))],
+        out_shape=[o((utts,) + BIG), o((utts,) + BIG), o((utts,) + BIG, f32), o((utts, 8, MAXLEN), f32), o((384, 384))],
+        name="enter",
+        **params(2 * 10**9, 16 * 10**6),
+    )(x, cot)
+
+
+def leave_body(out_ref, grad_ref, back_ref, xf_ref, rs_ref, cols_ref, pm_ref, done_ref, gin_ref):
+    done_ref[0] = permute_out(out_ref[0].astype(f32), pm_ref[...]).astype(bf16)
+    back = norm_back(back_ref[0], xf_ref[0], rs_ref[0, 0:1, :], column(cols_ref, C_F1))
+    gin_ref[0] = permute_out_wide(grad_ref[0] + back, pm_ref[...])
+
+
+def leave(out, grad, back, xf, rs, cols, pm):
+    utts = out.shape[0]
+    return pl.pallas_call(
+        leave_body,
+        grid=(utts,),
+        in_specs=[per_utt(BIG)] * 4 + [per_utt((8, MAXLEN)), whole(cols.shape), whole(pm.shape)],
+        out_specs=[per_utt(BIG)] * 2,
+        out_shape=[o((utts,) + BIG), o((utts,) + BIG, f32)],
+        name="leave",
+        **params(3 * 10**9, 20 * 10**6),
+    )(out, grad, back, xf, rs, cols, pm)
+
+
+def unpack(me_ref, g_ref, flat, tb):
     parts, part_rows = g_ref.shape[0], g_ref.shape[1]
     for d in range(parts):
         flat[part_rows * d : part_rows * (d + 1), :] = g_ref[place(me_ref[0] ^ d, parts)].astype(f32)
-    tb[...] = jnp.zeros_like(tb)
+    tb[ROWS_HEAD:TAIL, :] = jnp.zeros((TAIL - ROWS_HEAD, 128), f32)
     for start, count, base in ((0, ROWS_HEAD, 0), (TAIL_AT, ROWS_TAIL, TAIL)):
         for r in range(16):
             at = start + D * r
-            first, col = at // 128, at % 128
+            first_row, col = at // 128, at % 128
             many = (count - r + 15) // 16
-            here = flat[pl.ds(first, many, stride=15), :]
-            then = flat[pl.ds(first + 1, many, stride=15), :]
+            here = flat[pl.ds(first_row, many, stride=15), :]
+            then = flat[pl.ds(first_row + 1, many, stride=15), :]
             lanes = lane_iota((many, 128))
             got = jnp.where(lanes >= col, here, then)
             if col:
                 got = pltpu.roll(got, 128 - col, 1)
             tb[pl.ds(base + r, many, stride=16), :] = jnp.where(lanes < D, got, 0.0)
 
-    def with_row(block, row):
-        tail = jnp.where(row_iota((8, 128)) == 0, row, 0.0)
-        return jnp.concatenate([block, tail], axis=0)
-
-    for base, up_ref, upp_ref, dn_ref, dnp_ref in (
-        (F1, up1_ref, upp1_ref, dn1_ref, dnp1_ref),
-        (F2, up2_ref, upp2_ref, dn2_ref, dnp2_ref),
-    ):
-        parts_t = []
-        for q in range(4):
-            block = tb[pl.ds(base + 2 + q, D, stride=4), :]
-            parts_t.append(with_row(block, tb[base + 482 + q : base + 483 + q, :]).T[:D, :])
-        up_t = jnp.concatenate(parts_t, axis=0)
-        up_ref[...] = (0.5 * up_t).astype(bf16)
-        full = jnp.concatenate([up_t, jnp.zeros((32, 128), f32)], axis=0)
-        upp_ref[...] = full.T[:, :FF].astype(bf16)
-        down = tb[base + 486 : base + 966, :]
-        dnp_ref[...] = (0.25 * down).astype(bf16)
-        bias = jnp.where(row_iota((32, 128)) == 0, tb[base + 966 : base + 967, :], 0.0)
-        dn_ref[...] = (0.5 * jnp.concatenate([down, bias], axis=0)).T.astype(bf16)
-
+
+def with_row(block, row):
+    tail = jnp.where(row_iota((8, 128)) == 0, row, 0.0)
+    return jnp.concatenate([block, tail], axis=0)
+
+
+def up_rows(tb, base):
+    parts_t = []
+    for q in range(4):
+        block = tb[pl.ds(base + 2 + q, D, stride=4), :]
+        parts_t.append(with_row(block, tb[base + 482 + q : base + 483 + q, :]).T[:D, :])
+    return jnp.concatenate(parts_t, axis=0)
+
+
+def up_across(up_t):
+    return jnp.concatenate([up_t, jnp.zeros((32, 128), f32)], axis=0).T[:, :FF].astype(bf16)
+
+
+def down_across(tb, base):
+    bias = jnp.where(row_iota((32, 128)) == 0, tb[base + 966 : base + 967, :], 0.0)
+    down = jnp.concatenate([tb[base + 486 : base + 966, :], bias], axis=0)
+    return (0.5 * down).T.astype(bf16)
+
+
+def point_rows(tb):
     parts_t = []
     for q in range(2):
         block = tb[pl.ds(CV + 2 + q, D, stride=2), :]
         parts_t.append(with_row(block, tb[CV + 242 + q : CV + 243 + q, :]).T[:D, :])
-    pw_t = jnp.concatenate(parts_t, axis=0)
-    pw_ref[...] = (0.5 * pw_t).astype(bf16)
-    pwp_ref[...] = jnp.concatenate([pw_t, jnp.zeros((16, 128), f32)], axis=0).T[:, :240].astype(bf16)
-    block = with_row(tb[CV + 262 : CV + 382, :], tb[CV + 382 : CV + 383, :])
-    prp_ref[...] = (0.5 * block).astype(bf16)
-    pr_ref[...] = block.T.astype(bf16)
-
+    return jnp.concatenate(parts_t, axis=0)
+
+
+def fill_windows(tb, wt, wins):
     none = jnp.zeros((1, 128), f32)
     wins[...] = jnp.zeros_like(wins)
     for w, at, bias_at in ((0, AT + 2, AT + 122), (1, AT + 123, None), (2, AT + 243, AT + 363)):
@@ -253,17 +343,25 @@
         for to, r, src, many in segments():
             start = WROWS * w + to - WIN[r]
             wins[r, start : start + many, :] = wt[src : src + many, :]
-    for r in range(GROUP):
-        made = wins[r]
-        wqkv_ref[r] = made[: 3 * WROWS].astype(bf16)
-        wqkvt_ref[r] = made.T[:, : 3 * WROWS].astype(bf16)
-    wt[...] = with_row(tb[AT + 364 : AT + 484, :], none)
+
+
+def fill_output(tb, wins):
     wins[:, 0:256, :] = jnp.zeros((GROUP, 256, 128), f32)
     for to, r, src, many in segments():
         start = to - WIN[r]
-        wins[r, start : start + many, :] = wt[src : src + many, :]
+        wins[r, start : start + many, :] = tb[AT + 364 + src : AT + 364 + src + many, :]
+
+
+def early_body(me_ref, g_ref, up_ref, dn_ref, wqkv_ref, wo_ref, pw_ref, cols_ref, base_ref, flat, tb, wt, wins, rows):
+    unpack(me_ref, g_ref, flat, tb)
+    up_ref[...] = (0.5 * up_rows(tb, F1)).astype(bf16)
+    dn_ref[...] = down_across(tb, F1)
+    pw_ref[...] = (0.5 * point_rows(tb)).astype(bf16)
+    fill_windows(tb, wt, wins)
     for r in range(GROUP):
-        wob_ref[r] = wins[r, 0:WROWS, :].astype(bf16)
+        wqkv_ref[r] = wins[r, : 3 * WROWS].astype(bf16)
+    fill_output(tb, wins)
+    for r in range(GROUP):
         wins[r, MARKS[r] : MARKS[r] + 1, :] = tb[AT + 484 : AT + 485, :]
         wo_ref[r] = wins[r, 0:256, :].T[:, :WROWS].astype(bf16)
 
@@ -280,21 +378,40 @@
     lanes = lane_iota((1, 128))
     for h in range(HEADS):
         at = REL_AT + (2 * REL + 1) * h
-        first, col = at // 128, at % 128
+        first_row, col = at // 128, at % 128
         pieces = []
         for k in range(2):
-            got = jnp.where(lanes >= col, flat[first + k : first + k + 1, :], flat[first + k + 1 : first + k + 2, :])
+            here = flat[first_row + k : first_row + k + 1, :]
+            got = jnp.where(lanes >= col, here, flat[first_row + k + 1 : first_row + k + 2, :])
             pieces.append(pltpu.roll(got, (128 - col) % 128, 1) if col else got)
         rel_rows.append(jnp.concatenate(pieces, axis=1))
     rel = jnp.concatenate(rel_rows + [jnp.zeros((4, 256), f32)], axis=0)
     rel = jnp.where(lane_iota((8, 256)) < 2 * REL + 1, rel, 0.0)
-    base = dot(rel.astype(bf16), distance_select()) * LOG2E
-    for h in range(HEADS):
-        spread = jnp.broadcast_to(base[h : h + 1, :], (LG, 2 * LG))
-        tab_ref[h] = pltpu.roll(spread, 0, 1, stride=1, stride_axis=0)[:, :LG]
-    t = row_iota((384, 384))
-    c = lane_iota((384, 384))
-    pm_ref[...] = jnp.where(t == GROUP * (c % 128) + c // 128, 1.0, 0.0).astype(bf16)
+    base_ref[...] = dot(rel.astype(bf16), distance_select()) * LOG2E
+
+
+def late_body(
+    me_ref, g_ref, upp1_ref, dnp1_ref, up2_ref, upp2_ref, dn2_ref, dnp2_ref, pwp_ref, pr_ref, prp_ref, wqkvt_ref, wob_ref,
+    flat, tb, wt, wins,
+):
+    unpack(me_ref, g_ref, flat, tb)
+    upp1_ref[...] = up_across(up_rows(tb, F1))
+    dnp1_ref[...] = (0.25 * tb[F1 + 486 : F1 + 966, :]).astype(bf16)
+    up_t = up_rows(tb, F2)
+    up2_ref[...] = (0.5 * up_t).astype(bf16)
+    upp2_ref[...] = up_across(up_t)
+    dn2_ref[...] = down_across(tb, F2)
+    dnp2_ref[...] = (0.25 * tb[F2 + 486 : F2 + 966, :]).astype(bf16)
+    pwp_ref[...] = jnp.concatenate([point_rows(tb), jnp.zeros((16, 128), f32)], axis=0).T[:, :240].astype(bf16)
+    block = with_row(tb[CV + 262 : CV + 382, :], tb[CV + 382 : CV + 383, :])
+    prp_ref[...] = (0.5 * block).astype(bf16)
+    pr_ref[...] = block.T.astype(bf16)
+    fill_windows(tb, wt, wins)
+    for r in range(GROUP):
+        wqkvt_ref[r] = wins[r].T[:, : 3 * WROWS].astype(bf16)
+    fill_output(tb, wins)
+    for r in range(GROUP):
+        wob_ref[r] = wins[r, 0:WROWS, :].astype(bf16)
 
 
 def distance_select():
@@ -318,34 +435,33 @@
     return wide
 
 
-SMEM = pl.BlockSpec(memory_space=pltpu.SMEM)
-
-
 def prepare(me, gathered):
     total = gathered.shape[0] * gathered.shape[1]
-
-    def o(shape, kind=bf16):
-        return jax.ShapeDtypeStruct(shape, kind)
-
-    ffn = [o((FF, 128)), o((128, FF)), o((128, 512)), o((FF, 128))]
-    return pl.pallas_call(
-        prepare_body,
-        in_specs=[SMEM, pl.BlockSpec(memory_space=pltpu.VMEM)],
-        out_shape=ffn
-        + ffn
-        + [o((240, 128)), o((128, 240)), o((128, 128)), o((128, 128))]
-        + [o((GROUP, 3 * WROWS, 128)), o((GROUP, 128, 3 * WROWS)), o((GROUP, 128, WROWS)), o((GROUP, WROWS, 128))]
-        + [o((128, 128), f32), o((HEADS, LG, LG), f32), o((384, 384))],
-        scratch_shapes=[
-            pltpu.VMEM((total, 128), f32),
-            pltpu.VMEM((TABLE, 128), f32),
-            pltpu.VMEM((128, 128), f32),
-            pltpu.VMEM((GROUP, 512, 128), f32),
-            pltpu.VMEM((128, 128), f32),
-        ],
-        compiler_params=pltpu.CompilerParams(vmem_limit_bytes=VMEM_BYTES),
+    room = [
+        pltpu.VMEM((total, 128), f32),
+        pltpu.VMEM((TABLE, 128), f32),
+        pltpu.VMEM((128, 128), f32),
+        pltpu.VMEM((GROUP, 512, 128), f32),
+    ]
+    early = pl.pallas_call(
+        early_body,
+        in_specs=[SMEM, VMEM],
+        out_shape=[o((FF, 128)), o((128, 512)), o((GROUP, 3 * WROWS, 128)), o((GROUP, 128, WROWS)), o((240, 128))]
+        + [o((128, 128), f32), o((8, 2 * LG), f32)],
+        scratch_shapes=room + [pltpu.VMEM((128, 128), f32)],
         name="prepare",
+        **params(10**9, 2 * 10**6),
     )(me, gathered)
+    late = pl.pallas_call(
+        late_body,
+        in_specs=[SMEM, VMEM],
+        out_shape=[o((128, FF)), o((FF, 128)), o((FF, 128)), o((128, FF)), o((128, 512)), o((FF, 128))]
+        + [o((128, 240)), o((128, 128)), o((128, 128)), o((GROUP, 128, 3 * WROWS)), o((GROUP, WROWS, 128))],
+        scratch_shapes=room,
+        name="late",
+        **params(3 * 10**9, 10 * 10**6),
+    )(me, gathered)
+    return early, late
 
 
 def column(cols, k):
@@ -370,10 +486,10 @@
 
 
 def first_body(
-    len_ref, x_ref, cols_ref, up_ref, dn_ref, wqkv_ref, wo_ref, pw_ref, tab_ref, pm_ref,
-    xf_ref, lf_ref, xa_ref, nrm_ref, qkv_ref, prob_ref, att_ref, aa_ref, xc_ref, cn_ref, gat_ref, sig_ref, rgt_ref,
+    len_ref, xp_ref, xf_ref, cols_ref, up_ref, dn_ref, wqkv_ref, wo_ref, pw_ref, base_ref,
+    lf_ref, xa_ref, nrm_ref, qkv_ref, prob_ref, att_ref, aa_ref, xc_ref, cn_ref, gat_ref, sig_ref, rgt_ref,
     rs_ref, dep_ref, st_ref,
-    hid, xp, one, cb, run,
+    hid, one, cb, tab, run,
 ):
     u = pl.program_id(0)
     length = len_ref[u]
@@ -383,15 +499,14 @@
         set_tail(hid)
         run[...] = jnp.zeros_like(run)
         conv_columns(cols_ref, cb)
-
-    xp[...] = permute_in(x_ref[0].astype(f32), pm_ref[...])
+        for h in range(HEADS):
+            spread = jnp.broadcast_to(base_ref[h : h + 1, :], (LG, 2 * LG))
+            tab[h] = pltpu.roll(spread, 0, 1, stride=1, stride_axis=0)[:, :LG]
+
     cols = cols_ref
 
     def ffn_up(r, held):
-        xhat, rstd = norm(xp[:, span(r)])
-        xf_ref[0, :, span(r)] = xhat
-        rs_ref[0, 0:1, span(r)] = rstd
-        low = ext(xhat * column(cols, C_F1) + column(cols, C_F1 + 1))
+        low = ext(xf_ref[0, :, span(r)] * column(cols, C_F1) + column(cols, C_F1 + 1))
         lf_ref[0, :, span(r)] = low
         return dot(up_ref[...], low)
 
@@ -400,7 +515,7 @@
         return dot(dn_ref[...], hid[:, span(r)])[:D]
 
     def ffn_norm(r, branch):
-        after = xp[:, span(r)] + branch
+        after = xp_ref[0, :, span(r)].astype(f32) + branch
         one[:, span(r)] = after
         xhat, rstd = norm(after)
         xa_ref[0, :, span(r)] = xhat
@@ -427,18 +542,20 @@
         return dot_tn(qkv_ref[0, rows(1, h), :], qkv_ref[0, rows(0, h), :])
 
     def soften(h, raw):
-        scores = raw * (SCALE * LOG2E) + tab_ref[h]
+        scores = raw * (SCALE * LOG2E) + tab[h]
         scores = jnp.where(keys, scores, NEG_FILL * LOG2E)
         peak = jnp.max(scores, axis=0, keepdims=True)
         power = jnp.exp2(scores - peak)
         total = jnp.sum(power, axis=0, keepdims=True)
         prob_ref[0, h] = (power * (1.0 / total)).astype(bf16)
+
+    def mix(h, held):
         mixed = dot(qkv_ref[0, rows(2, h), :], prob_ref[0, h])
         if h < GROUP:
             mixed = jnp.where(row_iota((HP, LG)) == HEAD, 1.0, mixed)
         att_ref[0, rows(0, h), :] = mixed.astype(bf16)
 
-    skewed(HEADS, (score, soften))
+    skewed(HEADS, (score, soften, mix))
 
     def project(r, held):
         return dot(wo_ref[r], window(att_ref.at[0], r))[:D]
@@ -463,18 +580,22 @@
 
     skewed(GROUP, (project, gate_in, gate_out))
 
-    def shift(f, held):
-        return shifted_planes([gat_ref[0, 8 * f : 8 * f + 8, span(r)] for r in range(GROUP)])
-
-    def taps(f, moved):
+    def conv(f, carry):
         at = slice(8 * f, 8 * f + 8)
+        tiles = [gat_ref[0, at, span(r)] for r in range(GROUP)]
+        totals = [wide(cb[0, at, :])] * GROUP
+        for m in range(-HALF, HALF + GROUP):
+            here = shifted(tiles, m)
+            for r in range(GROUP):
+                k = m + HALF - r
+                if 0 <= k < KERNEL:
+                    totals[r] = totals[r] + wide(cb[1 + k, at, :]) * here
         for r in range(GROUP):
-            total = wide(cb[0, at, :])
-            for k in range(KERNEL):
-                total = total + wide(cb[1 + k, at, :]) * moved[r + k - HALF]
-            dep_ref[0, at, span(r)] = total
-
-    skewed(D // 8, (shift, taps))
+            dep_ref[0, at, span(r)] = totals[r]
+        return carry
+
+    for f in range(D // 8):
+        conv(f, 0)
 
     count = length.astype(f32)
     mask = jnp.concatenate([plane_mask(r, length) for r in range(GROUP)], axis=1)
@@ -500,60 +621,47 @@
             st_ref[d] = line
 
 
-def whole(shape):
-    zeros = (0,) * len(shape)
-    return pl.BlockSpec(shape, lambda u: zeros)
-
-
-def per_utt(shape):
-    zeros = (0,) * len(shape)
-    return pl.BlockSpec((1,) + shape, lambda u: (u,) + zeros)
-
-
-def first(devices, lengths, x, weights):
-    utts = x.shape[0]
-    big = (D, MAXLEN)
-    low = (128, MAXLEN)
+def first(devices, lengths, xp, xf, weights):
+    utts = xp.shape[0]
     per = [
-        (big, f32),
-        (low, bf16),
-        (big, f32),
+        (LOW, bf16),
+        (BIG, f32),
         ((GP, LG), bf16),
         ((3 * GP, LG), bf16),
         ((HEADS, LG, LG), bf16),
         ((GP, LG), bf16),
-        (big, f32),
-        (big, f32),
-        (low, bf16),
-        (big, f32),
-        (big, f32),
-        (big, f32),
+        (BIG, f32),
+        (BIG, f32),
+        (LOW, bf16),
+        (BIG, f32),
+        (BIG, f32),
+        (BIG, f32),
         ((8, MAXLEN), f32),
-        (big, f32),
+        (BIG, f32),
     ]
     line = (devices, 8, 128)
     return pl.pallas_call(
         first_body,
         grid=(utts,),
-        in_specs=[SMEM, per_utt(big)] + [whole(w.shape) for w in weights],
+        in_specs=[SMEM, per_utt(BIG), per_utt(BIG)] + [whole(w.shape) for w in weights],
         out_specs=[per_utt(s) for s, k in per] + [whole(line)],
-        out_shape=[jax.ShapeDtypeStruct((utts,) + s, k) for s, k in per] + [jax.ShapeDtypeStruct(line, f32)],
+        out_shape=[o((utts,) + s, k) for s, k in per] + [o(line, f32)],
         scratch_shapes=[
             pltpu.VMEM((512, MAXLEN), bf16),
-            pltpu.VMEM(big, f32),
-            pltpu.VMEM(big, f32),
+            pltpu.VMEM(BIG, f32),
             pltpu.VMEM((KERNEL + 1, D, 128), f32),
+            pltpu.VMEM((HEADS, LG, LG), f32),
             pltpu.VMEM((3, D, 128), f32),
         ],
-        compiler_params=pltpu.CompilerParams(vmem_limit_bytes=VMEM_BYTES),
         name="first",
-    )(lengths, x, *weights)
+        **params(10 * 10**9, 60 * 10**6),
+    )(lengths, xp, xf, *weights)
 
 
 def second_body(
-    len_ref, stats_ref, cot_ref, aa_ref, dep_ref, cols_ref, up_ref, upp_ref, dn_ref, dnp_ref, pr_ref, prp_ref, pm_ref,
+    len_ref, stats_ref, cot_ref, aa_ref, dep_ref, cols_ref, up_ref, upp_ref, dn_ref, dnp_ref, pr_ref, prp_ref,
     out_ref, bgd_ref, gc_ref, sums_ref, stc_ref, gdn_ref, gup_ref, gpr_ref, vec_ref,
-    hid, cotp, outp, acc,
+    hid, acc,
 ):
     u = pl.program_id(0)
     length = len_ref[u]
@@ -586,7 +694,6 @@
         vec_ref[...] = jnp.zeros_like(vec_ref)
         acc[...] = jnp.zeros_like(acc)
 
-    cotp[...] = permute_in(cot_ref[0].astype(f32), pm_ref[...])
     half_gain = 0.5 * column(cols, C_BN)
     half_bias = 0.5 * column(cols, C_BN + 1)
 
@@ -617,8 +724,9 @@
         act_low, normal, slope, after_conv, xhat, rstd, low, bend, branch = held
         mask = plane_mask(r, length)
         xhat_f, rstd_f = norm(after_conv + branch)
-        outp[:, span(r)] = (xhat_f * column(cols, C_FN) + column(cols, C_FN + 1)) * mask
-        up_grad = cotp[:, span(r)] * mask
+        made = (xhat_f * column(cols, C_FN) + column(cols, C_FN + 1)) * mask
+        out_ref[0, :, span(r)] = made.astype(bf16)
+        up_grad = cot_ref[0, :, span(r)].astype(f32) * mask
         vec_ref[2] += fold(up_grad * xhat_f)
         vec_ref[3] += fold(up_grad)
         grad_two = norm_back(up_grad, xhat_f, rstd_f, column(cols, C_FN))
@@ -650,7 +758,6 @@
         acc[1] += fold(batch)
 
     skewed(GROUP, (enter, ffn_up, ffn_down, finish, ffn_back, leave, last))
-    out_ref[0] = permute_out(outp[...], pm_ref[...]).astype(bf16)
 
     @pl.when(u == pl.num_programs(0) - 1)
     def _():
@@ -680,20 +787,18 @@
         out_shape=[jax.ShapeDtypeStruct(o[1], o[2]) for o in outs],
         scratch_shapes=[
             pltpu.VMEM((512, MAXLEN), bf16),
-            pltpu.VMEM(big, f32),
-            pltpu.VMEM(big, f32),
             pltpu.VMEM((2, D, 128), f32),
         ],
-        compiler_params=pltpu.CompilerParams(vmem_limit_bytes=VMEM_BYTES),
         name="second",
+        **params(15000000000, 30000000),
     )(lengths, stats, cot, aa, dep, *weights)
 
 
 def third_body(
     len_ref, sums_ref, stc_ref, bgd_ref, gc_ref, dep_ref, xf_ref, lf_ref, xa_ref, nrm_ref, qkv_ref, prob_ref, att_ref, xc_ref,
     cn_ref, gat_ref, sig_ref, rgt_ref, rs_ref,
-    cols_ref, up_ref, upp_ref, dnp_ref, wqkv_t_ref, wob_ref, pwp_ref, pm_ref,
-    gin_ref, gdn_ref, gup_ref, gpw_ref, gqkv_ref, go_ref, rel_ref, vec_ref,
+    cols_ref, up_ref, upp_ref, dnp_ref, wqkv_t_ref, wob_ref, pwp_ref,
+    grad_ref, back_ref, gdn_ref, gup_ref, gpw_ref, gqkv_ref, go_ref, rel_ref, vec_ref,
     hid, dgs, olg, agr, back_s, gg, relacc, cb, tot,
 ):
     u = pl.program_id(0)
@@ -722,28 +827,30 @@
         mask = plane_mask(r, length)
         dgs[:, span(r)] = bgd_ref[0, :, span(r)] * lead - mask * (shift_part + normal * gain_part)
 
-    def shift(f, held):
-        return shifted_planes([dgs[8 * f : 8 * f + 8, span(r)] for r in range(GROUP)])
-
-    def taps(f, moved):
+    def conv(f, carry):
         at = slice(8 * f, 8 * f + 8)
+        tiles = [dgs[at, span(r)] for r in range(GROUP)]
         gated = [gat_ref[0, at, span(r)] for r in range(GROUP)]
         totals = [None] * GROUP
+        taps = [None] * KERNEL
+        for m in range(-HALF, HALF + GROUP):
+            here = shifted(tiles, m)
+            for r in range(GROUP):
+                k = r + HALF - m
+                if 0 <= k < KERNEL:
+                    term = wide(cb[1 + k, at, :]) * here
+                    totals[r] = term if totals[r] is None else totals[r] + term
+                    part = fold(gated[r] * here)
+                    taps[k] = part if taps[k] is None else taps[k] + part
+        vec_ref[6, at, :] += fold(tiles[0] + tiles[1] + tiles[2])
         for k in range(KERNEL):
-            weight = wide(cb[1 + k, at, :])
-            tap = None
-            for r in range(GROUP):
-                here = moved[r - k + HALF]
-                term = weight * here
-                totals[r] = term if totals[r] is None else totals[r] + term
-                part = gated[r] * here
-                tap = part if tap is None else tap + part
-            vec_ref[7 + k, at, :] += fold(tap)
-        vec_ref[6, at, :] += fold(moved[0] + moved[1] + moved[2])
+            vec_ref[7 + k, at, :] += taps[k]
         for r in range(GROUP):
             gg[at, span(r)] = totals[r]
-
-    skewed(D // 8, (shift, taps))
+        return carry
+
+    for f in range(D // 8):
+        conv(f, 0)
 
     def gate(r, held):
         grad = gg[:, span(r)]
@@ -785,11 +892,13 @@
         inner = jnp.sum(probs * prob_grad, axis=0, keepdims=True)
         score = probs * (prob_grad - inner)
         relacc[h] += score
-        low = score.astype(bf16)
+        return score.astype(bf16)
+
+    def turn(h, low):
         back_s[rows(0, h), :] = (dot(qkv_ref[0, rows(1, h), :], low) * SCALE).astype(bf16)
         back_s[rows(1, h), :] = (dot_nt(qkv_ref[0, rows(0, h), :], low) * SCALE).astype(bf16)
 
-    skewed(HEADS, (enter, soften))
+    skewed(HEADS, (enter, soften, turn))
 
     def project(r, held):
         stack = jnp.concatenate([window(back_s, r, GP * w) for w in range(3)], axis=0)
@@ -802,27 +911,25 @@
         vec_ref[2] += fold(back * xhat)
         vec_ref[3] += fold(back)
         grad = dgs[:, span(r)] + norm_back(back, xhat, rs_ref[0, 1:2, span(r)], column(cols, C_AT))
+        grad_ref[0, :, span(r)] = grad
         low = pad8(grad).astype(bf16)
-        return grad, low, half, dot(dnp_ref[...], low)
+        return low, half, dot(dnp_ref[...], low)
 
     def ffn_mid(r, held):
-        grad, branch, half, back = held
+        branch, half, back = held
         t = jnp.tanh(half)
         hid[:FF, span(r)] = (half + half * t).astype(bf16)
         pre_low = ((1.0 + t) * (1.0 + half * (1.0 - t)) * back).astype(bf16)
         gdn_ref[...] += dot_nt(hid[:, span(r)], branch)
         gup_ref[...] += dot_nt(pre_low, lf_ref[0, :, span(r)])
-        return grad, dot(upp_ref[...], pre_low)[:D]
-
-    def ffn_out(r, held):
-        grad, back = held
-        xhat = xf_ref[0, :, span(r)]
-        vec_ref[4] += fold(back * xhat)
+        return dot(upp_ref[...], pre_low)[:D]
+
+    def ffn_out(r, back):
+        back_ref[0, :, span(r)] = back
+        vec_ref[4] += fold(back * xf_ref[0, :, span(r)])
         vec_ref[5] += fold(back)
-        gg[:, span(r)] = grad + norm_back(back, xhat, rs_ref[0, 0:1, span(r)], column(cols, C_F1))
 
     skewed(GROUP, (project, ffn_in, ffn_mid, ffn_out))
-    gin_ref[0] = permute_out_wide(gg[...], pm_ref[...])
 
     @pl.when(u == pl.num_programs(0) - 1)
     def _():
@@ -841,7 +948,7 @@
 def third(lengths, sums, stc, saved, weights):
     utts = saved[0].shape[0]
     big = (D, MAXLEN)
-    outs = [(per_utt(big), (utts,) + big)]
+    outs = [(per_utt(big), (utts,) + big)] * 2
     for s in ((512, 128), (FF, 128), (240, 128), (GROUP, 3 * WROWS, 128), (GROUP, WROWS, 128), (8, 256), (22, D, 128)):
         outs.append((whole(s), s))
     return pl.pallas_call(
@@ -863,42 +970,86 @@
             pltpu.VMEM((KERNEL + 1, D, 128), f32),
             pltpu.VMEM((128, 128), f32),
         ],
-        compiler_params=pltpu.CompilerParams(vmem_limit_bytes=VMEM_BYTES),
         name="third",
+        **params(20000000000, 80000000),
     )(lengths, sums, stc, *saved, *weights)
 
 
+def clean(block):
+    return jnp.where(lane_iota(block.shape) < D, block, 0.0)
+
+
+def set_rows(tb, wt, ref, at):
+    lanes = lane_iota((D, 128))
+    table = jnp.zeros((D, 128), f32)
+    for k in range(len(at)):
+        table = jnp.where(lanes == k, jnp.sum(ref[k], axis=1, keepdims=True), table)
+    wt[...] = pad8(table).T
+    for k, to in enumerate(at):
+        tb[to : to + 1, :] = wt[k : k + 1, :]
+
+
+def set_ffn(tb, base, dn_ref, up_ref):
+    tb[base + 486 : base + 967, :] = 0.5 * clean(dn_ref[0 : FF + 1, :])
+    for q in range(4):
+        block = pad8(up_ref[D * q : D * q + D, :]).T
+        tb[pl.ds(base + 2 + q, D, stride=4), :] = block[:D]
+        tb[base + 482 + q : base + 483 + q, :] = block[D : D + 1]
+
+
+def flatten(tb, base, flat, at_row, y_count, offset):
+    for k in range(15):
+        at = 128 * k + offset
+        first_row, col = at // D, at % D
+        many = (y_count - k + 14) // 15
+        here = lane_iota((many, 128))
+        got = tb[pl.ds(base + first_row, many, stride=16), :]
+        if col:
+            got = pltpu.roll(got, 128 - col, 1)
+        then = pltpu.roll(tb[pl.ds(base + first_row + 1, many, stride=16), :], D - col, 1)
+        got = jnp.where(here < D - col, got, then)
+        if 2 * D - col < 128:
+            then = pltpu.roll(tb[pl.ds(base + first_row + 2, many, stride=16), :], 2 * D - col, 1)
+            got = jnp.where(here < 2 * D - col, got, then)
+        flat[pl.ds(at_row + k, many, stride=15), :] = got
+
+
+SPLIT = F2 - TAIL
+ROWS_LAST = ROWS_TAIL - SPLIT
+LAST_AT = TAIL_AT + D * SPLIT
+LAST_Y = LAST_AT // 128
+LAST_COUNT = (LIVE - 1) // 128 - LAST_Y + 1
+
+
+def ahead_body(dn_ref, up_ref, vec_ref, out_ref, tb, wt):
+    tb[0:8, :] = jnp.zeros((8, 128), f32)
+    tb[8 + ROWS_LAST :, :] = jnp.zeros((tb.shape[0] - 8 - ROWS_LAST, 128), f32)
+    set_rows(tb, wt, vec_ref, (8, 9, 8 + FN - F2, 9 + FN - F2))
+    set_ffn(tb, 8, dn_ref, up_ref)
+    flatten(tb, 7, out_ref, 0, LAST_COUNT, D + 128 * LAST_Y - LAST_AT)
+
+
+def pack_ahead(dn, up, vec):
+    return pl.pallas_call(
+        ahead_body,
+        out_shape=o((LAST_COUNT, 128), f32),
+        scratch_shapes=[pltpu.VMEM((ROWS_LAST + 24, 128), f32), pltpu.VMEM((128, 128), f32)],
+        name="ahead",
+        **params(2 * 10**9, 8 * 10**6),
+    )(dn, up, vec)
+
+
 def pack_body(
-    me_ref, dn1_ref, up1_ref, dn2_ref, up2_ref, pr_ref, pw_ref, qkv_ref, o_ref, rel_ref, vecs2_ref, vecs3_ref, sums_ref,
+    me_ref, last_ref, dn1_ref, up1_ref, pr_ref, pw_ref, qkv_ref, o_ref, rel_ref, vec_ref, sums_ref,
     keep_ref, send_ref, tb, flat, stage, wt,
 ):
-    tb[...] = jnp.zeros_like(tb)
-    flat[...] = jnp.zeros_like(flat)
-    lanes = lane_iota((D, 128))
-    table = jnp.zeros((D, 128), f32)
-    listed = []
-    for ref, at in (
-        (vecs2_ref, (F2, F2 + 1, FN, FN + 1)),
-        (vecs3_ref, (CV, CV + 1, AT, AT + 1, F1, F1 + 1, CV + 259) + tuple(CV + 244 + k for k in range(KERNEL))),
-    ):
-        for k, to in enumerate(at):
-            table = jnp.where(lanes == len(listed), jnp.sum(ref[k], axis=1, keepdims=True), table)
-            listed.append(to)
-    wt[...] = pad8(table).T
-    keep = lane_iota((1, 128)) < D
-    for k, to in enumerate(listed):
-        tb[to : to + 1, :] = wt[k : k + 1, :]
+    tb[ROWS_HEAD:TAIL, :] = jnp.zeros((TAIL - ROWS_HEAD, 128), f32)
+    tb[F2:, :] = jnp.zeros((tb.shape[0] - F2, 128), f32)
+    set_rows(
+        tb, wt, vec_ref, (CV, CV + 1, AT, AT + 1, F1, F1 + 1, CV + 259) + tuple(CV + 244 + k for k in range(KERNEL))
+    )
     tb[CV + 260 : CV + 262, :] = sums_ref[0, 0:2, :]
-
-    def clean(block):
-        return jnp.where(lane_iota(block.shape) < D, block, 0.0)
-
-    for base, dn_ref, up_ref in ((F1, dn1_ref, up1_ref), (F2, dn2_ref, up2_ref)):
-        tb[base + 486 : base + 967, :] = 0.5 * clean(dn_ref[0 : FF + 1, :])
-        for q in range(4):
-            block = pad8(up_ref[D * q : D * q + D, :]).T
-            tb[pl.ds(base + 2 + q, D, stride=4), :] = block[:D]
-            tb[base + 482 + q : base + 483 + q, :] = block[D : D + 1]
+    set_ffn(tb, F1, dn1_ref, up1_ref)
     for q in range(2):
         block = pad8(pw_ref[D * q : D * q + D, :]).T
         tb[pl.ds(CV + 2 + q, D, stride=2), :] = block[:D]
@@ -919,27 +1070,15 @@
             tb[bias_at : bias_at + 1, :] = block[D : D + 1]
     tb[AT + 364 : AT + 484, :] = clean(gathered(o_ref, 0)[:D])
     bias = sum(o_ref[r, MARKS[r] : MARKS[r] + 1, :] for r in range(GROUP))
-    tb[AT + 484 : AT + 485, :] = jnp.where(keep, bias, 0.0)
-
-    last = (LIVE - 1) // 128
-    for y_first, y_count, offset, base in (
-        (0, REL_AT // 128 + 1, 0, 0),
-        (TAIL_AT // 128, last - TAIL_AT // 128 + 1, 128 * (TAIL_AT // 128) - TAIL_AT + D, TAIL - 1),
-    ):
-        for k in range(15):
-            at = 128 * k + offset
-            first_row, col = at // D, at % D
-            many = (y_count - k + 14) // 15
-            here = lane_iota((many, 128))
-            got = tb[pl.ds(base + first_row, many, stride=16), :]
-            if col:
-                got = pltpu.roll(got, 128 - col, 1)
-            then = pltpu.roll(tb[pl.ds(base + first_row + 1, many, stride=16), :], D - col, 1)
-            got = jnp.where(here < D - col, got, then)
-            if 2 * D - col < 128:
-                then = pltpu.roll(tb[pl.ds(base + first_row + 2, many, stride=16), :], 2 * D - col, 1)
-                got = jnp.where(here < 2 * D - col, got, then)
-            flat[pl.ds(y_first + k, many, stride=15), :] = got
+    tb[AT + 484 : AT + 485, :] = clean(bias)
+
+    tail_y = TAIL_AT // 128
+    flat[LAST_Y + LAST_COUNT :, :] = jnp.zeros((flat.shape[0] - LAST_Y - LAST_COUNT, 128), f32)
+    flat[REL_AT // 128 + 1 : tail_y, :] = jnp.zeros((tail_y - REL_AT // 128 - 1, 128), f32)
+    flatten(tb, 0, flat, 0, REL_AT // 128 + 1, 0)
+    flatten(tb, TAIL - 1, flat, tail_y, LAST_Y - tail_y + 1, 128 * tail_y - TAIL_AT + D)
+    flat[LAST_Y : LAST_Y + 1, :] += last_ref[0:1, :]
+    flat[LAST_Y + 1 : LAST_Y + LAST_COUNT, :] = last_ref[1:, :]
     here = lane_iota((1, 128))
     width = 2 * REL + 1
     for h in range(HEADS):
@@ -960,19 +1099,19 @@
 
 
 def pack(parts, rows, me, grads):
-    half = jax.ShapeDtypeStruct((parts // 2, rows, 128), f32)
+    half = o((parts // 2, rows, 128), f32)
     return pl.pallas_call(
         pack_body,
-        in_specs=[SMEM] + [pl.BlockSpec(memory_space=pltpu.VMEM)] * len(grads),
+        in_specs=[SMEM] + [VMEM] * len(grads),
         out_shape=[half, half],
         scratch_shapes=[
-            pltpu.VMEM((TABLE, 128), f32),
+            pltpu.VMEM((F2 + 24, 128), f32),
             pltpu.VMEM((parts * rows, 128), f32),
             pltpu.VMEM((parts, rows, 128), f32),
             pltpu.VMEM((128, 128), f32),
         ],
-        compiler_params=pltpu.CompilerParams(vmem_limit_bytes=VMEM_BYTES),
         name="pack",
+        **params(10**9, 5 * 10**6),
     )(me, *grads)
 
 
@@ -1015,11 +1154,15 @@
     return lax.ppermute(values, "dp", [(i, i ^ offset) for i in range(devices)])
 
 
-def gather(values, devices):
+def gather(values, devices, beside):
     held = values[None]
     for stride, size in reversed(digits(devices)):
-        held = jnp.concatenate([held] + [partner(held, stride * j, devices) for j in range(1, size)], axis=0)
-    return held
+        parts = [held] + [partner(held, stride * j, devices) for j in range(1, size)]
+        if beside is not None:
+            parts, made = lax.optimization_barrier((parts, beside))
+            beside = None
+        held = jnp.concatenate(parts, axis=0)
+    return held, made
 
 
 def scatter_sum(keep, send, devices):
@@ -1037,26 +1180,27 @@
     devices = lax.axis_size("dp")
     rows = shard_len // 128
     me = lax.axis_index("dp").astype(jnp.int32).reshape(1)
-    gathered = gather(master.astype(bf16).reshape(rows, 128), devices)
-    (
-        up1, upp1, dn1, dnp1, up2, upp2, dn2, dnp2, pw, pwp, pr, prp, wqkv, wqkvt, wo, wob, cols, tab, pm,
-    ) = prepare(me, gathered)
-    x = jnp.transpose(frames, (0, 2, 1))
-    cot = jnp.transpose(cotangent, (0, 2, 1))
-    xf, lf, xa, nrm, qkv, prob, att, aa, xc, cn, gat, sig, rgt, rs, dep, st = first(
-        devices, lengths, x, (cols, up1, dn1, wqkv, wo, pw, tab, pm)
+    entered = enter(jnp.transpose(frames, (0, 2, 1)), jnp.transpose(cotangent, (0, 2, 1)))
+    gathered, (xp, cp, xf, rs_in, pm) = gather(master.astype(bf16).reshape(rows, 128), devices, entered)
+    early, late = prepare(me, gathered)
+    up1, dn1, wqkv, wo, pw, cols, base = early
+    upp1, dnp1, up2, upp2, dn2, dnp2, pwp, pr, prp, wqkvt, wob = late
+    lf, xa, nrm, qkv, prob, att, aa, xc, cn, gat, sig, rgt, rs, dep, st = first(
+        devices, lengths, xp, xf, (cols, up1, dn1, wqkv, wo, pw, base)
     )
     stats = lax.all_to_all(st, "dp", 0, 0)
     out, bgd, gc, sums, stc, gdn2, gup2, gpr, vec2 = second(
-        lengths, stats, cot, aa, dep, (cols, up2, upp2, dn2, dnp2, pr, prp, pm)
+        lengths, stats, cp, aa, dep, (cols, up2, upp2, dn2, dnp2, pr, prp)
     )
     all_sums = lax.all_to_all(sums, "dp", 0, 0)
-    gin, gdn1, gup1, gpw, gqkv, go, rel, vec3 = third(
+    last = pack_ahead(gdn2, gup2, vec2)
+    grad, back, gdn1, gup1, gpw, gqkv, go, rel, vec3 = third(
         lengths, all_sums, stc,
         (bgd, gc, dep, xf, lf, xa, nrm, qkv, prob, att, xc, cn, gat, sig, rgt, rs),
-        (cols, up1, upp1, dnp1, wqkvt, wob, pwp, pm),
+        (cols, up1, upp1, dnp1, wqkvt, wob, pwp),
     )
-    keep, send = pack(devices, rows, me, (gdn1, gup1, gdn2, gup2, gpr, gpw, gqkv, go, rel, vec2, vec3, sums))
+    keep, send = pack(devices, rows, me, (last, gdn1, gup1, gpr, gpw, gqkv, go, rel, vec3, sums))
+    out, gin = leave(out, grad, back, xf, rs_in, cols, pm)
     reduced = scatter_sum(keep, send, devices).reshape(shard_len)
     rates_np, decays_np = update_tables(shard_len * devices)
     start_at = lax.axis_index("dp") * shard_len

time: 196 us -> 198 us (1.010)
  blocking collectives: 23 us -> 0 us
  Pallas kernels: 123 us -> 138 us
  starting transfers between devices: 17.5 us -> 24.5 us
    all_to_all x2 -> x0, blocking collectives: 23 us -> none  [the longest x1 11.5 us: local(): stats = lax.all_to_all(st, 'dp', 0, 0)]
    pallas_call x3 -> x7, Pallas kernels: 47.2 us -> 67.2 us  [the longest x1 34.7 us: first(): pl.pallas_call(first_body, grid=(utts,), in_specs=[SMEM, per_utt(BIG), pe...]
    all_to_all x0 -> x2, waiting for transfers between devices: none -> 9.87 us  [the longest x1 5.43 us: local(): all_sums = lax.all_to_all(sums, 'dp', 0, 0)]
    ppermute x14, waiting for transfers between devices: 25.2 us -> 16.6 us  [partner(): return lax.ppermute(values, 'dp', [(i, i ^ offset) for i in range(devices)])]
    all_to_all x0 -> x2, starting transfers between devices: none -> 6.95 us  [the longest x1 4.16 us: local(): stats = lax.all_to_all(st, 'dp', 0, 0)]
    pallas_call x1, Pallas kernels: 52.7 us -> 49.1 us  [third(): pl.pallas_call(third_body, grid=(utts,), in_specs=[SMEM, whole(sums.shape...]
  transfers between devices with their start and end apart: 14 -> 16, of which waited for: 13 -> 10; matrix products, arithmetic and copies ran while one was open for 0% -> 0% of each run, Pallas kernels for 0% -> 12%
where the time goes in v2:
time: 198 us; the launch traced here: 197 us
  Pallas kernels  138 us (70%)
  waiting for transfers between devices  26.5 us (13%)
  starting transfers between devices  24.5 us (12%)
  other arithmetic  3.74 us (2%)
  local copies, waits for them, and re-layouts  3.69 us (2%)
    pallas_call x1, Pallas kernels, third(): pl.pallas_call(third_body, grid=(utts,), in_specs=[SMEM, whole(sums.shape...  49.1 us
    pallas_call x1, Pallas kernels, first(): pl.pallas_call(first_body, grid=(utts,), in_specs=[SMEM, per_utt(BIG), pe...  34.7 us
    pallas_call x1, Pallas kernels, second(): pl.pallas_call(second_body, grid=(utts,), in_specs=[SMEM, whole(stats.sha...  21.5 us
    ppermute x14, starting transfers between devices, partner(): return lax.ppermute(values, 'dp', [(i, i ^ offset) for i in range(devices)])  17.5 us
    ppermute x14, waiting for transfers between devices, partner(): return lax.ppermute(values, 'dp', [(i, i ^ offset) for i in range(devices)])  16.6 us
    pallas_call x1, Pallas kernels, leave(): pl.pallas_call(leave_body, grid=(utts,), in_specs=[per_utt(BIG)] * 4 + [p...  10.8 us
    pallas_call x1, Pallas kernels, enter(): pl.pallas_call(enter_body, grid=(utts,), in_specs=[per_utt(BIG)] * 2, out...  7.64 us
    all_to_all x1, waiting for transfers between devices, local(): all_sums = lax.all_to_all(sums, 'dp', 0, 0)  5.43 us
  transfers between devices with their start and end apart: 16, of which 10 were waited for; matrix products, arithmetic and copies ran while one was open for 0% of the time, Pallas kernels for 12%

profile of v2, /device:TPU:0, one launch (start us, length us, event | category | flops | bytes accessed | tf_op | source)
XLA Modules:
  0.0 197.0 jit_solution(5141545860394246068)
XLA Ops:
  0.6 0.8 convert_bitcast_fusion
  1.4 3.0 %collective-permute-start = (bf16[1,83,128]{2,1,0:T(8,128)(2,1)S(1)}, bf16[1,83,128]{2,1,0:T(8,128)(2,1)S(1)}, u32[]{:S(2)}, u32[]{:S(2)}) collective-permute-start(bf16[1,83,128]{2,1,0:T(8,128)(2,1)S(1)} %convert_bitcast_fusion), channel_id=1, source_target_pairs={{0,8},{1,9},{2,10},{3,11},{4,12},{5,13},{6,14},{7,15},{8,0},{9,1},... | collective-permute-start | bytes 63752 | tf_op jit(solution)/shard_map/ppermute | solution.py:1154
  4.5 2.6 %collective-permute-start.1 = (bf16[1,83,128]{2,1,0:T(8,128)(2,1)S(1)}, bf16[1,83,128]{2,1,0:T(8,128)(2,1)S(1)}, u32[]{:S(2)}, u32[]{:S(2)}) collective-permute-start(bf16[1,83,128]{2,1,0:T(8,128)(2,1)S(1)} %convert_bitcast_fusion), channel_id=1, source_target_pairs={{0,16},{1,17},{2,18},{3,19},{4,20},{5,21},{6,22},{7,23},{8,24},{9,... | collective-permute-start | bytes 63752 | tf_op jit(solution)/shard_map/ppermute | solution.py:1154
  7.0 0.0 collective-permute-start.2
  7.0 7.6 %enter.1 = (bf16[5,120,1536]{2,1,0:T(8,128)(2,1)}, bf16[5,120,1536]{2,1,0:T(8,128)(2,1)}, f32[5,120,1536]{2,1,0:T(8,128)}, f32[5,8,1536]{2,1,0:T(8,128)}, bf16[384,384]{1,0:T(8,128)(2,1)}) custom-call(bf16[5,120,1536]{2,1,0:T(8,128)(2,1)} %bitcast.11, bf16[5,120,1536]{2,1,0:T(8,128)(2,1)} %bitcast.12), custom_call_target="tpu_custom_call" | custom-call | flops 2000000000 | bytes 16000000 | tf_op jit(solution)/shard_map/enter/pallas_call | solution.py:257
  14.7 0.0 collective-permute-done
  14.7 0.0 collective-permute-done.1
  14.7 0.0 collective-permute-done.2
  14.8 1.8 collective-permute-start.3
  16.6 1.5 collective-permute-start.4
  18.1 0.3 collective-permute-start.5
  18.3 1.3 collective-permute-done.3
  19.7 2.3 %collective-permute-done.4 = bf16[4,83,128]{2,1,0:T(8,128)(2,1)S(1)} collective-permute-done((bf16[4,83,128]{2,1,0:T(8,128)(2,1)S(1)}, bf16[4,83,128]{2,1,0:T(8,128)(2,1)S(1)}, u32[]{:S(2)}, u32[]{:S(2)}) %collective-permute-start.4) | collective-permute-done | bytes 85024 | tf_op jit(solution)/shard_map/ppermute | solution.py:1154
  22.1 1.5 collective-permute-done.5
  23.6 0.1 collective-permute-start.6
  23.6 1.7 collective-permute-done.6
  25.3 0.1 constant_dynamic-update-slice_fusion.11.g_ref
  25.3 0.0 copy-start.6
  25.4 0.9 copy-done.6
  26.2 3.3 %prepare.1 = (bf16[480,128]{1,0:T(8,128)(2,1)}, bf16[128,512]{1,0:T(8,128)(2,1)}, bf16[3,432,128]{2,1,0:T(8,128)(2,1)}, bf16[3,128,144]{2,1,0:T(8,128)(2,1)}, bf...) custom-call(s32[1]{0:T(128)} %bitcast.3.me_ref, bf16[32,83,128]{2,1,0:T(8,128)(2,1)} %copy-done.6), custom_call_target="tpu_custom_call" | custom-call | flops 1000000000 | bytes 2000000 | tf_op jit(solution)/shard_map/prepare/pallas_call | solution.py:446
  29.5 34.7 %first.1 = (bf16[5,128,1536]{2,1,0:T(8,128)(2,1)}, f32[5,120,1536]{2,1,0:T(8,128)}, bf16[5,384,512]{2,1,0:T(8,128)(2,1)}, bf16[5,1152,512]{2,1,0:T(8,128)(2,1)},...) custom-call(s32[5]{0:T(128)} %len_ref.5, ...), custom_call_target="tpu_custom_call" | custom-call | flops 10000000000 | bytes 60000000 | tf_op jit(solution)/shard_map/first/pallas_call | solution.py:643
  64.2 4.2 %all-to-all-start = ((f32[32,8,128]{2,1,0:T(8,128)}), f32[32,8,128]{2,1,0:T(8,128)S(1)}, u32[]{:S(2)}, u32[]{:S(2)}) async-start(f32[32,8,128]{2,1,0:T(8,128)} %get-tuple-element.94), calls=%async_computation | async-start | bytes 262144 | tf_op jit(solution)/shard_map/all_to_all | solution.py:1191
  68.4 3.6 %late.1 = (bf16[128,480]{1,0:T(8,128)(2,1)}, bf16[480,128]{1,0:T(8,128)(2,1)}, bf16[480,128]{1,0:T(8,128)(2,1)}, bf16[128,480]{1,0:T(8,128)(2,1)}, bf16[128,512]...) custom-call(s32[1]{0:T(128)} %bitcast.3.me_ref, ...), custom_call_target="tpu_custom_call" | custom-call | flops 3000000000 | bytes 10000000 | tf_op jit(solution)/shard_map/late/pallas_call | solution.py:455
  72.0 4.4 %all-to-all-done.stats_ref = f32[32,8,128]{2,1,0:T(8,128)S(1)} async-done(((f32[32,8,128]{2,1,0:T(8,128)}), f32[32,8,128]{2,1,0:T(8,128)S(1)}, u32[]{:S(2)}, u32[]{:S(2)}) %all-to-all-start) | async-done | bytes 131104 | tf_op jit(solution)/shard_map/all_to_all | solution.py:1191
  76.4 0.0 copy-start.2
  76.4 0.7 copy-done.2
  77.1 21.5 %second.1 = (bf16[5,120,1536]{2,1,0:T(8,128)(2,1)}, f32[5,120,1536]{2,1,0:T(8,128)}, f32[5,120,1536]{2,1,0:T(8,128)}, f32[32,8,128]{2,1,0:T(8,128)}, f32[128,128...) custom-call(s32[5]{0:T(128)} %len_ref.5, ...), custom_call_target="tpu_custom_call" | custom-call | flops 15000000512 | bytes 30000000 | tf_op jit(solution)/shard_map/second/pallas_call | solution.py:782
  98.6 2.8 %all-to-all-start.1 = ((f32[32,8,128]{2,1,0:T(8,128)}), f32[32,8,128]{2,1,0:T(8,128)S(1)}, u32[]{:S(2)}, u32[]{:S(2)}) async-start(f32[32,8,128]{2,1,0:T(8,128)} %get-tuple-element.105.sums_ref), calls=%async_computation.1 | async-start | bytes 262144 | tf_op jit(solution)/shard_map/all_to_all | solution.py:1195
  101.4 2.6 %ahead.1.last_ref = f32[909,128]{1,0:T(8,128)} custom-call(f32[512,128]{1,0:T(8,128)} %get-tuple-element.132.dn_ref, f32[480,128]{1,0:T(8,128)} %get-tuple-element.133.up_ref, f32[4,120,128]{2,1,0:T(8,128)} %get-tuple-element.134.vec_ref), custom_call_target="tpu_custom_call" | custom-call | flops 2000000000 | bytes 8000000 | tf_op jit(solution)/shard_map/ahead/pallas_call | solution.py:1033
  104.0 5.4 %all-to-all-done.1.sums_ref = f32[32,8,128]{2,1,0:T(8,128)S(1)} async-done(((f32[32,8,128]{2,1,0:T(8,128)}), f32[32,8,128]{2,1,0:T(8,128)S(1)}, u32[]{:S(2)}, u32[]{:S(2)}) %all-to-all-start.1) | async-done | bytes 131104 | tf_op jit(solution)/shard_map/all_to_all | solution.py:1195
  109.4 0.0 copy-start.1
  109.4 0.6 copy-done.1
  110.1 49.1 %third.1 = (f32[5,120,1536]{2,1,0:T(8,128)}, f32[5,120,1536]{2,1,0:T(8,128)}, f32[512,128]{1,0:T(8,128)}, f32[480,128]{1,0:T(8,128)}, f32[240,128]{1,0:T(8,128)}...) custom-call(s32[5]{0:T(128)} %len_ref.5, ...), custom_call_target="tpu_custom_call" | custom-call | flops 20000000000 | bytes 80000000 | tf_op jit(solution)/shard_map/third/pallas_call | solution.py:954
  159.2 4.6 %pack.1 = (f32[16,83,128]{2,1,0:T(8,128)}, f32[16,83,128]{2,1,0:T(8,128)}) custom-call(s32[1]{0:T(128)} %bitcast.3.me_ref, f32[909,128]{1,0:T(8,128)} %ahead.1.last_ref, f32[512,128]{1,0:T(8,128)} %get-tuple-element.135.dn1_ref, f32[480,128]{1,0:T(8,128)} %get-tuple-element.136.up1_ref, f32[128,128]{1,0:T(8,128)} %get-tuple-element.137.pr_ref, ...), custom_call_target="tpu_custom_call" | custom-call | flops 1000000000 | bytes 5000000 | tf_op jit(solution)/shard_map/pack/pallas_call | solution.py:1103
  163.7 1.2 copy.16
  165.0 0.3 collective-permute-start.7
  165.3 1.9 collective-permute-done.7
  167.2 1.3 copy_add_fusion
  168.6 0.9 collective-permute-start.10
  169.5 1.3 collective-permute-start.8
  170.8 1.4 collective-permute-start.9
  172.1 4.8 %collective-permute-done.10 = f32[4,83,128]{2,1,0:T(8,128)S(1)} collective-permute-done((f32[4,83,128]{2,1,0:T(8,128)S(1)}, f32[4,83,128]{2,1,0:T(8,128)S(1)}, u32[]{:S(2)}, u32[]{:S(2)}) %collective-permute-start.10) | collective-permute-done | bytes 170016 | tf_op jit(solution)/shard_map/ppermute | solution.py:1154
  177.0 2.2 %collective-permute-done.8 = f32[4,83,128]{2,1,0:T(8,128)S(1)} collective-permute-done((f32[4,83,128]{2,1,0:T(8,128)S(1)}, f32[4,83,128]{2,1,0:T(8,128)S(1)}, u32[]{:S(2)}, u32[]{:S(2)}) %collective-permute-start.8) | collective-permute-done | bytes 170016 | tf_op jit(solution)/shard_map/ppermute | solution.py:1154
  179.2 0.9 collective-permute-done.9
  180.1 0.6 collective-permute-start.11
  180.8 1.2 collective-permute-start.12
  181.9 2.7 %collective-permute-start.13 = (f32[1,83,128]{2,1,0:T(8,128)S(1)}, f32[1,83,128]{2,1,0:T(8,128)S(1)}, u32[]{:S(2)}, u32[]{:S(2)}) collective-permute-start(f32[1,83,128]{2,1,0:T(8,128)S(1)} %get-tuple-element.154), channel_id=1, source_target_pairs={{0,24},{1,25},{2,26},{3,27},{4,28},{5,29},{6,30},{7,31},{8,16},{9,... | collective-permute-start | bytes 127496 | tf_op jit(solution)/shard_map/ppermute | solution.py:1154
  184.6 0.0 copy-start
  184.6 0.0 copy-start.3
  184.6 0.0 copy-start.4
  184.6 0.0 copy-start.5
  184.6 10.8 %leave.1 = (bf16[5,120,1536]{2,1,0:T(8,128)(2,1)}, f32[5,120,1536]{2,1,0:T(8,128)}) custom-call(bf16[5,120,1536]{2,1,0:T(8,128)(2,1)} %get-tuple-element.104.out_ref, f32[5,120,1536]{2,1,0:T(8,128)} %get-tuple-element.126.grad_ref, f32[5,120,1536]{2,1,0:T(8,128)} %get-tuple-element.127.back_ref, f32[5,120,1536]{2,1,0:T(8,128)} %get-tuple-element.82.xf_ref, ...), custom_call_target="tpu_custom_call" | custom-call | flops 3000000000 | bytes 20000000 | tf_op jit(solution)/shard_map/leave/pallas_call | solution.py:276
  195.4 0.0 collective-permute-done.11
  195.4 0.0 collective-permute-done.12
  195.4 0.0 collective-permute-done.13
  195.4 0.0 copy-done
  195.4 0.0 copy-done.3
  195.4 0.0 copy-done.4
  195.4 0.0 copy-done.5
  195.4 1.6 multiply_add_fusion.1
  (10 shorter events, 0.3 us)
Async XLA Ops:
  1.4 13.3 %collective-permute-start = (bf16[1,83,128]{2,1,0:T(8,128)(2,1)S(1)}, bf16[1,83,128]{2,1,0:T(8,128)(2,1)S(1)}, u32[]{:S(2)}, u32[]{:S(2)}) collective-permute-start(bf16[1,83,128]{2,1,0:T(8,128)(2,1)S(1)} %convert_bitcast_fusion), channel_id=1, source_target_pairs={{0,8},{1,9},{2,10},{3,11},{4,12},{5,13},{6,14},{7,15},{8,0},{9,1},... | collective-permute-start | bytes 63752 | tf_op jit(solution)/shard_map/ppermute | solution.py:1154
  4.5 10.2 %collective-permute-start.1 = (bf16[1,83,128]{2,1,0:T(8,128)(2,1)S(1)}, bf16[1,83,128]{2,1,0:T(8,128)(2,1)S(1)}, u32[]{:S(2)}, u32[]{:S(2)}) collective-permute-start(bf16[1,83,128]{2,1,0:T(8,128)(2,1)S(1)} %convert_bitcast_fusion), channel_id=1, source_target_pairs={{0,16},{1,17},{2,18},{3,19},{4,20},{5,21},{6,22},{7,23},{8,24},{9,... | collective-permute-start | bytes 63752 | tf_op jit(solution)/shard_map/ppermute | solution.py:1154
  7.0 7.7 %collective-permute-start.2 = (bf16[1,83,128]{2,1,0:T(8,128)(2,1)S(1)}, bf16[1,83,128]{2,1,0:T(8,128)(2,1)S(1)}, u32[]{:S(2)}, u32[]{:S(2)}) collective-permute-start(bf16[1,83,128]{2,1,0:T(8,128)(2,1)S(1)} %convert_bitcast_fusion), channel_id=1, source_target_pairs={{0,24},{1,25},{2,26},{3,27},{4,28},{5,29},{6,30},{7,31},{8,16},{9,... | collective-permute-start | bytes 63752 | tf_op jit(solution)/shard_map/ppermute | solution.py:1154
  14.8 4.9 %collective-permute-start.3 = (bf16[4,83,128]{2,1,0:T(8,128)(2,1)S(1)}, bf16[4,83,128]{2,1,0:T(8,128)(2,1)S(1)}, u32[]{:S(2)}, u32[]{:S(2)}) collective-permute-start(bf16[4,83,128]{2,1,0:T(8,128)(2,1)S(1)} %get-tuple-element.164), channel_id=1, source_target_pairs={{0,2},{1,3},{2,0},{3,1},{4,6},{5,7},{6,4},{7,5},{8,10},{9,11},{10,... | collective-permute-start | bytes 254984 | tf_op jit(solution)/shard_map/ppermute | solution.py:1154
  16.6 5.4 %collective-permute-start.4 = (bf16[4,83,128]{2,1,0:T(8,128)(2,1)S(1)}, bf16[4,83,128]{2,1,0:T(8,128)(2,1)S(1)}, u32[]{:S(2)}, u32[]{:S(2)}) collective-permute-start(bf16[4,83,128]{2,1,0:T(8,128)(2,1)S(1)} %get-tuple-element.164), channel_id=1, source_target_pairs={{0,4},{1,5},{2,6},{3,7},{4,0},{5,1},{6,2},{7,3},{8,12},{9,13},{10,... | collective-permute-start | bytes 254984 | tf_op jit(solution)/shard_map/ppermute | solution.py:1154
  18.1 5.4 %collective-permute-start.5 = (bf16[4,83,128]{2,1,0:T(8,128)(2,1)S(1)}, bf16[4,83,128]{2,1,0:T(8,128)(2,1)S(1)}, u32[]{:S(2)}, u32[]{:S(2)}) collective-permute-start(bf16[4,83,128]{2,1,0:T(8,128)(2,1)S(1)} %get-tuple-element.164), channel_id=1, source_target_pairs={{0,6},{1,7},{2,4},{3,5},{4,2},{5,3},{6,0},{7,1},{8,14},{9,15},{10,... | collective-permute-start | bytes 254984 | tf_op jit(solution)/shard_map/ppermute | solution.py:1154
  23.6 1.7 collective-permute-start.6
  25.3 0.9 copy-start.6
  64.2 12.2 %all-to-all-start = ((f32[32,8,128]{2,1,0:T(8,128)}), f32[32,8,128]{2,1,0:T(8,128)S(1)}, u32[]{:S(2)}, u32[]{:S(2)}) async-start(f32[32,8,128]{2,1,0:T(8,128)} %get-tuple-element.94), calls=%async_computation | async-start | bytes 262144 | tf_op jit(solution)/shard_map/all_to_all | solution.py:1191
  76.4 0.7 copy-start.2
  98.6 10.8 %all-to-all-start.1 = ((f32[32,8,128]{2,1,0:T(8,128)}), f32[32,8,128]{2,1,0:T(8,128)S(1)}, u32[]{:S(2)}, u32[]{:S(2)}) async-start(f32[32,8,128]{2,1,0:T(8,128)} %get-tuple-element.105.sums_ref), calls=%async_computation.1 | async-start | bytes 262144 | tf_op jit(solution)/shard_map/all_to_all | solution.py:1195
  109.4 0.6 copy-start.1
  165.0 2.2 %collective-permute-start.7 = (f32[16,83,128]{2,0,1:T(8,128)S(1)}, f32[16,83,128]{2,0,1:T(8,128)S(1)}, u32[]{:S(2)}, u32[]{:S(2)}) collective-permute-start(f32[16,83,128]{2,0,1:T(8,128)S(1)} %copy.16), channel_id=1, source_target_pairs={{0,1},{1,0},{2,3},{3,2},{4,5},{5,4},{6,7},{7,6},{8,9},{9,8},{10,11... | collective-permute-start | bytes 2039816 | tf_op jit(solution)/shard_map/ppermute | solution.py:1154
  168.6 8.4 %collective-permute-start.10 = (f32[4,83,128]{2,1,0:T(8,128)S(1)}, f32[4,83,128]{2,1,0:T(8,128)S(1)}, u32[]{:S(2)}, u32[]{:S(2)}) collective-permute-start(f32[4,83,128]{2,1,0:T(8,128)S(1)} %get-tuple-element.151), channel_id=1, source_target_pairs={{0,6},{1,7},{2,4},{3,5},{4,2},{5,3},{6,0},{7,1},{8,14},{9,15},{10,... | collective-permute-start | bytes 509960 | tf_op jit(solution)/shard_map/ppermute | solution.py:1154
  169.5 9.7 %collective-permute-start.8 = (f32[4,83,128]{2,1,0:T(8,128)S(1)}, f32[4,83,128]{2,1,0:T(8,128)S(1)}, u32[]{:S(2)}, u32[]{:S(2)}) collective-permute-start(f32[4,83,128]{2,1,0:T(8,128)S(1)} %get-tuple-element.150), channel_id=1, source_target_pairs={{0,2},{1,3},{2,0},{3,1},{4,6},{5,7},{6,4},{7,5},{8,10},{9,11},{10,... | collective-permute-start | bytes 509960 | tf_op jit(solution)/shard_map/ppermute | solution.py:1154
  170.8 9.3 %collective-permute-start.9 = (f32[4,83,128]{2,1,0:T(8,128)S(1)}, f32[4,83,128]{2,1,0:T(8,128)S(1)}, u32[]{:S(2)}, u32[]{:S(2)}) collective-permute-start(f32[4,83,128]{2,1,0:T(8,128)S(1)} %get-tuple-element.152), channel_id=1, source_target_pairs={{0,4},{1,5},{2,6},{3,7},{4,0},{5,1},{6,2},{7,3},{8,12},{9,13},{10,... | collective-permute-start | bytes 509960 | tf_op jit(solution)/shard_map/ppermute | solution.py:1154
  180.1 15.3 %collective-permute-start.11 = (f32[1,83,128]{2,1,0:T(8,128)S(1)}, f32[1,83,128]{2,1,0:T(8,128)S(1)}, u32[]{:S(2)}, u32[]{:S(2)}) collective-permute-start(f32[1,83,128]{2,1,0:T(8,128)S(1)} %get-tuple-element.153), channel_id=1, source_target_pairs={{0,8},{1,9},{2,10},{3,11},{4,12},{5,13},{6,14},{7,15},{8,0},{9,1},... | collective-permute-start | bytes 127496 | tf_op jit(solution)/shard_map/ppermute | solution.py:1154
  180.8 14.6 %collective-permute-start.12 = (f32[1,83,128]{2,1,0:T(8,128)S(1)}, f32[1,83,128]{2,1,0:T(8,128)S(1)}, u32[]{:S(2)}, u32[]{:S(2)}) collective-permute-start(f32[1,83,128]{2,1,0:T(8,128)S(1)} %get-tuple-element.155), channel_id=1, source_target_pairs={{0,16},{1,17},{2,18},{3,19},{4,20},{5,21},{6,22},{7,23},{8,24},{9,... | collective-permute-start | bytes 127496 | tf_op jit(solution)/shard_map/ppermute | solution.py:1154
  181.9 13.5 %collective-permute-start.13 = (f32[1,83,128]{2,1,0:T(8,128)S(1)}, f32[1,83,128]{2,1,0:T(8,128)S(1)}, u32[]{:S(2)}, u32[]{:S(2)}) collective-permute-start(f32[1,83,128]{2,1,0:T(8,128)S(1)} %get-tuple-element.154), channel_id=1, source_target_pairs={{0,24},{1,25},{2,26},{3,27},{4,28},{5,29},{6,30},{7,31},{8,16},{9,... | collective-permute-start | bytes 127496 | tf_op jit(solution)/shard_map/ppermute | solution.py:1154
  184.6 10.8 %copy-start = (f32[10624]{0:T(1024)S(1)}, f32[10624]{0:T(1024)}, u32[]{:S(2)}) copy-start(f32[10624]{0:T(1024)} %param.12) | copy-start | bytes 127492
  184.6 10.8 %copy-start.3 = (f32[10624]{0:T(1024)S(1)}, f32[10624]{0:T(1024)}, u32[]{:S(2)}) copy-start(f32[10624]{0:T(1024)} %param.15) | copy-start | bytes 127492
  184.6 10.9 %copy-start.4 = (f32[10624]{0:T(1024)S(1)}, f32[10624]{0:T(1024)}, u32[]{:S(2)}) copy-start(f32[10624]{0:T(1024)} %param.13) | copy-start | bytes 127492
  184.6 10.9 %copy-start.5 = (f32[10624]{0:T(1024)S(1)}, f32[10624]{0:T(1024)}, u32[]{:S(2)}) copy-start(f32[10624]{0:T(1024)} %param.14) | copy-start | bytes 127492

commit v3 on v2

--- a/solution.py
+++ b/solution.py
@@ -239,7 +239,7 @@
     return jnp.where(t == GROUP * (c % 128) + c // 128, 1.0, 0.0).astype(bf16)
 
 
-def enter_body(x_ref, cot_ref, xp_ref, cp_ref, xf_ref, rs_ref, pm_ref):
+def enter_body(x_ref, xp_ref, xf_ref, rs_ref, pm_ref):
     @pl.when(pl.program_id(0) == 0)
     def _():
         pm_ref[...] = permutation()
@@ -249,39 +249,44 @@
     xhat, rstd = norm(x)
     xf_ref[0] = xhat
     rs_ref[0] = jnp.broadcast_to(rstd, (8, MAXLEN))
-    cp_ref[0] = permute_in(cot_ref[0].astype(f32), pm_ref[...]).astype(bf16)
-
-
-def enter(x, cot):
+
+
+def enter(x):
     utts = x.shape[0]
     return pl.pallas_call(
         enter_body,
         grid=(utts,),
-        in_specs=[per_utt(BIG)] * 2,
-        out_specs=[per_utt(BIG)] * 3 + [per_utt((8, MAXLEN)), whole((384, 384))],
-        out_shape=[o((utts,) + BIG), o((utts,) + BIG), o((utts,) + BIG, f32), o((utts, 8, MAXLEN), f32), o((384, 384))],
+        in_specs=[per_utt(BIG)],
+        out_specs=[per_utt(BIG)] * 2 + [per_utt((8, MAXLEN)), whole((384, 384))],
+        out_shape=[o((utts,) + BIG), o((utts,) + BIG, f32), o((utts, 8, MAXLEN), f32), o((384, 384))],
         name="enter",
-        **params(2 * 10**9, 16 * 10**6),
-    )(x, cot)
-
-
-def leave_body(out_ref, grad_ref, back_ref, xf_ref, rs_ref, cols_ref, pm_ref, done_ref, gin_ref):
+        **params(2 * 10**9, 8 * 10**6),
+    )(x)
+
+
+def inward_body(cot_ref, pm_ref, cp_ref):
+    cp_ref[0] = permute_in(cot_ref[0].astype(f32), pm_ref[...]).astype(bf16)
+
+
+def outward_body(out_ref, pm_ref, done_ref):
     done_ref[0] = permute_out(out_ref[0].astype(f32), pm_ref[...]).astype(bf16)
-    back = norm_back(back_ref[0], xf_ref[0], rs_ref[0, 0:1, :], column(cols_ref, C_F1))
-    gin_ref[0] = permute_out_wide(grad_ref[0] + back, pm_ref[...])
-
-
-def leave(out, grad, back, xf, rs, cols, pm):
-    utts = out.shape[0]
+
+
+def leave_body(grad_ref, pm_ref, gin_ref):
+    gin_ref[0] = permute_out_wide(grad_ref[0], pm_ref[...])
+
+
+def reorder(body, values, pm, name):
+    utts = values.shape[0]
     return pl.pallas_call(
-        leave_body,
+        body,
         grid=(utts,),
-        in_specs=[per_utt(BIG)] * 4 + [per_utt((8, MAXLEN)), whole(cols.shape), whole(pm.shape)],
-        out_specs=[per_utt(BIG)] * 2,
-        out_shape=[o((utts,) + BIG), o((utts,) + BIG, f32)],
-        name="leave",
-        **params(3 * 10**9, 20 * 10**6),
-    )(out, grad, back, xf, rs, cols, pm)
+        in_specs=[per_utt(BIG), whole(pm.shape)],
+        out_specs=per_utt(BIG),
+        out_shape=o((utts,) + BIG, values.dtype),
+        name=name,
+        **params(2 * 10**9, 8 * 10**6),
+    )(values, pm)
 
 
 def unpack(me_ref, g_ref, flat, tb):
@@ -796,9 +801,9 @@
 
 def third_body(
     len_ref, sums_ref, stc_ref, bgd_ref, gc_ref, dep_ref, xf_ref, lf_ref, xa_ref, nrm_ref, qkv_ref, prob_ref, att_ref, xc_ref,
-    cn_ref, gat_ref, sig_ref, rgt_ref, rs_ref,
+    cn_ref, gat_ref, sig_ref, rgt_ref, ri_ref, rs_ref,
     cols_ref, up_ref, upp_ref, dnp_ref, wqkv_t_ref, wob_ref, pwp_ref,
-    grad_ref, back_ref, gdn_ref, gup_ref, gpw_ref, gqkv_ref, go_ref, rel_ref, vec_ref,
+    grad_ref, gdn_ref, gup_ref, gpw_ref, gqkv_ref, go_ref, rel_ref, vec_ref,
     hid, dgs, olg, agr, back_s, gg, relacc, cb, tot,
 ):
     u = pl.program_id(0)
@@ -911,23 +916,24 @@
         vec_ref[2] += fold(back * xhat)
         vec_ref[3] += fold(back)
         grad = dgs[:, span(r)] + norm_back(back, xhat, rs_ref[0, 1:2, span(r)], column(cols, C_AT))
-        grad_ref[0, :, span(r)] = grad
         low = pad8(grad).astype(bf16)
-        return low, half, dot(dnp_ref[...], low)
+        return grad, low, half, dot(dnp_ref[...], low)
 
     def ffn_mid(r, held):
-        branch, half, back = held
+        grad, branch, half, back = held
         t = jnp.tanh(half)
         hid[:FF, span(r)] = (half + half * t).astype(bf16)
         pre_low = ((1.0 + t) * (1.0 + half * (1.0 - t)) * back).astype(bf16)
         gdn_ref[...] += dot_nt(hid[:, span(r)], branch)
         gup_ref[...] += dot_nt(pre_low, lf_ref[0, :, span(r)])
-        return dot(upp_ref[...], pre_low)[:D]
-
-    def ffn_out(r, back):
-        back_ref[0, :, span(r)] = back
-        vec_ref[4] += fold(back * xf_ref[0, :, span(r)])
+        return grad, dot(upp_ref[...], pre_low)[:D]
+
+    def ffn_out(r, held):
+        grad, back = held
+        xhat = xf_ref[0, :, span(r)]
+        vec_ref[4] += fold(back * xhat)
         vec_ref[5] += fold(back)
+        grad_ref[0, :, span(r)] = grad + norm_back(back, xhat, ri_ref[0, 0:1, span(r)], column(cols, C_F1))
 
     skewed(GROUP, (project, ffn_in, ffn_mid, ffn_out))
 
@@ -948,7 +954,7 @@
 def third(lengths, sums, stc, saved, weights):
     utts = saved[0].shape[0]
     big = (D, MAXLEN)
-    outs = [(per_utt(big), (utts,) + big)] * 2
+    outs = [(per_utt(big), (utts,) + big)]
     for s in ((512, 128), (FF, 128), (240, 128), (GROUP, 3 * WROWS, 128), (GROUP, WROWS, 128), (8, 256), (22, D, 128)):
         outs.append((whole(s), s))
     return pl.pallas_call(
@@ -1155,24 +1161,27 @@
 
 
 def gather(values, devices, beside):
-    held = values[None]
-    for stride, size in reversed(digits(devices)):
+    held, made = values[None], []
+    for k, (stride, size) in enumerate(reversed(digits(devices))):
         parts = [held] + [partner(held, stride * j, devices) for j in range(1, size)]
-        if beside is not None:
-            parts, made = lax.optimization_barrier((parts, beside))
-            beside = None
+        if k < len(beside):
+            parts, found = lax.optimization_barrier((parts, beside[k]))
+            made.append(found)
         held = jnp.concatenate(parts, axis=0)
-    return held, made
-
-
-def scatter_sum(keep, send, devices):
+    return held, made + beside[len(made) :]
+
+
+def scatter_sum(keep, send, devices, beside):
     total = keep + partner(send, 1, devices)
     for stride, size in digits(devices)[1:]:
         parts = total.reshape((size, total.shape[0] // size) + total.shape[1:])
+        found = [partner(parts[j], stride * j, devices) for j in range(1, size)]
+        if stride == 2:
+            found, beside = lax.optimization_barrier((found, beside))
         total = parts[0]
-        for j in range(1, size):
-            total = total + partner(parts[j], stride * j, devices)
-    return total
+        for part in found:
+            total = total + part
+    return total, beside
 
 
 def local(frames, lengths, cotangent, master, moment_one, moment_two, average):
@@ -1180,8 +1189,10 @@
     devices = lax.axis_size("dp")
     rows = shard_len // 128
     me = lax.axis_index("dp").astype(jnp.int32).reshape(1)
-    entered = enter(jnp.transpose(frames, (0, 2, 1)), jnp.transpose(cotangent, (0, 2, 1)))
-    gathered, (xp, cp, xf, rs_in, pm) = gather(master.astype(bf16).reshape(rows, 128), devices, entered)
+    entered = enter(jnp.transpose(frames, (0, 2, 1)))
+    cp = reorder(inward_body, jnp.transpose(cotangent, (0, 2, 1)), entered[3], "inward")
+    gathered, (entered, cp) = gather(master.astype(bf16).reshape(rows, 128), devices, [entered, cp])
+    xp, xf, rs_in, pm = entered
     early, late = prepare(me, gathered)
     up1, dn1, wqkv, wo, pw, cols, base = early
     upp1, dnp1, up2, upp2, dn2, dnp2, pwp, pr, prp, wqkvt, wob = late
@@ -1194,14 +1205,17 @@
     )
     all_sums = lax.all_to_all(sums, "dp", 0, 0)
     last = pack_ahead(gdn2, gup2, vec2)
-    grad, back, gdn1, gup1, gpw, gqkv, go, rel, vec3 = third(
+    out = reorder(outward_body, out, pm, "outward")
+    (all_sums, last, out) = lax.optimization_barrier((all_sums, last, out))
+    grad, gdn1, gup1, gpw, gqkv, go, rel, vec3 = third(
         lengths, all_sums, stc,
-        (bgd, gc, dep, xf, lf, xa, nrm, qkv, prob, att, xc, cn, gat, sig, rgt, rs),
+        (bgd, gc, dep, xf, lf, xa, nrm, qkv, prob, att, xc, cn, gat, sig, rgt, rs_in, rs),
         (cols, up1, upp1, dnp1, wqkvt, wob, pwp),
     )
     keep, send = pack(devices, rows, me, (last, gdn1, gup1, gpr, gpw, gqkv, go, rel, vec3, sums))
-    out, gin = leave(out, grad, back, xf, rs_in, cols, pm)
-    reduced = scatter_sum(keep, send, devices).reshape(shard_len)
+    gin = reorder(leave_body, grad, pm, "leave")
+    reduced, gin = scatter_sum(keep, send, devices, gin)
+    reduced = reduced.reshape(shard_len)
     rates_np, decays_np = update_tables(shard_len * devices)
     start_at = lax.axis_index("dp") * shard_len
     rates = lax.dynamic_slice_in_dim(jnp.asarray(rates_np), start_at, shard_len)

time: 198 us -> 193 us (0.975)
  waiting for transfers between devices: 26.5 us -> 13.5 us
  Pallas kernels: 138 us -> 144 us
    ppermute x14, waiting for transfers between devices: 16.6 us -> 8.69 us  [partner(): return lax.ppermute(values, 'dp', [(i, i ^ offset) for i in range(devices)])]
    pallas_call x2 -> x4, Pallas kernels: 18.4 us -> 23.7 us  [the longest x3 17.5 us: reorder(): pl.pallas_call(body, grid=(utts,), in_specs=[per_utt(BIG), whole(pm.shape...]
    all_to_all x1, waiting for transfers between devices: 5.43 us -> 0.32 us  [local(): all_sums = lax.all_to_all(sums, 'dp', 0, 0)]
    all_to_all x1, starting transfers between devices: 4.16 us -> 6.26 us  [local(): stats = lax.all_to_all(st, 'dp', 0, 0)]
  transfers between devices with their start and end apart: 16 -> 16, of which waited for: 10 -> 7; matrix products, arithmetic and copies ran while one was open for 0% -> 0% of each run, Pallas kernels for 12% -> 16%
where the time goes in v3:
time: 193 us; the launch traced here: 192 us
  Pallas kernels  144 us (75%)
  starting transfers between devices  26.4 us (14%)
  waiting for transfers between devices  13.5 us (7%)
  other arithmetic  3.79 us (2%)
  local copies, waits for them, and re-layouts  3.6 us (2%)
    pallas_call x1, Pallas kernels, third(): pl.pallas_call(third_body, grid=(utts,), in_specs=[SMEM, whole(sums.shape...  50.1 us
    pallas_call x1, Pallas kernels, first(): pl.pallas_call(first_body, grid=(utts,), in_specs=[SMEM, per_utt(BIG), pe...  34.7 us
    pallas_call x1, Pallas kernels, second(): pl.pallas_call(second_body, grid=(utts,), in_specs=[SMEM, whole(stats.sha...  21.6 us
    ppermute x14, starting transfers between devices, partner(): return lax.ppermute(values, 'dp', [(i, i ^ offset) for i in range(devices)])  17.5 us
    pallas_call x3, Pallas kernels, reorder(): pl.pallas_call(body, grid=(utts,), in_specs=[per_utt(BIG), whole(pm.shape...  17.5 us
    ppermute x14, waiting for transfers between devices, partner(): return lax.ppermute(values, 'dp', [(i, i ^ offset) for i in range(devices)])  8.69 us
    all_to_all x1, starting transfers between devices, local(): stats = lax.all_to_all(st, 'dp', 0, 0)  6.26 us
    pallas_call x1, Pallas kernels, enter(): pl.pallas_call(enter_body, grid=(utts,), in_specs=[per_utt(BIG)], out_spe...  6.18 us
  transfers between devices with their start and end apart: 16, of which 7 were waited for; matrix products, arithmetic and copies ran while one was open for 0% of the time, Pallas kernels for 16%

profile of v3, /device:TPU:0, one launch (start us, length us, event | category | flops | bytes accessed | tf_op | source)
XLA Modules:
  0.0 191.9 jit_solution(3213150130349597563)
XLA Ops:
  0.6 0.8 convert_bitcast_fusion
  1.4 3.0 %collective-permute-start = (bf16[1,83,128]{2,1,0:T(8,128)(2,1)S(1)}, bf16[1,83,128]{2,1,0:T(8,128)(2,1)S(1)}, u32[]{:S(2)}, u32[]{:S(2)}) collective-permute-start(bf16[1,83,128]{2,1,0:T(8,128)(2,1)S(1)} %convert_bitcast_fusion), channel_id=1, source_target_pairs={{0,8},{1,9},{2,10},{3,11},{4,12},{5,13},{6,14},{7,15},{8,0},{9,1},... | collective-permute-start | bytes 63752 | tf_op jit(solution)/shard_map/ppermute | solution.py:1160
  4.5 2.6 %collective-permute-start.1 = (bf16[1,83,128]{2,1,0:T(8,128)(2,1)S(1)}, bf16[1,83,128]{2,1,0:T(8,128)(2,1)S(1)}, u32[]{:S(2)}, u32[]{:S(2)}) collective-permute-start(bf16[1,83,128]{2,1,0:T(8,128)(2,1)S(1)} %convert_bitcast_fusion), channel_id=1, source_target_pairs={{0,16},{1,17},{2,18},{3,19},{4,20},{5,21},{6,22},{7,23},{8,24},{9,... | collective-permute-start | bytes 63752 | tf_op jit(solution)/shard_map/ppermute | solution.py:1160
  7.0 0.0 collective-permute-start.2
  7.0 6.2 %enter.1 = (bf16[5,120,1536]{2,1,0:T(8,128)(2,1)}, f32[5,120,1536]{2,1,0:T(8,128)}, f32[5,8,1536]{2,1,0:T(8,128)}, bf16[384,384]{1,0:T(8,128)(2,1)}) custom-call(bf16[5,120,1536]{2,1,0:T(8,128)(2,1)} %bitcast.11), custom_call_target="tpu_custom_call" | custom-call | flops 2000000000 | bytes 8000000 | tf_op jit(solution)/shard_map/enter/pallas_call | solution.py:256
  13.2 0.0 collective-permute-done
  13.2 0.0 collective-permute-done.1
  13.2 0.0 collective-permute-done.2
  13.3 1.8 collective-permute-start.3
  15.1 1.5 collective-permute-start.4
  16.6 0.3 collective-permute-start.5
  16.9 5.3 %inward.1.cot_ref = bf16[5,120,1536]{2,1,0:T(8,128)(2,1)} custom-call(bf16[5,120,1536]{2,1,0:T(8,128)(2,1)} %bitcast.12, bf16[384,384]{1,0:T(8,128)(2,1)} %get-tuple-element.119.pm_ref), custom_call_target="tpu_custom_call" | custom-call | flops 2000000000 | bytes 8000000 | tf_op jit(solution)/shard_map/inward/pallas_call | solution.py:281
  22.1 0.0 collective-permute-done.3
  22.1 0.0 collective-permute-done.4
  22.1 0.0 collective-permute-done.5
  22.2 0.1 pad_maximum_fusion
  22.2 0.1 collective-permute-start.6
  22.4 1.6 collective-permute-done.6
  24.0 0.1 constant_dynamic-update-slice_fusion.4.g_ref
  24.0 0.0 copy-start.6
  24.0 0.9 copy-done.6
  24.9 3.2 %prepare.1 = (bf16[480,128]{1,0:T(8,128)(2,1)}, bf16[128,512]{1,0:T(8,128)(2,1)}, bf16[3,432,128]{2,1,0:T(8,128)(2,1)}, bf16[3,128,144]{2,1,0:T(8,128)(2,1)}, bf...) custom-call(s32[1]{0:T(128)} %bitcast.2.me_ref, bf16[32,83,128]{2,1,0:T(8,128)(2,1)} %copy-done.6), custom_call_target="tpu_custom_call" | custom-call | flops 1000000000 | bytes 2000000 | tf_op jit(solution)/shard_map/prepare/pallas_call | solution.py:451
  28.1 34.7 %first.1 = (bf16[5,128,1536]{2,1,0:T(8,128)(2,1)}, f32[5,120,1536]{2,1,0:T(8,128)}, bf16[5,384,512]{2,1,0:T(8,128)(2,1)}, bf16[5,1152,512]{2,1,0:T(8,128)(2,1)},...) custom-call(s32[5]{0:T(128)} %len_ref.5, ...), custom_call_target="tpu_custom_call" | custom-call | flops 10000000000 | bytes 60000000 | tf_op jit(solution)/shard_map/first/pallas_call | solution.py:648
  62.8 6.3 %all-to-all-start = ((f32[32,8,128]{2,1,0:T(8,128)}), f32[32,8,128]{2,1,0:T(8,128)S(1)}, u32[]{:S(2)}, u32[]{:S(2)}) async-start(f32[32,8,128]{2,1,0:T(8,128)} %get-tuple-element.104), calls=%async_computation | async-start | bytes 262144 | tf_op jit(solution)/shard_map/all_to_all | solution.py:1202
  69.0 3.6 %late.1 = (bf16[128,480]{1,0:T(8,128)(2,1)}, bf16[480,128]{1,0:T(8,128)(2,1)}, bf16[480,128]{1,0:T(8,128)(2,1)}, bf16[128,480]{1,0:T(8,128)(2,1)}, bf16[128,512]...) custom-call(s32[1]{0:T(128)} %bitcast.2.me_ref, ...), custom_call_target="tpu_custom_call" | custom-call | flops 3000000000 | bytes 10000000 | tf_op jit(solution)/shard_map/late/pallas_call | solution.py:460
  72.6 4.4 %all-to-all-done.stats_ref = f32[32,8,128]{2,1,0:T(8,128)S(1)} async-done(((f32[32,8,128]{2,1,0:T(8,128)}), f32[32,8,128]{2,1,0:T(8,128)S(1)}, u32[]{:S(2)}, u32[]{:S(2)}) %all-to-all-start) | async-done | bytes 131104 | tf_op jit(solution)/shard_map/all_to_all | solution.py:1202
  77.1 0.0 copy-start.2
  77.1 0.7 copy-done.2
  77.7 21.6 %second.1 = (bf16[5,120,1536]{2,1,0:T(8,128)(2,1)}, f32[5,120,1536]{2,1,0:T(8,128)}, f32[5,120,1536]{2,1,0:T(8,128)}, f32[32,8,128]{2,1,0:T(8,128)}, f32[128,128...) custom-call(s32[5]{0:T(128)} %len_ref.5, ...), custom_call_target="tpu_custom_call" | custom-call | flops 15000000512 | bytes 30000000 | tf_op jit(solution)/shard_map/second/pallas_call | solution.py:787
  99.3 2.6 %all-to-all-start.1 = ((f32[32,8,128]{2,1,0:T(8,128)}), f32[32,8,128]{2,1,0:T(8,128)S(1)}, u32[]{:S(2)}, u32[]{:S(2)}) async-start(f32[32,8,128]{2,1,0:T(8,128)} %get-tuple-element.114.sums_ref), calls=%async_computation.1 | async-start | bytes 262144 | tf_op jit(solution)/shard_map/all_to_all | solution.py:1206
  101.9 5.3 %outward.1 = bf16[5,120,1536]{2,1,0:T(8,128)(2,1)} custom-call(bf16[5,120,1536]{2,1,0:T(8,128)(2,1)} %get-tuple-element.118.out_ref, bf16[384,384]{1,0:T(8,128)(2,1)} %get-tuple-element.119.pm_ref), custom_call_target="tpu_custom_call" | custom-call | flops 2000000000 | bytes 8000000 | tf_op jit(solution)/shard_map/outward/pallas_call | solution.py:281
  107.3 2.6 %ahead.1.last_ref = f32[909,128]{1,0:T(8,128)} custom-call(f32[512,128]{1,0:T(8,128)} %get-tuple-element.115.dn_ref, f32[480,128]{1,0:T(8,128)} %get-tuple-element.116.up_ref, f32[4,120,128]{2,1,0:T(8,128)} %get-tuple-element.117.vec_ref), custom_call_target="tpu_custom_call" | custom-call | flops 2000000000 | bytes 8000000 | tf_op jit(solution)/shard_map/ahead/pallas_call | solution.py:1039
  109.8 0.3 all-to-all-done.1.sums_ref
  110.2 0.0 copy-start.1
  110.2 0.6 copy-done.1
  110.8 50.1 %third.1 = (f32[5,120,1536]{2,1,0:T(8,128)}, f32[512,128]{1,0:T(8,128)}, f32[480,128]{1,0:T(8,128)}, f32[240,128]{1,0:T(8,128)}, f32[3,432,128]{2,1,0:T(8,128)},...) custom-call(s32[5]{0:T(128)} %len_ref.5, f32[32,8,128]{2,1,0:T(8,128)} %copy-done.1, ...), custom_call_target="tpu_custom_call" | custom-call | flops 20000000000 | bytes 80000000 | tf_op jit(solution)/shard_map/third/pallas_call | solution.py:960
  160.9 4.5 %pack.1 = (f32[16,83,128]{2,1,0:T(8,128)}, f32[16,83,128]{2,1,0:T(8,128)}) custom-call(s32[1]{0:T(128)} %bitcast.2.me_ref, f32[909,128]{1,0:T(8,128)} %ahead.1.last_ref, f32[512,128]{1,0:T(8,128)} %get-tuple-element.144.dn1_ref, f32[480,128]{1,0:T(8,128)} %get-tuple-element.145.up1_ref, f32[128,128]{1,0:T(8,128)} %get-tuple-element.146.pr_ref, ...), custom_call_target="tpu_custom_call" | custom-call | flops 1000000000 | bytes 5000000 | tf_op jit(solution)/shard_map/pack/pallas_call | solution.py:1109
  165.4 1.2 copy.16
  166.7 0.3 collective-permute-start.7
  166.9 1.9 collective-permute-done.7
  168.9 1.3 copy_add_fusion
  170.2 1.4 collective-permute-start.8
  171.6 1.5 collective-permute-start.9
  173.1 0.7 collective-permute-start.10
  173.8 0.0 copy-start
  173.8 0.0 copy-start.3
  173.8 0.0 copy-start.4
  173.8 0.0 copy-start.5
  173.8 6.9 %leave.1 = f32[5,120,1536]{2,1,0:T(8,128)} custom-call(f32[5,120,1536]{2,1,0:T(8,128)} %get-tuple-element.154.grad_ref, bf16[384,384]{1,0:T(8,128)(2,1)} %get-tuple-element.119.pm_ref), custom_call_target="tpu_custom_call" | custom-call | flops 2000000000 | bytes 8000000 | tf_op jit(solution)/shard_map/leave/pallas_call | solution.py:281
  180.7 0.0 collective-permute-done.8
  180.7 1.1 collective-permute-done.9
  181.8 0.0 collective-permute-done.10
  181.9 3.5 %collective-permute-start.13 = (f32[1,83,128]{2,1,0:T(8,128)S(1)}, f32[1,83,128]{2,1,0:T(8,128)S(1)}, u32[]{:S(2)}, u32[]{:S(2)}) collective-permute-start(f32[1,83,128]{2,1,0:T(8,128)S(1)} %get-tuple-element.168), channel_id=1, source_target_pairs={{0,24},{1,25},{2,26},{3,27},{4,28},{5,29},{6,30},{7,31},{8,16},{9,... | collective-permute-start | bytes 127496 | tf_op jit(solution)/shard_map/ppermute | solution.py:1160
  185.4 0.0 collective-permute-start.12
  185.4 0.9 collective-permute-start.11
  186.3 1.5 collective-permute-done.13
  187.8 2.5 %collective-permute-done.12 = f32[1,83,128]{2,1,0:T(8,128)S(1)} collective-permute-done((f32[1,83,128]{2,1,0:T(8,128)S(1)}, f32[1,83,128]{2,1,0:T(8,128)S(1)}, u32[]{:S(2)}, u32[]{:S(2)}) %collective-permute-start.12) | collective-permute-done | bytes 42528 | tf_op jit(solution)/shard_map/ppermute | solution.py:1160
  190.3 0.0 collective-permute-done.11
  190.3 0.0 copy-done
  190.4 0.0 copy-done.3
  190.4 0.0 copy-done.4
  190.4 0.0 copy-done.5
  190.4 1.6 multiply_add_fusion.1
  (11 shorter events, 0.2 us)
Async XLA Ops:
  1.4 11.8 %collective-permute-start = (bf16[1,83,128]{2,1,0:T(8,128)(2,1)S(1)}, bf16[1,83,128]{2,1,0:T(8,128)(2,1)S(1)}, u32[]{:S(2)}, u32[]{:S(2)}) collective-permute-start(bf16[1,83,128]{2,1,0:T(8,128)(2,1)S(1)} %convert_bitcast_fusion), channel_id=1, source_target_pairs={{0,8},{1,9},{2,10},{3,11},{4,12},{5,13},{6,14},{7,15},{8,0},{9,1},... | collective-permute-start | bytes 63752 | tf_op jit(solution)/shard_map/ppermute | solution.py:1160
  4.5 8.8 %collective-permute-start.1 = (bf16[1,83,128]{2,1,0:T(8,128)(2,1)S(1)}, bf16[1,83,128]{2,1,0:T(8,128)(2,1)S(1)}, u32[]{:S(2)}, u32[]{:S(2)}) collective-permute-start(bf16[1,83,128]{2,1,0:T(8,128)(2,1)S(1)} %convert_bitcast_fusion), channel_id=1, source_target_pairs={{0,16},{1,17},{2,18},{3,19},{4,20},{5,21},{6,22},{7,23},{8,24},{9,... | collective-permute-start | bytes 63752 | tf_op jit(solution)/shard_map/ppermute | solution.py:1160
  7.0 6.2 %collective-permute-start.2 = (bf16[1,83,128]{2,1,0:T(8,128)(2,1)S(1)}, bf16[1,83,128]{2,1,0:T(8,128)(2,1)S(1)}, u32[]{:S(2)}, u32[]{:S(2)}) collective-permute-start(bf16[1,83,128]{2,1,0:T(8,128)(2,1)S(1)} %convert_bitcast_fusion), channel_id=1, source_target_pairs={{0,24},{1,25},{2,26},{3,27},{4,28},{5,29},{6,30},{7,31},{8,16},{9,... | collective-permute-start | bytes 63752 | tf_op jit(solution)/shard_map/ppermute | solution.py:1160
  13.3 8.8 %collective-permute-start.3 = (bf16[4,83,128]{2,1,0:T(8,128)(2,1)S(1)}, bf16[4,83,128]{2,1,0:T(8,128)(2,1)S(1)}, u32[]{:S(2)}, u32[]{:S(2)}) collective-permute-start(bf16[4,83,128]{2,1,0:T(8,128)(2,1)S(1)} %constant_dynamic-update-slice_fusion), channel_id=1, source_target_pairs={{0,2},{1,3},{2,0},{3,1},{4,6},{5,7},{6,4},{7,5},{8,10},{9,11},{10,... | collective-permute-start | bytes 254984 | tf_op jit(solution)/shard_map/ppermute | solution.py:1160
  15.1 7.1 %collective-permute-start.4 = (bf16[4,83,128]{2,1,0:T(8,128)(2,1)S(1)}, bf16[4,83,128]{2,1,0:T(8,128)(2,1)S(1)}, u32[]{:S(2)}, u32[]{:S(2)}) collective-permute-start(bf16[4,83,128]{2,1,0:T(8,128)(2,1)S(1)} %constant_dynamic-update-slice_fusion), channel_id=1, source_target_pairs={{0,4},{1,5},{2,6},{3,7},{4,0},{5,1},{6,2},{7,3},{8,12},{9,13},{10,... | collective-permute-start | bytes 254984 | tf_op jit(solution)/shard_map/ppermute | solution.py:1160
  16.6 5.5 %collective-permute-start.5 = (bf16[4,83,128]{2,1,0:T(8,128)(2,1)S(1)}, bf16[4,83,128]{2,1,0:T(8,128)(2,1)S(1)}, u32[]{:S(2)}, u32[]{:S(2)}) collective-permute-start(bf16[4,83,128]{2,1,0:T(8,128)(2,1)S(1)} %constant_dynamic-update-slice_fusion), channel_id=1, source_target_pairs={{0,6},{1,7},{2,4},{3,5},{4,2},{5,3},{6,0},{7,1},{8,14},{9,15},{10,... | collective-permute-start | bytes 254984 | tf_op jit(solution)/shard_map/ppermute | solution.py:1160
  22.2 1.7 collective-permute-start.6
  24.0 0.9 copy-start.6
  62.8 14.3 %all-to-all-start = ((f32[32,8,128]{2,1,0:T(8,128)}), f32[32,8,128]{2,1,0:T(8,128)S(1)}, u32[]{:S(2)}, u32[]{:S(2)}) async-start(f32[32,8,128]{2,1,0:T(8,128)} %get-tuple-element.104), calls=%async_computation | async-start | bytes 262144 | tf_op jit(solution)/shard_map/all_to_all | solution.py:1202
  77.1 0.7 copy-start.2
  99.3 10.8 %all-to-all-start.1 = ((f32[32,8,128]{2,1,0:T(8,128)}), f32[32,8,128]{2,1,0:T(8,128)S(1)}, u32[]{:S(2)}, u32[]{:S(2)}) async-start(f32[32,8,128]{2,1,0:T(8,128)} %get-tuple-element.114.sums_ref), calls=%async_computation.1 | async-start | bytes 262144 | tf_op jit(solution)/shard_map/all_to_all | solution.py:1206
  110.2 0.6 copy-start.1
  166.7 2.2 %collective-permute-start.7 = (f32[16,83,128]{2,0,1:T(8,128)S(1)}, f32[16,83,128]{2,0,1:T(8,128)S(1)}, u32[]{:S(2)}, u32[]{:S(2)}) collective-permute-start(f32[16,83,128]{2,0,1:T(8,128)S(1)} %copy.16), channel_id=1, source_target_pairs={{0,1},{1,0},{2,3},{3,2},{4,5},{5,4},{6,7},{7,6},{8,9},{9,8},{10,11... | collective-permute-start | bytes 2039816 | tf_op jit(solution)/shard_map/ppermute | solution.py:1160
  170.2 10.4 %collective-permute-start.8 = (f32[4,83,128]{2,1,0:T(8,128)S(1)}, f32[4,83,128]{2,1,0:T(8,128)S(1)}, u32[]{:S(2)}, u32[]{:S(2)}) collective-permute-start(f32[4,83,128]{2,1,0:T(8,128)S(1)} %get-tuple-element.166), channel_id=1, source_target_pairs={{0,2},{1,3},{2,0},{3,1},{4,6},{5,7},{6,4},{7,5},{8,10},{9,11},{10,... | collective-permute-start | bytes 509960 | tf_op jit(solution)/shard_map/ppermute | solution.py:1160
  171.6 10.2 %collective-permute-start.9 = (f32[4,83,128]{2,1,0:T(8,128)S(1)}, f32[4,83,128]{2,1,0:T(8,128)S(1)}, u32[]{:S(2)}, u32[]{:S(2)}) collective-permute-start(f32[4,83,128]{2,1,0:T(8,128)S(1)} %get-tuple-element.165), channel_id=1, source_target_pairs={{0,4},{1,5},{2,6},{3,7},{4,0},{5,1},{6,2},{7,3},{8,12},{9,13},{10,... | collective-permute-start | bytes 509960 | tf_op jit(solution)/shard_map/ppermute | solution.py:1160
  173.1 8.7 %collective-permute-start.10 = (f32[4,83,128]{2,1,0:T(8,128)S(1)}, f32[4,83,128]{2,1,0:T(8,128)S(1)}, u32[]{:S(2)}, u32[]{:S(2)}) collective-permute-start(f32[4,83,128]{2,1,0:T(8,128)S(1)} %get-tuple-element.164), channel_id=1, source_target_pairs={{0,6},{1,7},{2,4},{3,5},{4,2},{5,3},{6,0},{7,1},{8,14},{9,15},{10,... | collective-permute-start | bytes 509960 | tf_op jit(solution)/shard_map/ppermute | solution.py:1160
  173.8 16.6 %copy-start = (f32[10624]{0:T(1024)S(1)}, f32[10624]{0:T(1024)}, u32[]{:S(2)}) copy-start(f32[10624]{0:T(1024)} %param.12) | copy-start | bytes 127492
  173.8 16.6 %copy-start.3 = (f32[10624]{0:T(1024)S(1)}, f32[10624]{0:T(1024)}, u32[]{:S(2)}) copy-start(f32[10624]{0:T(1024)} %param.15) | copy-start | bytes 127492
  173.8 16.6 %copy-start.4 = (f32[10624]{0:T(1024)S(1)}, f32[10624]{0:T(1024)}, u32[]{:S(2)}) copy-start(f32[10624]{0:T(1024)} %param.13) | copy-start | bytes 127492
  173.8 16.6 %copy-start.5 = (f32[10624]{0:T(1024)S(1)}, f32[10624]{0:T(1024)}, u32[]{:S(2)}) copy-start(f32[10624]{0:T(1024)} %param.14) | copy-start | bytes 127492
  181.9 6.0 %collective-permute-start.13 = (f32[1,83,128]{2,1,0:T(8,128)S(1)}, f32[1,83,128]{2,1,0:T(8,128)S(1)}, u32[]{:S(2)}, u32[]{:S(2)}) collective-permute-start(f32[1,83,128]{2,1,0:T(8,128)S(1)} %get-tuple-element.168), channel_id=1, source_target_pairs={{0,24},{1,25},{2,26},{3,27},{4,28},{5,29},{6,30},{7,31},{8,16},{9,... | collective-permute-start | bytes 127496 | tf_op jit(solution)/shard_map/ppermute | solution.py:1160
  185.4 4.9 %collective-permute-start.12 = (f32[1,83,128]{2,1,0:T(8,128)S(1)}, f32[1,83,128]{2,1,0:T(8,128)S(1)}, u32[]{:S(2)}, u32[]{:S(2)}) collective-permute-start(f32[1,83,128]{2,1,0:T(8,128)S(1)} %get-tuple-element.169), channel_id=1, source_target_pairs={{0,16},{1,17},{2,18},{3,19},{4,20},{5,21},{6,22},{7,23},{8,24},{9,... | collective-permute-start | bytes 127496 | tf_op jit(solution)/shard_map/ppermute | solution.py:1160
  185.4 4.9 %collective-permute-start.11 = (f32[1,83,128]{2,1,0:T(8,128)S(1)}, f32[1,83,128]{2,1,0:T(8,128)S(1)}, u32[]{:S(2)}, u32[]{:S(2)}) collective-permute-start(f32[1,83,128]{2,1,0:T(8,128)S(1)} %get-tuple-element.167), channel_id=1, source_target_pairs={{0,8},{1,9},{2,10},{3,11},{4,12},{5,13},{6,14},{7,15},{8,0},{9,1},... | collective-permute-start | bytes 127496 | tf_op jit(solution)/shard_map/ppermute | solution.py:1160

commit v4 on v3

--- a/solution.py
+++ b/solution.py
@@ -224,6 +224,16 @@
     return pl.BlockSpec((1,) + shape, lambda u: (u,) + zeros)
 
 
+def at_most(shape, utts):
+    zeros = (0,) * len(shape)
+    return pl.BlockSpec((1,) + shape, lambda u: (jnp.minimum(u, utts - 1),) + zeros)
+
+
+def one_late(shape):
+    zeros = (0,) * len(shape)
+    return pl.BlockSpec((1,) + shape, lambda u: (jnp.maximum(u - 1, 0),) + zeros)
+
+
 def o(shape, kind=bf16):
     return jax.ShapeDtypeStruct(shape, kind)
 
@@ -290,9 +300,10 @@
 
 
 def unpack(me_ref, g_ref, flat, tb):
-    parts, part_rows = g_ref.shape[0], g_ref.shape[1]
+    parts = g_ref.shape[0]
+    part_rows = flat.shape[0] // parts
     for d in range(parts):
-        flat[part_rows * d : part_rows * (d + 1), :] = g_ref[place(me_ref[0] ^ d, parts)].astype(f32)
+        flat[part_rows * d : part_rows * (d + 1), :] = g_ref[place(me_ref[0] ^ d, parts)].astype(f32)[:part_rows]
     tb[ROWS_HEAD:TAIL, :] = jnp.zeros((TAIL - ROWS_HEAD, 128), f32)
     for start, count, base in ((0, ROWS_HEAD, 0), (TAIL_AT, ROWS_TAIL, TAIL)):
         for r in range(16):
@@ -426,22 +437,53 @@
     return jnp.where(row_iota((256, 2 * LG)) == index, 1.0, 0.0).astype(bf16)
 
 
-def diagonal_sum(values):
-    wide = jnp.concatenate([values, jnp.zeros((LG, LG), f32)], axis=1)
-    half = LG // 2
+def spread_table(line, tab, h):
+    blocks = {}
+    for gap in (-1, 0, 1):
+        tiles = [line[:, 128 * (k % 8) : 128 * (k % 8) + 128] for k in (gap - 1, gap)]
+        both = jnp.broadcast_to(jnp.concatenate(tiles, axis=1), (128, 256))
+        blocks[gap] = pltpu.roll(both, 0, 1, stride=1, stride_axis=0)[:, 128:]
+    blocks[2] = jnp.broadcast_to(line[:, 256:257], (128, 128))
+    blocks[-2] = jnp.broadcast_to(line[:, 768:769], (128, 128))
+    for j in range(4):
+        for i in range(4):
+            tab[h, 128 * j : 128 * j + 128, 128 * i : 128 * i + 128] = blocks[max(-2, min(2, i - j))]
+
+
+def block_of(values, j, i):
+    return values[128 * j : 128 * j + 128, 128 * i : 128 * i + 128]
+
+
+def add_distances(values, near, far, h):
+    for gap in (-1, 0, 1):
+        parts = [block_of(values, j, j + gap) for j in range(4) if 0 <= j + gap < 4]
+        total = parts[0]
+        for part in parts[1:]:
+            total = total + part
+        near[h, :, 128 * (gap + 1) : 128 * (gap + 2)] += total
+    for k, blocks in enumerate((((0, 2), (0, 3), (1, 3)), ((2, 0), (3, 0), (3, 1)))):
+        total = sum(block_of(values, j, i) for j, i in blocks)
+        rows = total[0:8]
+        for at in range(8, 128, 8):
+            rows = rows + total[at : at + 8]
+        far[h, k] += rows
+
+
+def diagonal_sum(near, far):
+    wide_rows = jnp.concatenate([near, jnp.zeros((128, 128), f32)], axis=1)
+    half = 64
     while half:
-        upper, lower = wide[:half], wide[half : 2 * half]
-        if half % 128 == 0:
-            lower = jnp.concatenate([lower[:, half:], lower[:, :half]], axis=1)
-        else:
-            lower = pltpu.roll(lower, 2 * LG - half, 1)
-        wide = upper + lower
+        wide_rows = wide_rows[:half] + pltpu.roll(wide_rows[half : 2 * half], LG - half, 1)
         half //= 2
-    return wide
-
-
-def prepare(me, gathered):
-    total = gathered.shape[0] * gathered.shape[1]
+    tiles = [wide_rows[:, 128 * k : 128 * k + 128] for k in range(4)]
+    none = jnp.zeros((1, 128), f32)
+    plus = jnp.sum(far[0], axis=0, keepdims=True)
+    minus = jnp.sum(far[1], axis=0, keepdims=True)
+    return jnp.concatenate([tiles[1], tiles[2], plus, none, none, minus, tiles[3], tiles[0]], axis=1)
+
+
+def prepare(me, gathered, rows):
+    total = gathered.shape[0] * rows
     room = [
         pltpu.VMEM((total, 128), f32),
         pltpu.VMEM((TABLE, 128), f32),
@@ -493,7 +535,7 @@
 def first_body(
     len_ref, xp_ref, xf_ref, cols_ref, up_ref, dn_ref, wqkv_ref, wo_ref, pw_ref, base_ref,
     lf_ref, xa_ref, nrm_ref, qkv_ref, prob_ref, att_ref, aa_ref, xc_ref, cn_ref, gat_ref, sig_ref, rgt_ref,
-    rs_ref, dep_ref, st_ref,
+    ra_ref, rc_ref, dep_ref, st_ref,
     hid, one, cb, tab, run,
 ):
     u = pl.program_id(0)
@@ -505,8 +547,7 @@
         run[...] = jnp.zeros_like(run)
         conv_columns(cols_ref, cb)
         for h in range(HEADS):
-            spread = jnp.broadcast_to(base_ref[h : h + 1, :], (LG, 2 * LG))
-            tab[h] = pltpu.roll(spread, 0, 1, stride=1, stride_axis=0)[:, :LG]
+            spread_table(base_ref[h : h + 1, :], tab, h)
 
     cols = cols_ref
 
@@ -524,7 +565,7 @@
         one[:, span(r)] = after
         xhat, rstd = norm(after)
         xa_ref[0, :, span(r)] = xhat
-        rs_ref[0, 1:2, span(r)] = rstd
+        ra_ref[0, 0:1, span(r)] = rstd
         low = ext(xhat * column(cols, C_AT) + column(cols, C_AT + 1))
         nrm_ref[0, 128 * r : 128 * r + 128, :] = low
         return dot(wqkv_ref[r], low)
@@ -570,7 +611,7 @@
         aa_ref[0, :, span(r)] = after
         xhat, rstd = norm(after)
         xc_ref[0, :, span(r)] = xhat
-        rs_ref[0, 2:3, span(r)] = rstd
+        rc_ref[0, 0:1, span(r)] = rstd
         low = ext(xhat * column(cols, C_CV) + column(cols, C_CV + 1))
         cn_ref[0, :, span(r)] = low
         return dot(pw_ref[...], low)
@@ -641,6 +682,7 @@
         (BIG, f32),
         (BIG, f32),
         (BIG, f32),
+        ((8, MAXLEN), f32),
         ((8, MAXLEN), f32),
         (BIG, f32),
     ]
@@ -800,14 +842,23 @@
 
 
 def third_body(
-    len_ref, sums_ref, stc_ref, bgd_ref, gc_ref, dep_ref, xf_ref, lf_ref, xa_ref, nrm_ref, qkv_ref, prob_ref, att_ref, xc_ref,
-    cn_ref, gat_ref, sig_ref, rgt_ref, ri_ref, rs_ref,
+    len_ref, sums_ref, stc_ref, bgd_ref, dep_ref, gat_ref, ri_ref, ra_ref, rc_ref,
+    gc_far, xc_far, cn_far, sig_far, rgt_far, att_far, qkv_far, prob_far, nrm_far, lf_far, xa_far, xf_far,
     cols_ref, up_ref, upp_ref, dnp_ref, wqkv_t_ref, wob_ref, pwp_ref,
     grad_ref, gdn_ref, gup_ref, gpw_ref, gqkv_ref, go_ref, rel_ref, vec_ref,
-    hid, dgs, olg, agr, back_s, gg, relacc, cb, tot,
+    gc_ref, xc_ref, cn_ref, sig_ref, rgt_ref, att_ref, qkv_ref, prob_ref, nrm_ref, lf_ref, xa_ref, xf_ref, sems,
+    hid, dgx, dgs, olg, agr, back_s, gg, near_s, far_s, cb, tot,
 ):
+    far = (gc_far, xc_far, cn_far, sig_far, rgt_far, att_far, qkv_far, prob_far, nrm_far, lf_far, xa_far, xf_far)
+    near = (gc_ref, xc_ref, cn_ref, sig_ref, rgt_ref, att_ref, qkv_ref, prob_ref, nrm_ref, lf_ref, xa_ref, xf_ref)
     u = pl.program_id(0)
-    length = len_ref[u]
+    utts = pl.num_programs(0) - 1
+    slot = 1 - u % 2
+
+    def copies(step):
+        at = step % 2
+        return [pltpu.make_async_copy(far[i].at[step], near[i].at[at], sems.at[i, at]) for i in range(len(far))]
+
     cols = cols_ref
 
     @pl.when(u == 0)
@@ -819,129 +870,151 @@
         for d in range(1, parts):
             total = total + sums_ref[d]
         tot[...] = jnp.concatenate([total, jnp.zeros((120, 128), f32)], axis=0).T
-        for ref in (gdn_ref, gup_ref, gpw_ref, gqkv_ref, go_ref, vec_ref, relacc):
+        for ref in (gdn_ref, gup_ref, gpw_ref, gqkv_ref, go_ref, vec_ref, near_s, far_s):
             ref[...] = jnp.zeros_like(ref)
 
-    scale = stc_ref[:D, 1:2]
-    lead = column(cols, C_BN) * scale
-    share = lead * stc_ref[:D, 2:3]
-    shift_part = share * tot[:D, 1:2]
-    gain_part = share * tot[:D, 0:1] * scale
-    for r in range(GROUP):
-        normal = dep_ref[0, :, span(r)] - stc_ref[:D, 0:1]
-        mask = plane_mask(r, length)
-        dgs[:, span(r)] = bgd_ref[0, :, span(r)] * lead - mask * (shift_part + normal * gain_part)
-
-    def conv(f, carry):
-        at = slice(8 * f, 8 * f + 8)
-        tiles = [dgs[at, span(r)] for r in range(GROUP)]
-        gated = [gat_ref[0, at, span(r)] for r in range(GROUP)]
-        totals = [None] * GROUP
-        taps = [None] * KERNEL
-        for m in range(-HALF, HALF + GROUP):
-            here = shifted(tiles, m)
+    @pl.when(u < utts)
+    def _():
+        for copy in copies(u):
+            copy.start()
+
+    @pl.when(u > 0)
+    def _():
+        for copy in copies(u - 1):
+            copy.wait()
+
+    def front():
+        scale = stc_ref[:D, 1:2]
+        lead = column(cols, C_BN) * scale
+        share = lead * stc_ref[:D, 2:3]
+        shift_part = share * tot[:D, 1:2]
+        gain_part = share * tot[:D, 0:1] * scale
+        for r in range(GROUP):
+            normal = dep_ref[0, :, span(r)] - stc_ref[:D, 0:1]
+            mask = plane_mask(r, len_ref[u])
+            dgx[:, span(r)] = bgd_ref[0, :, span(r)] * lead - mask * (shift_part + normal * gain_part)
+
+        def conv(f, carry):
+            at = slice(8 * f, 8 * f + 8)
+            tiles = [dgx[at, span(r)] for r in range(GROUP)]
+            gated = [gat_ref[0, at, span(r)] for r in range(GROUP)]
+            totals = [None] * GROUP
+            taps = [None] * KERNEL
+            for m in range(-HALF, HALF + GROUP):
+                here = shifted(tiles, m)
+                for r in range(GROUP):
+                    k = r + HALF - m
+                    if 0 <= k < KERNEL:
+                        term = wide(cb[1 + k, at, :]) * here
+                        totals[r] = term if totals[r] is None else totals[r] + term
+                        part = fold(gated[r] * here)
+                        taps[k] = part if taps[k] is None else taps[k] + part
+            vec_ref[6, at, :] += fold(tiles[0] + tiles[1] + tiles[2])
+            for k in range(KERNEL):
+                vec_ref[7 + k, at, :] += taps[k]
             for r in range(GROUP):
-                k = r + HALF - m
-                if 0 <= k < KERNEL:
-                    term = wide(cb[1 + k, at, :]) * here
-                    totals[r] = term if totals[r] is None else totals[r] + term
-                    part = fold(gated[r] * here)
-                    taps[k] = part if taps[k] is None else taps[k] + part
-        vec_ref[6, at, :] += fold(tiles[0] + tiles[1] + tiles[2])
-        for k in range(KERNEL):
-            vec_ref[7 + k, at, :] += taps[k]
-        for r in range(GROUP):
-            gg[at, span(r)] = totals[r]
-        return carry
-
-    for f in range(D // 8):
-        conv(f, 0)
-
-    def gate(r, held):
-        grad = gg[:, span(r)]
-        left = grad * sig_ref[0, :, span(r)]
-        right = grad * rgt_ref[0, :, span(r)]
-        pre_low = jnp.concatenate([left, right], axis=0).astype(bf16)
-        gpw_ref[...] += dot_nt(pre_low, cn_ref[0, :, span(r)])
-        return dot(pwp_ref[...], pre_low)[:D]
-
-    def residual(r, back):
-        xhat = xc_ref[0, :, span(r)]
-        vec_ref[0] += fold(back * xhat)
-        vec_ref[1] += fold(back)
-        grad = gc_ref[0, :, span(r)] + norm_back(back, xhat, rs_ref[0, 2:3, span(r)], column(cols, C_CV))
-        dgs[:, span(r)] = grad
-        low = pad8(grad).astype(bf16)
-        olg[128 * r : 128 * r + 128, :] = low
-        return dot(wob_ref[r], low)
-
-    made = [None] * GROUP
-
-    def keep(r, found):
-        go_ref[r] += dot_nt(window(att_ref.at[0], r), olg[128 * r : 128 * r + 128, :])
-        made[r] = found
-
-    skewed(GROUP, (gate, residual, keep))
-    agr[...] = join_windows(made).astype(bf16)
-
-    def rows(w, h):
-        return slice(GP * w + HP * h, GP * w + HP * h + HP)
-
-    def enter(h, held):
-        grad = agr[rows(0, h), :]
-        back_s[rows(2, h), :] = dot_nt(grad, prob_ref[0, h]).astype(bf16)
-        return dot_tn(qkv_ref[0, rows(2, h), :], grad)
-
-    def soften(h, prob_grad):
-        probs = prob_ref[0, h].astype(f32)
-        inner = jnp.sum(probs * prob_grad, axis=0, keepdims=True)
-        score = probs * (prob_grad - inner)
-        relacc[h] += score
-        return score.astype(bf16)
-
-    def turn(h, low):
-        back_s[rows(0, h), :] = (dot(qkv_ref[0, rows(1, h), :], low) * SCALE).astype(bf16)
-        back_s[rows(1, h), :] = (dot_nt(qkv_ref[0, rows(0, h), :], low) * SCALE).astype(bf16)
-
-    skewed(HEADS, (enter, soften, turn))
-
-    def project(r, held):
-        stack = jnp.concatenate([window(back_s, r, GP * w) for w in range(3)], axis=0)
-        gqkv_ref[r] += dot_nt(stack, nrm_ref[0, 128 * r : 128 * r + 128, :])
-        return dot(wqkv_t_ref[r], stack)[:D], dot(up_ref[...], lf_ref[0, :, span(r)])
-
-    def ffn_in(r, held):
-        back, half = held
-        xhat = xa_ref[0, :, span(r)]
-        vec_ref[2] += fold(back * xhat)
-        vec_ref[3] += fold(back)
-        grad = dgs[:, span(r)] + norm_back(back, xhat, rs_ref[0, 1:2, span(r)], column(cols, C_AT))
-        low = pad8(grad).astype(bf16)
-        return grad, low, half, dot(dnp_ref[...], low)
-
-    def ffn_mid(r, held):
-        grad, branch, half, back = held
-        t = jnp.tanh(half)
-        hid[:FF, span(r)] = (half + half * t).astype(bf16)
-        pre_low = ((1.0 + t) * (1.0 + half * (1.0 - t)) * back).astype(bf16)
-        gdn_ref[...] += dot_nt(hid[:, span(r)], branch)
-        gup_ref[...] += dot_nt(pre_low, lf_ref[0, :, span(r)])
-        return grad, dot(upp_ref[...], pre_low)[:D]
-
-    def ffn_out(r, held):
-        grad, back = held
-        xhat = xf_ref[0, :, span(r)]
-        vec_ref[4] += fold(back * xhat)
-        vec_ref[5] += fold(back)
-        grad_ref[0, :, span(r)] = grad + norm_back(back, xhat, ri_ref[0, 0:1, span(r)], column(cols, C_F1))
-
-    skewed(GROUP, (project, ffn_in, ffn_mid, ffn_out))
-
-    @pl.when(u == pl.num_programs(0) - 1)
+                gg[at, span(r)] = totals[r]
+            return carry
+
+        for f in range(D // 8):
+            conv(f, 0)
+
+    def back():
+        def gate(r, held):
+            grad = gg[:, span(r)]
+            left = grad * sig_ref[slot, :, span(r)]
+            right = grad * rgt_ref[slot, :, span(r)]
+            pre_low = jnp.concatenate([left, right], axis=0).astype(bf16)
+            gpw_ref[...] += dot_nt(pre_low, cn_ref[slot, :, span(r)])
+            return dot(pwp_ref[...], pre_low)[:D]
+
+        def residual(r, back):
+            xhat = xc_ref[slot, :, span(r)]
+            vec_ref[0] += fold(back * xhat)
+            vec_ref[1] += fold(back)
+            grad = gc_ref[slot, :, span(r)] + norm_back(back, xhat, rc_ref[0, 0:1, span(r)], column(cols, C_CV))
+            dgs[:, span(r)] = grad
+            low = pad8(grad).astype(bf16)
+            olg[128 * r : 128 * r + 128, :] = low
+            return dot(wob_ref[r], low)
+
+        made = [None] * GROUP
+
+        def keep(r, found):
+            go_ref[r] += dot_nt(window(att_ref.at[slot], r), olg[128 * r : 128 * r + 128, :])
+            made[r] = found
+
+        skewed(GROUP, (gate, residual, keep))
+        agr[...] = join_windows(made).astype(bf16)
+
+        def rows(w, h):
+            return slice(GP * w + HP * h, GP * w + HP * h + HP)
+
+        def enter(h, held):
+            grad = agr[rows(0, h), :]
+            back_s[rows(2, h), :] = dot_nt(grad, prob_ref[slot, h]).astype(bf16)
+            return dot_tn(qkv_ref[slot, rows(2, h), :], grad)
+
+        def soften(h, prob_grad):
+            probs = prob_ref[slot, h].astype(f32)
+            inner = jnp.sum(probs * prob_grad, axis=0, keepdims=True)
+            score = probs * (prob_grad - inner)
+            add_distances(score, near_s, far_s, h)
+            return score.astype(bf16)
+
+        def turn(h, low):
+            back_s[rows(0, h), :] = (dot(qkv_ref[slot, rows(1, h), :], low) * SCALE).astype(bf16)
+            back_s[rows(1, h), :] = (dot_nt(qkv_ref[slot, rows(0, h), :], low) * SCALE).astype(bf16)
+
+        skewed(HEADS, (enter, soften, turn))
+
+        def project(r, held):
+            stack = jnp.concatenate([window(back_s, r, GP * w) for w in range(3)], axis=0)
+            gqkv_ref[r] += dot_nt(stack, nrm_ref[slot, 128 * r : 128 * r + 128, :])
+            return dot(wqkv_t_ref[r], stack)[:D], dot(up_ref[...], lf_ref[slot, :, span(r)])
+
+        def ffn_in(r, held):
+            back, half = held
+            xhat = xa_ref[slot, :, span(r)]
+            vec_ref[2] += fold(back * xhat)
+            vec_ref[3] += fold(back)
+            grad = dgs[:, span(r)] + norm_back(back, xhat, ra_ref[0, 0:1, span(r)], column(cols, C_AT))
+            low = pad8(grad).astype(bf16)
+            return grad, low, half, dot(dnp_ref[...], low)
+
+        def ffn_mid(r, held):
+            grad, branch, half, back = held
+            t = jnp.tanh(half)
+            hid[:FF, span(r)] = (half + half * t).astype(bf16)
+            pre_low = ((1.0 + t) * (1.0 + half * (1.0 - t)) * back).astype(bf16)
+            gdn_ref[...] += dot_nt(hid[:, span(r)], branch)
+            gup_ref[...] += dot_nt(pre_low, lf_ref[slot, :, span(r)])
+            return grad, dot(upp_ref[...], pre_low)[:D]
+
+        def ffn_out(r, held):
+            grad, back = held
+            xhat = xf_ref[slot, :, span(r)]
+            vec_ref[4] += fold(back * xhat)
+            vec_ref[5] += fold(back)
+            grad_ref[0, :, span(r)] = grad + norm_back(back, xhat, ri_ref[0, 0:1, span(r)], column(cols, C_F1))
+
+        skewed(GROUP, (project, ffn_in, ffn_mid, ffn_out))
+
+    @pl.when(u == 0)
     def _():
+        front()
+
+    @pl.when((u > 0) & (u < utts))
+    def _():
+        back()
+        front()
+
+    @pl.when(u == utts)
+    def _():
+        back()
         found = []
         for h in range(HEADS):
-            found.append(diagonal_sum(relacc[h]))
+            found.append(diagonal_sum(near_s[h], far_s[h]))
         stacked = jnp.concatenate(found + [jnp.zeros((4, 2 * LG), f32)], axis=0)
         high = stacked.astype(bf16)
         rest = stacked - high.astype(f32)
@@ -951,34 +1024,40 @@
         rel_ref[...] = dot_nt(high, select) + dot_nt(mid, select) + dot_nt(rest.astype(bf16), select)
 
 
-def third(lengths, sums, stc, saved, weights):
-    utts = saved[0].shape[0]
+def third(lengths, sums, stc, soon, later, weights):
+    utts = soon[0].shape[0]
     big = (D, MAXLEN)
-    outs = [(per_utt(big), (utts,) + big)]
+    outs = [(one_late(big), (utts,) + big)]
     for s in ((512, 128), (FF, 128), (240, 128), (GROUP, 3 * WROWS, 128), (GROUP, WROWS, 128), (8, 256), (22, D, 128)):
         outs.append((whole(s), s))
     return pl.pallas_call(
         third_body,
-        grid=(utts,),
+        grid=(utts + 1,),
         in_specs=[SMEM, whole(sums.shape), whole(stc.shape)]
-        + [per_utt(s.shape[1:]) for s in saved]
+        + [at_most(s.shape[1:], utts) for s in soon[:3]]
+        + [one_late(s.shape[1:]) for s in soon[3:]]
+        + [pl.BlockSpec(memory_space=pl.ANY)] * len(later)
         + [whole(w.shape) for w in weights],
         out_specs=[o[0] for o in outs],
         out_shape=[jax.ShapeDtypeStruct(o[1], f32) for o in outs],
-        scratch_shapes=[
+        scratch_shapes=[pltpu.VMEM((2,) + s.shape[1:], s.dtype) for s in later]
+        + [
+            pltpu.SemaphoreType.DMA((len(later), 2)),
             pltpu.VMEM((512, MAXLEN), bf16),
+            pltpu.VMEM(big, f32),
             pltpu.VMEM(big, f32),
             pltpu.VMEM((GP, LG), bf16),
             pltpu.VMEM((GP, LG), bf16),
             pltpu.VMEM((3 * GP, LG), bf16),
             pltpu.VMEM(big, f32),
-            pltpu.VMEM((HEADS, LG, LG), f32),
+            pltpu.VMEM((HEADS, 128, 384), f32),
+            pltpu.VMEM((HEADS, 2, 8, 128), f32),
             pltpu.VMEM((KERNEL + 1, D, 128), f32),
             pltpu.VMEM((128, 128), f32),
         ],
         name="third",
         **params(20000000000, 80000000),
-    )(lengths, sums, stc, *saved, *weights)
+    )(lengths, sums, stc, *soon, *later, *weights)
 
 
 def clean(block):
@@ -1096,16 +1175,19 @@
             if shift:
                 turned = pltpu.roll(turned, shift, 1)
             flat[y : y + 1, :] += jnp.where((here >= lo) & (here < hi), turned[:, :128], 0.0)
-    parts, rows = 2 * keep_ref.shape[0], keep_ref.shape[1]
+    parts, padded = 2 * keep_ref.shape[0], keep_ref.shape[1]
+    rows = flat.shape[0] // parts
     for d in range(parts):
-        stage[d] = flat[rows * d : rows * (d + 1), :]
+        stage[d, 0:rows, :] = flat[rows * d : rows * (d + 1), :]
+        if rows < padded:
+            stage[d, rows:padded, :] = jnp.zeros((padded - rows, 128), f32)
     for offset in range(0, parts, 2):
         keep_ref[place(offset, parts)] = stage[me_ref[0] ^ offset]
         send_ref[place(offset, parts)] = stage[me_ref[0] ^ (offset + 1)]
 
 
 def pack(parts, rows, me, grads):
-    half = o((parts // 2, rows, 128), f32)
+    half = o((parts // 2, whole_tiles(rows), 128), f32)
     return pl.pallas_call(
         pack_body,
         in_specs=[SMEM] + [VMEM] * len(grads),
@@ -1113,7 +1195,7 @@
         scratch_shapes=[
             pltpu.VMEM((F2 + 24, 128), f32),
             pltpu.VMEM((parts * rows, 128), f32),
-            pltpu.VMEM((parts, rows, 128), f32),
+            pltpu.VMEM((parts, whole_tiles(rows), 128), f32),
             pltpu.VMEM((128, 128), f32),
         ],
         name="pack",
@@ -1139,6 +1221,10 @@
     return rates, decays
 
 
+def whole_tiles(rows):
+    return -(-rows // 8) * 8
+
+
 def digits(devices):
     found, stride = [], 1
     while stride < devices:
@@ -1190,13 +1276,14 @@
     rows = shard_len // 128
     me = lax.axis_index("dp").astype(jnp.int32).reshape(1)
     entered = enter(jnp.transpose(frames, (0, 2, 1)))
+    mine = jnp.pad(master.astype(bf16).reshape(rows, 128), ((0, whole_tiles(rows) - rows), (0, 0)))
     cp = reorder(inward_body, jnp.transpose(cotangent, (0, 2, 1)), entered[3], "inward")
-    gathered, (entered, cp) = gather(master.astype(bf16).reshape(rows, 128), devices, [entered, cp])
+    gathered, (entered, cp) = gather(mine, devices, [entered, cp])
     xp, xf, rs_in, pm = entered
-    early, late = prepare(me, gathered)
+    early, late = prepare(me, gathered, rows)
     up1, dn1, wqkv, wo, pw, cols, base = early
     upp1, dnp1, up2, upp2, dn2, dnp2, pwp, pr, prp, wqkvt, wob = late
-    lf, xa, nrm, qkv, prob, att, aa, xc, cn, gat, sig, rgt, rs, dep, st = first(
+    lf, xa, nrm, qkv, prob, att, aa, xc, cn, gat, sig, rgt, ra, rc, dep, st = first(
         devices, lengths, xp, xf, (cols, up1, dn1, wqkv, wo, pw, base)
     )
     stats = lax.all_to_all(st, "dp", 0, 0)
@@ -1209,13 +1296,14 @@
     (all_sums, last, out) = lax.optimization_barrier((all_sums, last, out))
     grad, gdn1, gup1, gpw, gqkv, go, rel, vec3 = third(
         lengths, all_sums, stc,
-        (bgd, gc, dep, xf, lf, xa, nrm, qkv, prob, att, xc, cn, gat, sig, rgt, rs_in, rs),
+        (bgd, dep, gat, rs_in, ra, rc),
+        (gc, xc, cn, sig, rgt, att, qkv, prob, nrm, lf, xa, xf),
         (cols, up1, upp1, dnp1, wqkvt, wob, pwp),
     )
     keep, send = pack(devices, rows, me, (last, gdn1, gup1, gpr, gpw, gqkv, go, rel, vec3, sums))
     gin = reorder(leave_body, grad, pm, "leave")
     reduced, gin = scatter_sum(keep, send, devices, gin)
-    reduced = reduced.reshape(shard_len)
+    reduced = reduced.reshape(-1)[:shard_len]
     rates_np, decays_np = update_tables(shard_len * devices)
     start_at = lax.axis_index("dp") * shard_len
     rates = lax.dynamic_slice_in_dim(jnp.asarray(rates_np), start_at, shard_len)

time: 193 us -> 188 us (0.974)
  Pallas kernels: 144 us -> 140 us
    pallas_call x1, Pallas kernels: 50.1 us -> 46 us  [third(): pl.pallas_call(third_body, grid=(utts + 1,), in_specs=[SMEM, whole(sums.s...]
where the time goes in v4:
time: 188 us; the launch traced here: 187 us
  Pallas kernels  140 us (74%)
  starting transfers between devices  26.3 us (14%)
  waiting for transfers between devices  13.7 us (7%)
  other arithmetic  3.63 us (2%)
  local copies, waits for them, and re-layouts  2.43 us (1%)
    pallas_call x1, Pallas kernels, third(): pl.pallas_call(third_body, grid=(utts + 1,), in_specs=[SMEM, whole(sums.s...  46 us
    pallas_call x1, Pallas kernels, first(): pl.pallas_call(first_body, grid=(utts,), in_specs=[SMEM, per_utt(BIG), pe...  34.8 us
    pallas_call x1, Pallas kernels, second(): pl.pallas_call(second_body, grid=(utts,), in_specs=[SMEM, whole(stats.sha...  21.5 us
    ppermute x14, starting transfers between devices, partner(): return lax.ppermute(values, 'dp', [(i, i ^ offset) for i in range(devices)])  17.5 us
    pallas_call x3, Pallas kernels, reorder(): pl.pallas_call(body, grid=(utts,), in_specs=[per_utt(BIG), whole(pm.shape...  17.5 us
    ppermute x14, waiting for transfers between devices, partner(): return lax.ppermute(values, 'dp', [(i, i ^ offset) for i in range(devices)])  8.94 us
    all_to_all x1, starting transfers between devices, local(): stats = lax.all_to_all(st, 'dp', 0, 0)  6.26 us
    pallas_call x1, Pallas kernels, enter(): pl.pallas_call(enter_body, grid=(utts,), in_specs=[per_utt(BIG)], out_spe...  6.18 us
  transfers between devices with their start and end apart: 16, of which 7 were waited for; matrix products, arithmetic and copies ran while one was open for 0% of the time, Pallas kernels for 16%

profile of v4, /device:TPU:0, one launch (start us, length us, event | category | flops | bytes accessed | tf_op | source)
XLA Modules:
  0.0 186.8 jit_solution(3386609307121513827)
XLA Ops:
  0.6 0.8 convert_bitcast_fusion
  1.4 3.1 %collective-permute-start = (bf16[1,88,128]{2,1,0:T(8,128)(2,1)S(1)}, bf16[1,88,128]{2,1,0:T(8,128)(2,1)S(1)}, u32[]{:S(2)}, u32[]{:S(2)}) collective-permute-start(bf16[1,88,128]{2,1,0:T(8,128)(2,1)S(1)} %pad_bitcast_fusion), channel_id=1, source_target_pairs={{0,8},{1,9},{2,10},{3,11},{4,12},{5,13},{6,14},{7,15},{8,0},{9,1},... | collective-permute-start | bytes 67592 | tf_op jit(solution)/shard_map/ppermute | solution.py:1246
  4.5 2.6 %collective-permute-start.1 = (bf16[1,88,128]{2,1,0:T(8,128)(2,1)S(1)}, bf16[1,88,128]{2,1,0:T(8,128)(2,1)S(1)}, u32[]{:S(2)}, u32[]{:S(2)}) collective-permute-start(bf16[1,88,128]{2,1,0:T(8,128)(2,1)S(1)} %pad_bitcast_fusion), channel_id=1, source_target_pairs={{0,16},{1,17},{2,18},{3,19},{4,20},{5,21},{6,22},{7,23},{8,24},{9,... | collective-permute-start | bytes 67592 | tf_op jit(solution)/shard_map/ppermute | solution.py:1246
  7.1 0.0 collective-permute-start.2
  7.1 6.2 %enter.1 = (bf16[5,120,1536]{2,1,0:T(8,128)(2,1)}, f32[5,120,1536]{2,1,0:T(8,128)}, f32[5,8,1536]{2,1,0:T(8,128)}, bf16[384,384]{1,0:T(8,128)(2,1)}) custom-call(bf16[5,120,1536]{2,1,0:T(8,128)(2,1)} %bitcast.13), custom_call_target="tpu_custom_call" | custom-call | flops 2000000000 | bytes 8000000 | tf_op jit(solution)/shard_map/enter/pallas_call | solution.py:266
  13.3 0.0 collective-permute-done
  13.3 0.0 collective-permute-done.1
  13.3 0.0 collective-permute-done.2
  13.4 1.8 collective-permute-start.3
  15.1 1.5 collective-permute-start.4
  16.7 0.3 collective-permute-start.5
  16.9 5.3 %inward.1.cot_ref = bf16[5,120,1536]{2,1,0:T(8,128)(2,1)} custom-call(bf16[5,120,1536]{2,1,0:T(8,128)(2,1)} %bitcast.14, bf16[384,384]{1,0:T(8,128)(2,1)} %get-tuple-element.120.pm_ref), custom_call_target="tpu_custom_call" | custom-call | flops 2000000000 | bytes 8000000 | tf_op jit(solution)/shard_map/inward/pallas_call | solution.py:291
  22.2 0.0 collective-permute-done.3
  22.2 0.0 collective-permute-done.4
  22.2 0.0 collective-permute-done.5
  22.3 0.1 collective-permute-start.6
  22.4 1.6 collective-permute-done.6
  24.0 0.1 constant_dynamic-update-slice_fusion.4.g_ref
  24.1 0.0 copy-start.6
  24.1 0.9 copy-done.6
  25.0 3.2 %prepare.1 = (bf16[480,128]{1,0:T(8,128)(2,1)}, bf16[128,512]{1,0:T(8,128)(2,1)}, bf16[3,432,128]{2,1,0:T(8,128)(2,1)}, bf16[3,128,144]{2,1,0:T(8,128)(2,1)}, bf...) custom-call(s32[1]{0:T(128)} %bitcast.3.me_ref, bf16[32,88,128]{2,1,0:T(8,128)(2,1)} %copy-done.6), custom_call_target="tpu_custom_call" | custom-call | flops 1000000000 | bytes 2000000 | tf_op jit(solution)/shard_map/prepare/pallas_call | solution.py:493
  28.2 34.8 %first.1 = (bf16[5,128,1536]{2,1,0:T(8,128)(2,1)}, f32[5,120,1536]{2,1,0:T(8,128)}, bf16[5,384,512]{2,1,0:T(8,128)(2,1)}, bf16[5,1152,512]{2,1,0:T(8,128)(2,1)},...) custom-call(s32[5]{0:T(128)} %len_ref.5, ...), custom_call_target="tpu_custom_call" | custom-call | flops 10000000000 | bytes 60000000 | tf_op jit(solution)/shard_map/first/pallas_call | solution.py:690
  62.9 6.3 %all-to-all-start = ((f32[32,8,128]{2,1,0:T(8,128)}), f32[32,8,128]{2,1,0:T(8,128)S(1)}, u32[]{:S(2)}, u32[]{:S(2)}) async-start(f32[32,8,128]{2,1,0:T(8,128)} %get-tuple-element.105), calls=%async_computation | async-start | bytes 262144 | tf_op jit(solution)/shard_map/all_to_all | solution.py:1289
  69.2 3.6 %late.1 = (bf16[128,480]{1,0:T(8,128)(2,1)}, bf16[480,128]{1,0:T(8,128)(2,1)}, bf16[480,128]{1,0:T(8,128)(2,1)}, bf16[128,480]{1,0:T(8,128)(2,1)}, bf16[128,512]...) custom-call(s32[1]{0:T(128)} %bitcast.3.me_ref, ...), custom_call_target="tpu_custom_call" | custom-call | flops 3000000000 | bytes 10000000 | tf_op jit(solution)/shard_map/late/pallas_call | solution.py:502
  72.8 4.4 %all-to-all-done.stats_ref = f32[32,8,128]{2,1,0:T(8,128)S(1)} async-done(((f32[32,8,128]{2,1,0:T(8,128)}), f32[32,8,128]{2,1,0:T(8,128)S(1)}, u32[]{:S(2)}, u32[]{:S(2)}) %all-to-all-start) | async-done | bytes 131104 | tf_op jit(solution)/shard_map/all_to_all | solution.py:1289
  77.2 0.0 copy-start.2
  77.2 0.7 copy-done.2
  77.9 21.5 %second.1 = (bf16[5,120,1536]{2,1,0:T(8,128)(2,1)}, f32[5,120,1536]{2,1,0:T(8,128)}, f32[5,120,1536]{2,1,0:T(8,128)}, f32[32,8,128]{2,1,0:T(8,128)}, f32[128,128...) custom-call(s32[5]{0:T(128)} %len_ref.5, ...), custom_call_target="tpu_custom_call" | custom-call | flops 15000000512 | bytes 30000000 | tf_op jit(solution)/shard_map/second/pallas_call | solution.py:829
  99.4 2.6 %all-to-all-start.1 = ((f32[32,8,128]{2,1,0:T(8,128)}), f32[32,8,128]{2,1,0:T(8,128)S(1)}, u32[]{:S(2)}, u32[]{:S(2)}) async-start(f32[32,8,128]{2,1,0:T(8,128)} %get-tuple-element.115.sums_ref), calls=%async_computation.1 | async-start | bytes 262144 | tf_op jit(solution)/shard_map/all_to_all | solution.py:1293
  102.0 5.3 %outward.1 = bf16[5,120,1536]{2,1,0:T(8,128)(2,1)} custom-call(bf16[5,120,1536]{2,1,0:T(8,128)(2,1)} %get-tuple-element.119.out_ref, bf16[384,384]{1,0:T(8,128)(2,1)} %get-tuple-element.120.pm_ref), custom_call_target="tpu_custom_call" | custom-call | flops 2000000000 | bytes 8000000 | tf_op jit(solution)/shard_map/outward/pallas_call | solution.py:291
  107.4 2.6 %ahead.1.last_ref = f32[909,128]{1,0:T(8,128)} custom-call(f32[512,128]{1,0:T(8,128)} %get-tuple-element.116.dn_ref, f32[480,128]{1,0:T(8,128)} %get-tuple-element.117.up_ref, f32[4,120,128]{2,1,0:T(8,128)} %get-tuple-element.118.vec_ref), custom_call_target="tpu_custom_call" | custom-call | flops 2000000000 | bytes 8000000 | tf_op jit(solution)/shard_map/ahead/pallas_call | solution.py:1118
  109.9 0.3 all-to-all-done.1.sums_ref
  110.3 0.0 copy-start.1
  110.3 0.7 copy-done.1
  110.9 46.0 %third.1 = (f32[5,120,1536]{2,1,0:T(8,128)}, f32[512,128]{1,0:T(8,128)}, f32[480,128]{1,0:T(8,128)}, f32[240,128]{1,0:T(8,128)}, f32[3,432,128]{2,1,0:T(8,128)},...) custom-call(s32[5]{0:T(128)} %len_ref.5, f32[32,8,128]{2,1,0:T(8,128)} %copy-done.1, ...), custom_call_target="tpu_custom_call" | custom-call | flops 20000000000 | bytes 80000000 | tf_op jit(solution)/shard_map/third/pallas_call | solution.py:1033
  156.9 4.6 %pack.1 = (f32[16,88,128]{2,1,0:T(8,128)}, f32[16,88,128]{2,1,0:T(8,128)}) custom-call(s32[1]{0:T(128)} %bitcast.3.me_ref, f32[909,128]{1,0:T(8,128)} %ahead.1.last_ref, f32[512,128]{1,0:T(8,128)} %get-tuple-element.146.dn1_ref, f32[480,128]{1,0:T(8,128)} %get-tuple-element.147.up1_ref, f32[128,128]{1,0:T(8,128)} %get-tuple-element.148.pr_ref, ...), custom_call_target="tpu_custom_call" | custom-call | flops 1000000000 | bytes 5000000 | tf_op jit(solution)/shard_map/pack/pallas_call | solution.py:1191
  161.5 0.2 collective-permute-start.7
  161.7 2.2 %collective-permute-done.7 = f32[16,88,128]{2,1,0:T(8,128)S(1)} collective-permute-done((f32[16,88,128]{2,1,0:T(8,128)}, f32[16,88,128]{2,1,0:T(8,128)S(1)}, u32[]{:S(2)}, u32[]{:S(2)}) %collective-permute-start.7) | collective-permute-done | bytes 720928 | tf_op jit(solution)/shard_map/ppermute | solution.py:1246
  163.9 1.2 add.45
  165.1 1.4 collective-permute-start.8
  166.5 1.5 collective-permute-start.9
  168.0 0.7 collective-permute-start.10
  168.7 0.0 copy-start
  168.7 0.0 copy-start.3
  168.7 0.0 copy-start.4
  168.7 0.0 copy-start.5
  168.7 6.9 %leave.1 = f32[5,120,1536]{2,1,0:T(8,128)} custom-call(f32[5,120,1536]{2,1,0:T(8,128)} %get-tuple-element.156.grad_ref, bf16[384,384]{1,0:T(8,128)(2,1)} %get-tuple-element.120.pm_ref), custom_call_target="tpu_custom_call" | custom-call | flops 2000000000 | bytes 8000000 | tf_op jit(solution)/shard_map/leave/pallas_call | solution.py:291
  175.5 0.0 collective-permute-done.8
  175.6 1.1 collective-permute-done.9
  176.7 0.0 collective-permute-done.10
  176.7 3.5 %collective-permute-start.13 = (f32[1,88,128]{2,1,0:T(8,128)S(1)}, f32[1,88,128]{2,1,0:T(8,128)S(1)}, u32[]{:S(2)}, u32[]{:S(2)}) collective-permute-start(f32[1,88,128]{2,1,0:T(8,128)S(1)} %get-tuple-element.170), channel_id=1, source_target_pairs={{0,24},{1,25},{2,26},{3,27},{4,28},{5,29},{6,30},{7,31},{8,16},{9,... | collective-permute-start | bytes 135176 | tf_op jit(solution)/shard_map/ppermute | solution.py:1246
  180.3 0.0 collective-permute-start.12
  180.3 0.9 collective-permute-start.11
  181.2 1.5 collective-permute-done.13
  182.7 2.5 %collective-permute-done.12 = f32[1,88,128]{2,1,0:T(8,128)S(1)} collective-permute-done((f32[1,88,128]{2,1,0:T(8,128)S(1)}, f32[1,88,128]{2,1,0:T(8,128)S(1)}, u32[]{:S(2)}, u32[]{:S(2)}) %collective-permute-start.12) | collective-permute-done | bytes 45088 | tf_op jit(solution)/shard_map/ppermute | solution.py:1246
  185.2 0.0 collective-permute-done.11
  185.2 0.0 copy-done
  185.2 0.0 copy-done.3
  185.2 0.0 copy-done.4
  185.2 0.0 copy-done.5
  185.2 1.6 multiply_add_fusion.1
  (13 shorter events, 0.2 us)
Async XLA Ops:
  1.4 11.9 %collective-permute-start = (bf16[1,88,128]{2,1,0:T(8,128)(2,1)S(1)}, bf16[1,88,128]{2,1,0:T(8,128)(2,1)S(1)}, u32[]{:S(2)}, u32[]{:S(2)}) collective-permute-start(bf16[1,88,128]{2,1,0:T(8,128)(2,1)S(1)} %pad_bitcast_fusion), channel_id=1, source_target_pairs={{0,8},{1,9},{2,10},{3,11},{4,12},{5,13},{6,14},{7,15},{8,0},{9,1},... | collective-permute-start | bytes 67592 | tf_op jit(solution)/shard_map/ppermute | solution.py:1246
  4.5 8.8 %collective-permute-start.1 = (bf16[1,88,128]{2,1,0:T(8,128)(2,1)S(1)}, bf16[1,88,128]{2,1,0:T(8,128)(2,1)S(1)}, u32[]{:S(2)}, u32[]{:S(2)}) collective-permute-start(bf16[1,88,128]{2,1,0:T(8,128)(2,1)S(1)} %pad_bitcast_fusion), channel_id=1, source_target_pairs={{0,16},{1,17},{2,18},{3,19},{4,20},{5,21},{6,22},{7,23},{8,24},{9,... | collective-permute-start | bytes 67592 | tf_op jit(solution)/shard_map/ppermute | solution.py:1246
  7.1 6.2 %collective-permute-start.2 = (bf16[1,88,128]{2,1,0:T(8,128)(2,1)S(1)}, bf16[1,88,128]{2,1,0:T(8,128)(2,1)S(1)}, u32[]{:S(2)}, u32[]{:S(2)}) collective-permute-start(bf16[1,88,128]{2,1,0:T(8,128)(2,1)S(1)} %pad_bitcast_fusion), channel_id=1, source_target_pairs={{0,24},{1,25},{2,26},{3,27},{4,28},{5,29},{6,30},{7,31},{8,16},{9,... | collective-permute-start | bytes 67592 | tf_op jit(solution)/shard_map/ppermute | solution.py:1246
  13.4 8.8 %collective-permute-start.3 = (bf16[4,88,128]{2,1,0:T(8,128)(2,1)S(1)}, bf16[4,88,128]{2,1,0:T(8,128)(2,1)S(1)}, u32[]{:S(2)}, u32[]{:S(2)}) collective-permute-start(bf16[4,88,128]{2,1,0:T(8,128)(2,1)S(1)} %constant_dynamic-update-slice_fusion), channel_id=1, source_target_pairs={{0,2},{1,3},{2,0},{3,1},{4,6},{5,7},{6,4},{7,5},{8,10},{9,11},{10,... | collective-permute-start | bytes 270344 | tf_op jit(solution)/shard_map/ppermute | solution.py:1246
  15.1 7.1 %collective-permute-start.4 = (bf16[4,88,128]{2,1,0:T(8,128)(2,1)S(1)}, bf16[4,88,128]{2,1,0:T(8,128)(2,1)S(1)}, u32[]{:S(2)}, u32[]{:S(2)}) collective-permute-start(bf16[4,88,128]{2,1,0:T(8,128)(2,1)S(1)} %constant_dynamic-update-slice_fusion), channel_id=1, source_target_pairs={{0,4},{1,5},{2,6},{3,7},{4,0},{5,1},{6,2},{7,3},{8,12},{9,13},{10,... | collective-permute-start | bytes 270344 | tf_op jit(solution)/shard_map/ppermute | solution.py:1246
  16.7 5.6 %collective-permute-start.5 = (bf16[4,88,128]{2,1,0:T(8,128)(2,1)S(1)}, bf16[4,88,128]{2,1,0:T(8,128)(2,1)S(1)}, u32[]{:S(2)}, u32[]{:S(2)}) collective-permute-start(bf16[4,88,128]{2,1,0:T(8,128)(2,1)S(1)} %constant_dynamic-update-slice_fusion), channel_id=1, source_target_pairs={{0,6},{1,7},{2,4},{3,5},{4,2},{5,3},{6,0},{7,1},{8,14},{9,15},{10,... | collective-permute-start | bytes 270344 | tf_op jit(solution)/shard_map/ppermute | solution.py:1246
  22.3 1.7 collective-permute-start.6
  24.1 0.9 copy-start.6
  62.9 14.3 %all-to-all-start = ((f32[32,8,128]{2,1,0:T(8,128)}), f32[32,8,128]{2,1,0:T(8,128)S(1)}, u32[]{:S(2)}, u32[]{:S(2)}) async-start(f32[32,8,128]{2,1,0:T(8,128)} %get-tuple-element.105), calls=%async_computation | async-start | bytes 262144 | tf_op jit(solution)/shard_map/all_to_all | solution.py:1289
  77.2 0.7 copy-start.2
  99.4 10.8 %all-to-all-start.1 = ((f32[32,8,128]{2,1,0:T(8,128)}), f32[32,8,128]{2,1,0:T(8,128)S(1)}, u32[]{:S(2)}, u32[]{:S(2)}) async-start(f32[32,8,128]{2,1,0:T(8,128)} %get-tuple-element.115.sums_ref), calls=%async_computation.1 | async-start | bytes 262144 | tf_op jit(solution)/shard_map/all_to_all | solution.py:1293
  110.3 0.7 copy-start.1
  161.5 2.4 %collective-permute-start.7 = (f32[16,88,128]{2,1,0:T(8,128)}, f32[16,88,128]{2,1,0:T(8,128)S(1)}, u32[]{:S(2)}, u32[]{:S(2)}) collective-permute-start(f32[16,88,128]{2,1,0:T(8,128)} %get-tuple-element.155), channel_id=1, source_target_pairs={{0,1},{1,0},{2,3},{3,2},{4,5},{5,4},{6,7},{7,6},{8,9},{9,8},{10,11... | collective-permute-start | bytes 2162696 | tf_op jit(solution)/shard_map/ppermute | solution.py:1246
  165.1 10.4 %collective-permute-start.8 = (f32[4,88,128]{2,1,0:T(8,128)S(1)}, f32[4,88,128]{2,1,0:T(8,128)S(1)}, u32[]{:S(2)}, u32[]{:S(2)}) collective-permute-start(f32[4,88,128]{2,1,0:T(8,128)S(1)} %get-tuple-element.168), channel_id=1, source_target_pairs={{0,2},{1,3},{2,0},{3,1},{4,6},{5,7},{6,4},{7,5},{8,10},{9,11},{10,... | collective-permute-start | bytes 540680 | tf_op jit(solution)/shard_map/ppermute | solution.py:1246
  166.5 10.2 %collective-permute-start.9 = (f32[4,88,128]{2,1,0:T(8,128)S(1)}, f32[4,88,128]{2,1,0:T(8,128)S(1)}, u32[]{:S(2)}, u32[]{:S(2)}) collective-permute-start(f32[4,88,128]{2,1,0:T(8,128)S(1)} %get-tuple-element.167), channel_id=1, source_target_pairs={{0,4},{1,5},{2,6},{3,7},{4,0},{5,1},{6,2},{7,3},{8,12},{9,13},{10,... | collective-permute-start | bytes 540680 | tf_op jit(solution)/shard_map/ppermute | solution.py:1246
  168.0 8.7 %collective-permute-start.10 = (f32[4,88,128]{2,1,0:T(8,128)S(1)}, f32[4,88,128]{2,1,0:T(8,128)S(1)}, u32[]{:S(2)}, u32[]{:S(2)}) collective-permute-start(f32[4,88,128]{2,1,0:T(8,128)S(1)} %get-tuple-element.166), channel_id=1, source_target_pairs={{0,6},{1,7},{2,4},{3,5},{4,2},{5,3},{6,0},{7,1},{8,14},{9,15},{10,... | collective-permute-start | bytes 540680 | tf_op jit(solution)/shard_map/ppermute | solution.py:1246
  168.7 16.5 %copy-start = (f32[10624]{0:T(1024)S(1)}, f32[10624]{0:T(1024)}, u32[]{:S(2)}) copy-start(f32[10624]{0:T(1024)} %param.12) | copy-start | bytes 127492
  168.7 16.5 %copy-start.3 = (f32[10624]{0:T(1024)S(1)}, f32[10624]{0:T(1024)}, u32[]{:S(2)}) copy-start(f32[10624]{0:T(1024)} %param.15) | copy-start | bytes 127492
  168.7 16.5 %copy-start.4 = (f32[10624]{0:T(1024)S(1)}, f32[10624]{0:T(1024)}, u32[]{:S(2)}) copy-start(f32[10624]{0:T(1024)} %param.13) | copy-start | bytes 127492
  168.7 16.6 %copy-start.5 = (f32[10624]{0:T(1024)S(1)}, f32[10624]{0:T(1024)}, u32[]{:S(2)}) copy-start(f32[10624]{0:T(1024)} %param.14) | copy-start | bytes 127492
  176.7 6.0 %collective-permute-start.13 = (f32[1,88,128]{2,1,0:T(8,128)S(1)}, f32[1,88,128]{2,1,0:T(8,128)S(1)}, u32[]{:S(2)}, u32[]{:S(2)}) collective-permute-start(f32[1,88,128]{2,1,0:T(8,128)S(1)} %get-tuple-element.170), channel_id=1, source_target_pairs={{0,24},{1,25},{2,26},{3,27},{4,28},{5,29},{6,30},{7,31},{8,16},{9,... | collective-permute-start | bytes 135176 | tf_op jit(solution)/shard_map/ppermute | solution.py:1246
  180.3 4.9 %collective-permute-start.12 = (f32[1,88,128]{2,1,0:T(8,128)S(1)}, f32[1,88,128]{2,1,0:T(8,128)S(1)}, u32[]{:S(2)}, u32[]{:S(2)}) collective-permute-start(f32[1,88,128]{2,1,0:T(8,128)S(1)} %get-tuple-element.171), channel_id=1, source_target_pairs={{0,16},{1,17},{2,18},{3,19},{4,20},{5,21},{6,22},{7,23},{8,24},{9,... | collective-permute-start | bytes 135176 | tf_op jit(solution)/shard_map/ppermute | solution.py:1246
  180.3 4.9 %collective-permute-start.11 = (f32[1,88,128]{2,1,0:T(8,128)S(1)}, f32[1,88,128]{2,1,0:T(8,128)S(1)}, u32[]{:S(2)}, u32[]{:S(2)}) collective-permute-start(f32[1,88,128]{2,1,0:T(8,128)S(1)} %get-tuple-element.172), channel_id=1, source_target_pairs={{0,8},{1,9},{2,10},{3,11},{4,12},{5,13},{6,14},{7,15},{8,0},{9,1},... | collective-permute-start | bytes 135176 | tf_op jit(solution)/shard_map/ppermute | solution.py:1246

commit v5 on v4

--- a/solution.py
+++ b/solution.py
@@ -249,54 +249,93 @@
     return jnp.where(t == GROUP * (c % 128) + c // 128, 1.0, 0.0).astype(bf16)
 
 
-def enter_body(x_ref, xp_ref, xf_ref, rs_ref, pm_ref):
-    @pl.when(pl.program_id(0) == 0)
-    def _():
-        pm_ref[...] = permutation()
-
-    x = permute_in(x_ref[0].astype(f32), pm_ref[...])
-    xp_ref[0] = x.astype(bf16)
-    xhat, rstd = norm(x)
-    xf_ref[0] = xhat
-    rs_ref[0] = jnp.broadcast_to(rstd, (8, MAXLEN))
+ANY = pl.BlockSpec(memory_space=pl.ANY)
+
+
+def streamed(work, far_in, near_in, far_out, near_out, sems, first_utt):
+    count = near_in.shape[0]
+
+    def coming(u):
+        return pltpu.make_async_copy(far_in.at[u + first_utt], near_in.at[u], sems.at[0, u])
+
+    def going(u):
+        pairs = enumerate(zip(near_out, far_out))
+        return [pltpu.make_async_copy(near.at[u], far.at[u + first_utt], sems.at[k + 1, u]) for k, (near, far) in pairs]
+
+    for u in range(count):
+        coming(u).start()
+
+    def step(u, carry):
+        coming(u).wait()
+        work(u)
+        for copy in going(u):
+            copy.start()
+        return carry
+
+    lax.fori_loop(0, count, step, 0)
+    for u in range(count):
+        for copy in going(u):
+            copy.wait()
+
+
+def enter_body(x_far, xp_far, xf_far, rs_far, pm_ref, x_near, xp_near, xf_near, rs_near, sems):
+    pm_ref[...] = permutation()
+
+    def work(u):
+        x = permute_in(x_near[u].astype(f32), pm_ref[...])
+        xp_near[u] = x.astype(bf16)
+        xhat, rstd = norm(x)
+        xf_near[u] = xhat
+        rs_near[u] = jnp.broadcast_to(rstd, (8, MAXLEN))
+
+    streamed(work, x_far, x_near, (xp_far, xf_far, rs_far), (xp_near, xf_near, rs_near), sems, 0)
 
 
 def enter(x):
     utts = x.shape[0]
+    made = [o((utts,) + BIG), o((utts,) + BIG, f32), o((utts, 8, MAXLEN), f32)]
     return pl.pallas_call(
         enter_body,
-        grid=(utts,),
-        in_specs=[per_utt(BIG)],
-        out_specs=[per_utt(BIG)] * 2 + [per_utt((8, MAXLEN)), whole((384, 384))],
-        out_shape=[o((utts,) + BIG), o((utts,) + BIG, f32), o((utts, 8, MAXLEN), f32), o((384, 384))],
+        in_specs=[ANY],
+        out_specs=[ANY] * 3 + [VMEM],
+        out_shape=made + [o((384, 384))],
+        scratch_shapes=[pltpu.VMEM(m.shape, m.dtype) for m in [x] + made] + [pltpu.SemaphoreType.DMA((4, utts))],
         name="enter",
         **params(2 * 10**9, 8 * 10**6),
     )(x)
 
 
-def inward_body(cot_ref, pm_ref, cp_ref):
-    cp_ref[0] = permute_in(cot_ref[0].astype(f32), pm_ref[...]).astype(bf16)
-
-
-def outward_body(out_ref, pm_ref, done_ref):
-    done_ref[0] = permute_out(out_ref[0].astype(f32), pm_ref[...]).astype(bf16)
-
-
-def leave_body(grad_ref, pm_ref, gin_ref):
-    gin_ref[0] = permute_out_wide(grad_ref[0], pm_ref[...])
-
-
-def reorder(body, values, pm, name):
-    utts = values.shape[0]
+def inward(values, pm):
+    return permute_in(values.astype(f32), pm).astype(bf16)
+
+
+def outward(values, pm):
+    return permute_out(values.astype(f32), pm).astype(bf16)
+
+
+def reorder(turn, values, pm, name, first_utt=0, count=None, begun=None):
+    count = values.shape[0] if count is None else count
+    more = [] if begun is None else [begun]
+
+    def body(far_in, pm_ref, *refs):
+        far_out, near_in, near_out, sems = refs[len(more) :]
+
+        def work(u):
+            near_out[u] = turn(near_in[u], pm_ref[...])
+
+        streamed(work, far_in, near_in, (far_out,), (near_out,), sems, first_utt)
+
+    room = pltpu.VMEM((count,) + BIG, values.dtype)
     return pl.pallas_call(
         body,
-        grid=(utts,),
-        in_specs=[per_utt(BIG), whole(pm.shape)],
-        out_specs=per_utt(BIG),
-        out_shape=o((utts,) + BIG, values.dtype),
+        in_specs=[ANY, VMEM] + [ANY] * len(more),
+        out_specs=ANY,
+        out_shape=o(values.shape, values.dtype),
+        scratch_shapes=[room, room, pltpu.SemaphoreType.DMA((2, count))],
+        input_output_aliases={2: 0} if more else {},
         name=name,
         **params(2 * 10**9, 8 * 10**6),
-    )(values, pm)
+    )(values, pm, *more)
 
 
 def unpack(me_ref, g_ref, flat, tb):
@@ -1259,15 +1298,19 @@
 
 def scatter_sum(keep, send, devices, beside):
     total = keep + partner(send, 1, devices)
-    for stride, size in digits(devices)[1:]:
+    made = None
+    for k, (stride, size) in enumerate(digits(devices)[1:]):
         parts = total.reshape((size, total.shape[0] // size) + total.shape[1:])
-        found = [partner(parts[j], stride * j, devices) for j in range(1, size)]
-        if stride == 2:
-            found, beside = lax.optimization_barrier((found, beside))
+        kind = bf16 if stride == 2 else f32
+        found = [partner(parts[j].astype(kind), stride * j, devices) for j in range(1, size)]
+        if k < len(beside):
+            found, made = lax.optimization_barrier((found, beside[k](made)))
         total = parts[0]
         for part in found:
-            total = total + part
-    return total, beside
+            total = total + part.astype(f32)
+    for work in beside[max(0, len(digits(devices)) - 1) :]:
+        made = work(made)
+    return total, made
 
 
 def local(frames, lengths, cotangent, master, moment_one, moment_two, average):
@@ -1277,7 +1320,7 @@
     me = lax.axis_index("dp").astype(jnp.int32).reshape(1)
     entered = enter(jnp.transpose(frames, (0, 2, 1)))
     mine = jnp.pad(master.astype(bf16).reshape(rows, 128), ((0, whole_tiles(rows) - rows), (0, 0)))
-    cp = reorder(inward_body, jnp.transpose(cotangent, (0, 2, 1)), entered[3], "inward")
+    cp = reorder(inward, jnp.transpose(cotangent, (0, 2, 1)), entered[3], "inward")
     gathered, (entered, cp) = gather(mine, devices, [entered, cp])
     xp, xf, rs_in, pm = entered
     early, late = prepare(me, gathered, rows)
@@ -1292,7 +1335,7 @@
     )
     all_sums = lax.all_to_all(sums, "dp", 0, 0)
     last = pack_ahead(gdn2, gup2, vec2)
-    out = reorder(outward_body, out, pm, "outward")
+    out = reorder(outward, out, pm, "outward")
     (all_sums, last, out) = lax.optimization_barrier((all_sums, last, out))
     grad, gdn1, gup1, gpw, gqkv, go, rel, vec3 = third(
         lengths, all_sums, stc,
@@ -1301,8 +1344,17 @@
         (cols, up1, upp1, dnp1, wqkvt, wob, pwp),
     )
     keep, send = pack(devices, rows, me, (last, gdn1, gup1, gpr, gpw, gqkv, go, rel, vec3, sums))
-    gin = reorder(leave_body, grad, pm, "leave")
-    reduced, gin = scatter_sum(keep, send, devices, gin)
+    utts = grad.shape[0]
+    begin = (utts + 1) // 2
+    reduced, gin = scatter_sum(
+        keep,
+        send,
+        devices,
+        [
+            lambda made: reorder(permute_out_wide, grad, pm, "leave", 0, begin),
+            lambda made: reorder(permute_out_wide, grad, pm, "leave", begin, utts - begin, made),
+        ],
+    )
     reduced = reduced.reshape(-1)[:shard_len]
     rates_np, decays_np = update_tables(shard_len * devices)
     start_at = lax.axis_index("dp") * shard_len

time: 188 us -> 184 us (0.979)
  waiting for transfers between devices: 13.7 us -> 9.94 us
    ppermute x14, waiting for transfers between devices: 8.94 us -> 4.67 us  [partner(): return lax.ppermute(values, 'dp', [(i, i ^ offset) for i in range(devices)])]
    pallas_call x4 -> x5, Pallas kernels: 23.7 us -> 24.4 us  [the longest x4 18.8 us: reorder(): pl.pallas_call(body, in_specs=[ANY, VMEM] + [ANY] * len(more), out_specs=...]
  transfers between devices with their start and end apart: 16 -> 16, of which waited for: 7 -> 6; matrix products, arithmetic and copies ran while one was open for 0% -> 0% of each run, Pallas kernels for 16% -> 17%
where the time goes in v5:
time: 184 us
  Pallas kernels  141 us (77%)
  starting transfers between devices  26.1 us (14%)
  waiting for transfers between devices  9.94 us (5%)
  other arithmetic  3.67 us (2%)
  local copies, waits for them, and re-layouts  2.4 us (1%)
    pallas_call x1, Pallas kernels, third(): pl.pallas_call(third_body, grid=(utts + 1,), in_specs=[SMEM, whole(sums.s...  46.1 us
    pallas_call x1, Pallas kernels, first(): pl.pallas_call(first_body, grid=(utts,), in_specs=[SMEM, per_utt(BIG), pe...  34.7 us
    pallas_call x1, Pallas kernels, second(): pl.pallas_call(second_body, grid=(utts,), in_specs=[SMEM, whole(stats.sha...  21.5 us
    pallas_call x4, Pallas kernels, reorder(): pl.pallas_call(body, in_specs=[ANY, VMEM] + [ANY] * len(more), out_specs=...  18.8 us
    ppermute x14, starting transfers between devices, partner(): return lax.ppermute(values, 'dp', [(i, i ^ offset) for i in range(devices)])  17.6 us
    all_to_all x1, starting transfers between devices, local(): stats = lax.all_to_all(st, 'dp', 0, 0)  5.89 us
    pallas_call x1, Pallas kernels, enter(): pl.pallas_call(enter_body, in_specs=[ANY], out_specs=[ANY] * 3 + [VMEM],...  5.56 us
    ppermute x14, waiting for transfers between devices, partner(): return lax.ppermute(values, 'dp', [(i, i ^ offset) for i in range(devices)])  4.67 us
  transfers between devices with their start and end apart: 16, of which 6 were waited for; matrix products, arithmetic and copies ran while one was open for 0% of the time, Pallas kernels for 17%

profile of v5, /device:TPU:0, one launch (start us, length us, event | category | flops | bytes accessed | tf_op | source)
XLA Modules:
  0.0 183.6 jit_solution(1184946953242920870)
XLA Ops:
  0.6 0.8 convert_bitcast_fusion
  1.4 3.1 %collective-permute-start = (bf16[1,88,128]{2,1,0:T(8,128)(2,1)S(1)}, bf16[1,88,128]{2,1,0:T(8,128)(2,1)S(1)}, u32[]{:S(2)}, u32[]{:S(2)}) collective-permute-start(bf16[1,88,128]{2,1,0:T(8,128)(2,1)S(1)} %pad_bitcast_fusion), channel_id=1, source_target_pairs={{0,8},{1,9},{2,10},{3,11},{4,12},{5,13},{6,14},{7,15},{8,0},{9,1},... | collective-permute-start | bytes 67592 | tf_op jit(solution)/shard_map/ppermute | solution.py:1285
  4.5 2.6 %collective-permute-start.1 = (bf16[1,88,128]{2,1,0:T(8,128)(2,1)S(1)}, bf16[1,88,128]{2,1,0:T(8,128)(2,1)S(1)}, u32[]{:S(2)}, u32[]{:S(2)}) collective-permute-start(bf16[1,88,128]{2,1,0:T(8,128)(2,1)S(1)} %pad_bitcast_fusion), channel_id=1, source_target_pairs={{0,16},{1,17},{2,18},{3,19},{4,20},{5,21},{6,22},{7,23},{8,24},{9,... | collective-permute-start | bytes 67592 | tf_op jit(solution)/shard_map/ppermute | solution.py:1285
  7.1 0.0 collective-permute-start.2
  7.1 5.6 %enter.1 = (bf16[5,120,1536]{2,1,0:T(8,128)(2,1)}, f32[5,120,1536]{2,1,0:T(8,128)}, f32[5,8,1536]{2,1,0:T(8,128)}, bf16[384,384]{1,0:T(8,128)(2,1)}) custom-call(bf16[5,120,1536]{2,1,0:T(8,128)(2,1)} %bitcast.13), custom_call_target="tpu_custom_call" | custom-call | flops 2000000000 | bytes 8000000 | tf_op jit(solution)/shard_map/enter/pallas_call | solution.py:297
  12.7 0.0 collective-permute-done
  12.7 0.0 collective-permute-done.1
  12.7 0.0 collective-permute-done.2
  12.8 1.8 collective-permute-start.3
  14.5 1.5 collective-permute-start.4
  16.1 0.3 collective-permute-start.5
  16.3 4.8 %inward.1.cot_ref = bf16[5,120,1536]{2,1,0:T(8,128)(2,1)} custom-call(bf16[5,120,1536]{2,1,0:T(8,128)(2,1)} %bitcast.14, bf16[384,384]{1,0:T(8,128)(2,1)} %get-tuple-element.124.pm_ref), custom_call_target="tpu_custom_call" | custom-call | flops 2000000000 | bytes 8000000 | tf_op jit(solution)/shard_map/inward/pallas_call | solution.py:329
  21.1 0.0 collective-permute-done.3
  21.1 0.0 collective-permute-done.4
  21.1 0.4 collective-permute-done.5
  21.5 0.1 collective-permute-start.6
  21.7 1.6 collective-permute-done.6
  23.3 0.1 constant_dynamic-update-slice_fusion.4.g_ref
  23.3 0.0 copy-start.6
  23.4 0.9 copy-done.6
  24.2 3.2 %prepare.1 = (bf16[480,128]{1,0:T(8,128)(2,1)}, bf16[128,512]{1,0:T(8,128)(2,1)}, bf16[3,432,128]{2,1,0:T(8,128)(2,1)}, bf16[3,128,144]{2,1,0:T(8,128)(2,1)}, bf...) custom-call(s32[1]{0:T(128)} %bitcast.3.me_ref, bf16[32,88,128]{2,1,0:T(8,128)(2,1)} %copy-done.6), custom_call_target="tpu_custom_call" | custom-call | flops 1000000000 | bytes 2000000 | tf_op jit(solution)/shard_map/prepare/pallas_call | solution.py:532
  27.4 34.7 %first.1 = (bf16[5,128,1536]{2,1,0:T(8,128)(2,1)}, f32[5,120,1536]{2,1,0:T(8,128)}, bf16[5,384,512]{2,1,0:T(8,128)(2,1)}, bf16[5,1152,512]{2,1,0:T(8,128)(2,1)},...) custom-call(s32[5]{0:T(128)} %len_ref.5, ...), custom_call_target="tpu_custom_call" | custom-call | flops 10000000000 | bytes 60000000 | tf_op jit(solution)/shard_map/first/pallas_call | solution.py:729
  62.2 5.9 %all-to-all-start = ((f32[32,8,128]{2,1,0:T(8,128)}), f32[32,8,128]{2,1,0:T(8,128)S(1)}, u32[]{:S(2)}, u32[]{:S(2)}) async-start(f32[32,8,128]{2,1,0:T(8,128)} %get-tuple-element.109), calls=%async_computation | async-start | bytes 262144 | tf_op jit(solution)/shard_map/all_to_all | solution.py:1332
  68.1 3.6 %late.1 = (bf16[128,480]{1,0:T(8,128)(2,1)}, bf16[480,128]{1,0:T(8,128)(2,1)}, bf16[480,128]{1,0:T(8,128)(2,1)}, bf16[128,480]{1,0:T(8,128)(2,1)}, bf16[128,512]...) custom-call(s32[1]{0:T(128)} %bitcast.3.me_ref, ...), custom_call_target="tpu_custom_call" | custom-call | flops 3000000000 | bytes 10000000 | tf_op jit(solution)/shard_map/late/pallas_call | solution.py:541
  71.7 4.4 %all-to-all-done.stats_ref = f32[32,8,128]{2,1,0:T(8,128)S(1)} async-done(((f32[32,8,128]{2,1,0:T(8,128)}), f32[32,8,128]{2,1,0:T(8,128)S(1)}, u32[]{:S(2)}, u32[]{:S(2)}) %all-to-all-start) | async-done | bytes 131104 | tf_op jit(solution)/shard_map/all_to_all | solution.py:1332
  76.1 0.0 copy-start.2
  76.1 0.7 copy-done.2
  76.8 21.5 %second.1 = (bf16[5,120,1536]{2,1,0:T(8,128)(2,1)}, f32[5,120,1536]{2,1,0:T(8,128)}, f32[5,120,1536]{2,1,0:T(8,128)}, f32[32,8,128]{2,1,0:T(8,128)}, f32[128,128...) custom-call(s32[5]{0:T(128)} %len_ref.5, ...), custom_call_target="tpu_custom_call" | custom-call | flops 15000000512 | bytes 30000000 | tf_op jit(solution)/shard_map/second/pallas_call | solution.py:868
  98.3 2.6 %all-to-all-start.1 = ((f32[32,8,128]{2,1,0:T(8,128)}), f32[32,8,128]{2,1,0:T(8,128)S(1)}, u32[]{:S(2)}, u32[]{:S(2)}) async-start(f32[32,8,128]{2,1,0:T(8,128)} %get-tuple-element.119.sums_ref), calls=%async_computation.1 | async-start | bytes 262144 | tf_op jit(solution)/shard_map/all_to_all | solution.py:1336
  100.9 4.8 %outward.1 = bf16[5,120,1536]{2,1,0:T(8,128)(2,1)} custom-call(bf16[5,120,1536]{2,1,0:T(8,128)(2,1)} %get-tuple-element.123.far_in, bf16[384,384]{1,0:T(8,128)(2,1)} %get-tuple-element.124.pm_ref), custom_call_target="tpu_custom_call" | custom-call | flops 2000000000 | bytes 8000000 | tf_op jit(solution)/shard_map/outward/pallas_call | solution.py:329
  105.8 2.6 %ahead.1.last_ref = f32[909,128]{1,0:T(8,128)} custom-call(f32[512,128]{1,0:T(8,128)} %get-tuple-element.120.dn_ref, f32[480,128]{1,0:T(8,128)} %get-tuple-element.121.up_ref, f32[4,120,128]{2,1,0:T(8,128)} %get-tuple-element.122.vec_ref), custom_call_target="tpu_custom_call" | custom-call | flops 2000000000 | bytes 8000000 | tf_op jit(solution)/shard_map/ahead/pallas_call | solution.py:1157
  108.3 0.8 all-to-all-done.1.sums_ref
  109.2 0.0 copy-start.1
  109.2 0.7 copy-done.1
  109.8 46.1 %third.1 = (f32[5,120,1536]{2,1,0:T(8,128)}, f32[512,128]{1,0:T(8,128)}, f32[480,128]{1,0:T(8,128)}, f32[240,128]{1,0:T(8,128)}, f32[3,432,128]{2,1,0:T(8,128)},...) custom-call(s32[5]{0:T(128)} %len_ref.5, f32[32,8,128]{2,1,0:T(8,128)} %copy-done.1, ...), custom_call_target="tpu_custom_call" | custom-call | flops 20000000000 | bytes 80000000 | tf_op jit(solution)/shard_map/third/pallas_call | solution.py:1072
  155.9 4.5 %pack.1 = (f32[16,88,128]{2,1,0:T(8,128)}, f32[16,88,128]{2,1,0:T(8,128)}) custom-call(s32[1]{0:T(128)} %bitcast.3.me_ref, f32[909,128]{1,0:T(8,128)} %ahead.1.last_ref, f32[512,128]{1,0:T(8,128)} %get-tuple-element.150.dn1_ref, f32[480,128]{1,0:T(8,128)} %get-tuple-element.151.up1_ref, f32[128,128]{1,0:T(8,128)} %get-tuple-element.152.pr_ref, ...), custom_call_target="tpu_custom_call" | custom-call | flops 1000000000 | bytes 5000000 | tf_op jit(solution)/shard_map/pack/pallas_call | solution.py:1230
  160.4 0.2 collective-permute-start.7
  160.6 2.2 %collective-permute-done.7 = f32[16,88,128]{2,1,0:T(8,128)S(1)} collective-permute-done((f32[16,88,128]{2,1,0:T(8,128)}, f32[16,88,128]{2,1,0:T(8,128)S(1)}, u32[]{:S(2)}, u32[]{:S(2)}) %collective-permute-start.7) | collective-permute-done | bytes 720928 | tf_op jit(solution)/shard_map/ppermute | solution.py:1285
  162.8 1.2 fusion.6
  164.1 0.9 collective-permute-start.8
  164.9 1.5 collective-permute-start.9
  166.4 1.2 collective-permute-start.10
  167.6 5.0 %leave.2.refs_0_ = f32[5,120,1536]{2,1,0:T(8,128)} custom-call(f32[5,120,1536]{2,1,0:T(8,128)} %get-tuple-element.160.far_in, bf16[384,384]{1,0:T(8,128)(2,1)} %get-tuple-element.124.pm_ref), custom_call_target="tpu_custom_call" | custom-call | flops 2000000000 | bytes 8000000 | tf_op jit(solution)/shard_map/leave/pallas_call | solution.py:329
  172.6 0.0 collective-permute-done.8
  172.6 0.0 collective-permute-done.9
  172.6 0.0 collective-permute-done.10
  172.7 0.9 collective-permute-start.11
  173.6 2.5 %collective-permute-start.12 = (f32[1,88,128]{2,1,0:T(8,128)S(1)}, f32[1,88,128]{2,1,0:T(8,128)S(1)}, u32[]{:S(2)}, u32[]{:S(2)}) collective-permute-start(f32[1,88,128]{2,1,0:T(8,128)S(1)} %get-tuple-element.181), channel_id=1, source_target_pairs={{0,16},{1,17},{2,18},{3,19},{4,20},{5,21},{6,22},{7,23},{8,24},{9,... | collective-permute-start | bytes 135176 | tf_op jit(solution)/shard_map/ppermute | solution.py:1285
  176.1 0.0 copy-start
  176.1 0.0 copy-start.3
  176.1 0.0 copy-start.4
  176.1 0.0 copy-start.5
  176.1 1.1 collective-permute-start.13
  177.2 4.3 %leave.3 = f32[5,120,1536]{2,1,0:T(8,128)} custom-call(f32[5,120,1536]{2,1,0:T(8,128)} %get-tuple-element.160.far_in, bf16[384,384]{1,0:T(8,128)(2,1)} %get-tuple-element.124.pm_ref, f32[5,120,1536]{2,1,0:T(8,128)} %leave.2.refs_0_), custom_call_target="tpu_custom_call", output_to_operand_aliasing={{}: (2, {})} | custom-call | flops 2000000000 | bytes 8000000 | tf_op jit(solution)/shard_map/leave/pallas_call | solution.py:329
  181.5 0.0 collective-permute-done.11
  181.5 0.0 collective-permute-done.12
  181.5 0.5 collective-permute-done.13
  182.0 0.0 copy-done
  182.0 0.0 copy-done.3
  182.0 0.0 copy-done.4
  182.0 0.0 copy-done.5
  182.1 1.6 multiply_add_fusion.1
  (13 shorter events, 0.2 us)
Async XLA Ops:
  1.4 11.3 %collective-permute-start = (bf16[1,88,128]{2,1,0:T(8,128)(2,1)S(1)}, bf16[1,88,128]{2,1,0:T(8,128)(2,1)S(1)}, u32[]{:S(2)}, u32[]{:S(2)}) collective-permute-start(bf16[1,88,128]{2,1,0:T(8,128)(2,1)S(1)} %pad_bitcast_fusion), channel_id=1, source_target_pairs={{0,8},{1,9},{2,10},{3,11},{4,12},{5,13},{6,14},{7,15},{8,0},{9,1},... | collective-permute-start | bytes 67592 | tf_op jit(solution)/shard_map/ppermute | solution.py:1285
  4.5 8.2 %collective-permute-start.1 = (bf16[1,88,128]{2,1,0:T(8,128)(2,1)S(1)}, bf16[1,88,128]{2,1,0:T(8,128)(2,1)S(1)}, u32[]{:S(2)}, u32[]{:S(2)}) collective-permute-start(bf16[1,88,128]{2,1,0:T(8,128)(2,1)S(1)} %pad_bitcast_fusion), channel_id=1, source_target_pairs={{0,16},{1,17},{2,18},{3,19},{4,20},{5,21},{6,22},{7,23},{8,24},{9,... | collective-permute-start | bytes 67592 | tf_op jit(solution)/shard_map/ppermute | solution.py:1285
  7.1 5.6 %collective-permute-start.2 = (bf16[1,88,128]{2,1,0:T(8,128)(2,1)S(1)}, bf16[1,88,128]{2,1,0:T(8,128)(2,1)S(1)}, u32[]{:S(2)}, u32[]{:S(2)}) collective-permute-start(bf16[1,88,128]{2,1,0:T(8,128)(2,1)S(1)} %pad_bitcast_fusion), channel_id=1, source_target_pairs={{0,24},{1,25},{2,26},{3,27},{4,28},{5,29},{6,30},{7,31},{8,16},{9,... | collective-permute-start | bytes 67592 | tf_op jit(solution)/shard_map/ppermute | solution.py:1285
  12.8 8.3 %collective-permute-start.3 = (bf16[4,88,128]{2,1,0:T(8,128)(2,1)S(1)}, bf16[4,88,128]{2,1,0:T(8,128)(2,1)S(1)}, u32[]{:S(2)}, u32[]{:S(2)}) collective-permute-start(bf16[4,88,128]{2,1,0:T(8,128)(2,1)S(1)} %constant_dynamic-update-slice_fusion), channel_id=1, source_target_pairs={{0,2},{1,3},{2,0},{3,1},{4,6},{5,7},{6,4},{7,5},{8,10},{9,11},{10,... | collective-permute-start | bytes 270344 | tf_op jit(solution)/shard_map/ppermute | solution.py:1285
  14.5 6.6 %collective-permute-start.4 = (bf16[4,88,128]{2,1,0:T(8,128)(2,1)S(1)}, bf16[4,88,128]{2,1,0:T(8,128)(2,1)S(1)}, u32[]{:S(2)}, u32[]{:S(2)}) collective-permute-start(bf16[4,88,128]{2,1,0:T(8,128)(2,1)S(1)} %constant_dynamic-update-slice_fusion), channel_id=1, source_target_pairs={{0,4},{1,5},{2,6},{3,7},{4,0},{5,1},{6,2},{7,3},{8,12},{9,13},{10,... | collective-permute-start | bytes 270344 | tf_op jit(solution)/shard_map/ppermute | solution.py:1285
  16.1 5.4 %collective-permute-start.5 = (bf16[4,88,128]{2,1,0:T(8,128)(2,1)S(1)}, bf16[4,88,128]{2,1,0:T(8,128)(2,1)S(1)}, u32[]{:S(2)}, u32[]{:S(2)}) collective-permute-start(bf16[4,88,128]{2,1,0:T(8,128)(2,1)S(1)} %constant_dynamic-update-slice_fusion), channel_id=1, source_target_pairs={{0,6},{1,7},{2,4},{3,5},{4,2},{5,3},{6,0},{7,1},{8,14},{9,15},{10,... | collective-permute-start | bytes 270344 | tf_op jit(solution)/shard_map/ppermute | solution.py:1285
  21.5 1.7 collective-permute-start.6
  23.3 0.9 copy-start.6
  62.2 13.9 %all-to-all-start = ((f32[32,8,128]{2,1,0:T(8,128)}), f32[32,8,128]{2,1,0:T(8,128)S(1)}, u32[]{:S(2)}, u32[]{:S(2)}) async-start(f32[32,8,128]{2,1,0:T(8,128)} %get-tuple-element.109), calls=%async_computation | async-start | bytes 262144 | tf_op jit(solution)/shard_map/all_to_all | solution.py:1332
  76.1 0.7 copy-start.2
  98.3 10.8 %all-to-all-start.1 = ((f32[32,8,128]{2,1,0:T(8,128)}), f32[32,8,128]{2,1,0:T(8,128)S(1)}, u32[]{:S(2)}, u32[]{:S(2)}) async-start(f32[32,8,128]{2,1,0:T(8,128)} %get-tuple-element.119.sums_ref), calls=%async_computation.1 | async-start | bytes 262144 | tf_op jit(solution)/shard_map/all_to_all | solution.py:1336
  109.2 0.7 copy-start.1
  160.4 2.4 %collective-permute-start.7 = (f32[16,88,128]{2,1,0:T(8,128)}, f32[16,88,128]{2,1,0:T(8,128)S(1)}, u32[]{:S(2)}, u32[]{:S(2)}) collective-permute-start(f32[16,88,128]{2,1,0:T(8,128)} %get-tuple-element.159), channel_id=1, source_target_pairs={{0,1},{1,0},{2,3},{3,2},{4,5},{5,4},{6,7},{7,6},{8,9},{9,8},{10,11... | collective-permute-start | bytes 2162696 | tf_op jit(solution)/shard_map/ppermute | solution.py:1285
  164.1 8.5 %collective-permute-start.8 = (bf16[4,88,128]{2,1,0:T(8,128)(2,1)S(1)}, bf16[4,88,128]{2,1,0:T(8,128)(2,1)S(1)}, u32[]{:S(2)}, u32[]{:S(2)}) collective-permute-start(bf16[4,88,128]{2,1,0:T(8,128)(2,1)S(1)} %get-tuple-element.178), channel_id=1, source_target_pairs={{0,2},{1,3},{2,0},{3,1},{4,6},{5,7},{6,4},{7,5},{8,10},{9,11},{10,... | collective-permute-start | bytes 270344 | tf_op jit(solution)/shard_map/ppermute | solution.py:1285
  164.9 7.7 %collective-permute-start.9 = (bf16[4,88,128]{2,1,0:T(8,128)(2,1)S(1)}, bf16[4,88,128]{2,1,0:T(8,128)(2,1)S(1)}, u32[]{:S(2)}, u32[]{:S(2)}) collective-permute-start(bf16[4,88,128]{2,1,0:T(8,128)(2,1)S(1)} %get-tuple-element.177), channel_id=1, source_target_pairs={{0,4},{1,5},{2,6},{3,7},{4,0},{5,1},{6,2},{7,3},{8,12},{9,13},{10,... | collective-permute-start | bytes 270344 | tf_op jit(solution)/shard_map/ppermute | solution.py:1285
  166.4 6.2 %collective-permute-start.10 = (bf16[4,88,128]{2,1,0:T(8,128)(2,1)S(1)}, bf16[4,88,128]{2,1,0:T(8,128)(2,1)S(1)}, u32[]{:S(2)}, u32[]{:S(2)}) collective-permute-start(bf16[4,88,128]{2,1,0:T(8,128)(2,1)S(1)} %get-tuple-element.176), channel_id=1, source_target_pairs={{0,6},{1,7},{2,4},{3,5},{4,2},{5,3},{6,0},{7,1},{8,14},{9,15},{10,... | collective-permute-start | bytes 270344 | tf_op jit(solution)/shard_map/ppermute | solution.py:1285
  172.7 8.8 %collective-permute-start.11 = (f32[1,88,128]{2,1,0:T(8,128)S(1)}, f32[1,88,128]{2,1,0:T(8,128)S(1)}, u32[]{:S(2)}, u32[]{:S(2)}) collective-permute-start(f32[1,88,128]{2,1,0:T(8,128)S(1)} %get-tuple-element.182), channel_id=1, source_target_pairs={{0,8},{1,9},{2,10},{3,11},{4,12},{5,13},{6,14},{7,15},{8,0},{9,1},... | collective-permute-start | bytes 135176 | tf_op jit(solution)/shard_map/ppermute | solution.py:1285
  173.6 7.9 %collective-permute-start.12 = (f32[1,88,128]{2,1,0:T(8,128)S(1)}, f32[1,88,128]{2,1,0:T(8,128)S(1)}, u32[]{:S(2)}, u32[]{:S(2)}) collective-permute-start(f32[1,88,128]{2,1,0:T(8,128)S(1)} %get-tuple-element.181), channel_id=1, source_target_pairs={{0,16},{1,17},{2,18},{3,19},{4,20},{5,21},{6,22},{7,23},{8,24},{9,... | collective-permute-start | bytes 135176 | tf_op jit(solution)/shard_map/ppermute | solution.py:1285
  176.1 5.9 %copy-start = (f32[10624]{0:T(1024)S(1)}, f32[10624]{0:T(1024)}, u32[]{:S(2)}) copy-start(f32[10624]{0:T(1024)} %param.12) | copy-start | bytes 127492
  176.1 5.9 %copy-start.3 = (f32[10624]{0:T(1024)S(1)}, f32[10624]{0:T(1024)}, u32[]{:S(2)}) copy-start(f32[10624]{0:T(1024)} %param.15) | copy-start | bytes 127492
  176.1 5.9 %copy-start.4 = (f32[10624]{0:T(1024)S(1)}, f32[10624]{0:T(1024)}, u32[]{:S(2)}) copy-start(f32[10624]{0:T(1024)} %param.13) | copy-start | bytes 127492
  176.1 5.9 %copy-start.5 = (f32[10624]{0:T(1024)S(1)}, f32[10624]{0:T(1024)}, u32[]{:S(2)}) copy-start(f32[10624]{0:T(1024)} %param.14) | copy-start | bytes 127492
  176.1 5.9 %collective-permute-start.13 = (f32[1,88,128]{2,1,0:T(8,128)S(1)}, f32[1,88,128]{2,1,0:T(8,128)S(1)}, u32[]{:S(2)}, u32[]{:S(2)}) collective-permute-start(f32[1,88,128]{2,1,0:T(8,128)S(1)} %get-tuple-element.180), channel_id=1, source_target_pairs={{0,24},{1,25},{2,26},{3,27},{4,28},{5,29},{6,30},{7,31},{8,16},{9,... | collective-permute-start | bytes 135176 | tf_op jit(solution)/shard_map/ppermute | solution.py:1285

commit v6 on v5

--- a/solution.py
+++ b/solution.py
@@ -556,6 +556,14 @@
 
 def valid_keys(length):
     return row_iota((LG, 1)) * GROUP < length
+
+
+def lane_sums(vec):
+    lanes = lane_iota((D, 128))
+    table = jnp.zeros((D, 128), f32)
+    for k in range(vec.shape[0]):
+        table = jnp.where(lanes == k, jnp.sum(vec[k], axis=1, keepdims=True), table)
+    return pad8(table).T
 
 
 def set_tail(hid):
@@ -884,9 +892,9 @@
     len_ref, sums_ref, stc_ref, bgd_ref, dep_ref, gat_ref, ri_ref, ra_ref, rc_ref,
     gc_far, xc_far, cn_far, sig_far, rgt_far, att_far, qkv_far, prob_far, nrm_far, lf_far, xa_far, xf_far,
     cols_ref, up_ref, upp_ref, dnp_ref, wqkv_t_ref, wob_ref, pwp_ref,
-    grad_ref, gdn_ref, gup_ref, gpw_ref, gqkv_ref, go_ref, rel_ref, vec_ref,
+    grad_ref, gdn_ref, gup_ref, gpw_ref, gqkv_ref, go_ref, rel_ref, rows_ref,
     gc_ref, xc_ref, cn_ref, sig_ref, rgt_ref, att_ref, qkv_ref, prob_ref, nrm_ref, lf_ref, xa_ref, xf_ref, sems,
-    hid, dgx, dgs, olg, agr, back_s, gg, near_s, far_s, cb, tot,
+    hid, dgx, dgs, olg, agr, back_s, gg, near_s, far_s, vec_ref, cb, tot,
 ):
     far = (gc_far, xc_far, cn_far, sig_far, rgt_far, att_far, qkv_far, prob_far, nrm_far, lf_far, xa_far, xf_far)
     near = (gc_ref, xc_ref, cn_ref, sig_ref, rgt_ref, att_ref, qkv_ref, prob_ref, nrm_ref, lf_ref, xa_ref, xf_ref)
@@ -1051,6 +1059,7 @@
     @pl.when(u == utts)
     def _():
         back()
+        rows_ref[...] = lane_sums(vec_ref)
         found = []
         for h in range(HEADS):
             found.append(diagonal_sum(near_s[h], far_s[h]))
@@ -1067,7 +1076,7 @@
     utts = soon[0].shape[0]
     big = (D, MAXLEN)
     outs = [(one_late(big), (utts,) + big)]
-    for s in ((512, 128), (FF, 128), (240, 128), (GROUP, 3 * WROWS, 128), (GROUP, WROWS, 128), (8, 256), (22, D, 128)):
+    for s in ((512, 128), (FF, 128), (240, 128), (GROUP, 3 * WROWS, 128), (GROUP, WROWS, 128), (8, 256), (128, 128)):
         outs.append((whole(s), s))
     return pl.pallas_call(
         third_body,
@@ -1091,6 +1100,7 @@
             pltpu.VMEM(big, f32),
             pltpu.VMEM((HEADS, 128, 384), f32),
             pltpu.VMEM((HEADS, 2, 8, 128), f32),
+            pltpu.VMEM((22, D, 128), f32),
             pltpu.VMEM((KERNEL + 1, D, 128), f32),
             pltpu.VMEM((128, 128), f32),
         ],
@@ -1103,14 +1113,9 @@
     return jnp.where(lane_iota(block.shape) < D, block, 0.0)
 
 
-def set_rows(tb, wt, ref, at):
-    lanes = lane_iota((D, 128))
-    table = jnp.zeros((D, 128), f32)
-    for k in range(len(at)):
-        table = jnp.where(lanes == k, jnp.sum(ref[k], axis=1, keepdims=True), table)
-    wt[...] = pad8(table).T
+def set_rows(tb, ref, at):
     for k, to in enumerate(at):
-        tb[to : to + 1, :] = wt[k : k + 1, :]
+        tb[to : to + 1, :] = ref[k : k + 1, :]
 
 
 def set_ffn(tb, base, dn_ref, up_ref):
@@ -1148,7 +1153,8 @@
 def ahead_body(dn_ref, up_ref, vec_ref, out_ref, tb, wt):
     tb[0:8, :] = jnp.zeros((8, 128), f32)
     tb[8 + ROWS_LAST :, :] = jnp.zeros((tb.shape[0] - 8 - ROWS_LAST, 128), f32)
-    set_rows(tb, wt, vec_ref, (8, 9, 8 + FN - F2, 9 + FN - F2))
+    wt[...] = lane_sums(vec_ref)
+    set_rows(tb, wt, (8, 9, 8 + FN - F2, 9 + FN - F2))
     set_ffn(tb, 8, dn_ref, up_ref)
     flatten(tb, 7, out_ref, 0, LAST_COUNT, D + 128 * LAST_Y - LAST_AT)
 
@@ -1169,9 +1175,7 @@
 ):
     tb[ROWS_HEAD:TAIL, :] = jnp.zeros((TAIL - ROWS_HEAD, 128), f32)
     tb[F2:, :] = jnp.zeros((tb.shape[0] - F2, 128), f32)
-    set_rows(
-        tb, wt, vec_ref, (CV, CV + 1, AT, AT + 1, F1, F1 + 1, CV + 259) + tuple(CV + 244 + k for k in range(KERNEL))
-    )
+    set_rows(tb, vec_ref, (CV, CV + 1, AT, AT + 1, F1, F1 + 1, CV + 259) + tuple(CV + 244 + k for k in range(KERNEL)))
     tb[CV + 260 : CV + 262, :] = sums_ref[0, 0:2, :]
     set_ffn(tb, F1, dn1_ref, up1_ref)
     for q in range(2):

time: 184 us -> 183 us (level)
  Pallas kernels: 141 us -> 139 us
where the time goes in v6:
time: 183 us; the launch traced here: 182 us
  Pallas kernels  139 us (76%)
  starting transfers between devices  26.1 us (14%)
  waiting for transfers between devices  9.95 us (5%)
  other arithmetic  3.66 us (2%)
  local copies, waits for them, and re-layouts  2.39 us (1%)
    pallas_call x1, Pallas kernels, third(): pl.pallas_call(third_body, grid=(utts + 1,), in_specs=[SMEM, whole(sums.s...  45.6 us
    pallas_call x1, Pallas kernels, first(): pl.pallas_call(first_body, grid=(utts,), in_specs=[SMEM, per_utt(BIG), pe...  34.7 us
    pallas_call x1, Pallas kernels, second(): pl.pallas_call(second_body, grid=(utts,), in_specs=[SMEM, whole(stats.sha...  21.5 us
    pallas_call x4, Pallas kernels, reorder(): pl.pallas_call(body, in_specs=[ANY, VMEM] + [ANY] * len(more), out_specs=...  18.8 us
    ppermute x14, starting transfers between devices, partner(): return lax.ppermute(values, 'dp', [(i, i ^ offset) for i in range(devices)])  17.6 us
    all_to_all x1, starting transfers between devices, local(): stats = lax.all_to_all(st, 'dp', 0, 0)  5.89 us
    pallas_call x1, Pallas kernels, enter(): pl.pallas_call(enter_body, in_specs=[ANY], out_specs=[ANY] * 3 + [VMEM],...  5.56 us
    ppermute x14, waiting for transfers between devices, partner(): return lax.ppermute(values, 'dp', [(i, i ^ offset) for i in range(devices)])  4.69 us
  transfers between devices with their start and end apart: 16, of which 6 were waited for; matrix products, arithmetic and copies ran while one was open for 0% of the time, Pallas kernels for 17%

profile of v6, /device:TPU:0, one launch (start us, length us, event | category | flops | bytes accessed | tf_op | source)
XLA Modules:
  0.0 182.3 jit_solution(2136600989033279782)
XLA Ops:
  0.6 0.8 convert_bitcast_fusion
  1.4 3.1 %collective-permute-start = (bf16[1,88,128]{2,1,0:T(8,128)(2,1)S(1)}, bf16[1,88,128]{2,1,0:T(8,128)(2,1)S(1)}, u32[]{:S(2)}, u32[]{:S(2)}) collective-permute-start(bf16[1,88,128]{2,1,0:T(8,128)(2,1)S(1)} %pad_bitcast_fusion), channel_id=1, source_target_pairs={{0,8},{1,9},{2,10},{3,11},{4,12},{5,13},{6,14},{7,15},{8,0},{9,1},... | collective-permute-start | bytes 67592 | tf_op jit(solution)/shard_map/ppermute | solution.py:1289
  4.5 2.6 %collective-permute-start.1 = (bf16[1,88,128]{2,1,0:T(8,128)(2,1)S(1)}, bf16[1,88,128]{2,1,0:T(8,128)(2,1)S(1)}, u32[]{:S(2)}, u32[]{:S(2)}) collective-permute-start(bf16[1,88,128]{2,1,0:T(8,128)(2,1)S(1)} %pad_bitcast_fusion), channel_id=1, source_target_pairs={{0,16},{1,17},{2,18},{3,19},{4,20},{5,21},{6,22},{7,23},{8,24},{9,... | collective-permute-start | bytes 67592 | tf_op jit(solution)/shard_map/ppermute | solution.py:1289
  7.1 0.0 collective-permute-start.2
  7.1 5.6 %enter.1 = (bf16[5,120,1536]{2,1,0:T(8,128)(2,1)}, f32[5,120,1536]{2,1,0:T(8,128)}, f32[5,8,1536]{2,1,0:T(8,128)}, bf16[384,384]{1,0:T(8,128)(2,1)}) custom-call(bf16[5,120,1536]{2,1,0:T(8,128)(2,1)} %bitcast.13), custom_call_target="tpu_custom_call" | custom-call | flops 2000000000 | bytes 8000000 | tf_op jit(solution)/shard_map/enter/pallas_call | solution.py:297
  12.7 0.0 collective-permute-done
  12.7 0.0 collective-permute-done.1
  12.7 0.0 collective-permute-done.2
  12.8 1.8 collective-permute-start.3
  14.5 1.5 collective-permute-start.4
  16.1 0.3 collective-permute-start.5
  16.3 4.8 %inward.1.cot_ref = bf16[5,120,1536]{2,1,0:T(8,128)(2,1)} custom-call(bf16[5,120,1536]{2,1,0:T(8,128)(2,1)} %bitcast.14, bf16[384,384]{1,0:T(8,128)(2,1)} %get-tuple-element.124.pm_ref), custom_call_target="tpu_custom_call" | custom-call | flops 2000000000 | bytes 8000000 | tf_op jit(solution)/shard_map/inward/pallas_call | solution.py:329
  21.1 0.0 collective-permute-done.3
  21.1 0.0 collective-permute-done.4
  21.1 0.4 collective-permute-done.5
  21.5 0.1 collective-permute-start.6
  21.7 1.6 collective-permute-done.6
  23.3 0.1 constant_dynamic-update-slice_fusion.4.g_ref
  23.3 0.0 copy-start.6
  23.4 0.9 copy-done.6
  24.2 3.2 %prepare.1 = (bf16[480,128]{1,0:T(8,128)(2,1)}, bf16[128,512]{1,0:T(8,128)(2,1)}, bf16[3,432,128]{2,1,0:T(8,128)(2,1)}, bf16[3,128,144]{2,1,0:T(8,128)(2,1)}, bf...) custom-call(s32[1]{0:T(128)} %bitcast.3.me_ref, bf16[32,88,128]{2,1,0:T(8,128)(2,1)} %copy-done.6), custom_call_target="tpu_custom_call" | custom-call | flops 1000000000 | bytes 2000000 | tf_op jit(solution)/shard_map/prepare/pallas_call | solution.py:532
  27.4 34.7 %first.1 = (bf16[5,128,1536]{2,1,0:T(8,128)(2,1)}, f32[5,120,1536]{2,1,0:T(8,128)}, bf16[5,384,512]{2,1,0:T(8,128)(2,1)}, bf16[5,1152,512]{2,1,0:T(8,128)(2,1)},...) custom-call(s32[5]{0:T(128)} %len_ref.5, ...), custom_call_target="tpu_custom_call" | custom-call | flops 10000000000 | bytes 60000000 | tf_op jit(solution)/shard_map/first/pallas_call | solution.py:737
  62.2 5.9 %all-to-all-start = ((f32[32,8,128]{2,1,0:T(8,128)}), f32[32,8,128]{2,1,0:T(8,128)S(1)}, u32[]{:S(2)}, u32[]{:S(2)}) async-start(f32[32,8,128]{2,1,0:T(8,128)} %get-tuple-element.109), calls=%async_computation | async-start | bytes 262144 | tf_op jit(solution)/shard_map/all_to_all | solution.py:1336
  68.1 3.6 %late.1 = (bf16[128,480]{1,0:T(8,128)(2,1)}, bf16[480,128]{1,0:T(8,128)(2,1)}, bf16[480,128]{1,0:T(8,128)(2,1)}, bf16[128,480]{1,0:T(8,128)(2,1)}, bf16[128,512]...) custom-call(s32[1]{0:T(128)} %bitcast.3.me_ref, ...), custom_call_target="tpu_custom_call" | custom-call | flops 3000000000 | bytes 10000000 | tf_op jit(solution)/shard_map/late/pallas_call | solution.py:541
  71.7 4.4 %all-to-all-done.stats_ref = f32[32,8,128]{2,1,0:T(8,128)S(1)} async-done(((f32[32,8,128]{2,1,0:T(8,128)}), f32[32,8,128]{2,1,0:T(8,128)S(1)}, u32[]{:S(2)}, u32[]{:S(2)}) %all-to-all-start) | async-done | bytes 131104 | tf_op jit(solution)/shard_map/all_to_all | solution.py:1336
  76.1 0.0 copy-start.2
  76.1 0.7 copy-done.2
  76.8 21.5 %second.1 = (bf16[5,120,1536]{2,1,0:T(8,128)(2,1)}, f32[5,120,1536]{2,1,0:T(8,128)}, f32[5,120,1536]{2,1,0:T(8,128)}, f32[32,8,128]{2,1,0:T(8,128)}, f32[128,128...) custom-call(s32[5]{0:T(128)} %len_ref.5, ...), custom_call_target="tpu_custom_call" | custom-call | flops 15000000512 | bytes 30000000 | tf_op jit(solution)/shard_map/second/pallas_call | solution.py:876
  98.3 2.6 %all-to-all-start.1 = ((f32[32,8,128]{2,1,0:T(8,128)}), f32[32,8,128]{2,1,0:T(8,128)S(1)}, u32[]{:S(2)}, u32[]{:S(2)}) async-start(f32[32,8,128]{2,1,0:T(8,128)} %get-tuple-element.119.sums_ref), calls=%async_computation.1 | async-start | bytes 262144 | tf_op jit(solution)/shard_map/all_to_all | solution.py:1340
  100.9 4.8 %outward.1 = bf16[5,120,1536]{2,1,0:T(8,128)(2,1)} custom-call(bf16[5,120,1536]{2,1,0:T(8,128)(2,1)} %get-tuple-element.123.far_in, bf16[384,384]{1,0:T(8,128)(2,1)} %get-tuple-element.124.pm_ref), custom_call_target="tpu_custom_call" | custom-call | flops 2000000000 | bytes 8000000 | tf_op jit(solution)/shard_map/outward/pallas_call | solution.py:329
  105.8 2.6 %ahead.1.last_ref = f32[909,128]{1,0:T(8,128)} custom-call(f32[512,128]{1,0:T(8,128)} %get-tuple-element.120.dn_ref, f32[480,128]{1,0:T(8,128)} %get-tuple-element.121.up_ref, f32[4,120,128]{2,1,0:T(8,128)} %get-tuple-element.122.vec_ref), custom_call_target="tpu_custom_call" | custom-call | flops 2000000000 | bytes 8000000 | tf_op jit(solution)/shard_map/ahead/pallas_call | solution.py:1163
  108.3 0.8 all-to-all-done.1.sums_ref
  109.2 0.0 copy-start.1
  109.2 0.6 copy-done.1
  109.8 45.6 %third.1 = (f32[5,120,1536]{2,1,0:T(8,128)}, f32[512,128]{1,0:T(8,128)}, f32[480,128]{1,0:T(8,128)}, f32[240,128]{1,0:T(8,128)}, f32[3,432,128]{2,1,0:T(8,128)},...) custom-call(s32[5]{0:T(128)} %len_ref.5, f32[32,8,128]{2,1,0:T(8,128)} %copy-done.1, ...), custom_call_target="tpu_custom_call" | custom-call | flops 20000000000 | bytes 80000000 | tf_op jit(solution)/shard_map/third/pallas_call | solution.py:1081
  155.4 3.7 %pack.1 = (f32[16,88,128]{2,1,0:T(8,128)}, f32[16,88,128]{2,1,0:T(8,128)}) custom-call(s32[1]{0:T(128)} %bitcast.3.me_ref, f32[909,128]{1,0:T(8,128)} %ahead.1.last_ref, f32[512,128]{1,0:T(8,128)} %get-tuple-element.150.dn1_ref, f32[480,128]{1,0:T(8,128)} %get-tuple-element.151.up1_ref, f32[128,128]{1,0:T(8,128)} %get-tuple-element.152.pr_ref, ...), custom_call_target="tpu_custom_call" | custom-call | flops 1000000000 | bytes 5000000 | tf_op jit(solution)/shard_map/pack/pallas_call | solution.py:1234
  159.1 0.2 collective-permute-start.7
  159.3 2.2 %collective-permute-done.7 = f32[16,88,128]{2,1,0:T(8,128)S(1)} collective-permute-done((f32[16,88,128]{2,1,0:T(8,128)}, f32[16,88,128]{2,1,0:T(8,128)S(1)}, u32[]{:S(2)}, u32[]{:S(2)}) %collective-permute-start.7) | collective-permute-done | bytes 720928 | tf_op jit(solution)/shard_map/ppermute | solution.py:1289
  161.5 1.2 fusion.6
  162.7 1.8 collective-permute-start.10
  164.5 0.5 collective-permute-start.8
  165.1 1.2 collective-permute-start.9
  166.3 5.0 %leave.2.refs_0_ = f32[5,120,1536]{2,1,0:T(8,128)} custom-call(f32[5,120,1536]{2,1,0:T(8,128)} %get-tuple-element.160.far_in, bf16[384,384]{1,0:T(8,128)(2,1)} %get-tuple-element.124.pm_ref), custom_call_target="tpu_custom_call" | custom-call | flops 2000000000 | bytes 8000000 | tf_op jit(solution)/shard_map/leave/pallas_call | solution.py:329
  171.3 0.0 collective-permute-done.10
  171.3 0.0 collective-permute-done.8
  171.3 0.0 collective-permute-done.9
  171.4 0.9 collective-permute-start.11
  172.3 2.5 %collective-permute-start.12 = (f32[1,88,128]{2,1,0:T(8,128)S(1)}, f32[1,88,128]{2,1,0:T(8,128)S(1)}, u32[]{:S(2)}, u32[]{:S(2)}) collective-permute-start(f32[1,88,128]{2,1,0:T(8,128)S(1)} %get-tuple-element.181), channel_id=1, source_target_pairs={{0,16},{1,17},{2,18},{3,19},{4,20},{5,21},{6,22},{7,23},{8,24},{9,... | collective-permute-start | bytes 135176 | tf_op jit(solution)/shard_map/ppermute | solution.py:1289
  174.8 0.0 copy-start
  174.8 0.0 copy-start.3
  174.8 0.0 copy-start.4
  174.8 0.0 copy-start.5
  174.8 1.1 collective-permute-start.13
  175.9 4.3 %leave.3 = f32[5,120,1536]{2,1,0:T(8,128)} custom-call(f32[5,120,1536]{2,1,0:T(8,128)} %get-tuple-element.160.far_in, bf16[384,384]{1,0:T(8,128)(2,1)} %get-tuple-element.124.pm_ref, f32[5,120,1536]{2,1,0:T(8,128)} %leave.2.refs_0_), custom_call_target="tpu_custom_call", output_to_operand_aliasing={{}: (2, {})} | custom-call | flops 2000000000 | bytes 8000000 | tf_op jit(solution)/shard_map/leave/pallas_call | solution.py:329
  180.2 0.0 collective-permute-done.11
  180.2 0.0 collective-permute-done.12
  180.2 0.5 collective-permute-done.13
  180.7 0.0 copy-done
  180.7 0.0 copy-done.3
  180.7 0.0 copy-done.4
  180.7 0.0 copy-done.5
  180.7 1.6 multiply_add_fusion.1
  (13 shorter events, 0.2 us)
Async XLA Ops:
  1.4 11.3 %collective-permute-start = (bf16[1,88,128]{2,1,0:T(8,128)(2,1)S(1)}, bf16[1,88,128]{2,1,0:T(8,128)(2,1)S(1)}, u32[]{:S(2)}, u32[]{:S(2)}) collective-permute-start(bf16[1,88,128]{2,1,0:T(8,128)(2,1)S(1)} %pad_bitcast_fusion), channel_id=1, source_target_pairs={{0,8},{1,9},{2,10},{3,11},{4,12},{5,13},{6,14},{7,15},{8,0},{9,1},... | collective-permute-start | bytes 67592 | tf_op jit(solution)/shard_map/ppermute | solution.py:1289
  4.5 8.2 %collective-permute-start.1 = (bf16[1,88,128]{2,1,0:T(8,128)(2,1)S(1)}, bf16[1,88,128]{2,1,0:T(8,128)(2,1)S(1)}, u32[]{:S(2)}, u32[]{:S(2)}) collective-permute-start(bf16[1,88,128]{2,1,0:T(8,128)(2,1)S(1)} %pad_bitcast_fusion), channel_id=1, source_target_pairs={{0,16},{1,17},{2,18},{3,19},{4,20},{5,21},{6,22},{7,23},{8,24},{9,... | collective-permute-start | bytes 67592 | tf_op jit(solution)/shard_map/ppermute | solution.py:1289
  7.1 5.6 %collective-permute-start.2 = (bf16[1,88,128]{2,1,0:T(8,128)(2,1)S(1)}, bf16[1,88,128]{2,1,0:T(8,128)(2,1)S(1)}, u32[]{:S(2)}, u32[]{:S(2)}) collective-permute-start(bf16[1,88,128]{2,1,0:T(8,128)(2,1)S(1)} %pad_bitcast_fusion), channel_id=1, source_target_pairs={{0,24},{1,25},{2,26},{3,27},{4,28},{5,29},{6,30},{7,31},{8,16},{9,... | collective-permute-start | bytes 67592 | tf_op jit(solution)/shard_map/ppermute | solution.py:1289
  12.8 8.3 %collective-permute-start.3 = (bf16[4,88,128]{2,1,0:T(8,128)(2,1)S(1)}, bf16[4,88,128]{2,1,0:T(8,128)(2,1)S(1)}, u32[]{:S(2)}, u32[]{:S(2)}) collective-permute-start(bf16[4,88,128]{2,1,0:T(8,128)(2,1)S(1)} %constant_dynamic-update-slice_fusion), channel_id=1, source_target_pairs={{0,2},{1,3},{2,0},{3,1},{4,6},{5,7},{6,4},{7,5},{8,10},{9,11},{10,... | collective-permute-start | bytes 270344 | tf_op jit(solution)/shard_map/ppermute | solution.py:1289
  14.5 6.6 %collective-permute-start.4 = (bf16[4,88,128]{2,1,0:T(8,128)(2,1)S(1)}, bf16[4,88,128]{2,1,0:T(8,128)(2,1)S(1)}, u32[]{:S(2)}, u32[]{:S(2)}) collective-permute-start(bf16[4,88,128]{2,1,0:T(8,128)(2,1)S(1)} %constant_dynamic-update-slice_fusion), channel_id=1, source_target_pairs={{0,4},{1,5},{2,6},{3,7},{4,0},{5,1},{6,2},{7,3},{8,12},{9,13},{10,... | collective-permute-start | bytes 270344 | tf_op jit(solution)/shard_map/ppermute | solution.py:1289
  16.1 5.4 %collective-permute-start.5 = (bf16[4,88,128]{2,1,0:T(8,128)(2,1)S(1)}, bf16[4,88,128]{2,1,0:T(8,128)(2,1)S(1)}, u32[]{:S(2)}, u32[]{:S(2)}) collective-permute-start(bf16[4,88,128]{2,1,0:T(8,128)(2,1)S(1)} %constant_dynamic-update-slice_fusion), channel_id=1, source_target_pairs={{0,6},{1,7},{2,4},{3,5},{4,2},{5,3},{6,0},{7,1},{8,14},{9,15},{10,... | collective-permute-start | bytes 270344 | tf_op jit(solution)/shard_map/ppermute | solution.py:1289
  21.5 1.7 collective-permute-start.6
  23.3 0.9 copy-start.6
  62.2 13.9 %all-to-all-start = ((f32[32,8,128]{2,1,0:T(8,128)}), f32[32,8,128]{2,1,0:T(8,128)S(1)}, u32[]{:S(2)}, u32[]{:S(2)}) async-start(f32[32,8,128]{2,1,0:T(8,128)} %get-tuple-element.109), calls=%async_computation | async-start | bytes 262144 | tf_op jit(solution)/shard_map/all_to_all | solution.py:1336
  76.1 0.7 copy-start.2
  98.3 10.8 %all-to-all-start.1 = ((f32[32,8,128]{2,1,0:T(8,128)}), f32[32,8,128]{2,1,0:T(8,128)S(1)}, u32[]{:S(2)}, u32[]{:S(2)}) async-start(f32[32,8,128]{2,1,0:T(8,128)} %get-tuple-element.119.sums_ref), calls=%async_computation.1 | async-start | bytes 262144 | tf_op jit(solution)/shard_map/all_to_all | solution.py:1340
  109.2 0.6 copy-start.1
  159.1 2.4 %collective-permute-start.7 = (f32[16,88,128]{2,1,0:T(8,128)}, f32[16,88,128]{2,1,0:T(8,128)S(1)}, u32[]{:S(2)}, u32[]{:S(2)}) collective-permute-start(f32[16,88,128]{2,1,0:T(8,128)} %get-tuple-element.159), channel_id=1, source_target_pairs={{0,1},{1,0},{2,3},{3,2},{4,5},{5,4},{6,7},{7,6},{8,9},{9,8},{10,11... | collective-permute-start | bytes 2162696 | tf_op jit(solution)/shard_map/ppermute | solution.py:1289
  162.7 8.5 %collective-permute-start.10 = (bf16[4,88,128]{2,1,0:T(8,128)(2,1)S(1)}, bf16[4,88,128]{2,1,0:T(8,128)(2,1)S(1)}, u32[]{:S(2)}, u32[]{:S(2)}) collective-permute-start(bf16[4,88,128]{2,1,0:T(8,128)(2,1)S(1)} %get-tuple-element.176), channel_id=1, source_target_pairs={{0,6},{1,7},{2,4},{3,5},{4,2},{5,3},{6,0},{7,1},{8,14},{9,15},{10,... | collective-permute-start | bytes 270344 | tf_op jit(solution)/shard_map/ppermute | solution.py:1289
  164.5 6.7 %collective-permute-start.8 = (bf16[4,88,128]{2,1,0:T(8,128)(2,1)S(1)}, bf16[4,88,128]{2,1,0:T(8,128)(2,1)S(1)}, u32[]{:S(2)}, u32[]{:S(2)}) collective-permute-start(bf16[4,88,128]{2,1,0:T(8,128)(2,1)S(1)} %get-tuple-element.178), channel_id=1, source_target_pairs={{0,2},{1,3},{2,0},{3,1},{4,6},{5,7},{6,4},{7,5},{8,10},{9,11},{10,... | collective-permute-start | bytes 270344 | tf_op jit(solution)/shard_map/ppermute | solution.py:1289
  165.1 6.2 %collective-permute-start.9 = (bf16[4,88,128]{2,1,0:T(8,128)(2,1)S(1)}, bf16[4,88,128]{2,1,0:T(8,128)(2,1)S(1)}, u32[]{:S(2)}, u32[]{:S(2)}) collective-permute-start(bf16[4,88,128]{2,1,0:T(8,128)(2,1)S(1)} %get-tuple-element.177), channel_id=1, source_target_pairs={{0,4},{1,5},{2,6},{3,7},{4,0},{5,1},{6,2},{7,3},{8,12},{9,13},{10,... | collective-permute-start | bytes 270344 | tf_op jit(solution)/shard_map/ppermute | solution.py:1289
  171.4 8.8 %collective-permute-start.11 = (f32[1,88,128]{2,1,0:T(8,128)S(1)}, f32[1,88,128]{2,1,0:T(8,128)S(1)}, u32[]{:S(2)}, u32[]{:S(2)}) collective-permute-start(f32[1,88,128]{2,1,0:T(8,128)S(1)} %get-tuple-element.182), channel_id=1, source_target_pairs={{0,8},{1,9},{2,10},{3,11},{4,12},{5,13},{6,14},{7,15},{8,0},{9,1},... | collective-permute-start | bytes 135176 | tf_op jit(solution)/shard_map/ppermute | solution.py:1289
  172.3 7.9 %collective-permute-start.12 = (f32[1,88,128]{2,1,0:T(8,128)S(1)}, f32[1,88,128]{2,1,0:T(8,128)S(1)}, u32[]{:S(2)}, u32[]{:S(2)}) collective-permute-start(f32[1,88,128]{2,1,0:T(8,128)S(1)} %get-tuple-element.181), channel_id=1, source_target_pairs={{0,16},{1,17},{2,18},{3,19},{4,20},{5,21},{6,22},{7,23},{8,24},{9,... | collective-permute-start | bytes 135176 | tf_op jit(solution)/shard_map/ppermute | solution.py:1289
  174.8 5.9 %copy-start = (f32[10624]{0:T(1024)S(1)}, f32[10624]{0:T(1024)}, u32[]{:S(2)}) copy-start(f32[10624]{0:T(1024)} %param.12) | copy-start | bytes 127492
  174.8 5.9 %copy-start.3 = (f32[10624]{0:T(1024)S(1)}, f32[10624]{0:T(1024)}, u32[]{:S(2)}) copy-start(f32[10624]{0:T(1024)} %param.15) | copy-start | bytes 127492
  174.8 5.9 %copy-start.4 = (f32[10624]{0:T(1024)S(1)}, f32[10624]{0:T(1024)}, u32[]{:S(2)}) copy-start(f32[10624]{0:T(1024)} %param.13) | copy-start | bytes 127492
  174.8 5.9 %copy-start.5 = (f32[10624]{0:T(1024)S(1)}, f32[10624]{0:T(1024)}, u32[]{:S(2)}) copy-start(f32[10624]{0:T(1024)} %param.14) | copy-start | bytes 127492
  174.8 5.9 %collective-permute-start.13 = (f32[1,88,128]{2,1,0:T(8,128)S(1)}, f32[1,88,128]{2,1,0:T(8,128)S(1)}, u32[]{:S(2)}, u32[]{:S(2)}) collective-permute-start(f32[1,88,128]{2,1,0:T(8,128)S(1)} %get-tuple-element.180), channel_id=1, source_target_pairs={{0,24},{1,25},{2,26},{3,27},{4,28},{5,29},{6,30},{7,31},{8,16},{9,... | collective-permute-start | bytes 135176 | tf_op jit(solution)/shard_map/ppermute | solution.py:1289

commit v7 on v6

--- a/solution.py
+++ b/solution.py
@@ -21,6 +21,7 @@
 HP = 96
 GP = HEADS * HP
 HALF = KERNEL // 2
+SURE = 128
 WIN = (0, 112, 240)
 WROWS = 144
 MARKS = tuple(HP * r + HEAD - WIN[r] for r in range(GROUP))
@@ -338,14 +339,14 @@
     )(values, pm, *more)
 
 
-def unpack(me_ref, g_ref, flat, tb):
+def unpack(me_ref, g_ref, flat, tb, regions):
     parts = g_ref.shape[0]
     part_rows = flat.shape[0] // parts
     for d in range(parts):
         flat[part_rows * d : part_rows * (d + 1), :] = g_ref[place(me_ref[0] ^ d, parts)].astype(f32)[:part_rows]
-    tb[ROWS_HEAD:TAIL, :] = jnp.zeros((TAIL - ROWS_HEAD, 128), f32)
-    for start, count, base in ((0, ROWS_HEAD, 0), (TAIL_AT, ROWS_TAIL, TAIL)):
-        for r in range(16):
+    for base, count in regions:
+        start = D * base if base < TAIL else TAIL_AT + D * (base - TAIL)
+        for r in range(min(16, count)):
             at = start + D * r
             first_row, col = at // 128, at % 128
             many = (count - r + 15) // 16
@@ -408,7 +409,7 @@
 
 
 def early_body(me_ref, g_ref, up_ref, dn_ref, wqkv_ref, wo_ref, pw_ref, cols_ref, base_ref, flat, tb, wt, wins, rows):
-    unpack(me_ref, g_ref, flat, tb)
+    unpack(me_ref, g_ref, flat, tb, ((0, ROWS_HEAD), (CV, F2 + 2 - CV), (FN, 2)))
     up_ref[...] = (0.5 * up_rows(tb, F1)).astype(bf16)
     dn_ref[...] = down_across(tb, F1)
     pw_ref[...] = (0.5 * point_rows(tb)).astype(bf16)
@@ -449,7 +450,7 @@
     me_ref, g_ref, upp1_ref, dnp1_ref, up2_ref, upp2_ref, dn2_ref, dnp2_ref, pwp_ref, pr_ref, prp_ref, wqkvt_ref, wob_ref,
     flat, tb, wt, wins,
 ):
-    unpack(me_ref, g_ref, flat, tb)
+    unpack(me_ref, g_ref, flat, tb, ((0, ROWS_HEAD), (TAIL, ROWS_TAIL)))
     upp1_ref[...] = up_across(up_rows(tb, F1))
     dnp1_ref[...] = (0.25 * tb[F1 + 486 : F1 + 966, :]).astype(bf16)
     up_t = up_rows(tb, F2)
@@ -625,6 +626,8 @@
     skewed(GROUP, (ffn_up, ffn_down, ffn_norm, ffn_keep))
     for w in range(3):
         joined = join_windows([made[r][WROWS * w : WROWS * w + WROWS] for r in range(GROUP)])
+        if w == 0:
+            joined = joined * (SCALE * LOG2E)
         qkv_ref[0, GP * w : GP * w + GP, :] = joined.astype(bf16)
     keys = valid_keys(length)
 
@@ -635,8 +638,9 @@
         return dot_tn(qkv_ref[0, rows(1, h), :], qkv_ref[0, rows(0, h), :])
 
     def soften(h, raw):
-        scores = raw * (SCALE * LOG2E) + tab[h]
-        scores = jnp.where(keys, scores, NEG_FILL * LOG2E)
+        scores = raw + tab[h]
+        later = jnp.where(keys[SURE:], scores[SURE:], NEG_FILL * LOG2E)
+        scores = jnp.concatenate([scores[:SURE], later], axis=0)
         peak = jnp.max(scores, axis=0, keepdims=True)
         power = jnp.exp2(scores - peak)
         total = jnp.sum(power, axis=0, keepdims=True)
@@ -1011,7 +1015,7 @@
 
         def turn(h, low):
             back_s[rows(0, h), :] = (dot(qkv_ref[slot, rows(1, h), :], low) * SCALE).astype(bf16)
-            back_s[rows(1, h), :] = (dot_nt(qkv_ref[slot, rows(0, h), :], low) * SCALE).astype(bf16)
+            back_s[rows(1, h), :] = (dot_nt(qkv_ref[slot, rows(0, h), :], low) * (1.0 / LOG2E)).astype(bf16)
 
         skewed(HEADS, (enter, soften, turn))
 

time: 183 us -> 182 us (level)
  no operation moved by 1% of the time
where the time goes in v7:
time: 182 us; the launch traced here: 181 us
  Pallas kernels  138 us (76%)
  starting transfers between devices  26.1 us (14%)
  waiting for transfers between devices  9.99 us (5%)
  other arithmetic  3.66 us (2%)
  local copies, waits for them, and re-layouts  2.39 us (1%)
    pallas_call x1, Pallas kernels, third(): pl.pallas_call(third_body, grid=(utts + 1,), in_specs=[SMEM, whole(sums.s...  45.6 us
    pallas_call x1, Pallas kernels, first(): pl.pallas_call(first_body, grid=(utts,), in_specs=[SMEM, per_utt(BIG), pe...  34.1 us
    pallas_call x1, Pallas kernels, second(): pl.pallas_call(second_body, grid=(utts,), in_specs=[SMEM, whole(stats.sha...  21.5 us
    pallas_call x4, Pallas kernels, reorder(): pl.pallas_call(body, in_specs=[ANY, VMEM] + [ANY] * len(more), out_specs=...  18.8 us
    ppermute x14, starting transfers between devices, partner(): return lax.ppermute(values, 'dp', [(i, i ^ offset) for i in range(devices)])  17.6 us
    all_to_all x1, starting transfers between devices, local(): stats = lax.all_to_all(st, 'dp', 0, 0)  5.88 us
    pallas_call x1, Pallas kernels, enter(): pl.pallas_call(enter_body, in_specs=[ANY], out_specs=[ANY] * 3 + [VMEM],...  5.56 us
    ppermute x14, waiting for transfers between devices, partner(): return lax.ppermute(values, 'dp', [(i, i ^ offset) for i in range(devices)])  4.69 us
  transfers between devices with their start and end apart: 16, of which 6 were waited for; matrix products, arithmetic and copies ran while one was open for 0% of the time, Pallas kernels for 17%

profile of v7, /device:TPU:0, one launch (start us, length us, event | category | flops | bytes accessed | tf_op | source)
XLA Modules:
  0.0 181.4 jit_solution(6967138145242225965)
XLA Ops:
  0.6 0.8 convert_bitcast_fusion
  1.4 3.1 %collective-permute-start = (bf16[1,88,128]{2,1,0:T(8,128)(2,1)S(1)}, bf16[1,88,128]{2,1,0:T(8,128)(2,1)S(1)}, u32[]{:S(2)}, u32[]{:S(2)}) collective-permute-start(bf16[1,88,128]{2,1,0:T(8,128)(2,1)S(1)} %pad_bitcast_fusion), channel_id=1, source_target_pairs={{0,8},{1,9},{2,10},{3,11},{4,12},{5,13},{6,14},{7,15},{8,0},{9,1},... | collective-permute-start | bytes 67592 | tf_op jit(solution)/shard_map/ppermute | solution.py:1293
  4.5 2.6 %collective-permute-start.1 = (bf16[1,88,128]{2,1,0:T(8,128)(2,1)S(1)}, bf16[1,88,128]{2,1,0:T(8,128)(2,1)S(1)}, u32[]{:S(2)}, u32[]{:S(2)}) collective-permute-start(bf16[1,88,128]{2,1,0:T(8,128)(2,1)S(1)} %pad_bitcast_fusion), channel_id=1, source_target_pairs={{0,16},{1,17},{2,18},{3,19},{4,20},{5,21},{6,22},{7,23},{8,24},{9,... | collective-permute-start | bytes 67592 | tf_op jit(solution)/shard_map/ppermute | solution.py:1293
  7.1 0.0 collective-permute-start.2
  7.1 5.6 %enter.1 = (bf16[5,120,1536]{2,1,0:T(8,128)(2,1)}, f32[5,120,1536]{2,1,0:T(8,128)}, f32[5,8,1536]{2,1,0:T(8,128)}, bf16[384,384]{1,0:T(8,128)(2,1)}) custom-call(bf16[5,120,1536]{2,1,0:T(8,128)(2,1)} %bitcast.13), custom_call_target="tpu_custom_call" | custom-call | flops 2000000000 | bytes 8000000 | tf_op jit(solution)/shard_map/enter/pallas_call | solution.py:298
  12.7 0.0 collective-permute-done
  12.7 0.0 collective-permute-done.1
  12.7 0.0 collective-permute-done.2
  12.8 1.8 collective-permute-start.3
  14.5 1.5 collective-permute-start.4
  16.1 0.3 collective-permute-start.5
  16.3 4.8 %inward.1.cot_ref = bf16[5,120,1536]{2,1,0:T(8,128)(2,1)} custom-call(bf16[5,120,1536]{2,1,0:T(8,128)(2,1)} %bitcast.14, bf16[384,384]{1,0:T(8,128)(2,1)} %get-tuple-element.124.pm_ref), custom_call_target="tpu_custom_call" | custom-call | flops 2000000000 | bytes 8000000 | tf_op jit(solution)/shard_map/inward/pallas_call | solution.py:330
  21.1 0.0 collective-permute-done.3
  21.1 0.0 collective-permute-done.4
  21.1 0.4 collective-permute-done.5
  21.5 0.1 collective-permute-start.6
  21.7 1.6 collective-permute-done.6
  23.3 0.1 constant_dynamic-update-slice_fusion.4.g_ref
  23.3 0.0 copy-start.6
  23.4 0.9 copy-done.6
  24.2 2.9 %prepare.1 = (bf16[480,128]{1,0:T(8,128)(2,1)}, bf16[128,512]{1,0:T(8,128)(2,1)}, bf16[3,432,128]{2,1,0:T(8,128)(2,1)}, bf16[3,128,144]{2,1,0:T(8,128)(2,1)}, bf...) custom-call(s32[1]{0:T(128)} %bitcast.3.me_ref, bf16[32,88,128]{2,1,0:T(8,128)(2,1)} %copy-done.6), custom_call_target="tpu_custom_call" | custom-call | flops 1000000000 | bytes 2000000 | tf_op jit(solution)/shard_map/prepare/pallas_call | solution.py:533
  27.2 34.1 %first.1 = (bf16[5,128,1536]{2,1,0:T(8,128)(2,1)}, f32[5,120,1536]{2,1,0:T(8,128)}, bf16[5,384,512]{2,1,0:T(8,128)(2,1)}, bf16[5,1152,512]{2,1,0:T(8,128)(2,1)},...) custom-call(s32[5]{0:T(128)} %len_ref.5, ...), custom_call_target="tpu_custom_call" | custom-call | flops 10000000000 | bytes 60000000 | tf_op jit(solution)/shard_map/first/pallas_call | solution.py:741
  61.3 5.9 %all-to-all-start = ((f32[32,8,128]{2,1,0:T(8,128)}), f32[32,8,128]{2,1,0:T(8,128)S(1)}, u32[]{:S(2)}, u32[]{:S(2)}) async-start(f32[32,8,128]{2,1,0:T(8,128)} %get-tuple-element.109), calls=%async_computation | async-start | bytes 262144 | tf_op jit(solution)/shard_map/all_to_all | solution.py:1340
  67.2 3.6 %late.1 = (bf16[128,480]{1,0:T(8,128)(2,1)}, bf16[480,128]{1,0:T(8,128)(2,1)}, bf16[480,128]{1,0:T(8,128)(2,1)}, bf16[128,480]{1,0:T(8,128)(2,1)}, bf16[128,512]...) custom-call(s32[1]{0:T(128)} %bitcast.3.me_ref, ...), custom_call_target="tpu_custom_call" | custom-call | flops 3000000000 | bytes 10000000 | tf_op jit(solution)/shard_map/late/pallas_call | solution.py:542
  70.8 4.5 %all-to-all-done.stats_ref = f32[32,8,128]{2,1,0:T(8,128)S(1)} async-done(((f32[32,8,128]{2,1,0:T(8,128)}), f32[32,8,128]{2,1,0:T(8,128)S(1)}, u32[]{:S(2)}, u32[]{:S(2)}) %all-to-all-start) | async-done | bytes 131104 | tf_op jit(solution)/shard_map/all_to_all | solution.py:1340
  75.2 0.0 copy-start.2
  75.2 0.7 copy-done.2
  75.9 21.5 %second.1 = (bf16[5,120,1536]{2,1,0:T(8,128)(2,1)}, f32[5,120,1536]{2,1,0:T(8,128)}, f32[5,120,1536]{2,1,0:T(8,128)}, f32[32,8,128]{2,1,0:T(8,128)}, f32[128,128...) custom-call(s32[5]{0:T(128)} %len_ref.5, ...), custom_call_target="tpu_custom_call" | custom-call | flops 15000000512 | bytes 30000000 | tf_op jit(solution)/shard_map/second/pallas_call | solution.py:880
  97.4 2.6 %all-to-all-start.1 = ((f32[32,8,128]{2,1,0:T(8,128)}), f32[32,8,128]{2,1,0:T(8,128)S(1)}, u32[]{:S(2)}, u32[]{:S(2)}) async-start(f32[32,8,128]{2,1,0:T(8,128)} %get-tuple-element.119.sums_ref), calls=%async_computation.1 | async-start | bytes 262144 | tf_op jit(solution)/shard_map/all_to_all | solution.py:1344
  100.0 4.8 %outward.1 = bf16[5,120,1536]{2,1,0:T(8,128)(2,1)} custom-call(bf16[5,120,1536]{2,1,0:T(8,128)(2,1)} %get-tuple-element.123.far_in, bf16[384,384]{1,0:T(8,128)(2,1)} %get-tuple-element.124.pm_ref), custom_call_target="tpu_custom_call" | custom-call | flops 2000000000 | bytes 8000000 | tf_op jit(solution)/shard_map/outward/pallas_call | solution.py:330
  104.9 2.6 %ahead.1.last_ref = f32[909,128]{1,0:T(8,128)} custom-call(f32[512,128]{1,0:T(8,128)} %get-tuple-element.120.dn_ref, f32[480,128]{1,0:T(8,128)} %get-tuple-element.121.up_ref, f32[4,120,128]{2,1,0:T(8,128)} %get-tuple-element.122.vec_ref), custom_call_target="tpu_custom_call" | custom-call | flops 2000000000 | bytes 8000000 | tf_op jit(solution)/shard_map/ahead/pallas_call | solution.py:1167
  107.4 0.8 all-to-all-done.1.sums_ref
  108.3 0.0 copy-start.1
  108.3 0.6 copy-done.1
  108.9 45.6 %third.1 = (f32[5,120,1536]{2,1,0:T(8,128)}, f32[512,128]{1,0:T(8,128)}, f32[480,128]{1,0:T(8,128)}, f32[240,128]{1,0:T(8,128)}, f32[3,432,128]{2,1,0:T(8,128)},...) custom-call(s32[5]{0:T(128)} %len_ref.5, f32[32,8,128]{2,1,0:T(8,128)} %copy-done.1, ...), custom_call_target="tpu_custom_call" | custom-call | flops 20000000000 | bytes 80000000 | tf_op jit(solution)/shard_map/third/pallas_call | solution.py:1085
  154.5 3.7 %pack.1 = (f32[16,88,128]{2,1,0:T(8,128)}, f32[16,88,128]{2,1,0:T(8,128)}) custom-call(s32[1]{0:T(128)} %bitcast.3.me_ref, f32[909,128]{1,0:T(8,128)} %ahead.1.last_ref, f32[512,128]{1,0:T(8,128)} %get-tuple-element.150.dn1_ref, f32[480,128]{1,0:T(8,128)} %get-tuple-element.151.up1_ref, f32[128,128]{1,0:T(8,128)} %get-tuple-element.152.pr_ref, ...), custom_call_target="tpu_custom_call" | custom-call | flops 1000000000 | bytes 5000000 | tf_op jit(solution)/shard_map/pack/pallas_call | solution.py:1238
  158.2 0.2 collective-permute-start.7
  158.4 2.2 %collective-permute-done.7 = f32[16,88,128]{2,1,0:T(8,128)S(1)} collective-permute-done((f32[16,88,128]{2,1,0:T(8,128)}, f32[16,88,128]{2,1,0:T(8,128)S(1)}, u32[]{:S(2)}, u32[]{:S(2)}) %collective-permute-start.7) | collective-permute-done | bytes 720928 | tf_op jit(solution)/shard_map/ppermute | solution.py:1293
  160.6 1.2 fusion.6
  161.8 1.8 collective-permute-start.10
  163.7 0.5 collective-permute-start.8
  164.2 1.2 collective-permute-start.9
  165.4 5.0 %leave.2.refs_0_ = f32[5,120,1536]{2,1,0:T(8,128)} custom-call(f32[5,120,1536]{2,1,0:T(8,128)} %get-tuple-element.160.far_in, bf16[384,384]{1,0:T(8,128)(2,1)} %get-tuple-element.124.pm_ref), custom_call_target="tpu_custom_call" | custom-call | flops 2000000000 | bytes 8000000 | tf_op jit(solution)/shard_map/leave/pallas_call | solution.py:330
  170.4 0.0 collective-permute-done.10
  170.4 0.0 collective-permute-done.8
  170.4 0.0 collective-permute-done.9
  170.5 0.9 collective-permute-start.11
  171.4 2.5 %collective-permute-start.12 = (f32[1,88,128]{2,1,0:T(8,128)S(1)}, f32[1,88,128]{2,1,0:T(8,128)S(1)}, u32[]{:S(2)}, u32[]{:S(2)}) collective-permute-start(f32[1,88,128]{2,1,0:T(8,128)S(1)} %get-tuple-element.181), channel_id=1, source_target_pairs={{0,16},{1,17},{2,18},{3,19},{4,20},{5,21},{6,22},{7,23},{8,24},{9,... | collective-permute-start | bytes 135176 | tf_op jit(solution)/shard_map/ppermute | solution.py:1293
  173.9 0.0 copy-start
  173.9 0.0 copy-start.3
  173.9 0.0 copy-start.4
  173.9 0.0 copy-start.5
  173.9 1.1 collective-permute-start.13
  175.0 4.3 %leave.3 = f32[5,120,1536]{2,1,0:T(8,128)} custom-call(f32[5,120,1536]{2,1,0:T(8,128)} %get-tuple-element.160.far_in, bf16[384,384]{1,0:T(8,128)(2,1)} %get-tuple-element.124.pm_ref, f32[5,120,1536]{2,1,0:T(8,128)} %leave.2.refs_0_), custom_call_target="tpu_custom_call", output_to_operand_aliasing={{}: (2, {})} | custom-call | flops 2000000000 | bytes 8000000 | tf_op jit(solution)/shard_map/leave/pallas_call | solution.py:330
  179.3 0.0 collective-permute-done.11
  179.3 0.0 collective-permute-done.12
  179.3 0.5 collective-permute-done.13
  179.8 0.0 copy-done
  179.8 0.0 copy-done.3
  179.8 0.0 copy-done.4
  179.8 0.0 copy-done.5
  179.8 1.6 multiply_add_fusion.1
  (13 shorter events, 0.2 us)
Async XLA Ops:
  1.4 11.3 %collective-permute-start = (bf16[1,88,128]{2,1,0:T(8,128)(2,1)S(1)}, bf16[1,88,128]{2,1,0:T(8,128)(2,1)S(1)}, u32[]{:S(2)}, u32[]{:S(2)}) collective-permute-start(bf16[1,88,128]{2,1,0:T(8,128)(2,1)S(1)} %pad_bitcast_fusion), channel_id=1, source_target_pairs={{0,8},{1,9},{2,10},{3,11},{4,12},{5,13},{6,14},{7,15},{8,0},{9,1},... | collective-permute-start | bytes 67592 | tf_op jit(solution)/shard_map/ppermute | solution.py:1293
  4.5 8.2 %collective-permute-start.1 = (bf16[1,88,128]{2,1,0:T(8,128)(2,1)S(1)}, bf16[1,88,128]{2,1,0:T(8,128)(2,1)S(1)}, u32[]{:S(2)}, u32[]{:S(2)}) collective-permute-start(bf16[1,88,128]{2,1,0:T(8,128)(2,1)S(1)} %pad_bitcast_fusion), channel_id=1, source_target_pairs={{0,16},{1,17},{2,18},{3,19},{4,20},{5,21},{6,22},{7,23},{8,24},{9,... | collective-permute-start | bytes 67592 | tf_op jit(solution)/shard_map/ppermute | solution.py:1293
  7.1 5.6 %collective-permute-start.2 = (bf16[1,88,128]{2,1,0:T(8,128)(2,1)S(1)}, bf16[1,88,128]{2,1,0:T(8,128)(2,1)S(1)}, u32[]{:S(2)}, u32[]{:S(2)}) collective-permute-start(bf16[1,88,128]{2,1,0:T(8,128)(2,1)S(1)} %pad_bitcast_fusion), channel_id=1, source_target_pairs={{0,24},{1,25},{2,26},{3,27},{4,28},{5,29},{6,30},{7,31},{8,16},{9,... | collective-permute-start | bytes 67592 | tf_op jit(solution)/shard_map/ppermute | solution.py:1293
  12.8 8.3 %collective-permute-start.3 = (bf16[4,88,128]{2,1,0:T(8,128)(2,1)S(1)}, bf16[4,88,128]{2,1,0:T(8,128)(2,1)S(1)}, u32[]{:S(2)}, u32[]{:S(2)}) collective-permute-start(bf16[4,88,128]{2,1,0:T(8,128)(2,1)S(1)} %constant_dynamic-update-slice_fusion), channel_id=1, source_target_pairs={{0,2},{1,3},{2,0},{3,1},{4,6},{5,7},{6,4},{7,5},{8,10},{9,11},{10,... | collective-permute-start | bytes 270344 | tf_op jit(solution)/shard_map/ppermute | solution.py:1293
  14.5 6.6 %collective-permute-start.4 = (bf16[4,88,128]{2,1,0:T(8,128)(2,1)S(1)}, bf16[4,88,128]{2,1,0:T(8,128)(2,1)S(1)}, u32[]{:S(2)}, u32[]{:S(2)}) collective-permute-start(bf16[4,88,128]{2,1,0:T(8,128)(2,1)S(1)} %constant_dynamic-update-slice_fusion), channel_id=1, source_target_pairs={{0,4},{1,5},{2,6},{3,7},{4,0},{5,1},{6,2},{7,3},{8,12},{9,13},{10,... | collective-permute-start | bytes 270344 | tf_op jit(solution)/shard_map/ppermute | solution.py:1293
  16.1 5.4 %collective-permute-start.5 = (bf16[4,88,128]{2,1,0:T(8,128)(2,1)S(1)}, bf16[4,88,128]{2,1,0:T(8,128)(2,1)S(1)}, u32[]{:S(2)}, u32[]{:S(2)}) collective-permute-start(bf16[4,88,128]{2,1,0:T(8,128)(2,1)S(1)} %constant_dynamic-update-slice_fusion), channel_id=1, source_target_pairs={{0,6},{1,7},{2,4},{3,5},{4,2},{5,3},{6,0},{7,1},{8,14},{9,15},{10,... | collective-permute-start | bytes 270344 | tf_op jit(solution)/shard_map/ppermute | solution.py:1293
  21.5 1.7 collective-permute-start.6
  23.3 0.9 copy-start.6
  61.3 13.9 %all-to-all-start = ((f32[32,8,128]{2,1,0:T(8,128)}), f32[32,8,128]{2,1,0:T(8,128)S(1)}, u32[]{:S(2)}, u32[]{:S(2)}) async-start(f32[32,8,128]{2,1,0:T(8,128)} %get-tuple-element.109), calls=%async_computation | async-start | bytes 262144 | tf_op jit(solution)/shard_map/all_to_all | solution.py:1340
  75.2 0.7 copy-start.2
  97.4 10.8 %all-to-all-start.1 = ((f32[32,8,128]{2,1,0:T(8,128)}), f32[32,8,128]{2,1,0:T(8,128)S(1)}, u32[]{:S(2)}, u32[]{:S(2)}) async-start(f32[32,8,128]{2,1,0:T(8,128)} %get-tuple-element.119.sums_ref), calls=%async_computation.1 | async-start | bytes 262144 | tf_op jit(solution)/shard_map/all_to_all | solution.py:1344
  108.3 0.6 copy-start.1
  158.2 2.4 %collective-permute-start.7 = (f32[16,88,128]{2,1,0:T(8,128)}, f32[16,88,128]{2,1,0:T(8,128)S(1)}, u32[]{:S(2)}, u32[]{:S(2)}) collective-permute-start(f32[16,88,128]{2,1,0:T(8,128)} %get-tuple-element.159), channel_id=1, source_target_pairs={{0,1},{1,0},{2,3},{3,2},{4,5},{5,4},{6,7},{7,6},{8,9},{9,8},{10,11... | collective-permute-start | bytes 2162696 | tf_op jit(solution)/shard_map/ppermute | solution.py:1293
  161.8 8.5 %collective-permute-start.10 = (bf16[4,88,128]{2,1,0:T(8,128)(2,1)S(1)}, bf16[4,88,128]{2,1,0:T(8,128)(2,1)S(1)}, u32[]{:S(2)}, u32[]{:S(2)}) collective-permute-start(bf16[4,88,128]{2,1,0:T(8,128)(2,1)S(1)} %get-tuple-element.176), channel_id=1, source_target_pairs={{0,6},{1,7},{2,4},{3,5},{4,2},{5,3},{6,0},{7,1},{8,14},{9,15},{10,... | collective-permute-start | bytes 270344 | tf_op jit(solution)/shard_map/ppermute | solution.py:1293
  163.7 6.7 %collective-permute-start.8 = (bf16[4,88,128]{2,1,0:T(8,128)(2,1)S(1)}, bf16[4,88,128]{2,1,0:T(8,128)(2,1)S(1)}, u32[]{:S(2)}, u32[]{:S(2)}) collective-permute-start(bf16[4,88,128]{2,1,0:T(8,128)(2,1)S(1)} %get-tuple-element.178), channel_id=1, source_target_pairs={{0,2},{1,3},{2,0},{3,1},{4,6},{5,7},{6,4},{7,5},{8,10},{9,11},{10,... | collective-permute-start | bytes 270344 | tf_op jit(solution)/shard_map/ppermute | solution.py:1293
  164.2 6.2 %collective-permute-start.9 = (bf16[4,88,128]{2,1,0:T(8,128)(2,1)S(1)}, bf16[4,88,128]{2,1,0:T(8,128)(2,1)S(1)}, u32[]{:S(2)}, u32[]{:S(2)}) collective-permute-start(bf16[4,88,128]{2,1,0:T(8,128)(2,1)S(1)} %get-tuple-element.177), channel_id=1, source_target_pairs={{0,4},{1,5},{2,6},{3,7},{4,0},{5,1},{6,2},{7,3},{8,12},{9,13},{10,... | collective-permute-start | bytes 270344 | tf_op jit(solution)/shard_map/ppermute | solution.py:1293
  170.5 8.8 %collective-permute-start.11 = (f32[1,88,128]{2,1,0:T(8,128)S(1)}, f32[1,88,128]{2,1,0:T(8,128)S(1)}, u32[]{:S(2)}, u32[]{:S(2)}) collective-permute-start(f32[1,88,128]{2,1,0:T(8,128)S(1)} %get-tuple-element.182), channel_id=1, source_target_pairs={{0,8},{1,9},{2,10},{3,11},{4,12},{5,13},{6,14},{7,15},{8,0},{9,1},... | collective-permute-start | bytes 135176 | tf_op jit(solution)/shard_map/ppermute | solution.py:1293
  171.4 7.9 %collective-permute-start.12 = (f32[1,88,128]{2,1,0:T(8,128)S(1)}, f32[1,88,128]{2,1,0:T(8,128)S(1)}, u32[]{:S(2)}, u32[]{:S(2)}) collective-permute-start(f32[1,88,128]{2,1,0:T(8,128)S(1)} %get-tuple-element.181), channel_id=1, source_target_pairs={{0,16},{1,17},{2,18},{3,19},{4,20},{5,21},{6,22},{7,23},{8,24},{9,... | collective-permute-start | bytes 135176 | tf_op jit(solution)/shard_map/ppermute | solution.py:1293
  173.9 5.9 %copy-start = (f32[10624]{0:T(1024)S(1)}, f32[10624]{0:T(1024)}, u32[]{:S(2)}) copy-start(f32[10624]{0:T(1024)} %param.12) | copy-start | bytes 127492
  173.9 5.9 %copy-start.3 = (f32[10624]{0:T(1024)S(1)}, f32[10624]{0:T(1024)}, u32[]{:S(2)}) copy-start(f32[10624]{0:T(1024)} %param.15) | copy-start | bytes 127492
  173.9 5.9 %copy-start.4 = (f32[10624]{0:T(1024)S(1)}, f32[10624]{0:T(1024)}, u32[]{:S(2)}) copy-start(f32[10624]{0:T(1024)} %param.13) | copy-start | bytes 127492
  173.9 5.9 %copy-start.5 = (f32[10624]{0:T(1024)S(1)}, f32[10624]{0:T(1024)}, u32[]{:S(2)}) copy-start(f32[10624]{0:T(1024)} %param.14) | copy-start | bytes 127492
  173.9 5.9 %collective-permute-start.13 = (f32[1,88,128]{2,1,0:T(8,128)S(1)}, f32[1,88,128]{2,1,0:T(8,128)S(1)}, u32[]{:S(2)}, u32[]{:S(2)}) collective-permute-start(f32[1,88,128]{2,1,0:T(8,128)S(1)} %get-tuple-element.180), channel_id=1, source_target_pairs={{0,24},{1,25},{2,26},{3,27},{4,28},{5,29},{6,30},{7,31},{8,16},{9,... | collective-permute-start | bytes 135176 | tf_op jit(solution)/shard_map/ppermute | solution.py:1293

commit v8 on v7

--- a/solution.py
+++ b/solution.py
@@ -582,7 +582,7 @@
 
 def first_body(
     len_ref, xp_ref, xf_ref, cols_ref, up_ref, dn_ref, wqkv_ref, wo_ref, pw_ref, base_ref,
-    lf_ref, xa_ref, nrm_ref, qkv_ref, prob_ref, att_ref, aa_ref, xc_ref, cn_ref, gat_ref, sig_ref, rgt_ref,
+    lf_ref, xa_ref, nrm_ref, qkv_ref, prob_ref, att_ref, aa_ref, xc_ref, cn_ref, gat_ref, sig_ref,
     ra_ref, rc_ref, dep_ref, st_ref,
     hid, one, cb, tab, run,
 ):
@@ -673,7 +673,6 @@
         gated = (pre[:D] + pre[:D]) * sig
         gat_ref[0, :, span(r)] = gated
         sig_ref[0, :, span(r)] = sig
-        rgt_ref[0, :, span(r)] = gated * (1.0 - sig)
 
     skewed(GROUP, (project, gate_in, gate_out))
 
@@ -730,7 +729,6 @@
         (BIG, f32),
         (BIG, f32),
         (LOW, bf16),
-        (BIG, f32),
         (BIG, f32),
         (BIG, f32),
         ((8, MAXLEN), f32),
@@ -894,14 +892,14 @@
 
 def third_body(
     len_ref, sums_ref, stc_ref, bgd_ref, dep_ref, gat_ref, ri_ref, ra_ref, rc_ref,
-    gc_far, xc_far, cn_far, sig_far, rgt_far, att_far, qkv_far, prob_far, nrm_far, lf_far, xa_far, xf_far,
+    gc_far, xc_far, cn_far, sig_far, gated_far, att_far, qkv_far, prob_far, nrm_far, lf_far, xa_far, xf_far,
     cols_ref, up_ref, upp_ref, dnp_ref, wqkv_t_ref, wob_ref, pwp_ref,
     grad_ref, gdn_ref, gup_ref, gpw_ref, gqkv_ref, go_ref, rel_ref, rows_ref,
-    gc_ref, xc_ref, cn_ref, sig_ref, rgt_ref, att_ref, qkv_ref, prob_ref, nrm_ref, lf_ref, xa_ref, xf_ref, sems,
+    gc_ref, xc_ref, cn_ref, sig_ref, gated_ref, att_ref, qkv_ref, prob_ref, nrm_ref, lf_ref, xa_ref, xf_ref, sems,
     hid, dgx, dgs, olg, agr, back_s, gg, near_s, far_s, vec_ref, cb, tot,
 ):
-    far = (gc_far, xc_far, cn_far, sig_far, rgt_far, att_far, qkv_far, prob_far, nrm_far, lf_far, xa_far, xf_far)
-    near = (gc_ref, xc_ref, cn_ref, sig_ref, rgt_ref, att_ref, qkv_ref, prob_ref, nrm_ref, lf_ref, xa_ref, xf_ref)
+    far = (gc_far, xc_far, cn_far, sig_far, gated_far, att_far, qkv_far, prob_far, nrm_far, lf_far, xa_far, xf_far)
+    near = (gc_ref, xc_ref, cn_ref, sig_ref, gated_ref, att_ref, qkv_ref, prob_ref, nrm_ref, lf_ref, xa_ref, xf_ref)
     u = pl.program_id(0)
     utts = pl.num_programs(0) - 1
     slot = 1 - u % 2
@@ -973,8 +971,9 @@
     def back():
         def gate(r, held):
             grad = gg[:, span(r)]
-            left = grad * sig_ref[slot, :, span(r)]
-            right = grad * rgt_ref[slot, :, span(r)]
+            sig = sig_ref[slot, :, span(r)]
+            left = grad * sig
+            right = grad * gated_ref[slot, :, span(r)] * (1.0 - sig)
             pre_low = jnp.concatenate([left, right], axis=0).astype(bf16)
             gpw_ref[...] += dot_nt(pre_low, cn_ref[slot, :, span(r)])
             return dot(pwp_ref[...], pre_low)[:D]
@@ -1334,7 +1333,7 @@
     early, late = prepare(me, gathered, rows)
     up1, dn1, wqkv, wo, pw, cols, base = early
     upp1, dnp1, up2, upp2, dn2, dnp2, pwp, pr, prp, wqkvt, wob = late
-    lf, xa, nrm, qkv, prob, att, aa, xc, cn, gat, sig, rgt, ra, rc, dep, st = first(
+    lf, xa, nrm, qkv, prob, att, aa, xc, cn, gat, sig, ra, rc, dep, st = first(
         devices, lengths, xp, xf, (cols, up1, dn1, wqkv, wo, pw, base)
     )
     stats = lax.all_to_all(st, "dp", 0, 0)
@@ -1348,7 +1347,7 @@
     grad, gdn1, gup1, gpw, gqkv, go, rel, vec3 = third(
         lengths, all_sums, stc,
         (bgd, dep, gat, rs_in, ra, rc),
-        (gc, xc, cn, sig, rgt, att, qkv, prob, nrm, lf, xa, xf),
+        (gc, xc, cn, sig, gat, att, qkv, prob, nrm, lf, xa, xf),
         (cols, up1, upp1, dnp1, wqkvt, wob, pwp),
     )
     keep, send = pack(devices, rows, me, (last, gdn1, gup1, gpr, gpw, gqkv, go, rel, vec3, sums))

time: 182 us -> 182 us (level)
  no operation moved by 1% of the time
where the time goes in v8:
time: 182 us; the launch traced here: 181 us
  Pallas kernels  138 us (76%)
  starting transfers between devices  26.1 us (14%)
  waiting for transfers between devices  9.99 us (5%)
  other arithmetic  3.66 us (2%)
  local copies, waits for them, and re-layouts  2.39 us (1%)
    pallas_call x1, Pallas kernels, third(): pl.pallas_call(third_body, grid=(utts + 1,), in_specs=[SMEM, whole(sums.s...  45.9 us
    pallas_call x1, Pallas kernels, first(): pl.pallas_call(first_body, grid=(utts,), in_specs=[SMEM, per_utt(BIG), pe...  33.7 us
    pallas_call x1, Pallas kernels, second(): pl.pallas_call(second_body, grid=(utts,), in_specs=[SMEM, whole(stats.sha...  21.5 us
    pallas_call x4, Pallas kernels, reorder(): pl.pallas_call(body, in_specs=[ANY, VMEM] + [ANY] * len(more), out_specs=...  18.8 us
    ppermute x14, starting transfers between devices, partner(): return lax.ppermute(values, 'dp', [(i, i ^ offset) for i in range(devices)])  17.6 us
    all_to_all x1, starting transfers between devices, local(): stats = lax.all_to_all(st, 'dp', 0, 0)  5.89 us
    pallas_call x1, Pallas kernels, enter(): pl.pallas_call(enter_body, in_specs=[ANY], out_specs=[ANY] * 3 + [VMEM],...  5.56 us
    ppermute x14, waiting for transfers between devices, partner(): return lax.ppermute(values, 'dp', [(i, i ^ offset) for i in range(devices)])  4.7 us
  transfers between devices with their start and end apart: 16, of which 6 were waited for; matrix products, arithmetic and copies ran while one was open for 0% of the time, Pallas kernels for 17%

profile of v8, /device:TPU:0, one launch (start us, length us, event | category | flops | bytes accessed | tf_op | source)
XLA Modules:
  0.0 181.3 jit_solution(9779380177367599649)
XLA Ops:
  0.6 0.8 convert_bitcast_fusion
  1.4 3.1 %collective-permute-start = (bf16[1,88,128]{2,1,0:T(8,128)(2,1)S(1)}, bf16[1,88,128]{2,1,0:T(8,128)(2,1)S(1)}, u32[]{:S(2)}, u32[]{:S(2)}) collective-permute-start(bf16[1,88,128]{2,1,0:T(8,128)(2,1)S(1)} %pad_bitcast_fusion), channel_id=1, source_target_pairs={{0,8},{1,9},{2,10},{3,11},{4,12},{5,13},{6,14},{7,15},{8,0},{9,1},... | collective-permute-start | bytes 67592 | tf_op jit(solution)/shard_map/ppermute | solution.py:1292
  4.5 2.6 %collective-permute-start.1 = (bf16[1,88,128]{2,1,0:T(8,128)(2,1)S(1)}, bf16[1,88,128]{2,1,0:T(8,128)(2,1)S(1)}, u32[]{:S(2)}, u32[]{:S(2)}) collective-permute-start(bf16[1,88,128]{2,1,0:T(8,128)(2,1)S(1)} %pad_bitcast_fusion), channel_id=1, source_target_pairs={{0,16},{1,17},{2,18},{3,19},{4,20},{5,21},{6,22},{7,23},{8,24},{9,... | collective-permute-start | bytes 67592 | tf_op jit(solution)/shard_map/ppermute | solution.py:1292
  7.1 0.0 collective-permute-start.2
  7.1 5.6 %enter.1 = (bf16[5,120,1536]{2,1,0:T(8,128)(2,1)}, f32[5,120,1536]{2,1,0:T(8,128)}, f32[5,8,1536]{2,1,0:T(8,128)}, bf16[384,384]{1,0:T(8,128)(2,1)}) custom-call(bf16[5,120,1536]{2,1,0:T(8,128)(2,1)} %bitcast.13), custom_call_target="tpu_custom_call" | custom-call | flops 2000000000 | bytes 8000000 | tf_op jit(solution)/shard_map/enter/pallas_call | solution.py:298
  12.7 0.0 collective-permute-done
  12.7 0.0 collective-permute-done.1
  12.7 0.0 collective-permute-done.2
  12.8 1.8 collective-permute-start.3
  14.5 1.5 collective-permute-start.4
  16.1 0.3 collective-permute-start.5
  16.3 4.8 %inward.1.cot_ref = bf16[5,120,1536]{2,1,0:T(8,128)(2,1)} custom-call(bf16[5,120,1536]{2,1,0:T(8,128)(2,1)} %bitcast.14, bf16[384,384]{1,0:T(8,128)(2,1)} %get-tuple-element.123.pm_ref), custom_call_target="tpu_custom_call" | custom-call | flops 2000000000 | bytes 8000000 | tf_op jit(solution)/shard_map/inward/pallas_call | solution.py:330
  21.1 0.0 collective-permute-done.3
  21.1 0.0 collective-permute-done.4
  21.1 0.4 collective-permute-done.5
  21.5 0.1 collective-permute-start.6
  21.7 1.6 collective-permute-done.6
  23.3 0.1 constant_dynamic-update-slice_fusion.4.g_ref
  23.3 0.0 copy-start.6
  23.4 0.9 copy-done.6
  24.2 2.9 %prepare.1 = (bf16[480,128]{1,0:T(8,128)(2,1)}, bf16[128,512]{1,0:T(8,128)(2,1)}, bf16[3,432,128]{2,1,0:T(8,128)(2,1)}, bf16[3,128,144]{2,1,0:T(8,128)(2,1)}, bf...) custom-call(s32[1]{0:T(128)} %bitcast.3.me_ref, bf16[32,88,128]{2,1,0:T(8,128)(2,1)} %copy-done.6), custom_call_target="tpu_custom_call" | custom-call | flops 1000000000 | bytes 2000000 | tf_op jit(solution)/shard_map/prepare/pallas_call | solution.py:533
  27.2 33.7 %first.1 = (bf16[5,128,1536]{2,1,0:T(8,128)(2,1)}, f32[5,120,1536]{2,1,0:T(8,128)}, bf16[5,384,512]{2,1,0:T(8,128)(2,1)}, bf16[5,1152,512]{2,1,0:T(8,128)(2,1)},...) custom-call(s32[5]{0:T(128)} %len_ref.5, ...), custom_call_target="tpu_custom_call" | custom-call | flops 10000000000 | bytes 60000000 | tf_op jit(solution)/shard_map/first/pallas_call | solution.py:739
  60.9 5.9 %all-to-all-start = ((f32[32,8,128]{2,1,0:T(8,128)}), f32[32,8,128]{2,1,0:T(8,128)S(1)}, u32[]{:S(2)}, u32[]{:S(2)}) async-start(f32[32,8,128]{2,1,0:T(8,128)} %get-tuple-element.108), calls=%async_computation | async-start | bytes 262144 | tf_op jit(solution)/shard_map/all_to_all | solution.py:1339
  66.8 3.6 %late.1 = (bf16[128,480]{1,0:T(8,128)(2,1)}, bf16[480,128]{1,0:T(8,128)(2,1)}, bf16[480,128]{1,0:T(8,128)(2,1)}, bf16[128,480]{1,0:T(8,128)(2,1)}, bf16[128,512]...) custom-call(s32[1]{0:T(128)} %bitcast.3.me_ref, ...), custom_call_target="tpu_custom_call" | custom-call | flops 3000000000 | bytes 10000000 | tf_op jit(solution)/shard_map/late/pallas_call | solution.py:542
  70.4 4.5 %all-to-all-done.stats_ref = f32[32,8,128]{2,1,0:T(8,128)S(1)} async-done(((f32[32,8,128]{2,1,0:T(8,128)}), f32[32,8,128]{2,1,0:T(8,128)S(1)}, u32[]{:S(2)}, u32[]{:S(2)}) %all-to-all-start) | async-done | bytes 131104 | tf_op jit(solution)/shard_map/all_to_all | solution.py:1339
  74.9 0.0 copy-start.2
  74.9 0.7 copy-done.2
  75.5 21.5 %second.1 = (bf16[5,120,1536]{2,1,0:T(8,128)(2,1)}, f32[5,120,1536]{2,1,0:T(8,128)}, f32[5,120,1536]{2,1,0:T(8,128)}, f32[32,8,128]{2,1,0:T(8,128)}, f32[128,128...) custom-call(s32[5]{0:T(128)} %len_ref.5, ...), custom_call_target="tpu_custom_call" | custom-call | flops 15000000512 | bytes 30000000 | tf_op jit(solution)/shard_map/second/pallas_call | solution.py:878
  97.0 2.6 %all-to-all-start.1 = ((f32[32,8,128]{2,1,0:T(8,128)}), f32[32,8,128]{2,1,0:T(8,128)S(1)}, u32[]{:S(2)}, u32[]{:S(2)}) async-start(f32[32,8,128]{2,1,0:T(8,128)} %get-tuple-element.118.sums_ref), calls=%async_computation.1 | async-start | bytes 262144 | tf_op jit(solution)/shard_map/all_to_all | solution.py:1343
  99.6 4.8 %outward.1 = bf16[5,120,1536]{2,1,0:T(8,128)(2,1)} custom-call(bf16[5,120,1536]{2,1,0:T(8,128)(2,1)} %get-tuple-element.122.far_in, bf16[384,384]{1,0:T(8,128)(2,1)} %get-tuple-element.123.pm_ref), custom_call_target="tpu_custom_call" | custom-call | flops 2000000000 | bytes 8000000 | tf_op jit(solution)/shard_map/outward/pallas_call | solution.py:330
  104.5 2.6 %ahead.1.last_ref = f32[909,128]{1,0:T(8,128)} custom-call(f32[512,128]{1,0:T(8,128)} %get-tuple-element.119.dn_ref, f32[480,128]{1,0:T(8,128)} %get-tuple-element.120.up_ref, f32[4,120,128]{2,1,0:T(8,128)} %get-tuple-element.121.vec_ref), custom_call_target="tpu_custom_call" | custom-call | flops 2000000000 | bytes 8000000 | tf_op jit(solution)/shard_map/ahead/pallas_call | solution.py:1166
  107.0 0.8 all-to-all-done.1.sums_ref
  107.8 0.0 copy-start.1
  107.8 0.7 copy-done.1
  108.5 45.9 %third.1 = (f32[5,120,1536]{2,1,0:T(8,128)}, f32[512,128]{1,0:T(8,128)}, f32[480,128]{1,0:T(8,128)}, f32[240,128]{1,0:T(8,128)}, f32[3,432,128]{2,1,0:T(8,128)},...) custom-call(s32[5]{0:T(128)} %len_ref.5, f32[32,8,128]{2,1,0:T(8,128)} %copy-done.1, ...), custom_call_target="tpu_custom_call" | custom-call | flops 20000000000 | bytes 80000000 | tf_op jit(solution)/shard_map/third/pallas_call | solution.py:1084
  154.4 3.7 %pack.1 = (f32[16,88,128]{2,1,0:T(8,128)}, f32[16,88,128]{2,1,0:T(8,128)}) custom-call(s32[1]{0:T(128)} %bitcast.3.me_ref, f32[909,128]{1,0:T(8,128)} %ahead.1.last_ref, f32[512,128]{1,0:T(8,128)} %get-tuple-element.148.dn1_ref, f32[480,128]{1,0:T(8,128)} %get-tuple-element.149.up1_ref, f32[128,128]{1,0:T(8,128)} %get-tuple-element.150.pr_ref, ...), custom_call_target="tpu_custom_call" | custom-call | flops 1000000000 | bytes 5000000 | tf_op jit(solution)/shard_map/pack/pallas_call | solution.py:1237
  158.1 0.2 collective-permute-start.7
  158.3 2.2 %collective-permute-done.7 = f32[16,88,128]{2,1,0:T(8,128)S(1)} collective-permute-done((f32[16,88,128]{2,1,0:T(8,128)}, f32[16,88,128]{2,1,0:T(8,128)S(1)}, u32[]{:S(2)}, u32[]{:S(2)}) %collective-permute-start.7) | collective-permute-done | bytes 720928 | tf_op jit(solution)/shard_map/ppermute | solution.py:1292
  160.5 1.2 fusion.6
  161.7 1.8 %collective-permute-start.10 = (bf16[4,88,128]{2,1,0:T(8,128)(2,1)S(1)}, bf16[4,88,128]{2,1,0:T(8,128)(2,1)S(1)}, u32[]{:S(2)}, u32[]{:S(2)}) collective-permute-start(bf16[4,88,128]{2,1,0:T(8,128)(2,1)S(1)} %get-tuple-element.174), channel_id=1, source_target_pairs={{0,6},{1,7},{2,4},{3,5},{4,2},{5,3},{6,0},{7,1},{8,14},{9,15},{10,... | collective-permute-start | bytes 270344 | tf_op jit(solution)/shard_map/ppermute | solution.py:1292
  163.5 0.5 collective-permute-start.8
  164.1 1.2 collective-permute-start.9
  165.3 5.0 %leave.2.refs_0_ = f32[5,120,1536]{2,1,0:T(8,128)} custom-call(f32[5,120,1536]{2,1,0:T(8,128)} %get-tuple-element.158.far_in, bf16[384,384]{1,0:T(8,128)(2,1)} %get-tuple-element.123.pm_ref), custom_call_target="tpu_custom_call" | custom-call | flops 2000000000 | bytes 8000000 | tf_op jit(solution)/shard_map/leave/pallas_call | solution.py:330
  170.2 0.0 collective-permute-done.10
  170.2 0.0 collective-permute-done.8
  170.2 0.0 collective-permute-done.9
  170.3 0.9 collective-permute-start.11
  171.3 2.5 %collective-permute-start.12 = (f32[1,88,128]{2,1,0:T(8,128)S(1)}, f32[1,88,128]{2,1,0:T(8,128)S(1)}, u32[]{:S(2)}, u32[]{:S(2)}) collective-permute-start(f32[1,88,128]{2,1,0:T(8,128)S(1)} %get-tuple-element.179), channel_id=1, source_target_pairs={{0,16},{1,17},{2,18},{3,19},{4,20},{5,21},{6,22},{7,23},{8,24},{9,... | collective-permute-start | bytes 135176 | tf_op jit(solution)/shard_map/ppermute | solution.py:1292
  173.8 0.0 copy-start
  173.8 0.0 copy-start.3
  173.8 0.0 copy-start.4
  173.8 0.0 copy-start.5
  173.8 1.1 collective-permute-start.13
  174.9 4.3 %leave.3 = f32[5,120,1536]{2,1,0:T(8,128)} custom-call(f32[5,120,1536]{2,1,0:T(8,128)} %get-tuple-element.158.far_in, bf16[384,384]{1,0:T(8,128)(2,1)} %get-tuple-element.123.pm_ref, f32[5,120,1536]{2,1,0:T(8,128)} %leave.2.refs_0_), custom_call_target="tpu_custom_call", output_to_operand_aliasing={{}: (2, {})} | custom-call | flops 2000000000 | bytes 8000000 | tf_op jit(solution)/shard_map/leave/pallas_call | solution.py:330
  179.1 0.0 collective-permute-done.11
  179.2 0.0 collective-permute-done.12
  179.2 0.5 collective-permute-done.13
  179.7 0.0 copy-done
  179.7 0.0 copy-done.3
  179.7 0.0 copy-done.4
  179.7 0.0 copy-done.5
  179.7 1.6 multiply_add_fusion.1
  (13 shorter events, 0.2 us)
Async XLA Ops:
  1.4 11.3 %collective-permute-start = (bf16[1,88,128]{2,1,0:T(8,128)(2,1)S(1)}, bf16[1,88,128]{2,1,0:T(8,128)(2,1)S(1)}, u32[]{:S(2)}, u32[]{:S(2)}) collective-permute-start(bf16[1,88,128]{2,1,0:T(8,128)(2,1)S(1)} %pad_bitcast_fusion), channel_id=1, source_target_pairs={{0,8},{1,9},{2,10},{3,11},{4,12},{5,13},{6,14},{7,15},{8,0},{9,1},... | collective-permute-start | bytes 67592 | tf_op jit(solution)/shard_map/ppermute | solution.py:1292
  4.5 8.2 %collective-permute-start.1 = (bf16[1,88,128]{2,1,0:T(8,128)(2,1)S(1)}, bf16[1,88,128]{2,1,0:T(8,128)(2,1)S(1)}, u32[]{:S(2)}, u32[]{:S(2)}) collective-permute-start(bf16[1,88,128]{2,1,0:T(8,128)(2,1)S(1)} %pad_bitcast_fusion), channel_id=1, source_target_pairs={{0,16},{1,17},{2,18},{3,19},{4,20},{5,21},{6,22},{7,23},{8,24},{9,... | collective-permute-start | bytes 67592 | tf_op jit(solution)/shard_map/ppermute | solution.py:1292
  7.1 5.6 %collective-permute-start.2 = (bf16[1,88,128]{2,1,0:T(8,128)(2,1)S(1)}, bf16[1,88,128]{2,1,0:T(8,128)(2,1)S(1)}, u32[]{:S(2)}, u32[]{:S(2)}) collective-permute-start(bf16[1,88,128]{2,1,0:T(8,128)(2,1)S(1)} %pad_bitcast_fusion), channel_id=1, source_target_pairs={{0,24},{1,25},{2,26},{3,27},{4,28},{5,29},{6,30},{7,31},{8,16},{9,... | collective-permute-start | bytes 67592 | tf_op jit(solution)/shard_map/ppermute | solution.py:1292
  12.8 8.3 %collective-permute-start.3 = (bf16[4,88,128]{2,1,0:T(8,128)(2,1)S(1)}, bf16[4,88,128]{2,1,0:T(8,128)(2,1)S(1)}, u32[]{:S(2)}, u32[]{:S(2)}) collective-permute-start(bf16[4,88,128]{2,1,0:T(8,128)(2,1)S(1)} %constant_dynamic-update-slice_fusion), channel_id=1, source_target_pairs={{0,2},{1,3},{2,0},{3,1},{4,6},{5,7},{6,4},{7,5},{8,10},{9,11},{10,... | collective-permute-start | bytes 270344 | tf_op jit(solution)/shard_map/ppermute | solution.py:1292
  14.5 6.6 %collective-permute-start.4 = (bf16[4,88,128]{2,1,0:T(8,128)(2,1)S(1)}, bf16[4,88,128]{2,1,0:T(8,128)(2,1)S(1)}, u32[]{:S(2)}, u32[]{:S(2)}) collective-permute-start(bf16[4,88,128]{2,1,0:T(8,128)(2,1)S(1)} %constant_dynamic-update-slice_fusion), channel_id=1, source_target_pairs={{0,4},{1,5},{2,6},{3,7},{4,0},{5,1},{6,2},{7,3},{8,12},{9,13},{10,... | collective-permute-start | bytes 270344 | tf_op jit(solution)/shard_map/ppermute | solution.py:1292
  16.1 5.4 %collective-permute-start.5 = (bf16[4,88,128]{2,1,0:T(8,128)(2,1)S(1)}, bf16[4,88,128]{2,1,0:T(8,128)(2,1)S(1)}, u32[]{:S(2)}, u32[]{:S(2)}) collective-permute-start(bf16[4,88,128]{2,1,0:T(8,128)(2,1)S(1)} %constant_dynamic-update-slice_fusion), channel_id=1, source_target_pairs={{0,6},{1,7},{2,4},{3,5},{4,2},{5,3},{6,0},{7,1},{8,14},{9,15},{10,... | collective-permute-start | bytes 270344 | tf_op jit(solution)/shard_map/ppermute | solution.py:1292
  21.5 1.7 collective-permute-start.6
  23.3 0.9 copy-start.6
  60.9 13.9 %all-to-all-start = ((f32[32,8,128]{2,1,0:T(8,128)}), f32[32,8,128]{2,1,0:T(8,128)S(1)}, u32[]{:S(2)}, u32[]{:S(2)}) async-start(f32[32,8,128]{2,1,0:T(8,128)} %get-tuple-element.108), calls=%async_computation | async-start | bytes 262144 | tf_op jit(solution)/shard_map/all_to_all | solution.py:1339
  74.9 0.7 copy-start.2
  97.0 10.8 %all-to-all-start.1 = ((f32[32,8,128]{2,1,0:T(8,128)}), f32[32,8,128]{2,1,0:T(8,128)S(1)}, u32[]{:S(2)}, u32[]{:S(2)}) async-start(f32[32,8,128]{2,1,0:T(8,128)} %get-tuple-element.118.sums_ref), calls=%async_computation.1 | async-start | bytes 262144 | tf_op jit(solution)/shard_map/all_to_all | solution.py:1343
  107.8 0.7 copy-start.1
  158.1 2.4 %collective-permute-start.7 = (f32[16,88,128]{2,1,0:T(8,128)}, f32[16,88,128]{2,1,0:T(8,128)S(1)}, u32[]{:S(2)}, u32[]{:S(2)}) collective-permute-start(f32[16,88,128]{2,1,0:T(8,128)} %get-tuple-element.157), channel_id=1, source_target_pairs={{0,1},{1,0},{2,3},{3,2},{4,5},{5,4},{6,7},{7,6},{8,9},{9,8},{10,11... | collective-permute-start | bytes 2162696 | tf_op jit(solution)/shard_map/ppermute | solution.py:1292
  161.7 8.5 %collective-permute-start.10 = (bf16[4,88,128]{2,1,0:T(8,128)(2,1)S(1)}, bf16[4,88,128]{2,1,0:T(8,128)(2,1)S(1)}, u32[]{:S(2)}, u32[]{:S(2)}) collective-permute-start(bf16[4,88,128]{2,1,0:T(8,128)(2,1)S(1)} %get-tuple-element.174), channel_id=1, source_target_pairs={{0,6},{1,7},{2,4},{3,5},{4,2},{5,3},{6,0},{7,1},{8,14},{9,15},{10,... | collective-permute-start | bytes 270344 | tf_op jit(solution)/shard_map/ppermute | solution.py:1292
  163.5 6.7 %collective-permute-start.8 = (bf16[4,88,128]{2,1,0:T(8,128)(2,1)S(1)}, bf16[4,88,128]{2,1,0:T(8,128)(2,1)S(1)}, u32[]{:S(2)}, u32[]{:S(2)}) collective-permute-start(bf16[4,88,128]{2,1,0:T(8,128)(2,1)S(1)} %get-tuple-element.176), channel_id=1, source_target_pairs={{0,2},{1,3},{2,0},{3,1},{4,6},{5,7},{6,4},{7,5},{8,10},{9,11},{10,... | collective-permute-start | bytes 270344 | tf_op jit(solution)/shard_map/ppermute | solution.py:1292
  164.1 6.2 %collective-permute-start.9 = (bf16[4,88,128]{2,1,0:T(8,128)(2,1)S(1)}, bf16[4,88,128]{2,1,0:T(8,128)(2,1)S(1)}, u32[]{:S(2)}, u32[]{:S(2)}) collective-permute-start(bf16[4,88,128]{2,1,0:T(8,128)(2,1)S(1)} %get-tuple-element.175), channel_id=1, source_target_pairs={{0,4},{1,5},{2,6},{3,7},{4,0},{5,1},{6,2},{7,3},{8,12},{9,13},{10,... | collective-permute-start | bytes 270344 | tf_op jit(solution)/shard_map/ppermute | solution.py:1292
  170.3 8.8 %collective-permute-start.11 = (f32[1,88,128]{2,1,0:T(8,128)S(1)}, f32[1,88,128]{2,1,0:T(8,128)S(1)}, u32[]{:S(2)}, u32[]{:S(2)}) collective-permute-start(f32[1,88,128]{2,1,0:T(8,128)S(1)} %get-tuple-element.180), channel_id=1, source_target_pairs={{0,8},{1,9},{2,10},{3,11},{4,12},{5,13},{6,14},{7,15},{8,0},{9,1},... | collective-permute-start | bytes 135176 | tf_op jit(solution)/shard_map/ppermute | solution.py:1292
  171.3 7.9 %collective-permute-start.12 = (f32[1,88,128]{2,1,0:T(8,128)S(1)}, f32[1,88,128]{2,1,0:T(8,128)S(1)}, u32[]{:S(2)}, u32[]{:S(2)}) collective-permute-start(f32[1,88,128]{2,1,0:T(8,128)S(1)} %get-tuple-element.179), channel_id=1, source_target_pairs={{0,16},{1,17},{2,18},{3,19},{4,20},{5,21},{6,22},{7,23},{8,24},{9,... | collective-permute-start | bytes 135176 | tf_op jit(solution)/shard_map/ppermute | solution.py:1292
  173.8 5.9 %copy-start = (f32[10624]{0:T(1024)S(1)}, f32[10624]{0:T(1024)}, u32[]{:S(2)}) copy-start(f32[10624]{0:T(1024)} %param.12) | copy-start | bytes 127492
  173.8 5.9 %copy-start.3 = (f32[10624]{0:T(1024)S(1)}, f32[10624]{0:T(1024)}, u32[]{:S(2)}) copy-start(f32[10624]{0:T(1024)} %param.15) | copy-start | bytes 127492
  173.8 5.9 %copy-start.4 = (f32[10624]{0:T(1024)S(1)}, f32[10624]{0:T(1024)}, u32[]{:S(2)}) copy-start(f32[10624]{0:T(1024)} %param.13) | copy-start | bytes 127492
  173.8 5.9 %copy-start.5 = (f32[10624]{0:T(1024)S(1)}, f32[10624]{0:T(1024)}, u32[]{:S(2)}) copy-start(f32[10624]{0:T(1024)} %param.14) | copy-start | bytes 127492
  173.8 5.9 %collective-permute-start.13 = (f32[1,88,128]{2,1,0:T(8,128)S(1)}, f32[1,88,128]{2,1,0:T(8,128)S(1)}, u32[]{:S(2)}, u32[]{:S(2)}) collective-permute-start(f32[1,88,128]{2,1,0:T(8,128)S(1)} %get-tuple-element.178), channel_id=1, source_target_pairs={{0,24},{1,25},{2,26},{3,27},{4,28},{5,29},{6,30},{7,31},{8,16},{9,... | collective-permute-start | bytes 135176 | tf_op jit(solution)/shard_map/ppermute | solution.py:1292
